TPU v7x, 32 devices: a whole 2x2x4 slice. The times are simulated.
32 devices in a mesh: tm: 8 (over y, x, core), chan: 4 (over z).
Axes of the slice: x: 2, y: 2, z: 4, core: 2. Of those that a mesh axis runs over, the one named last changes fastest.
Arguments:
- record: bfloat16 [8192, 10240], P('tm', 'chan'), may hold values from -6 to 6
- fir_taps: bfloat16 [64], replicated, may hold values from -0.75 to 0.75
- gauge_lag: int32 [10240], P('chan'), may hold values from 1 to 16
- projector: bfloat16 [8192, 128], P('tm'), may hold values from -0.1875 to 0.1875
- compress: float32 [256, 128], replicated, may hold values from -0.5 to 0.5
Outputs:
- sketch: float32 [128, 10240], P('tm', 'chan')
Inputs may be any that keep to these rules, and one draw needn't show every extreme that they name: `gauge_lag`: some channel has lag 16.
All inputs are finite; a program needn't handle non-finite values.
Results may differ from a plain program's by a relative error of at most 0.0028.
Values may be sent and summed in bfloat16 or wider, within the bound.
No kernel may reach another device: no remote copies, remote signals or barrier semaphores. Data moves between devices by JAX's collectives and lax.ppermute only.
A program may use at most 64 MiB of HBM per device.

v0:
```python
import functools

import jax
import jax.numpy as jnp
from jax import lax
from jax.experimental import pallas as pl
from jax.experimental.pallas import tpu as pltpu
from jax.sharding import PartitionSpec as P

TAPS = 64
GAUGE_MAX = 16
K_ITERS = 8
HALO = TAPS + GAUGE_MAX
BLOCK = 128
EXTRA = 16
F32 = jnp.float32
BF16 = jnp.bfloat16
ANY = pl.BlockSpec(memory_space=pl.ANY)
SMEM = pl.BlockSpec(memory_space=pltpu.SMEM)
VMEM = pl.BlockSpec(memory_space=pltpu.VMEM)
PARAMS = pltpu.CompilerParams(vmem_limit_bytes=40 * 2**20)


def dot(a, b):
    return jnp.dot(a, b, preferred_element_type=F32)


def dot_nt(a, b):
    return lax.dot_general(a, b, (((1,), (1,)), ((), ())), preferred_element_type=F32)


def split(a):
    high = a.astype(BF16)
    return high, (a - high.astype(F32)).astype(BF16)


def dot3(a, b):
    ah, al = split(a)
    bh, bl = split(b)
    return dot(ah, bh) + (dot(ah, bl) + dot(al, bh))


def dot3_nt(a, b):
    ah, al = split(a)
    bh, bl = split(b)
    return dot_nt(ah, bh) + (dot_nt(ah, bl) + dot_nt(al, bh))


def eye_mask(n):
    row = lax.broadcasted_iota(jnp.int32, (n, n), 0)
    col = lax.broadcasted_iota(jnp.int32, (n, n), 1)
    return row == col


def front_kernel(record, halo, lag, taps, projector, out, band, proj_t):
    rows = record.shape[0]
    cols = record.shape[1]

    @pl.when(pl.program_id(0) == 0)
    def _():
        line = jnp.broadcast_to(taps[...], (BLOCK, taps.shape[1]))
        rolled = pltpu.roll(line, 0, 1, stride=1, stride_axis=0)
        band[...] = rolled[:, : BLOCK + TAPS].astype(BF16)
        proj_t[...] = projector[...].astype(F32).T.astype(BF16)

    lane = min(128, cols)
    before = dot(band[0:GAUGE_MAX, 0:HALO], halo[...])
    total = jnp.zeros(out.shape, F32)
    for b in range(rows // BLOCK):
        if b == 0:
            segment = jnp.concatenate([halo[GAUGE_MAX:HALO, :], record[0:BLOCK, :]], 0)
        else:
            segment = record[b * BLOCK - TAPS : (b + 1) * BLOCK, :]
        current = dot(band[...], segment)
        parts = []
        for c in range(0, cols, lane):
            span = slice(c, c + lane)
            shift = GAUGE_MAX - lag[:, span]
            here = current[:, span]
            wide = jnp.concatenate([before[:, span], here], 0)
            picked = jnp.where((shift & 8) != 0, wide[8:], wide[:-8])
            for step in (4, 2, 1):
                moved = pltpu.roll(picked, picked.shape[0] - step, 0)
                picked = jnp.where((shift & step) != 0, moved, picked)
            parts.append((here - picked[:BLOCK]).astype(BF16))
        strain = jnp.concatenate(parts, 1) if len(parts) > 1 else parts[0]
        total = total + dot(proj_t[:, b * BLOCK : (b + 1) * BLOCK], strain)
        before = current[BLOCK - GAUGE_MAX :]
    out[...] = total.astype(BF16)


def front(record, halo, lag, taps, projector):
    rows, cols = record.shape
    rank = projector.shape[1]
    tile = next((t for t in (512, 640, 256, 128) if cols % t == 0), cols)
    whole = lambda a: pl.BlockSpec(a.shape, lambda i: (0, 0))
    return pl.pallas_call(
        front_kernel,
        grid=(cols // tile,),
        in_specs=[
            pl.BlockSpec((rows, tile), lambda i: (0, i)),
            pl.BlockSpec((HALO, tile), lambda i: (0, i)),
            pl.BlockSpec((1, tile), lambda i: (0, i)),
            whole(taps),
            whole(projector),
        ],
        out_specs=pl.BlockSpec((rank, tile), lambda i: (0, i)),
        out_shape=jax.ShapeDtypeStruct((rank, cols), BF16),
        scratch_shapes=[
            pltpu.VMEM((BLOCK, BLOCK + TAPS), BF16),
            pltpu.VMEM((rank, rows), BF16),
        ],
        compiler_params=PARAMS,
        name="front",
    )(record, halo, lag, taps, projector)


def pair_kernel(own, other, out):
    rank = own.shape[0]
    a, b = own[...], other[...]
    aa, ab, bb = dot_nt(a, a), dot_nt(a, b), dot_nt(b, b)
    diag = eye_mask(rank)
    trace = jnp.sum(jnp.where(diag, aa + bb, 0.0), axis=(0, 1), keepdims=True)
    mean = trace / (2 * rank)
    aa = aa - jnp.where(diag, mean, 0.0)
    bb = bb - jnp.where(diag, mean, 0.0)
    row = lax.broadcasted_iota(jnp.int32, (rank, rank), 0)
    col = lax.broadcasted_iota(jnp.int32, (rank, rank), 1)
    out[0:rank, :] = jnp.where(row <= col, aa, bb).astype(BF16)
    out[rank : 2 * rank, :] = ab.astype(BF16)
    bottom = jnp.sum(jnp.where(diag, bb, 0.0), axis=0, keepdims=True)
    full = jnp.broadcast_to(mean, (EXTRA, rank))
    high = full.astype(BF16).astype(F32)
    mid = (full - high).astype(BF16).astype(F32)
    low = full - high - mid
    line = lax.broadcasted_iota(jnp.int32, (EXTRA, rank), 0)
    extra = jnp.where(line == 0, high, jnp.where(line == 1, mid, jnp.where(line == 2, low, 0.0)))
    out[2 * rank :, :] = jnp.where(line == 3, jnp.broadcast_to(bottom, (EXTRA, rank)), extra).astype(
        BF16
    )


def pair_gram(own, other):
    rank = own.shape[0]
    return pl.pallas_call(
        pair_kernel,
        out_shape=jax.ShapeDtypeStruct((2 * rank + EXTRA, rank), BF16),
        compiler_params=PARAMS,
        name="pair_gram",
    )(own, other)


def cross_kernel(own, other, out):
    out[...] = dot_nt(own[...], other[...]).astype(out.dtype)


def cross_gram(own, other):
    return pl.pallas_call(
        cross_kernel,
        out_shape=jax.ShapeDtypeStruct((own.shape[0], other.shape[0]), BF16),
        compiler_params=PARAMS,
        name="cross_gram",
    )(own, other)


def summed(parts):
    total = parts[0][...].astype(F32)
    for part in parts[1:]:
        total = total + part[...].astype(F32)
    return total


def square_of(aa, ab, bb):
    return jnp.concatenate(
        [jnp.concatenate([aa, ab], 1), jnp.concatenate([ab.T, bb], 1)], 0
    )


def first_gram(parts):
    total = summed(parts)
    rank = total.shape[1]
    both = total[0:rank]
    ab = total[rank : 2 * rank]
    extra = total[2 * rank :]
    mean = extra[0:1, 0:1] + extra[1:2, 0:1] + extra[2:3, 0:1]
    row = lax.broadcasted_iota(jnp.int32, (rank, rank), 0)
    col = lax.broadcasted_iota(jnp.int32, (rank, rank), 1)
    turned = both.T
    aa = jnp.where(row <= col, both, turned)
    bb = jnp.where(row > col, both, jnp.where(row < col, turned, extra[3:4, :]))
    return square_of(aa, ab, bb), mean


def later_gram(parts, own_level, other_level):
    gram = square_of(own_level[...], summed(parts), other_level[...])
    diag = eye_mask(gram.shape[0])
    mean = jnp.sum(jnp.where(diag, gram, 0.0), axis=(0, 1), keepdims=True) / gram.shape[0]
    return gram - jnp.where(diag, mean, 0.0), mean


def filter_kernel(count, first, last, *refs):
    parts, refs = refs[:count], refs[count:]
    if first:
        levels = ()
    else:
        levels, refs = refs[:2], refs[2:]
    compress_t, offset, own, other, refs = *refs[:4], refs[4:]
    if last:
        sketch, pair, sems = refs
    else:
        sketch, level, pair, sems = refs
    rank, width = own.shape[0], pair.shape[1]
    start = pl.multiple_of(offset[0], 128) if width % 128 == 0 else 0
    copies = [
        pltpu.make_async_copy(
            source.at[:, pl.ds(start, width)] if width < own.shape[1] else source,
            pair.at[slice(i * rank, (i + 1) * rank)],
            sems.at[i],
        )
        for i, source in enumerate((own, other))
    ]
    for copy in copies:
        copy.start()
    gram, mean = first_gram(parts) if first else later_gram(parts, *levels)
    size = gram.shape[0]
    eye = jnp.where(eye_mask(size), 1.0, 0.0)
    z = gram * lax.rsqrt(jnp.sum(gram * gram, axis=(0, 1), keepdims=True) + 1e-6)
    for _ in range(K_ITERS):
        zh, zl = split(z)
        square = dot(zh, zh) + (dot(zh, zl) + dot(zl, zh))
        ph, low = split(1.5 * eye - 0.5 * square)
        z = dot(zh, ph) + (dot(zh, low) + dot(zl, ph))
    mixing = dot3(compress_t[...], 0.5 * (eye + z))
    for copy in copies:
        copy.wait()
    high, low = split(mixing)
    both = jnp.concatenate([high, low], 0)
    rows = mixing.shape[0]
    tile = next((t for t in (640, 512, 256, 128) if width % t == 0), width)
    for c in range(0, width, tile):
        wide = dot(both, pair[:, c : c + tile])
        sketch[:, c : c + tile] = (wide[:rows] + wide[rows:]).astype(sketch.dtype)
    if not last:
        level[...] = dot3_nt(dot3(mixing, gram + mean * eye), mixing)


def filter_call(parts, levels, compress_t, offset, own, other, width, first, last):
    rank = own.shape[0]
    rows = compress_t.shape[0]
    out = [jax.ShapeDtypeStruct((rows, width), F32 if last else BF16)]
    if not last:
        out.append(jax.ShapeDtypeStruct((rank, rank), F32))
    args = [*parts, *levels, compress_t]
    return pl.pallas_call(
        functools.partial(filter_kernel, len(parts), first, last),
        in_specs=[VMEM] * len(args) + [SMEM, ANY, ANY],
        out_shape=out,
        scratch_shapes=[pltpu.VMEM((2 * rank, width), BF16), pltpu.SemaphoreType.DMA((2,))],
        compiler_params=PARAMS,
        name="sign_filter",
    )(*args, offset, own, other)


def swap(value, axis, mask):
    count = lax.axis_size(axis)
    return lax.ppermute(value, axis, [(source, source ^ mask) for source in range(count)])


def gather_parts(value, axis):
    count = lax.axis_size(axis)
    if count > 4 or count & (count - 1):
        return [lax.psum(value.astype(F32), axis)]
    return [value] + [swap(value, axis, mask) for mask in range(1, count)]


def join_kernel(offsets, *refs):
    out = refs[-1]
    width = refs[0].shape[1]
    for i, piece in enumerate(refs[:-1]):
        out[:, pl.ds(pl.multiple_of(offsets[i], 128), width)] = piece[...]


def join(offsets, pieces):
    share, width = pieces[0].shape
    return pl.pallas_call(
        join_kernel,
        in_specs=[SMEM] + [VMEM] * len(pieces),
        out_shape=jax.ShapeDtypeStruct((share, width * len(pieces)), F32),
        name="join",
    )(offsets, *pieces)


def on_device(record, fir_taps, gauge_lag, projector, compress):
    rows, cols = record.shape
    rank = projector.shape[1]
    count = lax.axis_size("tm")
    position = lax.axis_index("tm")
    depths = count.bit_length() - 1
    share = rank // count
    halo = lax.ppermute(
        record[rows - HALO :], "tm", [(source, source + 1) for source in range(count - 1)]
    )
    taps = jnp.pad(fir_taps.astype(F32)[::-1], (1, 2 * BLOCK - TAPS - 1))[None, :]
    sketch = front(record, halo, gauge_lag[None, :], taps, projector)

    widths = []
    width = cols
    for depth in range(1, depths):
        if width % 256 == 0:
            width //= 2
        widths.append(width)
    narrowed = [depth for depth in range(depths - 1) if widths[depth] < ([cols] + widths)[depth]]
    assert narrowed == list(range(len(narrowed)))
    span = 2 ** len(narrowed)

    def bit_of(where, bit):
        return where // 2**bit % 2

    compress_t = compress.T
    flipped = jnp.concatenate([compress_t[:, rank:], compress_t[:, :rank]], 1)

    level = None
    for depth in range(depths):
        first, last = depth == 0, depth == depths - 1
        mask = 2**depth
        weights = jnp.where(bit_of(position, depth) == 0, compress_t, flipped)
        if last:
            weights = jnp.concatenate(
                [
                    lax.dynamic_slice_in_dim(weights, (position ^ part) * share, share, 0)
                    for part in range(span)
                ],
                0,
            )
        here = sketch.shape[1]
        narrow = not last and widths[depth] < here
        offset = bit_of(position, depth) * (here // 2) if narrow else jnp.int32(0)
        offset = jnp.reshape(offset, (1,)).astype(jnp.int32)
        other = swap(sketch, "tm", mask)
        if first:
            parts = gather_parts(pair_gram(sketch, other), "chan")
            levels = []
        else:
            levels = [level, swap(level, "tm", mask)]
            part = cross_gram(sketch, other)
            for bit in [b for b in narrowed if b < depth]:
                part = (part.astype(F32) + swap(part, "tm", 2**bit).astype(F32)).astype(BF16)
            parts = gather_parts(part, "chan")
        results = filter_call(
            parts, levels, weights, offset, sketch, other, here if last else widths[depth], first, last
        )
        sketch = results[0]
        level = None if last else results[1]
    if span == 1:
        return sketch
    width = sketch.shape[1]
    pieces = [sketch[:share]] + [
        swap(sketch[part * share : (part + 1) * share], "tm", part) for part in range(1, span)
    ]
    offsets = []
    for part in range(span):
        source = position ^ part
        offsets.append(sum(bit_of(source, bit) * (cols >> (bit + 1)) for bit in narrowed))
    return join(jnp.stack(offsets).astype(jnp.int32), pieces)


def solution(mesh):
    return jax.shard_map(
        on_device,
        mesh=mesh,
        in_specs=(P("tm", "chan"), P(), P("chan"), P("tm", None), P()),
        out_specs=P("tm", "chan"),
        check_vma=False,
    )
```

profile of v0, /device:TPU:0, one launch (start us, length us, event | category | flops | bytes accessed | tf_op | source)
XLA Modules:
  0.0 104.2 jit_solution(2816202801261058985)
XLA Ops:
  0.0 1.1 %slice.21 = bf16[80,2560]{1,0:T(8,128)(2,1)S(1)} slice(bf16[1024,2560]{1,0:T(8,128)(2,1)} %record.1), slice={[944:1024], [0:2560]} | slice | bytes 819200 | tf_op jit(solution)/shard_map/slice | solution.py:301
  1.1 2.4 %collective-permute-start = (bf16[80,2560]{1,0:T(8,128)(2,1)S(1)}, bf16[80,2560]{1,0:T(8,128)(2,1)S(1)}, u32[]{:S(2)}, u32[]{:S(2)}) collective-permute-start(bf16[80,2560]{1,0:T(8,128)(2,1)S(1)} %slice.21), channel_id=1, source_target_pairs={{0,4},{4,8},{8,12},{12,16},{16,20},{20,24},{24,28},{1,5},{5,9},{9,... | collective-permute-start | bytes 1228808 | tf_op jit(solution)/shard_map/ppermute | solution.py:300
  5.0 2.5 %copy-done = bf16[1024,2560]{1,0:T(8,128)(2,1)S(1)} copy-done((bf16[1024,2560]{1,0:T(8,128)(2,1)S(1)}, bf16[1024,2560]{1,0:T(8,128)(2,1)}, u32[]{:S(2)}) %copy-start) | copy-done | bytes 5242904
  8.4 12.6 %front.1.own.refs_6_ = bf16[128,2560]{1,0:T(8,128)(2,1)S(1)} custom-call(bf16[1024,2560]{1,0:T(8,128)(2,1)S(1)} %copy-done, bf16[80,2560]{1,0:T(8,128)(2,1)S(1)} %collective-permute-done.halo, s32[1,2560]{1,0:T(1,128)S(1)} %broadcast_in_dim.6.lag, f32[1,256]{1,0:T(1,128)S(1)} %bitcast.11, bf16[1024,128]{1,0:T(8,128)(2,1)S(1)} %copy-done.1), custom_call_target="tpu_custom_call" | custom-call | tf_op jit(solution)/shard_map/front/pallas_call | solution.py:97
  21.0 6.0 %collective-permute-start.1 = (bf16[128,2560]{1,0:T(8,128)(2,1)S(1)}, bf16[128,2560]{1,0:T(8,128)(2,1)S(1)}, u32[]{:S(2)}, u32[]{:S(2)}) collective-permute-start(bf16[128,2560]{1,0:T(8,128)(2,1)S(1)} %front.1.own.refs_6_), channel_id=1, source_target_pairs={{0,4},{4,0},{8,12},{12,8},{16,20},{20,16},{24,28},{28,24},{1,5},{5... | collective-permute-start | bytes 1966088 | tf_op jit(solution)/shard_map/ppermute | solution.py:266
  27.1 1.6 %collective-permute-done.1.other.refs_7_ = bf16[128,2560]{1,0:T(8,128)(2,1)S(1)} collective-permute-done((bf16[128,2560]{1,0:T(8,128)(2,1)S(1)}, bf16[128,2560]{1,0:T(8,128)(2,1)S(1)}, u32[]{:S(2)}, u32[]{:S(2)}) %collective-permute-start.1) | collective-permute-done | bytes 655392 | tf_op jit(solution)/shard_map/ppermute | solution.py:266
  29.5 3.7 %collective-permute-start.4 = (bf16[272,128]{1,0:T(8,128)(2,1)S(1)}, bf16[272,128]{1,0:T(8,128)(2,1)S(1)}, u32[]{:S(2)}, u32[]{:S(2)}) collective-permute-start(bf16[272,128]{1,0:T(8,128)(2,1)S(1)} %pair_gram.1.refs_0_), channel_id=1, source_target_pairs={{0,3},{1,2},{2,1},{3,0},{4,7},{5,6},{6,5},{7,4},{8,11},{9,10},{10,... | collective-permute-start | bytes 208904 | tf_op jit(solution)/shard_map/ppermute | solution.py:266
  34.0 2.2 %collective-permute-done.4.refs_3_ = bf16[272,128]{1,0:T(8,128)(2,1)S(1)} collective-permute-done((bf16[272,128]{1,0:T(8,128)(2,1)S(1)}, bf16[272,128]{1,0:T(8,128)(2,1)S(1)}, u32[]{:S(2)}, u32[]{:S(2)}) %collective-permute-start.4) | collective-permute-done | bytes 69664 | tf_op jit(solution)/shard_map/ppermute | solution.py:266
  36.3 3.3 %collective-permute-done.3.refs_2_ = bf16[272,128]{1,0:T(8,128)(2,1)S(1)} collective-permute-done((bf16[272,128]{1,0:T(8,128)(2,1)S(1)}, bf16[272,128]{1,0:T(8,128)(2,1)S(1)}, u32[]{:S(2)}, u32[]{:S(2)}) %collective-permute-start.3) | collective-permute-done | bytes 69664 | tf_op jit(solution)/shard_map/ppermute | solution.py:266
  39.5 6.3 %sign_filter.3 = (bf16[128,1280]{1,0:T(8,128)(2,1)S(1)}, f32[128,128]{1,0:T(8,128)S(1)}) custom-call(bf16[272,128]{1,0:T(8,128)(2,1)S(1)} %pair_gram.1.refs_0_, bf16[272,128]{1,0:T(8,128)(2,1)S(1)} %collective-permute-done.2.refs_1_, bf16[272,128]{1,0:T(8,128)(2,1)S(1)} %collective-permute-done.3.refs_2_, ...), custom_call_target="tpu_custom_call" | custom-call | tf_op jit(solution)/shard_map/sign_filter/pallas_call | solution.py:254
  45.9 2.7 %collective-permute-start.5 = (bf16[128,1280]{1,0:T(8,128)(2,1)S(1)}, bf16[128,1280]{1,0:T(8,128)(2,1)S(1)}, u32[]{:S(2)}, u32[]{:S(2)}) collective-permute-start(bf16[128,1280]{1,0:T(8,128)(2,1)S(1)} %get-tuple-element.9.own.refs_8_), channel_id=1, source_target_pairs={{0,8},{4,12},{8,0},{12,4},{16,24},{20,28},{24,16},{28,20},{1,9},{5... | collective-permute-start | bytes 983048 | tf_op jit(solution)/shard_map/ppermute | solution.py:266
  48.6 7.4 %collective-permute-done.5.other.refs_9_ = bf16[128,1280]{1,0:T(8,128)(2,1)S(1)} collective-permute-done((bf16[128,1280]{1,0:T(8,128)(2,1)S(1)}, bf16[128,1280]{1,0:T(8,128)(2,1)S(1)}, u32[]{:S(2)}, u32[]{:S(2)}) %collective-permute-start.5) | collective-permute-done | bytes 327712 | tf_op jit(solution)/shard_map/ppermute | solution.py:266
  56.2 1.8 %collective-permute-start.10 = (f32[128,128]{1,0:T(8,128)S(1)}, f32[128,128]{1,0:T(8,128)S(1)}, u32[]{:S(2)}, u32[]{:S(2)}) collective-permute-start(f32[128,128]{1,0:T(8,128)S(1)} %get-tuple-element.10.refs_4_), channel_id=1, source_target_pairs={{0,8},{4,12},{8,0},{12,4},{16,24},{20,28},{24,16},{28,20},{1,9},{5... | collective-permute-start | bytes 196616 | tf_op jit(solution)/shard_map/ppermute | solution.py:266
  58.1 2.5 %collective-permute-start.9 = (bf16[128,128]{1,0:T(8,128)(2,1)S(1)}, bf16[128,128]{1,0:T(8,128)(2,1)S(1)}, u32[]{:S(2)}, u32[]{:S(2)}) collective-permute-start(bf16[128,128]{1,0:T(8,128)(2,1)S(1)} %add_convert_fusion.2.refs_0_), channel_id=1, source_target_pairs={{0,3},{1,2},{2,1},{3,0},{4,7},{5,6},{6,5},{7,4},{8,11},{9,10},{10,... | collective-permute-start | bytes 98312 | tf_op jit(solution)/shard_map/ppermute | solution.py:266
  60.5 2.0 %collective-permute-start.7 = (bf16[128,128]{1,0:T(8,128)(2,1)S(1)}, bf16[128,128]{1,0:T(8,128)(2,1)S(1)}, u32[]{:S(2)}, u32[]{:S(2)}) collective-permute-start(bf16[128,128]{1,0:T(8,128)(2,1)S(1)} %add_convert_fusion.2.refs_0_), channel_id=1, source_target_pairs={{0,1},{1,0},{2,3},{3,2},{4,5},{5,4},{6,7},{7,6},{8,9},{9,8},{10,11... | collective-permute-start | bytes 98312 | tf_op jit(solution)/shard_map/ppermute | solution.py:266
  62.5 1.3 %collective-permute-done.9.refs_3_ = bf16[128,128]{1,0:T(8,128)(2,1)S(1)} collective-permute-done((bf16[128,128]{1,0:T(8,128)(2,1)S(1)}, bf16[128,128]{1,0:T(8,128)(2,1)S(1)}, u32[]{:S(2)}, u32[]{:S(2)}) %collective-permute-start.9) | collective-permute-done | bytes 32800 | tf_op jit(solution)/shard_map/ppermute | solution.py:266
  63.9 1.5 %collective-permute-done.8.refs_2_ = bf16[128,128]{1,0:T(8,128)(2,1)S(1)} collective-permute-done((bf16[128,128]{1,0:T(8,128)(2,1)S(1)}, bf16[128,128]{1,0:T(8,128)(2,1)S(1)}, u32[]{:S(2)}, u32[]{:S(2)}) %collective-permute-start.8) | collective-permute-done | bytes 32800 | tf_op jit(solution)/shard_map/ppermute | solution.py:266
  65.4 6.3 %sign_filter.4 = (bf16[128,640]{1,0:T(8,128)(2,1)S(1)}, f32[128,128]{1,0:T(8,128)S(1)}) custom-call(bf16[128,128]{1,0:T(8,128)(2,1)S(1)} %add_convert_fusion.2.refs_0_, bf16[128,128]{1,0:T(8,128)(2,1)S(1)} %collective-permute-done.7.refs_1_, bf16[128,128]{1,0:T(8,128)(2,1)S(1)} %collective-permute-done.8.refs_2_, ...), custom_call_target="tpu_custom_call" | custom-call | tf_op jit(solution)/shard_map/sign_filter/pallas_call | solution.py:254
  71.7 2.1 %collective-permute-start.11 = (bf16[128,640]{1,0:T(8,128)(2,1)S(1)}, bf16[128,640]{1,0:T(8,128)(2,1)S(1)}, u32[]{:S(2)}, u32[]{:S(2)}) collective-permute-start(bf16[128,640]{1,0:T(8,128)(2,1)S(1)} %get-tuple-element.11.own.refs_8_), channel_id=1, source_target_pairs={{0,16},{4,20},{8,24},{12,28},{16,0},{20,4},{24,8},{28,12},{1,17},{... | collective-permute-start | bytes 491528 | tf_op jit(solution)/shard_map/ppermute | solution.py:266
  73.9 3.5 %collective-permute-done.11.other.refs_9_ = bf16[128,640]{1,0:T(8,128)(2,1)S(1)} collective-permute-done((bf16[128,640]{1,0:T(8,128)(2,1)S(1)}, bf16[128,640]{1,0:T(8,128)(2,1)S(1)}, u32[]{:S(2)}, u32[]{:S(2)}) %collective-permute-start.11) | collective-permute-done | bytes 163872 | tf_op jit(solution)/shard_map/ppermute | solution.py:266
  77.6 1.2 %collective-permute-done.12 = bf16[128,128]{1,0:T(8,128)(2,1)S(1)} collective-permute-done((bf16[128,128]{1,0:T(8,128)(2,1)S(1)}, bf16[128,128]{1,0:T(8,128)(2,1)S(1)}, u32[]{:S(2)}, u32[]{:S(2)}) %collective-permute-start.12) | collective-permute-done | bytes 32800 | tf_op jit(solution)/shard_map/ppermute | solution.py:266
  78.8 1.0 collective-permute-start.13
  79.8 1.8 %collective-permute-start.17 = (f32[128,128]{1,0:T(8,128)S(1)}, f32[128,128]{1,0:T(8,128)S(1)}, u32[]{:S(2)}, u32[]{:S(2)}) collective-permute-start(f32[128,128]{1,0:T(8,128)S(1)} %get-tuple-element.12.refs_4_), channel_id=1, source_target_pairs={{0,16},{4,20},{8,24},{12,28},{16,0},{20,4},{24,8},{28,12},{1,17},{... | collective-permute-start | bytes 196616 | tf_op jit(solution)/shard_map/ppermute | solution.py:266
  81.6 1.2 %collective-permute-done.13 = bf16[128,128]{1,0:T(8,128)(2,1)S(1)} collective-permute-done((bf16[128,128]{1,0:T(8,128)(2,1)S(1)}, bf16[128,128]{1,0:T(8,128)(2,1)S(1)}, u32[]{:S(2)}, u32[]{:S(2)}) %collective-permute-start.13) | collective-permute-done | bytes 32800 | tf_op jit(solution)/shard_map/ppermute | solution.py:266
  82.8 2.8 %collective-permute-start.16 = (bf16[128,128]{1,0:T(8,128)(2,1)S(1)}, bf16[128,128]{1,0:T(8,128)(2,1)S(1)}, u32[]{:S(2)}, u32[]{:S(2)}) collective-permute-start(bf16[128,128]{1,0:T(8,128)(2,1)S(1)} %add_convert_fusion.refs_0_), channel_id=1, source_target_pairs={{0,3},{1,2},{2,1},{3,0},{4,7},{5,6},{6,5},{7,4},{8,11},{9,10},{10,... | collective-permute-start | bytes 98312 | tf_op jit(solution)/shard_map/ppermute | solution.py:266
  85.6 1.6 %collective-permute-start.14 = (bf16[128,128]{1,0:T(8,128)(2,1)S(1)}, bf16[128,128]{1,0:T(8,128)(2,1)S(1)}, u32[]{:S(2)}, u32[]{:S(2)}) collective-permute-start(bf16[128,128]{1,0:T(8,128)(2,1)S(1)} %add_convert_fusion.refs_0_), channel_id=1, source_target_pairs={{0,1},{1,0},{2,3},{3,2},{4,5},{5,4},{6,7},{7,6},{8,9},{9,8},{10,11... | collective-permute-start | bytes 98312 | tf_op jit(solution)/shard_map/ppermute | solution.py:266
  87.3 1.3 %collective-permute-done.16.refs_3_ = bf16[128,128]{1,0:T(8,128)(2,1)S(1)} collective-permute-done((bf16[128,128]{1,0:T(8,128)(2,1)S(1)}, bf16[128,128]{1,0:T(8,128)(2,1)S(1)}, u32[]{:S(2)}, u32[]{:S(2)}) %collective-permute-start.16) | collective-permute-done | bytes 32800 | tf_op jit(solution)/shard_map/ppermute | solution.py:266
  88.6 1.8 %collective-permute-done.15.refs_2_ = bf16[128,128]{1,0:T(8,128)(2,1)S(1)} collective-permute-done((bf16[128,128]{1,0:T(8,128)(2,1)S(1)}, bf16[128,128]{1,0:T(8,128)(2,1)S(1)}, u32[]{:S(2)}, u32[]{:S(2)}) %collective-permute-start.15) | collective-permute-done | bytes 32800 | tf_op jit(solution)/shard_map/ppermute | solution.py:266
  90.4 6.6 %sign_filter.5 = f32[64,640]{1,0:T(8,128)S(1)} custom-call(bf16[128,128]{1,0:T(8,128)(2,1)S(1)} %add_convert_fusion.refs_0_, bf16[128,128]{1,0:T(8,128)(2,1)S(1)} %collective-permute-done.14.refs_1_, bf16[128,128]{1,0:T(8,128)(2,1)S(1)} %collective-permute-done.15.refs_2_, bf16[128,128]{1,0:T(8,128)(2,1)S(1)} %collective-permute-done.16.refs_3_, ...), custom_call_target="tpu_custom_call" | custom-call | tf_op jit(solution)/shard_map/sign_filter/pallas_call | solution.py:254
  100.1 1.0 collective-permute-done.20.refs_3_
  101.1 1.0 collective-permute-done.19.refs_2_
  102.7 1.5 %join.1 = f32[16,2560]{1,0:T(8,128)} custom-call(s32[4]{0:T(128)} %pad_add_fusion.offsets, f32[16,640]{1,0:T(8,128)} %get-tuple-element.19.refs_0_, f32[16,640]{1,0:T(8,128)} %copy-done.5, f32[16,640]{1,0:T(8,128)} %copy-done.4, f32[16,640]{1,0:T(8,128)} %copy-done.3), custom_call_target="tpu_custom_call" | custom-call | tf_op jit(solution)/shard_map/join/pallas_call | solution.py:285
  (44 shorter events, 8.6 us)
Async XLA Ops:
  0.0 27.0 %copy-start.2 = (f32[256,128]{1,0:T(8,128)S(1)}, f32[256,128]{1,0:T(8,128)}, u32[]{:S(2)}) copy-start(f32[256,128]{1,0:T(8,128)} %param.9) | copy-start | bytes 393220
  1.1 3.9 %collective-permute-start = (bf16[80,2560]{1,0:T(8,128)(2,1)S(1)}, bf16[80,2560]{1,0:T(8,128)(2,1)S(1)}, u32[]{:S(2)}, u32[]{:S(2)}) collective-permute-start(bf16[80,2560]{1,0:T(8,128)(2,1)S(1)} %slice.21), channel_id=1, source_target_pairs={{0,4},{4,8},{8,12},{12,16},{16,20},{20,24},{24,28},{1,5},{5,9},{9,... | collective-permute-start | bytes 1228808 | tf_op jit(solution)/shard_map/ppermute | solution.py:300
  5.0 2.5 %copy-start = (bf16[1024,2560]{1,0:T(8,128)(2,1)S(1)}, bf16[1024,2560]{1,0:T(8,128)(2,1)}, u32[]{:S(2)}) copy-start(bf16[1024,2560]{1,0:T(8,128)(2,1)} %record.1) | copy-start | bytes 15728644
  7.5 0.9 copy-start.1
  21.0 7.7 %collective-permute-start.1 = (bf16[128,2560]{1,0:T(8,128)(2,1)S(1)}, bf16[128,2560]{1,0:T(8,128)(2,1)S(1)}, u32[]{:S(2)}, u32[]{:S(2)}) collective-permute-start(bf16[128,2560]{1,0:T(8,128)(2,1)S(1)} %front.1.own.refs_6_), channel_id=1, source_target_pairs={{0,4},{4,0},{8,12},{12,8},{16,20},{20,16},{24,28},{28,24},{1,5},{5... | collective-permute-start | bytes 1966088 | tf_op jit(solution)/shard_map/ppermute | solution.py:266
  29.5 6.7 %collective-permute-start.4 = (bf16[272,128]{1,0:T(8,128)(2,1)S(1)}, bf16[272,128]{1,0:T(8,128)(2,1)S(1)}, u32[]{:S(2)}, u32[]{:S(2)}) collective-permute-start(bf16[272,128]{1,0:T(8,128)(2,1)S(1)} %pair_gram.1.refs_0_), channel_id=1, source_target_pairs={{0,3},{1,2},{2,1},{3,0},{4,7},{5,6},{6,5},{7,4},{8,11},{9,10},{10,... | collective-permute-start | bytes 208904 | tf_op jit(solution)/shard_map/ppermute | solution.py:266
  33.2 6.3 %collective-permute-start.3 = (bf16[272,128]{1,0:T(8,128)(2,1)S(1)}, bf16[272,128]{1,0:T(8,128)(2,1)S(1)}, u32[]{:S(2)}, u32[]{:S(2)}) collective-permute-start(bf16[272,128]{1,0:T(8,128)(2,1)S(1)} %pair_gram.1.refs_0_), channel_id=1, source_target_pairs={{0,2},{1,3},{2,0},{3,1},{4,6},{5,7},{6,4},{7,5},{8,10},{9,11},{10,... | collective-permute-start | bytes 208904 | tf_op jit(solution)/shard_map/ppermute | solution.py:266
  33.2 6.3 %collective-permute-start.2 = (bf16[272,128]{1,0:T(8,128)(2,1)S(1)}, bf16[272,128]{1,0:T(8,128)(2,1)S(1)}, u32[]{:S(2)}, u32[]{:S(2)}) collective-permute-start(bf16[272,128]{1,0:T(8,128)(2,1)S(1)} %pair_gram.1.refs_0_), channel_id=1, source_target_pairs={{0,1},{1,0},{2,3},{3,2},{4,5},{5,4},{6,7},{7,6},{8,9},{9,8},{10,11... | collective-permute-start | bytes 208904 | tf_op jit(solution)/shard_map/ppermute | solution.py:266
  45.9 10.0 %collective-permute-start.5 = (bf16[128,1280]{1,0:T(8,128)(2,1)S(1)}, bf16[128,1280]{1,0:T(8,128)(2,1)S(1)}, u32[]{:S(2)}, u32[]{:S(2)}) collective-permute-start(bf16[128,1280]{1,0:T(8,128)(2,1)S(1)} %get-tuple-element.9.own.refs_8_), channel_id=1, source_target_pairs={{0,8},{4,12},{8,0},{12,4},{16,24},{20,28},{24,16},{28,20},{1,9},{5... | collective-permute-start | bytes 983048 | tf_op jit(solution)/shard_map/ppermute | solution.py:266
  56.2 1.9 %collective-permute-start.6 = (bf16[128,128]{1,0:T(8,128)(2,1)S(1)}, bf16[128,128]{1,0:T(8,128)(2,1)S(1)}, u32[]{:S(2)}, u32[]{:S(2)}) collective-permute-start(bf16[128,128]{1,0:T(8,128)(2,1)S(1)} %cross_gram.2), channel_id=1, source_target_pairs={{0,4},{4,0},{8,12},{12,8},{16,20},{20,16},{24,28},{28,24},{1,5},{5... | collective-permute-start | bytes 98312 | tf_op jit(solution)/shard_map/ppermute | solution.py:266
  56.2 6.3 %collective-permute-start.10 = (f32[128,128]{1,0:T(8,128)S(1)}, f32[128,128]{1,0:T(8,128)S(1)}, u32[]{:S(2)}, u32[]{:S(2)}) collective-permute-start(f32[128,128]{1,0:T(8,128)S(1)} %get-tuple-element.10.refs_4_), channel_id=1, source_target_pairs={{0,8},{4,12},{8,0},{12,4},{16,24},{20,28},{24,16},{28,20},{1,9},{5... | collective-permute-start | bytes 196616 | tf_op jit(solution)/shard_map/ppermute | solution.py:266
  58.1 5.8 %collective-permute-start.9 = (bf16[128,128]{1,0:T(8,128)(2,1)S(1)}, bf16[128,128]{1,0:T(8,128)(2,1)S(1)}, u32[]{:S(2)}, u32[]{:S(2)}) collective-permute-start(bf16[128,128]{1,0:T(8,128)(2,1)S(1)} %add_convert_fusion.2.refs_0_), channel_id=1, source_target_pairs={{0,3},{1,2},{2,1},{3,0},{4,7},{5,6},{6,5},{7,4},{8,11},{9,10},{10,... | collective-permute-start | bytes 98312 | tf_op jit(solution)/shard_map/ppermute | solution.py:266
  60.5 4.8 %collective-permute-start.8 = (bf16[128,128]{1,0:T(8,128)(2,1)S(1)}, bf16[128,128]{1,0:T(8,128)(2,1)S(1)}, u32[]{:S(2)}, u32[]{:S(2)}) collective-permute-start(bf16[128,128]{1,0:T(8,128)(2,1)S(1)} %add_convert_fusion.2.refs_0_), channel_id=1, source_target_pairs={{0,2},{1,3},{2,0},{3,1},{4,6},{5,7},{6,4},{7,5},{8,10},{9,11},{10,... | collective-permute-start | bytes 98312 | tf_op jit(solution)/shard_map/ppermute | solution.py:266
  60.5 4.8 %collective-permute-start.7 = (bf16[128,128]{1,0:T(8,128)(2,1)S(1)}, bf16[128,128]{1,0:T(8,128)(2,1)S(1)}, u32[]{:S(2)}, u32[]{:S(2)}) collective-permute-start(bf16[128,128]{1,0:T(8,128)(2,1)S(1)} %add_convert_fusion.2.refs_0_), channel_id=1, source_target_pairs={{0,1},{1,0},{2,3},{3,2},{4,5},{5,4},{6,7},{7,6},{8,9},{9,8},{10,11... | collective-permute-start | bytes 98312 | tf_op jit(solution)/shard_map/ppermute | solution.py:266
  71.7 5.6 %collective-permute-start.11 = (bf16[128,640]{1,0:T(8,128)(2,1)S(1)}, bf16[128,640]{1,0:T(8,128)(2,1)S(1)}, u32[]{:S(2)}, u32[]{:S(2)}) collective-permute-start(bf16[128,640]{1,0:T(8,128)(2,1)S(1)} %get-tuple-element.11.own.refs_8_), channel_id=1, source_target_pairs={{0,16},{4,20},{8,24},{12,28},{16,0},{20,4},{24,8},{28,12},{1,17},{... | collective-permute-start | bytes 491528 | tf_op jit(solution)/shard_map/ppermute | solution.py:266
  77.5 1.3 %collective-permute-start.12 = (bf16[128,128]{1,0:T(8,128)(2,1)S(1)}, bf16[128,128]{1,0:T(8,128)(2,1)S(1)}, u32[]{:S(2)}, u32[]{:S(2)}) collective-permute-start(bf16[128,128]{1,0:T(8,128)(2,1)S(1)} %cross_gram.3), channel_id=1, source_target_pairs={{0,4},{4,0},{8,12},{12,8},{16,20},{20,16},{24,28},{28,24},{1,5},{5... | collective-permute-start | bytes 98312 | tf_op jit(solution)/shard_map/ppermute | solution.py:266
  78.8 4.0 %collective-permute-start.13 = (bf16[128,128]{1,0:T(8,128)(2,1)S(1)}, bf16[128,128]{1,0:T(8,128)(2,1)S(1)}, u32[]{:S(2)}, u32[]{:S(2)}) collective-permute-start(bf16[128,128]{1,0:T(8,128)(2,1)S(1)} %add_convert_fusion.1), channel_id=1, source_target_pairs={{0,8},{4,12},{8,0},{12,4},{16,24},{20,28},{24,16},{28,20},{1,9},{5... | collective-permute-start | bytes 98312 | tf_op jit(solution)/shard_map/ppermute | solution.py:266
  79.8 7.5 %collective-permute-start.17 = (f32[128,128]{1,0:T(8,128)S(1)}, f32[128,128]{1,0:T(8,128)S(1)}, u32[]{:S(2)}, u32[]{:S(2)}) collective-permute-start(f32[128,128]{1,0:T(8,128)S(1)} %get-tuple-element.12.refs_4_), channel_id=1, source_target_pairs={{0,16},{4,20},{8,24},{12,28},{16,0},{20,4},{24,8},{28,12},{1,17},{... | collective-permute-start | bytes 196616 | tf_op jit(solution)/shard_map/ppermute | solution.py:266
  82.8 5.8 %collective-permute-start.16 = (bf16[128,128]{1,0:T(8,128)(2,1)S(1)}, bf16[128,128]{1,0:T(8,128)(2,1)S(1)}, u32[]{:S(2)}, u32[]{:S(2)}) collective-permute-start(bf16[128,128]{1,0:T(8,128)(2,1)S(1)} %add_convert_fusion.refs_0_), channel_id=1, source_target_pairs={{0,3},{1,2},{2,1},{3,0},{4,7},{5,6},{6,5},{7,4},{8,11},{9,10},{10,... | collective-permute-start | bytes 98312 | tf_op jit(solution)/shard_map/ppermute | solution.py:266
  85.6 4.8 %collective-permute-start.15 = (bf16[128,128]{1,0:T(8,128)(2,1)S(1)}, bf16[128,128]{1,0:T(8,128)(2,1)S(1)}, u32[]{:S(2)}, u32[]{:S(2)}) collective-permute-start(bf16[128,128]{1,0:T(8,128)(2,1)S(1)} %add_convert_fusion.refs_0_), channel_id=1, source_target_pairs={{0,2},{1,3},{2,0},{3,1},{4,6},{5,7},{6,4},{7,5},{8,10},{9,11},{10,... | collective-permute-start | bytes 98312 | tf_op jit(solution)/shard_map/ppermute | solution.py:266
  85.6 4.8 %collective-permute-start.14 = (bf16[128,128]{1,0:T(8,128)(2,1)S(1)}, bf16[128,128]{1,0:T(8,128)(2,1)S(1)}, u32[]{:S(2)}, u32[]{:S(2)}) collective-permute-start(bf16[128,128]{1,0:T(8,128)(2,1)S(1)} %add_convert_fusion.refs_0_), channel_id=1, source_target_pairs={{0,1},{1,0},{2,3},{3,2},{4,5},{5,4},{6,7},{7,6},{8,9},{9,8},{10,11... | collective-permute-start | bytes 98312 | tf_op jit(solution)/shard_map/ppermute | solution.py:266
  97.6 3.4 %collective-permute-start.20 = (f32[16,640]{1,0:T(8,128)S(1)}, f32[16,640]{1,0:T(8,128)S(1)}, u32[]{:S(2)}, u32[]{:S(2)}) collective-permute-start(f32[16,640]{1,0:T(8,128)S(1)} %get-tuple-element.16), channel_id=1, source_target_pairs={{0,12},{4,8},{8,4},{12,0},{16,28},{20,24},{24,20},{28,16},{1,13},{... | collective-permute-start | bytes 122888 | tf_op jit(solution)/shard_map/ppermute | solution.py:266
  97.6 4.5 %collective-permute-start.19 = (f32[16,640]{1,0:T(8,128)S(1)}, f32[16,640]{1,0:T(8,128)S(1)}, u32[]{:S(2)}, u32[]{:S(2)}) collective-permute-start(f32[16,640]{1,0:T(8,128)S(1)} %get-tuple-element.17), channel_id=1, source_target_pairs={{0,8},{4,12},{8,0},{12,4},{16,24},{20,28},{24,16},{28,20},{1,9},{5... | collective-permute-start | bytes 122888 | tf_op jit(solution)/shard_map/ppermute | solution.py:266
  98.6 3.5 %collective-permute-start.18 = (f32[16,640]{1,0:T(8,128)S(1)}, f32[16,640]{1,0:T(8,128)S(1)}, u32[]{:S(2)}, u32[]{:S(2)}) collective-permute-start(f32[16,640]{1,0:T(8,128)S(1)} %get-tuple-element.18), channel_id=1, source_target_pairs={{0,4},{4,0},{8,12},{12,8},{16,20},{20,16},{24,28},{28,24},{1,5},{5... | collective-permute-start | bytes 122888 | tf_op jit(solution)/shard_map/ppermute | solution.py:266
  101.1 1.0 copy-start.3
  102.1 0.6 copy-start.4
  102.1 0.6 copy-start.5
where the time goes:
time: 105 us; the launch traced here: 104 us
  Pallas kernels  34.6 us (33%)
  starting transfers between devices  33.1 us (32%)
  waiting for transfers between devices  28.3 us (27%)
  local copies, waits for them, and re-layouts  7.4 us (7%)
    ppermute x20, starting transfers between devices, swap(): lax.ppermute(value, axis, [(source, source ^ mask) for source in range(co...  30.8 us
    ppermute x20, waiting for transfers between devices, swap(): lax.ppermute(value, axis, [(source, source ^ mask) for source in range(co...  28.3 us
    pallas_call x3, Pallas kernels, filter_call(): pl.pallas_call(functools.partial(filter_kernel, len(parts), first, last),...  19.2 us
    pallas_call x1, Pallas kernels, front(): pl.pallas_call(front_kernel, grid=(cols // tile,), in_specs=[pl.BlockSpec...  12.6 us
    unnamed x13, local copies, waits for them, and re-layouts  4.16 us
    ppermute x1, starting transfers between devices, on_device(): lax.ppermute(record[rows - HALO:], 'tm', [(source, source + 1) for source...  2.38 us
  transfers between devices with their start and end apart: 21, of which 13 were waited for; matrix products, arithmetic and copies ran while one was open for 2% of the time, Pallas kernels for 0%

commit v1 on v0

--- a/solution.py
+++ b/solution.py
@@ -11,7 +11,8 @@
 GAUGE_MAX = 16
 K_ITERS = 8
 HALO = TAPS + GAUGE_MAX
-BLOCK = 128
+BLOCK = 192
+CHUNK = 256
 EXTRA = 16
 F32 = jnp.float32
 BF16 = jnp.bfloat16
@@ -52,27 +53,27 @@
     return row == col
 
 
-def front_kernel(record, halo, lag, taps, projector, out, band, proj_t):
+def front_kernel(record, halo, lag, taps, projector, out, band, proj_t, strain):
     rows = record.shape[0]
     cols = record.shape[1]
 
     @pl.when(pl.program_id(0) == 0)
     def _():
         line = jnp.broadcast_to(taps[...], (BLOCK, taps.shape[1]))
-        rolled = pltpu.roll(line, 0, 1, stride=1, stride_axis=0)
-        band[...] = rolled[:, : BLOCK + TAPS].astype(BF16)
+        band[...] = pltpu.roll(line, 0, 1, stride=1, stride_axis=0).astype(BF16)
         proj_t[...] = projector[...].astype(F32).T.astype(BF16)
 
     lane = min(128, cols)
     before = dot(band[0:GAUGE_MAX, 0:HALO], halo[...])
     total = jnp.zeros(out.shape, F32)
-    for b in range(rows // BLOCK):
-        if b == 0:
-            segment = jnp.concatenate([halo[GAUGE_MAX:HALO, :], record[0:BLOCK, :]], 0)
+    used = 0
+    for first in range(0, rows, BLOCK):
+        size = min(BLOCK, rows - first)
+        if first == 0:
+            segment = jnp.concatenate([halo[GAUGE_MAX:HALO, :], record[0:size, :]], 0)
         else:
-            segment = record[b * BLOCK - TAPS : (b + 1) * BLOCK, :]
-        current = dot(band[...], segment)
-        parts = []
+            segment = record[first - TAPS : first + size, :]
+        current = dot(band[:size, : size + TAPS], segment)
         for c in range(0, cols, lane):
             span = slice(c, c + lane)
             shift = GAUGE_MAX - lag[:, span]
@@ -82,10 +83,12 @@
             for step in (4, 2, 1):
                 moved = pltpu.roll(picked, picked.shape[0] - step, 0)
                 picked = jnp.where((shift & step) != 0, moved, picked)
-            parts.append((here - picked[:BLOCK]).astype(BF16))
-        strain = jnp.concatenate(parts, 1) if len(parts) > 1 else parts[0]
-        total = total + dot(proj_t[:, b * BLOCK : (b + 1) * BLOCK], strain)
-        before = current[BLOCK - GAUGE_MAX :]
+            strain[first : first + size, span] = (here - picked[:size]).astype(BF16)
+        before = current[size - GAUGE_MAX :]
+        while used < rows and min(used + CHUNK, rows) <= first + size:
+            part = slice(used, min(used + CHUNK, rows))
+            total = total + dot(proj_t[:, part], strain[part, :])
+            used = part.stop
     out[...] = total.astype(BF16)
 
 
@@ -109,8 +112,9 @@
         scratch_shapes=[
             pltpu.VMEM((BLOCK, BLOCK + TAPS), BF16),
             pltpu.VMEM((rank, rows), BF16),
+            pltpu.VMEM((rows, tile), BF16),
         ],
-        compiler_params=PARAMS,
+        compiler_params=pltpu.CompilerParams(vmem_limit_bytes=58 * 2**20),
         name="front",
     )(record, halo, lag, taps, projector)
 
@@ -150,17 +154,21 @@
     )(own, other)
 
 
-def cross_kernel(own, other, out):
-    out[...] = dot_nt(own[...], other[...]).astype(out.dtype)
-
-
-def cross_gram(own, other):
+def ahead_kernel(own, sibling, partner, out):
+    rank = own.shape[0]
+    there = partner[...]
+    out[0:rank, :] = dot_nt(own[...], there).astype(out.dtype)
+    out[rank:, :] = dot_nt(sibling[...], there).astype(out.dtype)
+
+
+def ahead_gram(own, sibling, partner):
+    rank = own.shape[0]
     return pl.pallas_call(
-        cross_kernel,
-        out_shape=jax.ShapeDtypeStruct((own.shape[0], other.shape[0]), BF16),
+        ahead_kernel,
+        out_shape=jax.ShapeDtypeStruct((2 * rank, rank), BF16),
         compiler_params=PARAMS,
-        name="cross_gram",
-    )(own, other)
+        name="ahead_gram",
+    )(own, sibling, partner)
 
 
 def summed(parts):
@@ -191,24 +199,35 @@
     return square_of(aa, ab, bb), mean
 
 
-def later_gram(parts, own_level, other_level):
-    gram = square_of(own_level[...], summed(parts), other_level[...])
+def later_gram(own_mix, own_level, packed, ahead, sibling_ahead):
+    rank = own_mix.shape[0]
+    mine, theirs = ahead[...], sibling_ahead[...]
+    cross = jnp.concatenate(
+        [
+            jnp.concatenate([mine[:rank], theirs[rank:]], 1),
+            jnp.concatenate([mine[rank:], theirs[:rank]], 1),
+        ],
+        0,
+    )
+    high, low = split(own_mix[...])
+    half = dot(high, cross) + dot(low, cross)
+    high, low = split(half)
+    other_mix = packed[:, : 2 * rank]
+    ab = dot_nt(high, other_mix) + dot_nt(low, other_mix)
+    other_level = packed[:, 2 * rank : 3 * rank].astype(F32) + packed[:, 3 * rank :].astype(F32)
+    gram = square_of(own_level[...], ab, other_level)
     diag = eye_mask(gram.shape[0])
     mean = jnp.sum(jnp.where(diag, gram, 0.0), axis=(0, 1), keepdims=True) / gram.shape[0]
     return gram - jnp.where(diag, mean, 0.0), mean
 
 
 def filter_kernel(count, first, last, *refs):
-    parts, refs = refs[:count], refs[count:]
-    if first:
-        levels = ()
-    else:
-        levels, refs = refs[:2], refs[2:]
+    grams, refs = refs[:count], refs[count:]
     compress_t, offset, own, other, refs = *refs[:4], refs[4:]
     if last:
         sketch, pair, sems = refs
     else:
-        sketch, level, pair, sems = refs
+        sketch, mix_out, level, packed, pair, sems = refs
     rank, width = own.shape[0], pair.shape[1]
     start = pl.multiple_of(offset[0], 128) if width % 128 == 0 else 0
     copies = [
@@ -221,7 +240,7 @@
     ]
     for copy in copies:
         copy.start()
-    gram, mean = first_gram(parts) if first else later_gram(parts, *levels)
+    gram, mean = first_gram(grams) if first else later_gram(*grams)
     size = gram.shape[0]
     eye = jnp.where(eye_mask(size), 1.0, 0.0)
     z = gram * lax.rsqrt(jnp.sum(gram * gram, axis=(0, 1), keepdims=True) + 1e-6)
@@ -241,18 +260,26 @@
         wide = dot(both, pair[:, c : c + tile])
         sketch[:, c : c + tile] = (wide[:rows] + wide[rows:]).astype(sketch.dtype)
     if not last:
-        level[...] = dot3_nt(dot3(mixing, gram + mean * eye), mixing)
-
-
-def filter_call(parts, levels, compress_t, offset, own, other, width, first, last):
+        block = dot3_nt(dot3(mixing, gram + mean * eye), mixing)
+        mix_out[...] = mixing
+        level[...] = block
+        packed[:, : 2 * rank] = high
+        high, low = split(block)
+        packed[:, 2 * rank : 3 * rank] = high
+        packed[:, 3 * rank :] = low
+
+
+def filter_call(grams, compress_t, offset, own, other, width, first, last):
     rank = own.shape[0]
     rows = compress_t.shape[0]
     out = [jax.ShapeDtypeStruct((rows, width), F32 if last else BF16)]
     if not last:
+        out.append(jax.ShapeDtypeStruct((rank, 2 * rank), F32))
         out.append(jax.ShapeDtypeStruct((rank, rank), F32))
-    args = [*parts, *levels, compress_t]
+        out.append(jax.ShapeDtypeStruct((rank, 4 * rank), BF16))
+    args = [*grams, compress_t]
     return pl.pallas_call(
-        functools.partial(filter_kernel, len(parts), first, last),
+        functools.partial(filter_kernel, len(grams), first, last),
         in_specs=[VMEM] * len(args) + [SMEM, ANY, ANY],
         out_shape=out,
         scratch_shapes=[pltpu.VMEM((2 * rank, width), BF16), pltpu.SemaphoreType.DMA((2,))],
@@ -300,7 +327,7 @@
     halo = lax.ppermute(
         record[rows - HALO :], "tm", [(source, source + 1) for source in range(count - 1)]
     )
-    taps = jnp.pad(fir_taps.astype(F32)[::-1], (1, 2 * BLOCK - TAPS - 1))[None, :]
+    taps = jnp.pad(fir_taps.astype(F32)[::-1], (1, BLOCK - 1))[None, :]
     sketch = front(record, halo, gauge_lag[None, :], taps, projector)
 
     widths = []
@@ -319,7 +346,7 @@
     compress_t = compress.T
     flipped = jnp.concatenate([compress_t[:, rank:], compress_t[:, :rank]], 1)
 
-    level = None
+    kept = ahead = None
     for depth in range(depths):
         first, last = depth == 0, depth == depths - 1
         mask = 2**depth
@@ -338,19 +365,20 @@
         offset = jnp.reshape(offset, (1,)).astype(jnp.int32)
         other = swap(sketch, "tm", mask)
         if first:
-            parts = gather_parts(pair_gram(sketch, other), "chan")
-            levels = []
+            grams = gather_parts(pair_gram(sketch, other), "chan")
         else:
-            levels = [level, swap(level, "tm", mask)]
-            part = cross_gram(sketch, other)
+            mixing, level, packed = kept
+            grams = [mixing, level, swap(packed, "tm", mask), *ahead]
+        if not last:
+            part = ahead_gram(sketch, other, swap(sketch, "tm", 2 * mask))
             for bit in [b for b in narrowed if b < depth]:
                 part = (part.astype(F32) + swap(part, "tm", 2**bit).astype(F32)).astype(BF16)
             parts = gather_parts(part, "chan")
-        results = filter_call(
-            parts, levels, weights, offset, sketch, other, here if last else widths[depth], first, last
+            total = sum(piece.astype(F32) for piece in parts).astype(BF16)
+            ahead = total, swap(total, "tm", mask)
+        sketch, *kept = filter_call(
+            grams, weights, offset, sketch, other, here if last else widths[depth], first, last
         )
-        sketch = results[0]
-        level = None if last else results[1]
     if span == 1:
         return sketch
     width = sketch.shape[1]

time: 105 us -> 94.9 us (0.904)
  waiting for transfers between devices: 28.3 us -> 15.8 us
  local copies, waits for them, and re-layouts: 7.4 us -> 9.16 us
    ppermute x20 -> x22, waiting for transfers between devices: 28.3 us -> 15.8 us  [swap(): lax.ppermute(value, axis, [(source, source ^ mask) for source in range(co...]
    unnamed x13 -> x17, local copies, waits for them, and re-layouts: 4.16 us -> 4.75 us
    ppermute x20 -> x22, starting transfers between devices: 30.8 us -> 31.2 us  [swap(): lax.ppermute(value, axis, [(source, source ^ mask) for source in range(co...]
  transfers between devices with their start and end apart: 21 -> 23, of which waited for: 13 -> 9; matrix products, arithmetic and copies ran while one was open for 2% -> 4% of each run, Pallas kernels for 0% -> 15%
where the time goes in v1:
time: 94.9 us; the launch traced here: 94.5 us
  Pallas kernels  35 us (37%)
  starting transfers between devices  33.6 us (35%)
  waiting for transfers between devices  15.8 us (17%)
  local copies, waits for them, and re-layouts  9.16 us (10%)
    ppermute x22, starting transfers between devices, swap(): lax.ppermute(value, axis, [(source, source ^ mask) for source in range(co...  31.2 us
    pallas_call x3, Pallas kernels, filter_call(): pl.pallas_call(functools.partial(filter_kernel, len(grams), first, last),...  19.7 us
    ppermute x22, waiting for transfers between devices, swap(): lax.ppermute(value, axis, [(source, source ^ mask) for source in range(co...  15.8 us
    pallas_call x1, Pallas kernels, front(): pl.pallas_call(front_kernel, grid=(cols // tile,), in_specs=[pl.BlockSpec...  12.1 us
    unnamed x17, local copies, waits for them, and re-layouts  4.75 us
    ppermute x1, starting transfers between devices, on_device(): lax.ppermute(record[rows - HALO:], 'tm', [(source, source + 1) for source...  2.38 us
  transfers between devices with their start and end apart: 23, of which 9 were waited for; matrix products, arithmetic and copies ran while one was open for 4% of the time, Pallas kernels for 15%

profile of v1, /device:TPU:0, one launch (start us, length us, event | category | flops | bytes accessed | tf_op | source)
XLA Modules:
  0.0 94.5 jit_solution(1758530517339570342)
XLA Ops:
  0.0 1.1 %slice.21 = bf16[80,2560]{1,0:T(8,128)(2,1)S(1)} slice(bf16[1024,2560]{1,0:T(8,128)(2,1)} %record.1), slice={[944:1024], [0:2560]} | slice | bytes 819200 | tf_op jit(solution)/shard_map/slice | solution.py:328
  1.1 2.4 %collective-permute-start = (bf16[80,2560]{1,0:T(8,128)(2,1)S(1)}, bf16[80,2560]{1,0:T(8,128)(2,1)S(1)}, u32[]{:S(2)}, u32[]{:S(2)}) collective-permute-start(bf16[80,2560]{1,0:T(8,128)(2,1)S(1)} %slice.21), channel_id=1, source_target_pairs={{0,4},{4,8},{8,12},{12,16},{16,20},{20,24},{24,28},{1,5},{5,9},{9,... | collective-permute-start | bytes 1228808 | tf_op jit(solution)/shard_map/ppermute | solution.py:327
  4.2 1.3 %broadcast_in_dim.6.lag = s32[1,2560]{1,0:T(1,128)} reshape(s32[2560]{0:T(1024)} %param.7) | data formatting | bytes 20480 | tf_op jit(solution)/shard_map/broadcast_in_dim | solution.py:331
  6.9 12.1 %front.1.own.refs_6_ = bf16[128,2560]{1,0:T(8,128)(2,1)} custom-call(bf16[1024,2560]{1,0:T(8,128)(2,1)} %record.1, bf16[80,2560]{1,0:T(8,128)(2,1)} %copy-done.3, s32[1,2560]{1,0:T(1,128)} %broadcast_in_dim.6.lag, f32[1,256]{1,0:T(1,128)} %bitcast.12, bf16[1024,128]{1,0:T(8,128)(2,1)} %projector.1), custom_call_target="tpu_custom_call" | custom-call | tf_op jit(solution)/shard_map/front/pallas_call | solution.py:100
  19.0 4.8 %collective-permute-start.1 = (bf16[128,2560]{1,0:T(8,128)(2,1)}, bf16[128,2560]{1,0:T(8,128)(2,1)S(1)}, u32[]{:S(2)}, u32[]{:S(2)}) collective-permute-start(bf16[128,2560]{1,0:T(8,128)(2,1)} %front.1.own.refs_6_), channel_id=1, source_target_pairs={{0,4},{4,0},{8,12},{12,8},{16,20},{20,16},{24,28},{28,24},{1,5},{5... | collective-permute-start | bytes 1966088 | tf_op jit(solution)/shard_map/ppermute | solution.py:293
  23.9 2.4 %collective-permute-start.6 = (bf16[128,2560]{1,0:T(8,128)(2,1)}, bf16[128,2560]{1,0:T(8,128)(2,1)S(1)}, u32[]{:S(2)}, u32[]{:S(2)}) collective-permute-start(bf16[128,2560]{1,0:T(8,128)(2,1)} %front.1.own.refs_6_), channel_id=1, source_target_pairs={{0,8},{4,12},{8,0},{12,4},{16,24},{20,28},{24,16},{28,20},{1,9},{5... | collective-permute-start | bytes 1966088 | tf_op jit(solution)/shard_map/ppermute | solution.py:293
  26.4 1.1 %copy-done = bf16[128,2560]{1,0:T(8,128)(2,1)S(1)} copy-done((bf16[128,2560]{1,0:T(8,128)(2,1)S(1)}, bf16[128,2560]{1,0:T(8,128)(2,1)}, u32[]{:S(2)}) %copy-start) | copy-done | bytes 655384
  27.5 0.8 pair_gram.1.refs_0_
  28.3 3.7 %collective-permute-start.4 = (bf16[272,128]{1,0:T(8,128)(2,1)S(1)}, bf16[272,128]{1,0:T(8,128)(2,1)S(1)}, u32[]{:S(2)}, u32[]{:S(2)}) collective-permute-start(bf16[272,128]{1,0:T(8,128)(2,1)S(1)} %pair_gram.1.refs_0_), channel_id=1, source_target_pairs={{0,3},{1,2},{2,1},{3,0},{4,7},{5,6},{6,5},{7,4},{8,11},{9,10},{10,... | collective-permute-start | bytes 208904 | tf_op jit(solution)/shard_map/ppermute | solution.py:293
  32.0 0.8 collective-permute-start.2
  32.8 2.1 %collective-permute-done.4.refs_3_ = bf16[272,128]{1,0:T(8,128)(2,1)S(1)} collective-permute-done((bf16[272,128]{1,0:T(8,128)(2,1)S(1)}, bf16[272,128]{1,0:T(8,128)(2,1)S(1)}, u32[]{:S(2)}, u32[]{:S(2)}) %collective-permute-start.4) | collective-permute-done | bytes 69664 | tf_op jit(solution)/shard_map/ppermute | solution.py:293
  34.9 3.3 %collective-permute-done.3.refs_2_ = bf16[272,128]{1,0:T(8,128)(2,1)S(1)} collective-permute-done((bf16[272,128]{1,0:T(8,128)(2,1)S(1)}, bf16[272,128]{1,0:T(8,128)(2,1)S(1)}, u32[]{:S(2)}, u32[]{:S(2)}) %collective-permute-start.3) | collective-permute-done | bytes 69664 | tf_op jit(solution)/shard_map/ppermute | solution.py:293
  38.2 1.1 %copy-done.1 = bf16[128,2560]{1,0:T(8,128)(2,1)S(1)} copy-done((bf16[128,2560]{1,0:T(8,128)(2,1)S(1)}, bf16[128,2560]{1,0:T(8,128)(2,1)}, u32[]{:S(2)}) %copy-start.1) | copy-done | bytes 655384
  39.3 6.3 %sign_filter.3 = (bf16[128,1280]{1,0:T(8,128)(2,1)S(1)}, f32[128,256]{1,0:T(8,128)S(1)}, f32[128,128]{1,0:T(8,128)S(1)}, bf16[128,512]{1,0:T(8,128)(2,1)S(1)}) custom-call(bf16[272,128]{1,0:T(8,128)(2,1)S(1)} %pair_gram.1.refs_0_, bf16[272,128]{1,0:T(8,128)(2,1)S(1)} %collective-permute-done.2.refs_1_, bf16[272,128]{1,0:T(8,128)(2,1)S(1)} %collective-permute-done.3.refs_2_, ...), custom_call_target="tpu_custom_call" | custom-call | tf_op jit(solution)/shard_map/sign_filter/pallas_call | solution.py:281
  45.6 3.1 %collective-permute-start.13 = (bf16[128,1280]{1,0:T(8,128)(2,1)S(1)}, bf16[128,1280]{1,0:T(8,128)(2,1)S(1)}, u32[]{:S(2)}, u32[]{:S(2)}) collective-permute-start(bf16[128,1280]{1,0:T(8,128)(2,1)S(1)} %get-tuple-element.16.refs_7_.own), channel_id=1, source_target_pairs={{0,16},{4,20},{8,24},{12,28},{16,0},{20,4},{24,8},{28,12},{1,17},{... | collective-permute-start | bytes 983048 | tf_op jit(solution)/shard_map/ppermute | solution.py:293
  49.3 1.1 %copy-done.2 = bf16[128,2560]{1,0:T(8,128)(2,1)S(1)} copy-done((bf16[128,2560]{1,0:T(8,128)(2,1)S(1)}, bf16[128,2560]{1,0:T(8,128)(2,1)}, u32[]{:S(2)}) %copy-start.2) | copy-done | bytes 655384
  50.9 2.5 %collective-permute-start.9 = (bf16[256,128]{1,0:T(8,128)(2,1)S(1)}, bf16[256,128]{1,0:T(8,128)(2,1)S(1)}, u32[]{:S(2)}, u32[]{:S(2)}) collective-permute-start(bf16[256,128]{1,0:T(8,128)(2,1)S(1)} %ahead_gram.2), channel_id=1, source_target_pairs={{0,3},{1,2},{2,1},{3,0},{4,7},{5,6},{6,5},{7,4},{8,11},{9,10},{10,... | collective-permute-start | bytes 196616 | tf_op jit(solution)/shard_map/ppermute | solution.py:293
  53.5 1.9 %collective-permute-start.7 = (bf16[256,128]{1,0:T(8,128)(2,1)S(1)}, bf16[256,128]{1,0:T(8,128)(2,1)S(1)}, u32[]{:S(2)}, u32[]{:S(2)}) collective-permute-start(bf16[256,128]{1,0:T(8,128)(2,1)S(1)} %ahead_gram.2), channel_id=1, source_target_pairs={{0,1},{1,0},{2,3},{3,2},{4,5},{5,4},{6,7},{7,6},{8,9},{9,8},{10,11... | collective-permute-start | bytes 196616 | tf_op jit(solution)/shard_map/ppermute | solution.py:293
  56.1 1.5 %collective-permute-done.11.refs_8_.sibling = bf16[128,1280]{1,0:T(8,128)(2,1)S(1)} collective-permute-done((bf16[128,1280]{1,0:T(8,128)(2,1)S(1)}, bf16[128,1280]{1,0:T(8,128)(2,1)S(1)}, u32[]{:S(2)}, u32[]{:S(2)}) %collective-permute-start.11) | collective-permute-done | bytes 327712 | tf_op jit(solution)/shard_map/ppermute | solution.py:293
  57.9 1.2 %collective-permute-done.8 = bf16[256,128]{1,0:T(8,128)(2,1)S(1)} collective-permute-done((bf16[256,128]{1,0:T(8,128)(2,1)S(1)}, bf16[256,128]{1,0:T(8,128)(2,1)S(1)}, u32[]{:S(2)}, u32[]{:S(2)}) %collective-permute-start.8) | collective-permute-done | bytes 65568 | tf_op jit(solution)/shard_map/ppermute | solution.py:293
  59.3 1.5 %collective-permute-start.5 = (bf16[128,512]{1,0:T(8,128)(2,1)S(1)}, bf16[128,512]{1,0:T(8,128)(2,1)S(1)}, u32[]{:S(2)}, u32[]{:S(2)}) collective-permute-start(bf16[128,512]{1,0:T(8,128)(2,1)S(1)} %get-tuple-element.15), channel_id=1, source_target_pairs={{0,8},{4,12},{8,0},{12,4},{16,24},{20,28},{24,16},{28,20},{1,9},{5... | collective-permute-start | bytes 393224 | tf_op jit(solution)/shard_map/ppermute | solution.py:293
  60.8 2.4 %collective-permute-start.17 = (bf16[256,128]{1,0:T(8,128)(2,1)S(1)}, bf16[256,128]{1,0:T(8,128)(2,1)S(1)}, u32[]{:S(2)}, u32[]{:S(2)}) collective-permute-start(bf16[256,128]{1,0:T(8,128)(2,1)S(1)} %add_convert_fusion.1), channel_id=1, source_target_pairs={{0,3},{1,2},{2,1},{3,0},{4,7},{5,6},{6,5},{7,4},{8,11},{9,10},{10,... | collective-permute-start | bytes 196616 | tf_op jit(solution)/shard_map/ppermute | solution.py:293
  63.2 2.0 %collective-permute-start.15 = (bf16[256,128]{1,0:T(8,128)(2,1)S(1)}, bf16[256,128]{1,0:T(8,128)(2,1)S(1)}, u32[]{:S(2)}, u32[]{:S(2)}) collective-permute-start(bf16[256,128]{1,0:T(8,128)(2,1)S(1)} %add_convert_fusion.1), channel_id=1, source_target_pairs={{0,1},{1,0},{2,3},{3,2},{4,5},{5,4},{6,7},{7,6},{8,9},{9,8},{10,11... | collective-permute-start | bytes 196616 | tf_op jit(solution)/shard_map/ppermute | solution.py:293
  65.3 6.6 %sign_filter.4 = (bf16[128,640]{1,0:T(8,128)(2,1)S(1)}, f32[128,256]{1,0:T(8,128)S(1)}, f32[128,128]{1,0:T(8,128)S(1)}, bf16[128,512]{1,0:T(8,128)(2,1)S(1)}) custom-call(f32[128,256]{1,0:T(8,128)S(1)} %get-tuple-element.13.refs_0_, f32[128,128]{1,0:T(8,128)S(1)} %get-tuple-element.14.refs_1_, bf16[128,512]{1,0:T(8,128)(2,1)S(1)} %collective-permute-done.5.refs_2_, ...), custom_call_target="tpu_custom_call" | custom-call | tf_op jit(solution)/shard_map/sign_filter/pallas_call | solution.py:281
  72.4 1.6 %collective-permute-start.19 = (bf16[128,640]{1,0:T(8,128)(2,1)S(1)}, bf16[128,640]{1,0:T(8,128)(2,1)S(1)}, u32[]{:S(2)}, u32[]{:S(2)}) collective-permute-start(bf16[128,640]{1,0:T(8,128)(2,1)S(1)} %get-tuple-element.20.refs_7_), channel_id=1, source_target_pairs={{0,16},{4,20},{8,24},{12,28},{16,0},{20,4},{24,8},{28,12},{1,17},{... | collective-permute-start | bytes 491528 | tf_op jit(solution)/shard_map/ppermute | solution.py:293
  74.1 1.4 %collective-permute-start.18 = (bf16[256,128]{1,0:T(8,128)(2,1)S(1)}, bf16[256,128]{1,0:T(8,128)(2,1)S(1)}, u32[]{:S(2)}, u32[]{:S(2)}) collective-permute-start(bf16[256,128]{1,0:T(8,128)(2,1)S(1)} %add_convert_fusion.refs_3_), channel_id=1, source_target_pairs={{0,8},{4,12},{8,0},{12,4},{16,24},{20,28},{24,16},{28,20},{1,9},{5... | collective-permute-start | bytes 196616 | tf_op jit(solution)/shard_map/ppermute | solution.py:293
  75.5 2.9 %collective-permute-done.12.refs_2_ = bf16[128,512]{1,0:T(8,128)(2,1)S(1)} collective-permute-done((bf16[128,512]{1,0:T(8,128)(2,1)S(1)}, bf16[128,512]{1,0:T(8,128)(2,1)S(1)}, u32[]{:S(2)}, u32[]{:S(2)}) %collective-permute-start.12) | collective-permute-done | bytes 131104 | tf_op jit(solution)/shard_map/ppermute | solution.py:293
  78.4 2.1 %collective-permute-done.19.refs_8_ = bf16[128,640]{1,0:T(8,128)(2,1)S(1)} collective-permute-done((bf16[128,640]{1,0:T(8,128)(2,1)S(1)}, bf16[128,640]{1,0:T(8,128)(2,1)S(1)}, u32[]{:S(2)}, u32[]{:S(2)}) %collective-permute-start.19) | collective-permute-done | bytes 163872 | tf_op jit(solution)/shard_map/ppermute | solution.py:293
  80.5 6.8 %sign_filter.5 = f32[64,640]{1,0:T(8,128)S(1)} custom-call(f32[128,256]{1,0:T(8,128)S(1)} %get-tuple-element.17.refs_0_, f32[128,128]{1,0:T(8,128)S(1)} %get-tuple-element.18.refs_1_, bf16[128,512]{1,0:T(8,128)(2,1)S(1)} %collective-permute-done.12.refs_2_, bf16[256,128]{1,0:T(8,128)(2,1)S(1)} %add_convert_fusion.refs_3_, ...), custom_call_target="tpu_custom_call" | custom-call | tf_op jit(solution)/shard_map/sign_filter/pallas_call | solution.py:281
  87.9 1.5 %collective-permute-start.21 = (f32[16,640]{1,0:T(8,128)S(1)}, f32[16,640]{1,0:T(8,128)S(1)}, u32[]{:S(2)}, u32[]{:S(2)}) collective-permute-start(f32[16,640]{1,0:T(8,128)S(1)} %get-tuple-element.25), channel_id=1, source_target_pairs={{0,8},{4,12},{8,0},{12,4},{16,24},{20,28},{24,16},{28,20},{1,9},{5... | collective-permute-start | bytes 122888 | tf_op jit(solution)/shard_map/ppermute | solution.py:293
  90.3 1.4 %collective-permute-done.22.refs_3_ = f32[16,640]{1,0:T(8,128)S(1)} collective-permute-done((f32[16,640]{1,0:T(8,128)S(1)}, f32[16,640]{1,0:T(8,128)S(1)}, u32[]{:S(2)}, u32[]{:S(2)}) %collective-permute-start.22) | collective-permute-done | bytes 40992 | tf_op jit(solution)/shard_map/ppermute | solution.py:293
  92.9 1.5 %join.1 = f32[16,2560]{1,0:T(8,128)} custom-call(s32[4]{0:T(128)} %pad_add_fusion.offsets, f32[16,640]{1,0:T(8,128)} %get-tuple-element.27.refs_0_, f32[16,640]{1,0:T(8,128)} %copy-done.7, f32[16,640]{1,0:T(8,128)} %copy-done.6, f32[16,640]{1,0:T(8,128)} %copy-done.5), custom_call_target="tpu_custom_call" | custom-call | tf_op jit(solution)/shard_map/join/pallas_call | solution.py:312
  (52 shorter events, 8.0 us)
Async XLA Ops:
  0.0 23.8 %copy-start.4 = (f32[256,128]{1,0:T(8,128)S(1)}, f32[256,128]{1,0:T(8,128)}, u32[]{:S(2)}) copy-start(f32[256,128]{1,0:T(8,128)} %param.9) | copy-start | bytes 393220
  1.1 5.1 %collective-permute-start = (bf16[80,2560]{1,0:T(8,128)(2,1)S(1)}, bf16[80,2560]{1,0:T(8,128)(2,1)S(1)}, u32[]{:S(2)}, u32[]{:S(2)}) collective-permute-start(bf16[80,2560]{1,0:T(8,128)(2,1)S(1)} %slice.21), channel_id=1, source_target_pairs={{0,4},{4,8},{8,12},{12,16},{16,20},{20,24},{24,28},{1,5},{5,9},{9,... | collective-permute-start | bytes 1228808 | tf_op jit(solution)/shard_map/ppermute | solution.py:327
  6.2 0.8 copy-start.3
  19.0 7.3 %collective-permute-start.1 = (bf16[128,2560]{1,0:T(8,128)(2,1)}, bf16[128,2560]{1,0:T(8,128)(2,1)S(1)}, u32[]{:S(2)}, u32[]{:S(2)}) collective-permute-start(bf16[128,2560]{1,0:T(8,128)(2,1)} %front.1.own.refs_6_), channel_id=1, source_target_pairs={{0,4},{4,0},{8,12},{12,8},{16,20},{20,16},{24,28},{28,24},{1,5},{5... | collective-permute-start | bytes 1966088 | tf_op jit(solution)/shard_map/ppermute | solution.py:293
  23.9 25.4 %collective-permute-start.6 = (bf16[128,2560]{1,0:T(8,128)(2,1)}, bf16[128,2560]{1,0:T(8,128)(2,1)S(1)}, u32[]{:S(2)}, u32[]{:S(2)}) collective-permute-start(bf16[128,2560]{1,0:T(8,128)(2,1)} %front.1.own.refs_6_), channel_id=1, source_target_pairs={{0,8},{4,12},{8,0},{12,4},{16,24},{20,28},{24,16},{28,20},{1,9},{5... | collective-permute-start | bytes 1966088 | tf_op jit(solution)/shard_map/ppermute | solution.py:293
  26.4 1.1 %copy-start = (bf16[128,2560]{1,0:T(8,128)(2,1)S(1)}, bf16[128,2560]{1,0:T(8,128)(2,1)}, u32[]{:S(2)}) copy-start(bf16[128,2560]{1,0:T(8,128)(2,1)} %front.1.own.refs_6_) | copy-start | bytes 1966084
  28.3 6.6 %collective-permute-start.4 = (bf16[272,128]{1,0:T(8,128)(2,1)S(1)}, bf16[272,128]{1,0:T(8,128)(2,1)S(1)}, u32[]{:S(2)}, u32[]{:S(2)}) collective-permute-start(bf16[272,128]{1,0:T(8,128)(2,1)S(1)} %pair_gram.1.refs_0_), channel_id=1, source_target_pairs={{0,3},{1,2},{2,1},{3,0},{4,7},{5,6},{6,5},{7,4},{8,11},{9,10},{10,... | collective-permute-start | bytes 208904 | tf_op jit(solution)/shard_map/ppermute | solution.py:293
  32.0 6.2 %collective-permute-start.3 = (bf16[272,128]{1,0:T(8,128)(2,1)S(1)}, bf16[272,128]{1,0:T(8,128)(2,1)S(1)}, u32[]{:S(2)}, u32[]{:S(2)}) collective-permute-start(bf16[272,128]{1,0:T(8,128)(2,1)S(1)} %pair_gram.1.refs_0_), channel_id=1, source_target_pairs={{0,2},{1,3},{2,0},{3,1},{4,6},{5,7},{6,4},{7,5},{8,10},{9,11},{10,... | collective-permute-start | bytes 208904 | tf_op jit(solution)/shard_map/ppermute | solution.py:293
  32.0 6.2 %collective-permute-start.2 = (bf16[272,128]{1,0:T(8,128)(2,1)S(1)}, bf16[272,128]{1,0:T(8,128)(2,1)S(1)}, u32[]{:S(2)}, u32[]{:S(2)}) collective-permute-start(bf16[272,128]{1,0:T(8,128)(2,1)S(1)} %pair_gram.1.refs_0_), channel_id=1, source_target_pairs={{0,1},{1,0},{2,3},{3,2},{4,5},{5,4},{6,7},{7,6},{8,9},{9,8},{10,11... | collective-permute-start | bytes 208904 | tf_op jit(solution)/shard_map/ppermute | solution.py:293
  38.2 1.1 %copy-start.1 = (bf16[128,2560]{1,0:T(8,128)(2,1)S(1)}, bf16[128,2560]{1,0:T(8,128)(2,1)}, u32[]{:S(2)}) copy-start(bf16[128,2560]{1,0:T(8,128)(2,1)} %front.1.own.refs_6_) | copy-start | bytes 1966084
  45.6 10.5 %collective-permute-start.13 = (bf16[128,1280]{1,0:T(8,128)(2,1)S(1)}, bf16[128,1280]{1,0:T(8,128)(2,1)S(1)}, u32[]{:S(2)}, u32[]{:S(2)}) collective-permute-start(bf16[128,1280]{1,0:T(8,128)(2,1)S(1)} %get-tuple-element.16.refs_7_.own), channel_id=1, source_target_pairs={{0,16},{4,20},{8,24},{12,28},{16,0},{20,4},{24,8},{28,12},{1,17},{... | collective-permute-start | bytes 983048 | tf_op jit(solution)/shard_map/ppermute | solution.py:293
  48.7 8.8 %collective-permute-start.11 = (bf16[128,1280]{1,0:T(8,128)(2,1)S(1)}, bf16[128,1280]{1,0:T(8,128)(2,1)S(1)}, u32[]{:S(2)}, u32[]{:S(2)}) collective-permute-start(bf16[128,1280]{1,0:T(8,128)(2,1)S(1)} %get-tuple-element.16.refs_7_.own), channel_id=1, source_target_pairs={{0,8},{4,12},{8,0},{12,4},{16,24},{20,28},{24,16},{28,20},{1,9},{5... | collective-permute-start | bytes 983048 | tf_op jit(solution)/shard_map/ppermute | solution.py:293
  49.3 1.1 %copy-start.2 = (bf16[128,2560]{1,0:T(8,128)(2,1)S(1)}, bf16[128,2560]{1,0:T(8,128)(2,1)}, u32[]{:S(2)}) copy-start(bf16[128,2560]{1,0:T(8,128)(2,1)} %front.1.own.refs_6_) | copy-start | bytes 1966084
  50.9 7.1 %collective-permute-start.9 = (bf16[256,128]{1,0:T(8,128)(2,1)S(1)}, bf16[256,128]{1,0:T(8,128)(2,1)S(1)}, u32[]{:S(2)}, u32[]{:S(2)}) collective-permute-start(bf16[256,128]{1,0:T(8,128)(2,1)S(1)} %ahead_gram.2), channel_id=1, source_target_pairs={{0,3},{1,2},{2,1},{3,0},{4,7},{5,6},{6,5},{7,4},{8,11},{9,10},{10,... | collective-permute-start | bytes 196616 | tf_op jit(solution)/shard_map/ppermute | solution.py:293
  53.4 5.8 %collective-permute-start.8 = (bf16[256,128]{1,0:T(8,128)(2,1)S(1)}, bf16[256,128]{1,0:T(8,128)(2,1)S(1)}, u32[]{:S(2)}, u32[]{:S(2)}) collective-permute-start(bf16[256,128]{1,0:T(8,128)(2,1)S(1)} %ahead_gram.2), channel_id=1, source_target_pairs={{0,2},{1,3},{2,0},{3,1},{4,6},{5,7},{6,4},{7,5},{8,10},{9,11},{10,... | collective-permute-start | bytes 196616 | tf_op jit(solution)/shard_map/ppermute | solution.py:293
  53.5 5.7 %collective-permute-start.7 = (bf16[256,128]{1,0:T(8,128)(2,1)S(1)}, bf16[256,128]{1,0:T(8,128)(2,1)S(1)}, u32[]{:S(2)}, u32[]{:S(2)}) collective-permute-start(bf16[256,128]{1,0:T(8,128)(2,1)S(1)} %ahead_gram.2), channel_id=1, source_target_pairs={{0,1},{1,0},{2,3},{3,2},{4,5},{5,4},{6,7},{7,6},{8,9},{9,8},{10,11... | collective-permute-start | bytes 196616 | tf_op jit(solution)/shard_map/ppermute | solution.py:293
  57.9 3.0 %collective-permute-start.14 = (bf16[256,128]{1,0:T(8,128)(2,1)S(1)}, bf16[256,128]{1,0:T(8,128)(2,1)S(1)}, u32[]{:S(2)}, u32[]{:S(2)}) collective-permute-start(bf16[256,128]{1,0:T(8,128)(2,1)S(1)} %ahead_gram.3), channel_id=1, source_target_pairs={{0,4},{4,0},{8,12},{12,8},{16,20},{20,16},{24,28},{28,24},{1,5},{5... | collective-permute-start | bytes 196616 | tf_op jit(solution)/shard_map/ppermute | solution.py:293
  59.2 6.1 %collective-permute-start.10 = (bf16[256,128]{1,0:T(8,128)(2,1)S(1)}, bf16[256,128]{1,0:T(8,128)(2,1)S(1)}, u32[]{:S(2)}, u32[]{:S(2)}) collective-permute-start(bf16[256,128]{1,0:T(8,128)(2,1)S(1)} %add_convert_fusion.2.refs_3_), channel_id=1, source_target_pairs={{0,4},{4,0},{8,12},{12,8},{16,20},{20,16},{24,28},{28,24},{1,5},{5... | collective-permute-start | bytes 196616 | tf_op jit(solution)/shard_map/ppermute | solution.py:293
  59.3 6.0 %collective-permute-start.5 = (bf16[128,512]{1,0:T(8,128)(2,1)S(1)}, bf16[128,512]{1,0:T(8,128)(2,1)S(1)}, u32[]{:S(2)}, u32[]{:S(2)}) collective-permute-start(bf16[128,512]{1,0:T(8,128)(2,1)S(1)} %get-tuple-element.15), channel_id=1, source_target_pairs={{0,8},{4,12},{8,0},{12,4},{16,24},{20,28},{24,16},{28,20},{1,9},{5... | collective-permute-start | bytes 393224 | tf_op jit(solution)/shard_map/ppermute | solution.py:293
  60.8 13.2 %collective-permute-start.17 = (bf16[256,128]{1,0:T(8,128)(2,1)S(1)}, bf16[256,128]{1,0:T(8,128)(2,1)S(1)}, u32[]{:S(2)}, u32[]{:S(2)}) collective-permute-start(bf16[256,128]{1,0:T(8,128)(2,1)S(1)} %add_convert_fusion.1), channel_id=1, source_target_pairs={{0,3},{1,2},{2,1},{3,0},{4,7},{5,6},{6,5},{7,4},{8,11},{9,10},{10,... | collective-permute-start | bytes 196616 | tf_op jit(solution)/shard_map/ppermute | solution.py:293
  63.2 10.8 %collective-permute-start.16 = (bf16[256,128]{1,0:T(8,128)(2,1)S(1)}, bf16[256,128]{1,0:T(8,128)(2,1)S(1)}, u32[]{:S(2)}, u32[]{:S(2)}) collective-permute-start(bf16[256,128]{1,0:T(8,128)(2,1)S(1)} %add_convert_fusion.1), channel_id=1, source_target_pairs={{0,2},{1,3},{2,0},{3,1},{4,6},{5,7},{6,4},{7,5},{8,10},{9,11},{10,... | collective-permute-start | bytes 196616 | tf_op jit(solution)/shard_map/ppermute | solution.py:293
  63.2 10.8 %collective-permute-start.15 = (bf16[256,128]{1,0:T(8,128)(2,1)S(1)}, bf16[256,128]{1,0:T(8,128)(2,1)S(1)}, u32[]{:S(2)}, u32[]{:S(2)}) collective-permute-start(bf16[256,128]{1,0:T(8,128)(2,1)S(1)} %add_convert_fusion.1), channel_id=1, source_target_pairs={{0,1},{1,0},{2,3},{3,2},{4,5},{5,4},{6,7},{7,6},{8,9},{9,8},{10,11... | collective-permute-start | bytes 196616 | tf_op jit(solution)/shard_map/ppermute | solution.py:293
  71.9 6.5 %collective-permute-start.12 = (bf16[128,512]{1,0:T(8,128)(2,1)S(1)}, bf16[128,512]{1,0:T(8,128)(2,1)S(1)}, u32[]{:S(2)}, u32[]{:S(2)}) collective-permute-start(bf16[128,512]{1,0:T(8,128)(2,1)S(1)} %get-tuple-element.19), channel_id=1, source_target_pairs={{0,16},{4,20},{8,24},{12,28},{16,0},{20,4},{24,8},{28,12},{1,17},{... | collective-permute-start | bytes 393224 | tf_op jit(solution)/shard_map/ppermute | solution.py:293
  72.4 8.1 %collective-permute-start.19 = (bf16[128,640]{1,0:T(8,128)(2,1)S(1)}, bf16[128,640]{1,0:T(8,128)(2,1)S(1)}, u32[]{:S(2)}, u32[]{:S(2)}) collective-permute-start(bf16[128,640]{1,0:T(8,128)(2,1)S(1)} %get-tuple-element.20.refs_7_), channel_id=1, source_target_pairs={{0,16},{4,20},{8,24},{12,28},{16,0},{20,4},{24,8},{28,12},{1,17},{... | collective-permute-start | bytes 491528 | tf_op jit(solution)/shard_map/ppermute | solution.py:293
  74.1 6.4 %collective-permute-start.18 = (bf16[256,128]{1,0:T(8,128)(2,1)S(1)}, bf16[256,128]{1,0:T(8,128)(2,1)S(1)}, u32[]{:S(2)}, u32[]{:S(2)}) collective-permute-start(bf16[256,128]{1,0:T(8,128)(2,1)S(1)} %add_convert_fusion.refs_3_), channel_id=1, source_target_pairs={{0,8},{4,12},{8,0},{12,4},{16,24},{20,28},{24,16},{28,20},{1,9},{5... | collective-permute-start | bytes 196616 | tf_op jit(solution)/shard_map/ppermute | solution.py:293
  87.9 3.9 %collective-permute-start.22 = (f32[16,640]{1,0:T(8,128)S(1)}, f32[16,640]{1,0:T(8,128)S(1)}, u32[]{:S(2)}, u32[]{:S(2)}) collective-permute-start(f32[16,640]{1,0:T(8,128)S(1)} %get-tuple-element.24), channel_id=1, source_target_pairs={{0,12},{4,8},{8,4},{12,0},{16,28},{20,24},{24,20},{28,16},{1,13},{... | collective-permute-start | bytes 122888 | tf_op jit(solution)/shard_map/ppermute | solution.py:293
  87.9 4.4 %collective-permute-start.21 = (f32[16,640]{1,0:T(8,128)S(1)}, f32[16,640]{1,0:T(8,128)S(1)}, u32[]{:S(2)}, u32[]{:S(2)}) collective-permute-start(f32[16,640]{1,0:T(8,128)S(1)} %get-tuple-element.25), channel_id=1, source_target_pairs={{0,8},{4,12},{8,0},{12,4},{16,24},{20,28},{24,16},{28,20},{1,9},{5... | collective-permute-start | bytes 122888 | tf_op jit(solution)/shard_map/ppermute | solution.py:293
  89.4 2.9 %collective-permute-start.20 = (f32[16,640]{1,0:T(8,128)S(1)}, f32[16,640]{1,0:T(8,128)S(1)}, u32[]{:S(2)}, u32[]{:S(2)}) collective-permute-start(f32[16,640]{1,0:T(8,128)S(1)} %get-tuple-element.26), channel_id=1, source_target_pairs={{0,4},{4,0},{8,12},{12,8},{16,20},{20,16},{24,28},{28,24},{1,5},{5... | collective-permute-start | bytes 122888 | tf_op jit(solution)/shard_map/ppermute | solution.py:293
  91.8 0.6 copy-start.5
  92.3 0.6 copy-start.6
  92.3 0.6 copy-start.7

commit v2 on v1

--- a/solution.py
+++ b/solution.py
@@ -11,7 +11,8 @@
 GAUGE_MAX = 16
 K_ITERS = 8
 HALO = TAPS + GAUGE_MAX
-BLOCK = 192
+BLOCK = 128
+STEP = 16
 CHUNK = 256
 EXTRA = 16
 F32 = jnp.float32
@@ -53,74 +54,132 @@
     return row == col
 
 
-def front_kernel(record, halo, lag, taps, projector, out, band, proj_t, strain):
-    rows = record.shape[0]
+def one_hot(shape, place):
+    row = lax.broadcasted_iota(jnp.int32, shape, 0)
+    col = lax.broadcasted_iota(jnp.int32, shape, 1)
+    return jnp.where(place(row) == col, 1.0, 0.0).astype(BF16)
+
+
+def front_kernel(first, last, *refs):
+    if first == 0:
+        record, halo, lag, band, proj_t, begun, out, strain = refs
+    else:
+        record, lag, taps, projector, out, band, proj_t, strain = refs
+        halo = begun = None
+
+        @pl.when(pl.program_id(0) == 0)
+        def _():
+            turn = one_hot((TAPS, 256), lambda tap: TAPS - tap)
+            line = dot(jnp.broadcast_to(taps[...], (8, TAPS)), turn)[0:1]
+            line = jnp.broadcast_to(line, (BLOCK + GAUGE_MAX, 256))
+            rolled = pltpu.roll(line, 0, 1, stride=1, stride_axis=0)[:, : BLOCK + HALO]
+            order = one_hot((2 * BLOCK, BLOCK + GAUGE_MAX), lambda row: row // 8 + STEP * (row % 8))
+            band[...] = dot(order, rolled.astype(BF16)).astype(BF16)
+            order = one_hot((BLOCK, BLOCK), lambda row: row // 8 + STEP * (row % 8))
+            for block in range(projector.shape[0] // BLOCK):
+                part = slice(block * BLOCK, (block + 1) * BLOCK)
+                moved = dot(order, projector[part, :])
+                proj_t[:, part] = moved.T.astype(BF16)
+
     cols = record.shape[1]
-
-    @pl.when(pl.program_id(0) == 0)
-    def _():
-        line = jnp.broadcast_to(taps[...], (BLOCK, taps.shape[1]))
-        band[...] = pltpu.roll(line, 0, 1, stride=1, stride_axis=0).astype(BF16)
-        proj_t[...] = projector[...].astype(F32).T.astype(BF16)
-
     lane = min(128, cols)
-    before = dot(band[0:GAUGE_MAX, 0:HALO], halo[...])
-    total = jnp.zeros(out.shape, F32)
-    used = 0
-    for first in range(0, rows, BLOCK):
-        size = min(BLOCK, rows - first)
-        if first == 0:
-            segment = jnp.concatenate([halo[GAUGE_MAX:HALO, :], record[0:size, :]], 0)
+    lanes = cols // lane
+    total = jnp.zeros(out.shape, F32) if begun is None else begun[...]
+    used = first * BLOCK
+    for block in range(first, last):
+        start = block * BLOCK
+        if block == 0:
+            segment = jnp.concatenate([halo[...], record[0:BLOCK, :]], 0)
         else:
-            segment = record[first - TAPS : first + size, :]
-        current = dot(band[:size, : size + TAPS], segment)
-        for c in range(0, cols, lane):
-            span = slice(c, c + lane)
-            shift = GAUGE_MAX - lag[:, span]
-            here = current[:, span]
-            wide = jnp.concatenate([before[:, span], here], 0)
-            picked = jnp.where((shift & 8) != 0, wide[8:], wide[:-8])
-            for step in (4, 2, 1):
-                moved = pltpu.roll(picked, picked.shape[0] - step, 0)
-                picked = jnp.where((shift & step) != 0, moved, picked)
-            strain[first : first + size, span] = (here - picked[:size]).astype(BF16)
-        before = current[size - GAUGE_MAX :]
-        while used < rows and min(used + CHUNK, rows) <= first + size:
-            part = slice(used, min(used + CHUNK, rows))
-            total = total + dot(proj_t[:, part], strain[part, :])
-            used = part.stop
-    out[...] = total.astype(BF16)
+            segment = record[start - HALO : start + BLOCK, :]
+        result = dot(band[...], segment)
+        for c in range(lanes):
+            span = slice(c * lane, (c + 1) * lane)
+            shift = GAUGE_MAX - lag[pl.ds(pl.program_id(0) * lanes + c, 1), :]
+            wide = result[:, span]
+            picked = wide
+            length = 2 * BLOCK
+            for step in (8, 4, 2, 1):
+                length = BLOCK + 8 * (step - 1)
+                picked = jnp.where(
+                    (shift & step) != 0, picked[8 * step : 8 * step + length], picked[:length]
+                )
+            strain[start : start + BLOCK, span] = (wide[BLOCK:] - picked).astype(BF16)
+        done = start + BLOCK
+        if done % CHUNK == 0 or block == last - 1:
+            total = total + dot(proj_t[:, used:done], strain[used:done, :])
+            used = done
+    out[...] = total.astype(out.dtype)
+
+
+def front_call(blocks, tile, args, in_specs, shape, more, scratch_rows):
+    cols = shape.shape[1]
+    specs = [pl.BlockSpec((shape.shape[0], tile), lambda i: (0, i))]
+    specs += [pl.BlockSpec(a.shape, lambda i: (0, 0)) for a in more]
+    return pl.pallas_call(
+        functools.partial(front_kernel, *blocks),
+        grid=(cols // tile,),
+        in_specs=in_specs,
+        out_specs=specs,
+        out_shape=[shape, *more],
+        scratch_shapes=[pltpu.VMEM((scratch_rows, tile), BF16)],
+        compiler_params=pltpu.CompilerParams(vmem_limit_bytes=58 * 2**20),
+        name="front",
+    )(*args)
 
 
 def front(record, halo, lag, taps, projector):
     rows, cols = record.shape
     rank = projector.shape[1]
+    lag = lag.reshape(cols // 128, 128) if cols % 128 == 0 else lag[None, :]
+    whole = lambda a: pl.BlockSpec(a.shape, lambda i: (0, 0))
+    columns = lambda count, tile: pl.BlockSpec((count, tile), lambda i: (0, i))
     tile = next((t for t in (512, 640, 256, 128) if cols % t == 0), cols)
-    whole = lambda a: pl.BlockSpec(a.shape, lambda i: (0, 0))
-    return pl.pallas_call(
-        front_kernel,
-        grid=(cols // tile,),
-        in_specs=[
-            pl.BlockSpec((rows, tile), lambda i: (0, i)),
-            pl.BlockSpec((HALO, tile), lambda i: (0, i)),
-            pl.BlockSpec((1, tile), lambda i: (0, i)),
-            whole(taps),
-            whole(projector),
+    begun, band, proj_t = front_call(
+        (1, rows // BLOCK),
+        tile,
+        (record, lag, taps, projector),
+        [columns(rows, tile), whole(lag), whole(taps), whole(projector)],
+        jax.ShapeDtypeStruct((rank, cols), F32),
+        [
+            jax.ShapeDtypeStruct((2 * BLOCK, BLOCK + HALO), BF16),
+            jax.ShapeDtypeStruct((rank, rows), BF16),
         ],
-        out_specs=pl.BlockSpec((rank, tile), lambda i: (0, i)),
-        out_shape=jax.ShapeDtypeStruct((rank, cols), BF16),
-        scratch_shapes=[
-            pltpu.VMEM((BLOCK, BLOCK + TAPS), BF16),
-            pltpu.VMEM((rank, rows), BF16),
-            pltpu.VMEM((rows, tile), BF16),
+        rows,
+    )
+    tile = next((t for t in (1280, 640, 512, 256, 128) if cols % t == 0), cols)
+    return front_call(
+        (0, 1),
+        tile,
+        (record, halo, lag, band, proj_t, begun),
+        [
+            columns(BLOCK, tile),
+            columns(HALO, tile),
+            whole(lag),
+            whole(band),
+            pl.BlockSpec((rank, BLOCK), lambda i: (0, 0)),
+            columns(rank, tile),
         ],
-        compiler_params=pltpu.CompilerParams(vmem_limit_bytes=58 * 2**20),
-        name="front",
-    )(record, halo, lag, taps, projector)
-
-
-def pair_kernel(own, other, out):
+        jax.ShapeDtypeStruct((rank, cols), BF16),
+        [],
+        BLOCK,
+    )[0]
+
+
+def fetch(sources, targets, sems):
+    copies = [
+        pltpu.make_async_copy(source, target, sems.at[i])
+        for i, (source, target) in enumerate(zip(sources, targets))
+    ]
+    for copy in copies:
+        copy.start()
+    for copy in copies:
+        copy.wait()
+
+
+def pair_kernel(own_ref, other_ref, out, own, other, sems):
     rank = own.shape[0]
+    fetch((own_ref, other_ref), (own, other), sems)
     a, b = own[...], other[...]
     aa, ab, bb = dot_nt(a, a), dot_nt(a, b), dot_nt(b, b)
     diag = eye_mask(rank)
@@ -148,14 +207,17 @@
     rank = own.shape[0]
     return pl.pallas_call(
         pair_kernel,
+        in_specs=[ANY, ANY],
+        scratch_shapes=[pltpu.VMEM(own.shape, BF16)] * 2 + [pltpu.SemaphoreType.DMA((2,))],
         out_shape=jax.ShapeDtypeStruct((2 * rank + EXTRA, rank), BF16),
         compiler_params=PARAMS,
         name="pair_gram",
     )(own, other)
 
 
-def ahead_kernel(own, sibling, partner, out):
+def ahead_kernel(own_ref, sibling_ref, partner_ref, out, own, sibling, partner, sems):
     rank = own.shape[0]
+    fetch((own_ref, sibling_ref, partner_ref), (own, sibling, partner), sems)
     there = partner[...]
     out[0:rank, :] = dot_nt(own[...], there).astype(out.dtype)
     out[rank:, :] = dot_nt(sibling[...], there).astype(out.dtype)
@@ -165,6 +227,8 @@
     rank = own.shape[0]
     return pl.pallas_call(
         ahead_kernel,
+        in_specs=[ANY] * 3,
+        scratch_shapes=[pltpu.VMEM(own.shape, BF16)] * 3 + [pltpu.SemaphoreType.DMA((3,))],
         out_shape=jax.ShapeDtypeStruct((2 * rank, rank), BF16),
         compiler_params=PARAMS,
         name="ahead_gram",
@@ -225,7 +289,7 @@
     grams, refs = refs[:count], refs[count:]
     compress_t, offset, own, other, refs = *refs[:4], refs[4:]
     if last:
-        sketch, pair, sems = refs
+        *sketch, pair, sems = refs
     else:
         sketch, mix_out, level, packed, pair, sems = refs
     rank, width = own.shape[0], pair.shape[1]
@@ -258,7 +322,13 @@
     tile = next((t for t in (640, 512, 256, 128) if width % t == 0), width)
     for c in range(0, width, tile):
         wide = dot(both, pair[:, c : c + tile])
-        sketch[:, c : c + tile] = (wide[:rows] + wide[rows:]).astype(sketch.dtype)
+        wide = wide[:rows] + wide[rows:]
+        if last:
+            share = rows // len(sketch)
+            for i, piece in enumerate(sketch):
+                piece[:, c : c + tile] = wide[i * share : (i + 1) * share]
+        else:
+            sketch[:, c : c + tile] = wide.astype(BF16)
     if not last:
         block = dot3_nt(dot3(mixing, gram + mean * eye), mixing)
         mix_out[...] = mixing
@@ -269,11 +339,13 @@
         packed[:, 3 * rank :] = low
 
 
-def filter_call(grams, compress_t, offset, own, other, width, first, last):
+def filter_call(grams, compress_t, offset, own, other, width, first, last, pieces):
     rank = own.shape[0]
     rows = compress_t.shape[0]
-    out = [jax.ShapeDtypeStruct((rows, width), F32 if last else BF16)]
-    if not last:
+    if last:
+        out = [jax.ShapeDtypeStruct((rows // pieces, width), F32)] * pieces
+    else:
+        out = [jax.ShapeDtypeStruct((rows, width), BF16)]
         out.append(jax.ShapeDtypeStruct((rank, 2 * rank), F32))
         out.append(jax.ShapeDtypeStruct((rank, rank), F32))
         out.append(jax.ShapeDtypeStruct((rank, 4 * rank), BF16))
@@ -301,18 +373,23 @@
 
 
 def join_kernel(offsets, *refs):
-    out = refs[-1]
-    width = refs[0].shape[1]
-    for i, piece in enumerate(refs[:-1]):
-        out[:, pl.ds(pl.multiple_of(offsets[i], 128), width)] = piece[...]
+    pieces, out, sems = refs[:-2], refs[-2], refs[-1]
+    width = pieces[0].shape[1]
+    targets = [
+        out.at[:, pl.ds(pl.multiple_of(offsets[i], 128), width)] for i in range(len(pieces))
+    ]
+    fetch(pieces, targets, sems)
 
 
 def join(offsets, pieces):
     share, width = pieces[0].shape
+    count = len(pieces)
     return pl.pallas_call(
         join_kernel,
-        in_specs=[SMEM] + [VMEM] * len(pieces),
-        out_shape=jax.ShapeDtypeStruct((share, width * len(pieces)), F32),
+        in_specs=[SMEM] + [ANY] * count,
+        out_specs=ANY,
+        scratch_shapes=[pltpu.SemaphoreType.DMA((count,))],
+        out_shape=jax.ShapeDtypeStruct((share, width * count), F32),
         name="join",
     )(offsets, *pieces)
 
@@ -327,8 +404,7 @@
     halo = lax.ppermute(
         record[rows - HALO :], "tm", [(source, source + 1) for source in range(count - 1)]
     )
-    taps = jnp.pad(fir_taps.astype(F32)[::-1], (1, BLOCK - 1))[None, :]
-    sketch = front(record, halo, gauge_lag[None, :], taps, projector)
+    sketch = front(record, halo, gauge_lag, fir_taps[None, :], projector)
 
     widths = []
     width = cols
@@ -376,14 +452,14 @@
             parts = gather_parts(part, "chan")
             total = sum(piece.astype(F32) for piece in parts).astype(BF16)
             ahead = total, swap(total, "tm", mask)
+        width = here if last else widths[depth]
         sketch, *kept = filter_call(
-            grams, weights, offset, sketch, other, here if last else widths[depth], first, last
+            grams, weights, offset, sketch, other, width, first, last, span
         )
     if span == 1:
         return sketch
-    width = sketch.shape[1]
-    pieces = [sketch[:share]] + [
-        swap(sketch[part * share : (part + 1) * share], "tm", part) for part in range(1, span)
+    pieces = [sketch] + [
+        swap(piece, "tm", part) for part, piece in enumerate(kept, 1)
     ]
     offsets = []
     for part in range(span):

time: 94.9 us -> 95.9 us (1.011)
  Pallas kernels: 35 us -> 42.3 us
  starting transfers between devices: 33.6 us -> 29.2 us
  local copies, waits for them, and re-layouts: 9.16 us -> 6.37 us
    pallas_call x5 -> x6, Pallas kernels: 15.3 us -> 22.6 us  [the longest x2 12.8 us: front_call(): pl.pallas_call(functools.partial(front_kernel, *blocks), grid=(cols // ti...]
    ppermute x22, starting transfers between devices: 31.2 us -> 26.9 us  [swap(): lax.ppermute(value, axis, [(source, source ^ mask) for source in range(co...]
    broadcast_in_dim x1 -> x0, local copies, waits for them, and re-layouts: 1.31 us -> none  [on_device(): sketch = front(record, halo, gauge_lag[None, :], taps, projector)]
    unnamed x17 -> x19, local copies, waits for them, and re-layouts: 4.75 us -> 5.32 us
  transfers between devices with their start and end apart: 23 -> 23, of which waited for: 9 -> 10; matrix products, arithmetic and copies ran while one was open for 4% -> 1% of each run, Pallas kernels for 15% -> 27%
where the time goes in v2:
time: 95.9 us; the launch traced here: 95.6 us
  Pallas kernels  42.3 us (44%)
  starting transfers between devices  29.2 us (30%)
  waiting for transfers between devices  16.5 us (17%)
  local copies, waits for them, and re-layouts  6.37 us (7%)
    ppermute x22, starting transfers between devices, swap(): lax.ppermute(value, axis, [(source, source ^ mask) for source in range(co...  26.9 us
    pallas_call x3, Pallas kernels, filter_call(): pl.pallas_call(functools.partial(filter_kernel, len(grams), first, last),...  19.7 us
    ppermute x22, waiting for transfers between devices, swap(): lax.ppermute(value, axis, [(source, source ^ mask) for source in range(co...  16.5 us
    pallas_call x2, Pallas kernels, front_call(): pl.pallas_call(functools.partial(front_kernel, *blocks), grid=(cols // ti...  12.8 us
    pallas_call x1, Pallas kernels, join(): pl.pallas_call(join_kernel, in_specs=[SMEM] + [ANY] * count, out_specs=AN...  6.76 us
    unnamed x19, local copies, waits for them, and re-layouts  5.32 us
    ppermute x1, starting transfers between devices, on_device(): lax.ppermute(record[rows - HALO:], 'tm', [(source, source + 1) for source...  2.38 us
  transfers between devices with their start and end apart: 23, of which 10 were waited for; matrix products, arithmetic and copies ran while one was open for 1% of the time, Pallas kernels for 27%

profile of v2, /device:TPU:0, one launch (start us, length us, event | category | flops | bytes accessed | tf_op | source)
XLA Modules:
  0.0 95.6 jit_solution(983599197384061525)
XLA Ops:
  0.0 1.0 %slice.9 = bf16[80,2560]{1,0:T(8,128)(2,1)S(1)} slice(bf16[1024,2560]{1,0:T(8,128)(2,1)} %refs_0_.3), slice={[944:1024], [0:2560]} | slice | bytes 819200 | tf_op jit(solution)/shard_map/slice | solution.py:405
  1.0 2.4 %collective-permute-start = (bf16[80,2560]{1,0:T(8,128)(2,1)S(1)}, bf16[80,2560]{1,0:T(8,128)(2,1)S(1)}, u32[]{:S(2)}, u32[]{:S(2)}) collective-permute-start(bf16[80,2560]{1,0:T(8,128)(2,1)S(1)} %slice.9), channel_id=1, source_target_pairs={{0,4},{4,8},{8,12},{12,16},{16,20},{20,24},{24,28},{1,5},{5,9},{9,... | collective-permute-start | bytes 1228808 | tf_op jit(solution)/shard_map/ppermute | solution.py:404
  3.4 9.5 %front.2 = (f32[128,2560]{1,0:T(8,128)}, bf16[256,208]{1,0:T(8,128)(2,1)}, bf16[128,1024]{1,0:T(8,128)(2,1)}) custom-call(bf16[1024,2560]{1,0:T(8,128)(2,1)} %refs_0_.3, s32[20,128]{1,0:T(8,128)} %bitcast.13, bf16[1,64]{1,0:T(2,128)(2,1)} %bitcast.15, bf16[1024,128]{1,0:T(8,128)(2,1)} %refs_3_.1), custom_call_target="tpu_custom_call" | custom-call | tf_op jit(solution)/shard_map/front/pallas_call | solution.py:119
  13.7 3.2 %front.3.own_ref.refs_6_ = bf16[128,2560]{1,0:T(8,128)(2,1)} custom-call(bf16[1024,2560]{1,0:T(8,128)(2,1)} %refs_0_.3, bf16[80,2560]{1,0:T(8,128)(2,1)} %copy-done.4, s32[20,128]{1,0:T(8,128)} %bitcast.14, bf16[256,208]{1,0:T(8,128)(2,1)} %get-tuple-element.20.refs_3_, bf16[128,1024]{1,0:T(8,128)(2,1)} %get-tuple-element.21.refs_4_, ...), custom_call_target="tpu_custom_call" | custom-call | tf_op jit(solution)/shard_map/front/pallas_call | solution.py:119
  16.9 2.6 %collective-permute-start.1 = (bf16[128,2560]{1,0:T(8,128)(2,1)}, bf16[128,2560]{1,0:T(8,128)(2,1)S(1)}, u32[]{:S(2)}, u32[]{:S(2)}) collective-permute-start(bf16[128,2560]{1,0:T(8,128)(2,1)} %front.3.own_ref.refs_6_), channel_id=1, source_target_pairs={{0,4},{4,0},{8,12},{12,8},{16,20},{20,16},{24,28},{28,24},{1,5},{5... | collective-permute-start | bytes 1966088 | tf_op jit(solution)/shard_map/ppermute | solution.py:365
  19.6 1.6 %collective-permute-start.6 = (bf16[128,2560]{1,0:T(8,128)(2,1)}, bf16[128,2560]{1,0:T(8,128)(2,1)S(1)}, u32[]{:S(2)}, u32[]{:S(2)}) collective-permute-start(bf16[128,2560]{1,0:T(8,128)(2,1)} %front.3.own_ref.refs_6_), channel_id=1, source_target_pairs={{0,8},{4,12},{8,0},{12,4},{16,24},{20,28},{24,16},{28,20},{1,9},{5... | collective-permute-start | bytes 1966088 | tf_op jit(solution)/shard_map/ppermute | solution.py:365
  21.5 1.1 %copy-done = bf16[128,2560]{1,0:T(8,128)(2,1)S(1)} copy-done((bf16[128,2560]{1,0:T(8,128)(2,1)S(1)}, bf16[128,2560]{1,0:T(8,128)(2,1)}, u32[]{:S(2)}) %copy-start) | copy-done | bytes 655384
  22.5 1.3 %pair_gram.1.refs_0_ = bf16[272,128]{1,0:T(8,128)(2,1)S(1)} custom-call(bf16[128,2560]{1,0:T(8,128)(2,1)S(1)} %copy-done, bf16[128,2560]{1,0:T(8,128)(2,1)S(1)} %collective-permute-done.1.other_ref.refs_7_.sibling_ref), custom_call_target="tpu_custom_call" | custom-call | tf_op jit(solution)/shard_map/pair_gram/pallas_call | solution.py:208
  23.8 1.7 %collective-permute-start.2 = (bf16[272,128]{1,0:T(8,128)(2,1)S(1)}, bf16[272,128]{1,0:T(8,128)(2,1)S(1)}, u32[]{:S(2)}, u32[]{:S(2)}) collective-permute-start(bf16[272,128]{1,0:T(8,128)(2,1)S(1)} %pair_gram.1.refs_0_), channel_id=1, source_target_pairs={{0,1},{1,0},{2,3},{3,2},{4,5},{5,4},{6,7},{7,6},{8,9},{9,8},{10,11... | collective-permute-start | bytes 208904 | tf_op jit(solution)/shard_map/ppermute | solution.py:365
  25.5 2.6 %collective-permute-start.3 = (bf16[272,128]{1,0:T(8,128)(2,1)S(1)}, bf16[272,128]{1,0:T(8,128)(2,1)S(1)}, u32[]{:S(2)}, u32[]{:S(2)}) collective-permute-start(bf16[272,128]{1,0:T(8,128)(2,1)S(1)} %pair_gram.1.refs_0_), channel_id=1, source_target_pairs={{0,2},{1,3},{2,0},{3,1},{4,6},{5,7},{6,4},{7,5},{8,10},{9,11},{10,... | collective-permute-start | bytes 208904 | tf_op jit(solution)/shard_map/ppermute | solution.py:365
  28.3 5.1 %collective-permute-done.3.refs_2_ = bf16[272,128]{1,0:T(8,128)(2,1)S(1)} collective-permute-done((bf16[272,128]{1,0:T(8,128)(2,1)S(1)}, bf16[272,128]{1,0:T(8,128)(2,1)S(1)}, u32[]{:S(2)}, u32[]{:S(2)}) %collective-permute-start.3) | collective-permute-done | bytes 69664 | tf_op jit(solution)/shard_map/ppermute | solution.py:365
  34.2 1.1 %copy-done.1 = bf16[128,2560]{1,0:T(8,128)(2,1)S(1)} copy-done((bf16[128,2560]{1,0:T(8,128)(2,1)S(1)}, bf16[128,2560]{1,0:T(8,128)(2,1)}, u32[]{:S(2)}) %copy-start.1) | copy-done | bytes 655384
  35.3 6.3 %sign_filter.3 = (bf16[128,1280]{1,0:T(8,128)(2,1)S(1)}, f32[128,256]{1,0:T(8,128)S(1)}, f32[128,128]{1,0:T(8,128)S(1)}, bf16[128,512]{1,0:T(8,128)(2,1)S(1)}) custom-call(bf16[272,128]{1,0:T(8,128)(2,1)S(1)} %pair_gram.1.refs_0_, bf16[272,128]{1,0:T(8,128)(2,1)S(1)} %collective-permute-done.2.refs_1_, bf16[272,128]{1,0:T(8,128)(2,1)S(1)} %collective-permute-done.3.refs_2_, ...), custom_call_target="tpu_custom_call" | custom-call | tf_op jit(solution)/shard_map/sign_filter/pallas_call | solution.py:353
  41.7 1.6 %collective-permute-start.11 = (bf16[128,1280]{1,0:T(8,128)(2,1)S(1)}, bf16[128,1280]{1,0:T(8,128)(2,1)S(1)}, u32[]{:S(2)}, u32[]{:S(2)}) collective-permute-start(bf16[128,1280]{1,0:T(8,128)(2,1)S(1)} %get-tuple-element.26.refs_7_.own_ref), channel_id=1, source_target_pairs={{0,8},{4,12},{8,0},{12,4},{16,24},{20,28},{24,16},{28,20},{1,9},{5... | collective-permute-start | bytes 983048 | tf_op jit(solution)/shard_map/ppermute | solution.py:365
  43.6 1.1 %copy-done.2 = bf16[128,2560]{1,0:T(8,128)(2,1)S(1)} copy-done((bf16[128,2560]{1,0:T(8,128)(2,1)S(1)}, bf16[128,2560]{1,0:T(8,128)(2,1)}, u32[]{:S(2)}) %copy-start.2) | copy-done | bytes 655384
  44.7 1.1 %ahead_gram.2 = bf16[256,128]{1,0:T(8,128)(2,1)S(1)} custom-call(bf16[128,2560]{1,0:T(8,128)(2,1)S(1)} %copy-done.2, bf16[128,2560]{1,0:T(8,128)(2,1)S(1)} %collective-permute-done.1.other_ref.refs_7_.sibling_ref, bf16[128,2560]{1,0:T(8,128)(2,1)S(1)} %collective-permute-done.6.partner_ref), custom_call_target="tpu_custom_call" | custom-call | tf_op jit(solution)/shard_map/ahead_gram/pallas_call | solution.py:228
  45.8 2.3 %collective-permute-start.9 = (bf16[256,128]{1,0:T(8,128)(2,1)S(1)}, bf16[256,128]{1,0:T(8,128)(2,1)S(1)}, u32[]{:S(2)}, u32[]{:S(2)}) collective-permute-start(bf16[256,128]{1,0:T(8,128)(2,1)S(1)} %ahead_gram.2), channel_id=1, source_target_pairs={{0,3},{1,2},{2,1},{3,0},{4,7},{5,6},{6,5},{7,4},{8,11},{9,10},{10,... | collective-permute-start | bytes 196616 | tf_op jit(solution)/shard_map/ppermute | solution.py:365
  48.5 1.8 %collective-permute-start.7 = (bf16[256,128]{1,0:T(8,128)(2,1)S(1)}, bf16[256,128]{1,0:T(8,128)(2,1)S(1)}, u32[]{:S(2)}, u32[]{:S(2)}) collective-permute-start(bf16[256,128]{1,0:T(8,128)(2,1)S(1)} %ahead_gram.2), channel_id=1, source_target_pairs={{0,1},{1,0},{2,3},{3,2},{4,5},{5,4},{6,7},{7,6},{8,9},{9,8},{10,11... | collective-permute-start | bytes 196616 | tf_op jit(solution)/shard_map/ppermute | solution.py:365
  52.3 1.6 %collective-permute-done.8 = bf16[256,128]{1,0:T(8,128)(2,1)S(1)} collective-permute-done((bf16[256,128]{1,0:T(8,128)(2,1)S(1)}, bf16[256,128]{1,0:T(8,128)(2,1)S(1)}, u32[]{:S(2)}, u32[]{:S(2)}) %collective-permute-start.8) | collective-permute-done | bytes 65568 | tf_op jit(solution)/shard_map/ppermute | solution.py:365
  54.1 1.9 %collective-permute-start.5 = (bf16[128,512]{1,0:T(8,128)(2,1)S(1)}, bf16[128,512]{1,0:T(8,128)(2,1)S(1)}, u32[]{:S(2)}, u32[]{:S(2)}) collective-permute-start(bf16[128,512]{1,0:T(8,128)(2,1)S(1)} %get-tuple-element.25), channel_id=1, source_target_pairs={{0,8},{4,12},{8,0},{12,4},{16,24},{20,28},{24,16},{28,20},{1,9},{5... | collective-permute-start | bytes 393224 | tf_op jit(solution)/shard_map/ppermute | solution.py:365
  56.0 2.0 %collective-permute-start.17 = (bf16[256,128]{1,0:T(8,128)(2,1)S(1)}, bf16[256,128]{1,0:T(8,128)(2,1)S(1)}, u32[]{:S(2)}, u32[]{:S(2)}) collective-permute-start(bf16[256,128]{1,0:T(8,128)(2,1)S(1)} %add_convert_fusion.1), channel_id=1, source_target_pairs={{0,3},{1,2},{2,1},{3,0},{4,7},{5,6},{6,5},{7,4},{8,11},{9,10},{10,... | collective-permute-start | bytes 196616 | tf_op jit(solution)/shard_map/ppermute | solution.py:365
  58.1 2.4 %collective-permute-start.15 = (bf16[256,128]{1,0:T(8,128)(2,1)S(1)}, bf16[256,128]{1,0:T(8,128)(2,1)S(1)}, u32[]{:S(2)}, u32[]{:S(2)}) collective-permute-start(bf16[256,128]{1,0:T(8,128)(2,1)S(1)} %add_convert_fusion.1), channel_id=1, source_target_pairs={{0,1},{1,0},{2,3},{3,2},{4,5},{5,4},{6,7},{7,6},{8,9},{9,8},{10,11... | collective-permute-start | bytes 196616 | tf_op jit(solution)/shard_map/ppermute | solution.py:365
  60.5 6.6 %sign_filter.4 = (bf16[128,640]{1,0:T(8,128)(2,1)S(1)}, f32[128,256]{1,0:T(8,128)S(1)}, f32[128,128]{1,0:T(8,128)S(1)}, bf16[128,512]{1,0:T(8,128)(2,1)S(1)}) custom-call(f32[128,256]{1,0:T(8,128)S(1)} %get-tuple-element.23.refs_0_, f32[128,128]{1,0:T(8,128)S(1)} %get-tuple-element.24.refs_1_, bf16[128,512]{1,0:T(8,128)(2,1)S(1)} %collective-permute-done.5.refs_2_, ...), custom_call_target="tpu_custom_call" | custom-call | tf_op jit(solution)/shard_map/sign_filter/pallas_call | solution.py:353
  67.1 1.4 %collective-permute-start.12 = (bf16[128,512]{1,0:T(8,128)(2,1)S(1)}, bf16[128,512]{1,0:T(8,128)(2,1)S(1)}, u32[]{:S(2)}, u32[]{:S(2)}) collective-permute-start(bf16[128,512]{1,0:T(8,128)(2,1)S(1)} %get-tuple-element.29), channel_id=1, source_target_pairs={{0,16},{4,20},{8,24},{12,28},{16,0},{20,4},{24,8},{28,12},{1,17},{... | collective-permute-start | bytes 393224 | tf_op jit(solution)/shard_map/ppermute | solution.py:365
  69.2 1.4 %collective-permute-start.18 = (bf16[256,128]{1,0:T(8,128)(2,1)S(1)}, bf16[256,128]{1,0:T(8,128)(2,1)S(1)}, u32[]{:S(2)}, u32[]{:S(2)}) collective-permute-start(bf16[256,128]{1,0:T(8,128)(2,1)S(1)} %add_convert_fusion.refs_3_), channel_id=1, source_target_pairs={{0,8},{4,12},{8,0},{12,4},{16,24},{20,28},{24,16},{28,20},{1,9},{5... | collective-permute-start | bytes 196616 | tf_op jit(solution)/shard_map/ppermute | solution.py:365
  70.6 2.9 %collective-permute-done.12.refs_2_ = bf16[128,512]{1,0:T(8,128)(2,1)S(1)} collective-permute-done((bf16[128,512]{1,0:T(8,128)(2,1)S(1)}, bf16[128,512]{1,0:T(8,128)(2,1)S(1)}, u32[]{:S(2)}, u32[]{:S(2)}) %collective-permute-start.12) | collective-permute-done | bytes 131104 | tf_op jit(solution)/shard_map/ppermute | solution.py:365
  73.6 1.8 %collective-permute-done.19.refs_8_ = bf16[128,640]{1,0:T(8,128)(2,1)S(1)} collective-permute-done((bf16[128,640]{1,0:T(8,128)(2,1)S(1)}, bf16[128,640]{1,0:T(8,128)(2,1)S(1)}, u32[]{:S(2)}, u32[]{:S(2)}) %collective-permute-start.19) | collective-permute-done | bytes 163872 | tf_op jit(solution)/shard_map/ppermute | solution.py:365
  75.4 6.8 %sign_filter.5 = (f32[16,640]{1,0:T(8,128)S(1)}, f32[16,640]{1,0:T(8,128)S(1)}, f32[16,640]{1,0:T(8,128)S(1)}, f32[16,640]{1,0:T(8,128)S(1)}) custom-call(f32[128,256]{1,0:T(8,128)S(1)} %get-tuple-element.27.refs_0_, f32[128,128]{1,0:T(8,128)S(1)} %get-tuple-element.28.refs_1_, bf16[128,512]{1,0:T(8,128)(2,1)S(1)} %collective-permute-done.12.refs_2_, ...), custom_call_target="tpu_custom_call" | custom-call | tf_op jit(solution)/shard_map/sign_filter/pallas_call | solution.py:353
  82.8 1.6 %collective-permute-start.21 = (f32[16,640]{1,0:T(8,128)S(1)}, f32[16,640]{1,0:T(8,128)S(1)}, u32[]{:S(2)}, u32[]{:S(2)}) collective-permute-start(f32[16,640]{1,0:T(8,128)S(1)} %get-tuple-element.33), channel_id=1, source_target_pairs={{0,8},{4,12},{8,0},{12,4},{16,24},{20,28},{24,16},{28,20},{1,9},{5... | collective-permute-start | bytes 122888 | tf_op jit(solution)/shard_map/ppermute | solution.py:365
  85.3 1.5 %collective-permute-done.21.refs_2_ = f32[16,640]{1,0:T(8,128)S(1)} collective-permute-done((f32[16,640]{1,0:T(8,128)S(1)}, f32[16,640]{1,0:T(8,128)S(1)}, u32[]{:S(2)}, u32[]{:S(2)}) %collective-permute-start.21) | collective-permute-done | bytes 40992 | tf_op jit(solution)/shard_map/ppermute | solution.py:365
  86.8 1.2 %collective-permute-done.22.refs_3_ = f32[16,640]{1,0:T(8,128)S(1)} collective-permute-done((f32[16,640]{1,0:T(8,128)S(1)}, f32[16,640]{1,0:T(8,128)S(1)}, u32[]{:S(2)}, u32[]{:S(2)}) %collective-permute-start.22) | collective-permute-done | bytes 40992 | tf_op jit(solution)/shard_map/ppermute | solution.py:365
  88.6 6.8 %join.1 = f32[16,2560]{1,0:T(8,128)} custom-call(s32[4]{0:T(128)} %pad_add_fusion.offsets, f32[16,640]{1,0:T(8,128)} %copy-done.3, f32[16,640]{1,0:T(8,128)} %copy-done.6, f32[16,640]{1,0:T(8,128)} %copy-done.7, f32[16,640]{1,0:T(8,128)} %copy-done.8), custom_call_target="tpu_custom_call" | custom-call | tf_op jit(solution)/shard_map/join/pallas_call | solution.py:387
  (51 shorter events, 8.0 us)
Async XLA Ops:
  1.0 11.9 %collective-permute-start = (bf16[80,2560]{1,0:T(8,128)(2,1)S(1)}, bf16[80,2560]{1,0:T(8,128)(2,1)S(1)}, u32[]{:S(2)}, u32[]{:S(2)}) collective-permute-start(bf16[80,2560]{1,0:T(8,128)(2,1)S(1)} %slice.9), channel_id=1, source_target_pairs={{0,4},{4,8},{8,12},{12,16},{16,20},{20,24},{24,28},{1,5},{5,9},{9,... | collective-permute-start | bytes 1228808 | tf_op jit(solution)/shard_map/ppermute | solution.py:404
  12.9 6.6 %copy-start.5 = (f32[256,128]{1,0:T(8,128)S(1)}, f32[256,128]{1,0:T(8,128)}, u32[]{:S(2)}) copy-start(f32[256,128]{1,0:T(8,128)} %param.9) | copy-start | bytes 393220
  12.9 0.7 copy-start.4
  16.9 4.5 %collective-permute-start.1 = (bf16[128,2560]{1,0:T(8,128)(2,1)}, bf16[128,2560]{1,0:T(8,128)(2,1)S(1)}, u32[]{:S(2)}, u32[]{:S(2)}) collective-permute-start(bf16[128,2560]{1,0:T(8,128)(2,1)} %front.3.own_ref.refs_6_), channel_id=1, source_target_pairs={{0,4},{4,0},{8,12},{12,8},{16,20},{20,16},{24,28},{28,24},{1,5},{5... | collective-permute-start | bytes 1966088 | tf_op jit(solution)/shard_map/ppermute | solution.py:365
  19.6 24.0 %collective-permute-start.6 = (bf16[128,2560]{1,0:T(8,128)(2,1)}, bf16[128,2560]{1,0:T(8,128)(2,1)S(1)}, u32[]{:S(2)}, u32[]{:S(2)}) collective-permute-start(bf16[128,2560]{1,0:T(8,128)(2,1)} %front.3.own_ref.refs_6_), channel_id=1, source_target_pairs={{0,8},{4,12},{8,0},{12,4},{16,24},{20,28},{24,16},{28,20},{1,9},{5... | collective-permute-start | bytes 1966088 | tf_op jit(solution)/shard_map/ppermute | solution.py:365
  21.4 1.1 %copy-start = (bf16[128,2560]{1,0:T(8,128)(2,1)S(1)}, bf16[128,2560]{1,0:T(8,128)(2,1)}, u32[]{:S(2)}) copy-start(bf16[128,2560]{1,0:T(8,128)(2,1)} %front.3.own_ref.refs_6_) | copy-start | bytes 1966084
  23.8 4.5 %collective-permute-start.2 = (bf16[272,128]{1,0:T(8,128)(2,1)S(1)}, bf16[272,128]{1,0:T(8,128)(2,1)S(1)}, u32[]{:S(2)}, u32[]{:S(2)}) collective-permute-start(bf16[272,128]{1,0:T(8,128)(2,1)S(1)} %pair_gram.1.refs_0_), channel_id=1, source_target_pairs={{0,1},{1,0},{2,3},{3,2},{4,5},{5,4},{6,7},{7,6},{8,9},{9,8},{10,11... | collective-permute-start | bytes 208904 | tf_op jit(solution)/shard_map/ppermute | solution.py:365
  25.5 7.9 %collective-permute-start.3 = (bf16[272,128]{1,0:T(8,128)(2,1)S(1)}, bf16[272,128]{1,0:T(8,128)(2,1)S(1)}, u32[]{:S(2)}, u32[]{:S(2)}) collective-permute-start(bf16[272,128]{1,0:T(8,128)(2,1)S(1)} %pair_gram.1.refs_0_), channel_id=1, source_target_pairs={{0,2},{1,3},{2,0},{3,1},{4,6},{5,7},{6,4},{7,5},{8,10},{9,11},{10,... | collective-permute-start | bytes 208904 | tf_op jit(solution)/shard_map/ppermute | solution.py:365
  28.0 6.2 %collective-permute-start.4 = (bf16[272,128]{1,0:T(8,128)(2,1)S(1)}, bf16[272,128]{1,0:T(8,128)(2,1)S(1)}, u32[]{:S(2)}, u32[]{:S(2)}) collective-permute-start(bf16[272,128]{1,0:T(8,128)(2,1)S(1)} %pair_gram.1.refs_0_), channel_id=1, source_target_pairs={{0,3},{1,2},{2,1},{3,0},{4,7},{5,6},{6,5},{7,4},{8,11},{9,10},{10,... | collective-permute-start | bytes 208904 | tf_op jit(solution)/shard_map/ppermute | solution.py:365
  34.2 1.1 %copy-start.1 = (bf16[128,2560]{1,0:T(8,128)(2,1)S(1)}, bf16[128,2560]{1,0:T(8,128)(2,1)}, u32[]{:S(2)}) copy-start(bf16[128,2560]{1,0:T(8,128)(2,1)} %front.3.own_ref.refs_6_) | copy-start | bytes 1966084
  41.7 8.6 %collective-permute-start.11 = (bf16[128,1280]{1,0:T(8,128)(2,1)S(1)}, bf16[128,1280]{1,0:T(8,128)(2,1)S(1)}, u32[]{:S(2)}, u32[]{:S(2)}) collective-permute-start(bf16[128,1280]{1,0:T(8,128)(2,1)S(1)} %get-tuple-element.26.refs_7_.own_ref), channel_id=1, source_target_pairs={{0,8},{4,12},{8,0},{12,4},{16,24},{20,28},{24,16},{28,20},{1,9},{5... | collective-permute-start | bytes 983048 | tf_op jit(solution)/shard_map/ppermute | solution.py:365
  43.2 7.9 %collective-permute-start.13 = (bf16[128,1280]{1,0:T(8,128)(2,1)S(1)}, bf16[128,1280]{1,0:T(8,128)(2,1)S(1)}, u32[]{:S(2)}, u32[]{:S(2)}) collective-permute-start(bf16[128,1280]{1,0:T(8,128)(2,1)S(1)} %get-tuple-element.26.refs_7_.own_ref), channel_id=1, source_target_pairs={{0,16},{4,20},{8,24},{12,28},{16,0},{20,4},{24,8},{28,12},{1,17},{... | collective-permute-start | bytes 983048 | tf_op jit(solution)/shard_map/ppermute | solution.py:365
  43.6 1.1 %copy-start.2 = (bf16[128,2560]{1,0:T(8,128)(2,1)S(1)}, bf16[128,2560]{1,0:T(8,128)(2,1)}, u32[]{:S(2)}) copy-start(bf16[128,2560]{1,0:T(8,128)(2,1)} %front.3.own_ref.refs_6_) | copy-start | bytes 1966084
  45.8 6.5 %collective-permute-start.9 = (bf16[256,128]{1,0:T(8,128)(2,1)S(1)}, bf16[256,128]{1,0:T(8,128)(2,1)S(1)}, u32[]{:S(2)}, u32[]{:S(2)}) collective-permute-start(bf16[256,128]{1,0:T(8,128)(2,1)S(1)} %ahead_gram.2), channel_id=1, source_target_pairs={{0,3},{1,2},{2,1},{3,0},{4,7},{5,6},{6,5},{7,4},{8,11},{9,10},{10,... | collective-permute-start | bytes 196616 | tf_op jit(solution)/shard_map/ppermute | solution.py:365
  48.1 5.8 %collective-permute-start.8 = (bf16[256,128]{1,0:T(8,128)(2,1)S(1)}, bf16[256,128]{1,0:T(8,128)(2,1)S(1)}, u32[]{:S(2)}, u32[]{:S(2)}) collective-permute-start(bf16[256,128]{1,0:T(8,128)(2,1)S(1)} %ahead_gram.2), channel_id=1, source_target_pairs={{0,2},{1,3},{2,0},{3,1},{4,6},{5,7},{6,4},{7,5},{8,10},{9,11},{10,... | collective-permute-start | bytes 196616 | tf_op jit(solution)/shard_map/ppermute | solution.py:365
  48.5 5.4 %collective-permute-start.7 = (bf16[256,128]{1,0:T(8,128)(2,1)S(1)}, bf16[256,128]{1,0:T(8,128)(2,1)S(1)}, u32[]{:S(2)}, u32[]{:S(2)}) collective-permute-start(bf16[256,128]{1,0:T(8,128)(2,1)S(1)} %ahead_gram.2), channel_id=1, source_target_pairs={{0,1},{1,0},{2,3},{3,2},{4,5},{5,4},{6,7},{7,6},{8,9},{9,8},{10,11... | collective-permute-start | bytes 196616 | tf_op jit(solution)/shard_map/ppermute | solution.py:365
  51.8 4.2 %collective-permute-start.14 = (bf16[256,128]{1,0:T(8,128)(2,1)S(1)}, bf16[256,128]{1,0:T(8,128)(2,1)S(1)}, u32[]{:S(2)}, u32[]{:S(2)}) collective-permute-start(bf16[256,128]{1,0:T(8,128)(2,1)S(1)} %ahead_gram.3), channel_id=1, source_target_pairs={{0,4},{4,0},{8,12},{12,8},{16,20},{20,16},{24,28},{28,24},{1,5},{5... | collective-permute-start | bytes 196616 | tf_op jit(solution)/shard_map/ppermute | solution.py:365
  54.0 6.5 %collective-permute-start.10 = (bf16[256,128]{1,0:T(8,128)(2,1)S(1)}, bf16[256,128]{1,0:T(8,128)(2,1)S(1)}, u32[]{:S(2)}, u32[]{:S(2)}) collective-permute-start(bf16[256,128]{1,0:T(8,128)(2,1)S(1)} %add_convert_fusion.2.refs_3_), channel_id=1, source_target_pairs={{0,4},{4,0},{8,12},{12,8},{16,20},{20,16},{24,28},{28,24},{1,5},{5... | collective-permute-start | bytes 196616 | tf_op jit(solution)/shard_map/ppermute | solution.py:365
  54.1 6.4 %collective-permute-start.5 = (bf16[128,512]{1,0:T(8,128)(2,1)S(1)}, bf16[128,512]{1,0:T(8,128)(2,1)S(1)}, u32[]{:S(2)}, u32[]{:S(2)}) collective-permute-start(bf16[128,512]{1,0:T(8,128)(2,1)S(1)} %get-tuple-element.25), channel_id=1, source_target_pairs={{0,8},{4,12},{8,0},{12,4},{16,24},{20,28},{24,16},{28,20},{1,9},{5... | collective-permute-start | bytes 393224 | tf_op jit(solution)/shard_map/ppermute | solution.py:365
  56.0 13.2 %collective-permute-start.17 = (bf16[256,128]{1,0:T(8,128)(2,1)S(1)}, bf16[256,128]{1,0:T(8,128)(2,1)S(1)}, u32[]{:S(2)}, u32[]{:S(2)}) collective-permute-start(bf16[256,128]{1,0:T(8,128)(2,1)S(1)} %add_convert_fusion.1), channel_id=1, source_target_pairs={{0,3},{1,2},{2,1},{3,0},{4,7},{5,6},{6,5},{7,4},{8,11},{9,10},{10,... | collective-permute-start | bytes 196616 | tf_op jit(solution)/shard_map/ppermute | solution.py:365
  58.1 11.1 %collective-permute-start.16 = (bf16[256,128]{1,0:T(8,128)(2,1)S(1)}, bf16[256,128]{1,0:T(8,128)(2,1)S(1)}, u32[]{:S(2)}, u32[]{:S(2)}) collective-permute-start(bf16[256,128]{1,0:T(8,128)(2,1)S(1)} %add_convert_fusion.1), channel_id=1, source_target_pairs={{0,2},{1,3},{2,0},{3,1},{4,6},{5,7},{6,4},{7,5},{8,10},{9,11},{10,... | collective-permute-start | bytes 196616 | tf_op jit(solution)/shard_map/ppermute | solution.py:365
  58.1 11.1 %collective-permute-start.15 = (bf16[256,128]{1,0:T(8,128)(2,1)S(1)}, bf16[256,128]{1,0:T(8,128)(2,1)S(1)}, u32[]{:S(2)}, u32[]{:S(2)}) collective-permute-start(bf16[256,128]{1,0:T(8,128)(2,1)S(1)} %add_convert_fusion.1), channel_id=1, source_target_pairs={{0,1},{1,0},{2,3},{3,2},{4,5},{5,4},{6,7},{7,6},{8,9},{9,8},{10,11... | collective-permute-start | bytes 196616 | tf_op jit(solution)/shard_map/ppermute | solution.py:365
  67.1 6.5 %collective-permute-start.12 = (bf16[128,512]{1,0:T(8,128)(2,1)S(1)}, bf16[128,512]{1,0:T(8,128)(2,1)S(1)}, u32[]{:S(2)}, u32[]{:S(2)}) collective-permute-start(bf16[128,512]{1,0:T(8,128)(2,1)S(1)} %get-tuple-element.29), channel_id=1, source_target_pairs={{0,16},{4,20},{8,24},{12,28},{16,0},{20,4},{24,8},{28,12},{1,17},{... | collective-permute-start | bytes 393224 | tf_op jit(solution)/shard_map/ppermute | solution.py:365
  68.5 7.0 %collective-permute-start.19 = (bf16[128,640]{1,0:T(8,128)(2,1)S(1)}, bf16[128,640]{1,0:T(8,128)(2,1)S(1)}, u32[]{:S(2)}, u32[]{:S(2)}) collective-permute-start(bf16[128,640]{1,0:T(8,128)(2,1)S(1)} %get-tuple-element.30.refs_7_), channel_id=1, source_target_pairs={{0,16},{4,20},{8,24},{12,28},{16,0},{20,4},{24,8},{28,12},{1,17},{... | collective-permute-start | bytes 491528 | tf_op jit(solution)/shard_map/ppermute | solution.py:365
  69.2 6.2 %collective-permute-start.18 = (bf16[256,128]{1,0:T(8,128)(2,1)S(1)}, bf16[256,128]{1,0:T(8,128)(2,1)S(1)}, u32[]{:S(2)}, u32[]{:S(2)}) collective-permute-start(bf16[256,128]{1,0:T(8,128)(2,1)S(1)} %add_convert_fusion.refs_3_), channel_id=1, source_target_pairs={{0,8},{4,12},{8,0},{12,4},{16,24},{20,28},{24,16},{28,20},{1,9},{5... | collective-permute-start | bytes 196616 | tf_op jit(solution)/shard_map/ppermute | solution.py:365
  82.2 0.6 copy-start.3
  82.8 2.5 %collective-permute-start.20 = (f32[16,640]{1,0:T(8,128)S(1)}, f32[16,640]{1,0:T(8,128)S(1)}, u32[]{:S(2)}, u32[]{:S(2)}) collective-permute-start(f32[16,640]{1,0:T(8,128)S(1)} %get-tuple-element.32), channel_id=1, source_target_pairs={{0,4},{4,0},{8,12},{12,8},{16,20},{20,16},{24,28},{28,24},{1,5},{5... | collective-permute-start | bytes 122888 | tf_op jit(solution)/shard_map/ppermute | solution.py:365
  82.8 4.0 %collective-permute-start.21 = (f32[16,640]{1,0:T(8,128)S(1)}, f32[16,640]{1,0:T(8,128)S(1)}, u32[]{:S(2)}, u32[]{:S(2)}) collective-permute-start(f32[16,640]{1,0:T(8,128)S(1)} %get-tuple-element.33), channel_id=1, source_target_pairs={{0,8},{4,12},{8,0},{12,4},{16,24},{20,28},{24,16},{28,20},{1,9},{5... | collective-permute-start | bytes 122888 | tf_op jit(solution)/shard_map/ppermute | solution.py:365
  84.5 3.5 %collective-permute-start.22 = (f32[16,640]{1,0:T(8,128)S(1)}, f32[16,640]{1,0:T(8,128)S(1)}, u32[]{:S(2)}, u32[]{:S(2)}) collective-permute-start(f32[16,640]{1,0:T(8,128)S(1)} %get-tuple-element.34), channel_id=1, source_target_pairs={{0,12},{4,8},{8,4},{12,0},{16,28},{20,24},{24,20},{28,16},{1,13},{... | collective-permute-start | bytes 122888 | tf_op jit(solution)/shard_map/ppermute | solution.py:365
  85.3 2.7 %copy-start.6 = (f32[16,640]{1,0:T(8,128)}, f32[16,640]{1,0:T(8,128)S(1)}, u32[]{:S(2)}) copy-start(f32[16,640]{1,0:T(8,128)S(1)} %collective-permute-done.20.refs_1_) | copy-start | bytes 122884
  86.8 1.2 %copy-start.7 = (f32[16,640]{1,0:T(8,128)}, f32[16,640]{1,0:T(8,128)S(1)}, u32[]{:S(2)}) copy-start(f32[16,640]{1,0:T(8,128)S(1)} %collective-permute-done.21.refs_2_) | copy-start | bytes 122884
  88.0 0.6 copy-start.8

commit v3 on v2

--- a/solution.py
+++ b/solution.py
@@ -36,10 +36,14 @@
     return high, (a - high.astype(F32)).astype(BF16)
 
 
+def dot3_split(ah, al, bh, bl):
+    rows = ah.shape[0]
+    wide = dot(jnp.concatenate([ah, al], 0), bh)
+    return wide[:rows] + (wide[rows:] + dot(ah, bl))
+
+
 def dot3(a, b):
-    ah, al = split(a)
-    bh, bl = split(b)
-    return dot(ah, bh) + (dot(ah, bl) + dot(al, bh))
+    return dot3_split(*split(a), *split(b))
 
 
 def dot3_nt(a, b):
@@ -62,9 +66,9 @@
 
 def front_kernel(first, last, *refs):
     if first == 0:
-        record, halo, lag, band, proj_t, begun, out, strain = refs
+        record, halo, lag, band, weights, begun, out, strain = refs
     else:
-        record, lag, taps, projector, out, band, proj_t, strain = refs
+        record, lag, taps, projector, out, band, head_weights, head, strain, weights = refs
         halo = begun = None
 
         @pl.when(pl.program_id(0) == 0)
@@ -78,14 +82,16 @@
             order = one_hot((BLOCK, BLOCK), lambda row: row // 8 + STEP * (row % 8))
             for block in range(projector.shape[0] // BLOCK):
                 part = slice(block * BLOCK, (block + 1) * BLOCK)
-                moved = dot(order, projector[part, :])
-                proj_t[:, part] = moved.T.astype(BF16)
+                weights[part, :] = dot(order, projector[part, :]).astype(BF16)
+            head_weights[...] = weights[0:BLOCK, :]
 
     cols = record.shape[1]
     lane = min(128, cols)
     lanes = cols // lane
-    total = jnp.zeros(out.shape, F32) if begun is None else begun[...]
+    total = None
     used = first * BLOCK
+    if first > 0:
+        head[...] = record[0:BLOCK, :]
     for block in range(first, last):
         start = block * BLOCK
         if block == 0:
@@ -104,26 +110,27 @@
                 picked = jnp.where(
                     (shift & step) != 0, picked[8 * step : 8 * step + length], picked[:length]
                 )
-            strain[start : start + BLOCK, span] = (wide[BLOCK:] - picked).astype(BF16)
+            strain[span, start : start + BLOCK] = (wide[BLOCK:] - picked).T.astype(BF16)
         done = start + BLOCK
         if done % CHUNK == 0 or block == last - 1:
-            total = total + dot(proj_t[:, used:done], strain[used:done, :])
+            part = dot(strain[:, used:done], weights[used:done, :])
+            total = part if total is None else total + part
             used = done
+    total = total.T
+    if begun is not None:
+        total = total + begun[...]
     out[...] = total.astype(out.dtype)
 
 
-def front_call(blocks, tile, args, in_specs, shape, more, scratch_rows):
-    cols = shape.shape[1]
-    specs = [pl.BlockSpec((shape.shape[0], tile), lambda i: (0, i))]
-    specs += [pl.BlockSpec(a.shape, lambda i: (0, 0)) for a in more]
+def front_call(blocks, args, in_specs, out_specs, out_shape, scratch, steps, grant):
     return pl.pallas_call(
         functools.partial(front_kernel, *blocks),
-        grid=(cols // tile,),
+        grid=(steps,),
         in_specs=in_specs,
-        out_specs=specs,
-        out_shape=[shape, *more],
-        scratch_shapes=[pltpu.VMEM((scratch_rows, tile), BF16)],
-        compiler_params=pltpu.CompilerParams(vmem_limit_bytes=58 * 2**20),
+        out_specs=out_specs,
+        out_shape=out_shape,
+        scratch_shapes=[pltpu.VMEM(shape, BF16) for shape in scratch],
+        compiler_params=pltpu.CompilerParams(vmem_limit_bytes=grant * 2**20),
         name="front",
     )(*args)
 
@@ -135,51 +142,44 @@
     whole = lambda a: pl.BlockSpec(a.shape, lambda i: (0, 0))
     columns = lambda count, tile: pl.BlockSpec((count, tile), lambda i: (0, i))
     tile = next((t for t in (512, 640, 256, 128) if cols % t == 0), cols)
-    begun, band, proj_t = front_call(
+    shapes = [
+        jax.ShapeDtypeStruct((rank, cols), F32),
+        jax.ShapeDtypeStruct((2 * BLOCK, BLOCK + HALO), BF16),
+        jax.ShapeDtypeStruct((BLOCK, rank), BF16),
+        jax.ShapeDtypeStruct((BLOCK, cols), BF16),
+    ]
+    begun, band, weights, head = front_call(
         (1, rows // BLOCK),
-        tile,
         (record, lag, taps, projector),
         [columns(rows, tile), whole(lag), whole(taps), whole(projector)],
-        jax.ShapeDtypeStruct((rank, cols), F32),
-        [
-            jax.ShapeDtypeStruct((2 * BLOCK, BLOCK + HALO), BF16),
-            jax.ShapeDtypeStruct((rank, rows), BF16),
-        ],
-        rows,
+        [columns(rank, tile), whole(shapes[1]), whole(shapes[2]), columns(BLOCK, tile)],
+        shapes,
+        [(tile, rows), (rows, rank)],
+        cols // tile,
+        58,
     )
     tile = next((t for t in (1280, 640, 512, 256, 128) if cols % t == 0), cols)
     return front_call(
         (0, 1),
-        tile,
-        (record, halo, lag, band, proj_t, begun),
+        (head, halo, lag, band, weights, begun),
         [
             columns(BLOCK, tile),
             columns(HALO, tile),
             whole(lag),
             whole(band),
-            pl.BlockSpec((rank, BLOCK), lambda i: (0, 0)),
+            whole(weights),
             columns(rank, tile),
         ],
+        columns(rank, tile),
         jax.ShapeDtypeStruct((rank, cols), BF16),
-        [],
-        BLOCK,
-    )[0]
-
-
-def fetch(sources, targets, sems):
-    copies = [
-        pltpu.make_async_copy(source, target, sems.at[i])
-        for i, (source, target) in enumerate(zip(sources, targets))
-    ]
-    for copy in copies:
-        copy.start()
-    for copy in copies:
-        copy.wait()
-
-
-def pair_kernel(own_ref, other_ref, out, own, other, sems):
+        [(tile, BLOCK)],
+        cols // tile,
+        32,
+    )
+
+
+def pair_kernel(own, other, out):
     rank = own.shape[0]
-    fetch((own_ref, other_ref), (own, other), sems)
     a, b = own[...], other[...]
     aa, ab, bb = dot_nt(a, a), dot_nt(a, b), dot_nt(b, b)
     diag = eye_mask(rank)
@@ -207,17 +207,14 @@
     rank = own.shape[0]
     return pl.pallas_call(
         pair_kernel,
-        in_specs=[ANY, ANY],
-        scratch_shapes=[pltpu.VMEM(own.shape, BF16)] * 2 + [pltpu.SemaphoreType.DMA((2,))],
         out_shape=jax.ShapeDtypeStruct((2 * rank + EXTRA, rank), BF16),
         compiler_params=PARAMS,
         name="pair_gram",
     )(own, other)
 
 
-def ahead_kernel(own_ref, sibling_ref, partner_ref, out, own, sibling, partner, sems):
+def ahead_kernel(own, sibling, partner, out):
     rank = own.shape[0]
-    fetch((own_ref, sibling_ref, partner_ref), (own, sibling, partner), sems)
     there = partner[...]
     out[0:rank, :] = dot_nt(own[...], there).astype(out.dtype)
     out[rank:, :] = dot_nt(sibling[...], there).astype(out.dtype)
@@ -227,8 +224,6 @@
     rank = own.shape[0]
     return pl.pallas_call(
         ahead_kernel,
-        in_specs=[ANY] * 3,
-        scratch_shapes=[pltpu.VMEM(own.shape, BF16)] * 3 + [pltpu.SemaphoreType.DMA((3,))],
         out_shape=jax.ShapeDtypeStruct((2 * rank, rank), BF16),
         compiler_params=PARAMS,
         name="ahead_gram",
@@ -310,9 +305,8 @@
     z = gram * lax.rsqrt(jnp.sum(gram * gram, axis=(0, 1), keepdims=True) + 1e-6)
     for _ in range(K_ITERS):
         zh, zl = split(z)
-        square = dot(zh, zh) + (dot(zh, zl) + dot(zl, zh))
-        ph, low = split(1.5 * eye - 0.5 * square)
-        z = dot(zh, ph) + (dot(zh, low) + dot(zl, ph))
+        square = dot3_split(zh, zl, zh, zl)
+        z = dot3_split(zh, zl, *split(1.5 * eye - 0.5 * square))
     mixing = dot3(compress_t[...], 0.5 * (eye + z))
     for copy in copies:
         copy.wait()
@@ -373,23 +367,18 @@
 
 
 def join_kernel(offsets, *refs):
-    pieces, out, sems = refs[:-2], refs[-2], refs[-1]
-    width = pieces[0].shape[1]
-    targets = [
-        out.at[:, pl.ds(pl.multiple_of(offsets[i], 128), width)] for i in range(len(pieces))
-    ]
-    fetch(pieces, targets, sems)
+    out = refs[-1]
+    width = refs[0].shape[1]
+    for i, piece in enumerate(refs[:-1], 1):
+        out[:, pl.ds(pl.multiple_of(offsets[i], 128), width)] = piece[...]
 
 
 def join(offsets, pieces):
     share, width = pieces[0].shape
-    count = len(pieces)
     return pl.pallas_call(
         join_kernel,
-        in_specs=[SMEM] + [ANY] * count,
-        out_specs=ANY,
-        scratch_shapes=[pltpu.SemaphoreType.DMA((count,))],
-        out_shape=jax.ShapeDtypeStruct((share, width * count), F32),
+        in_specs=[SMEM] + [VMEM] * len(pieces),
+        out_shape=jax.ShapeDtypeStruct((share, width * len(pieces)), F32),
         name="join",
     )(offsets, *pieces)
 
@@ -422,6 +411,11 @@
     compress_t = compress.T
     flipped = jnp.concatenate([compress_t[:, rank:], compress_t[:, :rank]], 1)
 
+    places = [position * 0]
+    for part in range(span):
+        source = position ^ part
+        places.append(sum([bit_of(source, bit) * (cols >> (bit + 1)) for bit in narrowed], position * 0))
+    places = jnp.stack(places).astype(jnp.int32)
     kept = ahead = None
     for depth in range(depths):
         first, last = depth == 0, depth == depths - 1
@@ -438,7 +432,7 @@
         here = sketch.shape[1]
         narrow = not last and widths[depth] < here
         offset = bit_of(position, depth) * (here // 2) if narrow else jnp.int32(0)
-        offset = jnp.reshape(offset, (1,)).astype(jnp.int32)
+        offset = places if last else jnp.reshape(offset, (1,)).astype(jnp.int32)
         other = swap(sketch, "tm", mask)
         if first:
             grams = gather_parts(pair_gram(sketch, other), "chan")
@@ -461,11 +455,7 @@
     pieces = [sketch] + [
         swap(piece, "tm", part) for part, piece in enumerate(kept, 1)
     ]
-    offsets = []
-    for part in range(span):
-        source = position ^ part
-        offsets.append(sum(bit_of(source, bit) * (cols >> (bit + 1)) for bit in narrowed))
-    return join(jnp.stack(offsets).astype(jnp.int32), pieces)
+    return join(places, pieces)
 
 
 def solution(mesh):

time: 95.9 us -> 89.8 us (0.936)
  Pallas kernels: 42.3 us -> 35.8 us
    pallas_call x6, Pallas kernels: 22.6 us -> 15.6 us  [the longest x2 12.4 us: front_call(): pl.pallas_call(functools.partial(front_kernel, *blocks), grid=(steps,), i...]
    unnamed x19 -> x23, local copies, waits for them, and re-layouts: 5.32 us -> 5.38 us
  transfers between devices with their start and end apart: 23 -> 23, of which waited for: 10 -> 9; matrix products, arithmetic and copies ran while one was open for 1% -> 2% of each run, Pallas kernels for 27% -> 28%
where the time goes in v3:
time: 89.8 us; the launch traced here: 89.4 us
  Pallas kernels  35.8 us (40%)
  starting transfers between devices  28.7 us (32%)
  waiting for transfers between devices  16.5 us (18%)
  local copies, waits for them, and re-layouts  7.32 us (8%)
    ppermute x22, starting transfers between devices, swap(): lax.ppermute(value, axis, [(source, source ^ mask) for source in range(co...  26.4 us
    pallas_call x3, Pallas kernels, filter_call(): pl.pallas_call(functools.partial(filter_kernel, len(grams), first, last),...  20.2 us
    ppermute x22, waiting for transfers between devices, swap(): lax.ppermute(value, axis, [(source, source ^ mask) for source in range(co...  16.5 us
    pallas_call x2, Pallas kernels, front_call(): pl.pallas_call(functools.partial(front_kernel, *blocks), grid=(steps,), i...  12.4 us
    unnamed x23, local copies, waits for them, and re-layouts  5.38 us
    ppermute x1, starting transfers between devices, on_device(): lax.ppermute(record[rows - HALO:], 'tm', [(source, source + 1) for source...  2.38 us
  transfers between devices with their start and end apart: 23, of which 9 were waited for; matrix products, arithmetic and copies ran while one was open for 2% of the time, Pallas kernels for 28%

profile of v3, /device:TPU:0, one launch (start us, length us, event | category | flops | bytes accessed | tf_op | source)
XLA Modules:
  0.0 89.4 jit_solution(15434229904641886078)
XLA Ops:
  0.0 1.1 %slice.9 = bf16[80,2560]{1,0:T(8,128)(2,1)S(1)} slice(bf16[1024,2560]{1,0:T(8,128)(2,1)} %refs_0_.1), slice={[944:1024], [0:2560]} | slice | bytes 819200 | tf_op jit(solution)/shard_map/slice | solution.py:394
  1.1 2.4 %collective-permute-start = (bf16[80,2560]{1,0:T(8,128)(2,1)S(1)}, bf16[80,2560]{1,0:T(8,128)(2,1)S(1)}, u32[]{:S(2)}, u32[]{:S(2)}) collective-permute-start(bf16[80,2560]{1,0:T(8,128)(2,1)S(1)} %slice.9), channel_id=1, source_target_pairs={{0,4},{4,8},{8,12},{12,16},{16,20},{20,24},{24,28},{1,5},{5,9},{9,... | collective-permute-start | bytes 1228808 | tf_op jit(solution)/shard_map/ppermute | solution.py:393
  3.5 10.7 %front.2 = (f32[128,2560]{1,0:T(8,128)}, bf16[256,208]{1,0:T(8,128)(2,1)}, bf16[128,128]{1,0:T(8,128)(2,1)}, bf16[128,2560]{1,0:T(8,128)(2,1)}) custom-call(bf16[1024,2560]{1,0:T(8,128)(2,1)} %refs_0_.1, s32[20,128]{1,0:T(8,128)} %bitcast.12, bf16[1,64]{1,0:T(2,128)(2,1)} %bitcast.15, bf16[1024,128]{1,0:T(8,128)(2,1)} %refs_3_.1), custom_call_target="tpu_custom_call" | custom-call | tf_op jit(solution)/shard_map/front/pallas_call | solution.py:126
  14.2 1.3 %copy-done = f32[128,2560]{1,0:T(8,128)S(1)} copy-done((f32[128,2560]{1,0:T(8,128)S(1)}, f32[128,2560]{1,0:T(8,128)}, u32[]{:S(2)}) %copy-start) | copy-done | bytes 1310744
  15.5 1.1 %copy-done.1 = bf16[128,2560]{1,0:T(8,128)(2,1)S(1)} copy-done((bf16[128,2560]{1,0:T(8,128)(2,1)S(1)}, bf16[128,2560]{1,0:T(8,128)(2,1)}, u32[]{:S(2)}) %copy-start.1) | copy-done | bytes 655384
  16.6 0.9 %copy-done.2 = bf16[256,208]{1,0:T(8,128)(2,1)S(1)} copy-done((bf16[256,208]{1,0:T(8,128)(2,1)S(1)}, bf16[256,208]{1,0:T(8,128)(2,1)}, u32[]{:S(2)}) %copy-start.2) | copy-done | bytes 106520
  18.2 1.8 %front.3.own.refs_6_ = bf16[128,2560]{1,0:T(8,128)(2,1)S(1)} custom-call(bf16[128,2560]{1,0:T(8,128)(2,1)S(1)} %copy-done.1, bf16[80,2560]{1,0:T(8,128)(2,1)S(1)} %collective-permute-done.refs_1_, s32[20,128]{1,0:T(8,128)S(1)} %bitcast.13, bf16[256,208]{1,0:T(8,128)(2,1)S(1)} %copy-done.2, bf16[128,128]{1,0:T(8,128)(2,1)S(1)} %copy-done.5, ...), custom_call_target="tpu_custom_call" | custom-call | tf_op jit(solution)/shard_map/front/pallas_call | solution.py:126
  20.0 2.6 %collective-permute-start.1 = (bf16[128,2560]{1,0:T(8,128)(2,1)S(1)}, bf16[128,2560]{1,0:T(8,128)(2,1)S(1)}, u32[]{:S(2)}, u32[]{:S(2)}) collective-permute-start(bf16[128,2560]{1,0:T(8,128)(2,1)S(1)} %front.3.own.refs_6_), channel_id=1, source_target_pairs={{0,4},{4,0},{8,12},{12,8},{16,20},{20,16},{24,28},{28,24},{1,5},{5... | collective-permute-start | bytes 1966088 | tf_op jit(solution)/shard_map/ppermute | solution.py:359
  22.8 1.6 %collective-permute-start.6 = (bf16[128,2560]{1,0:T(8,128)(2,1)S(1)}, bf16[128,2560]{1,0:T(8,128)(2,1)S(1)}, u32[]{:S(2)}, u32[]{:S(2)}) collective-permute-start(bf16[128,2560]{1,0:T(8,128)(2,1)S(1)} %front.3.own.refs_6_), channel_id=1, source_target_pairs={{0,8},{4,12},{8,0},{12,4},{16,24},{20,28},{24,16},{28,20},{1,9},{5... | collective-permute-start | bytes 1966088 | tf_op jit(solution)/shard_map/ppermute | solution.py:359
  24.4 0.8 pair_gram.1.refs_0_
  25.2 1.7 %collective-permute-start.2 = (bf16[272,128]{1,0:T(8,128)(2,1)S(1)}, bf16[272,128]{1,0:T(8,128)(2,1)S(1)}, u32[]{:S(2)}, u32[]{:S(2)}) collective-permute-start(bf16[272,128]{1,0:T(8,128)(2,1)S(1)} %pair_gram.1.refs_0_), channel_id=1, source_target_pairs={{0,1},{1,0},{2,3},{3,2},{4,5},{5,4},{6,7},{7,6},{8,9},{9,8},{10,11... | collective-permute-start | bytes 208904 | tf_op jit(solution)/shard_map/ppermute | solution.py:359
  26.8 2.6 %collective-permute-start.3 = (bf16[272,128]{1,0:T(8,128)(2,1)S(1)}, bf16[272,128]{1,0:T(8,128)(2,1)S(1)}, u32[]{:S(2)}, u32[]{:S(2)}) collective-permute-start(bf16[272,128]{1,0:T(8,128)(2,1)S(1)} %pair_gram.1.refs_0_), channel_id=1, source_target_pairs={{0,2},{1,3},{2,0},{3,1},{4,6},{5,7},{6,4},{7,5},{8,10},{9,11},{10,... | collective-permute-start | bytes 208904 | tf_op jit(solution)/shard_map/ppermute | solution.py:359
  30.3 4.4 %collective-permute-done.3.refs_2_ = bf16[272,128]{1,0:T(8,128)(2,1)S(1)} collective-permute-done((bf16[272,128]{1,0:T(8,128)(2,1)S(1)}, bf16[272,128]{1,0:T(8,128)(2,1)S(1)}, u32[]{:S(2)}, u32[]{:S(2)}) %collective-permute-start.3) | collective-permute-done | bytes 69664 | tf_op jit(solution)/shard_map/ppermute | solution.py:359
  34.8 0.8 collective-permute-done.4.refs_3_
  35.6 6.3 %sign_filter.3 = (bf16[128,1280]{1,0:T(8,128)(2,1)S(1)}, f32[128,256]{1,0:T(8,128)S(1)}, f32[128,128]{1,0:T(8,128)S(1)}, bf16[128,512]{1,0:T(8,128)(2,1)S(1)}) custom-call(bf16[272,128]{1,0:T(8,128)(2,1)S(1)} %pair_gram.1.refs_0_, bf16[272,128]{1,0:T(8,128)(2,1)S(1)} %collective-permute-done.2.refs_1_, bf16[272,128]{1,0:T(8,128)(2,1)S(1)} %collective-permute-done.3.refs_2_, ...), custom_call_target="tpu_custom_call" | custom-call | tf_op jit(solution)/shard_map/sign_filter/pallas_call | solution.py:347
  41.9 1.6 %collective-permute-start.11 = (bf16[128,1280]{1,0:T(8,128)(2,1)S(1)}, bf16[128,1280]{1,0:T(8,128)(2,1)S(1)}, u32[]{:S(2)}, u32[]{:S(2)}) collective-permute-start(bf16[128,1280]{1,0:T(8,128)(2,1)S(1)} %get-tuple-element.28.refs_7_.own), channel_id=1, source_target_pairs={{0,8},{4,12},{8,0},{12,4},{16,24},{20,28},{24,16},{28,20},{1,9},{5... | collective-permute-start | bytes 983048 | tf_op jit(solution)/shard_map/ppermute | solution.py:359
  44.6 2.1 %collective-permute-start.9 = (bf16[256,128]{1,0:T(8,128)(2,1)S(1)}, bf16[256,128]{1,0:T(8,128)(2,1)S(1)}, u32[]{:S(2)}, u32[]{:S(2)}) collective-permute-start(bf16[256,128]{1,0:T(8,128)(2,1)S(1)} %ahead_gram.2), channel_id=1, source_target_pairs={{0,3},{1,2},{2,1},{3,0},{4,7},{5,6},{6,5},{7,4},{8,11},{9,10},{10,... | collective-permute-start | bytes 196616 | tf_op jit(solution)/shard_map/ppermute | solution.py:359
  47.1 2.0 %collective-permute-start.7 = (bf16[256,128]{1,0:T(8,128)(2,1)S(1)}, bf16[256,128]{1,0:T(8,128)(2,1)S(1)}, u32[]{:S(2)}, u32[]{:S(2)}) collective-permute-start(bf16[256,128]{1,0:T(8,128)(2,1)S(1)} %ahead_gram.2), channel_id=1, source_target_pairs={{0,1},{1,0},{2,3},{3,2},{4,5},{5,4},{6,7},{7,6},{8,9},{9,8},{10,11... | collective-permute-start | bytes 196616 | tf_op jit(solution)/shard_map/ppermute | solution.py:359
  49.1 1.1 %collective-permute-done.11.refs_8_.sibling = bf16[128,1280]{1,0:T(8,128)(2,1)S(1)} collective-permute-done((bf16[128,1280]{1,0:T(8,128)(2,1)S(1)}, bf16[128,1280]{1,0:T(8,128)(2,1)S(1)}, u32[]{:S(2)}, u32[]{:S(2)}) %collective-permute-start.11) | collective-permute-done | bytes 327712 | tf_op jit(solution)/shard_map/ppermute | solution.py:359
  50.2 1.2 %collective-permute-done.13.partner = bf16[128,1280]{1,0:T(8,128)(2,1)S(1)} collective-permute-done((bf16[128,1280]{1,0:T(8,128)(2,1)S(1)}, bf16[128,1280]{1,0:T(8,128)(2,1)S(1)}, u32[]{:S(2)}, u32[]{:S(2)}) %collective-permute-start.13) | collective-permute-done | bytes 327712 | tf_op jit(solution)/shard_map/ppermute | solution.py:359
  52.6 1.9 %collective-permute-start.5 = (bf16[128,512]{1,0:T(8,128)(2,1)S(1)}, bf16[128,512]{1,0:T(8,128)(2,1)S(1)}, u32[]{:S(2)}, u32[]{:S(2)}) collective-permute-start(bf16[128,512]{1,0:T(8,128)(2,1)S(1)} %get-tuple-element.27), channel_id=1, source_target_pairs={{0,8},{4,12},{8,0},{12,4},{16,24},{20,28},{24,16},{28,20},{1,9},{5... | collective-permute-start | bytes 393224 | tf_op jit(solution)/shard_map/ppermute | solution.py:359
  54.6 2.0 %collective-permute-start.17 = (bf16[256,128]{1,0:T(8,128)(2,1)S(1)}, bf16[256,128]{1,0:T(8,128)(2,1)S(1)}, u32[]{:S(2)}, u32[]{:S(2)}) collective-permute-start(bf16[256,128]{1,0:T(8,128)(2,1)S(1)} %add_convert_fusion.1), channel_id=1, source_target_pairs={{0,3},{1,2},{2,1},{3,0},{4,7},{5,6},{6,5},{7,4},{8,11},{9,10},{10,... | collective-permute-start | bytes 196616 | tf_op jit(solution)/shard_map/ppermute | solution.py:359
  57.0 2.0 %collective-permute-start.15 = (bf16[256,128]{1,0:T(8,128)(2,1)S(1)}, bf16[256,128]{1,0:T(8,128)(2,1)S(1)}, u32[]{:S(2)}, u32[]{:S(2)}) collective-permute-start(bf16[256,128]{1,0:T(8,128)(2,1)S(1)} %add_convert_fusion.1), channel_id=1, source_target_pairs={{0,1},{1,0},{2,3},{3,2},{4,5},{5,4},{6,7},{7,6},{8,9},{9,8},{10,11... | collective-permute-start | bytes 196616 | tf_op jit(solution)/shard_map/ppermute | solution.py:359
  59.8 6.6 %sign_filter.4 = (bf16[128,640]{1,0:T(8,128)(2,1)S(1)}, f32[128,256]{1,0:T(8,128)S(1)}, f32[128,128]{1,0:T(8,128)S(1)}, bf16[128,512]{1,0:T(8,128)(2,1)S(1)}) custom-call(f32[128,256]{1,0:T(8,128)S(1)} %get-tuple-element.25.refs_0_, f32[128,128]{1,0:T(8,128)S(1)} %get-tuple-element.26.refs_1_, bf16[128,512]{1,0:T(8,128)(2,1)S(1)} %collective-permute-done.5.refs_2_, ...), custom_call_target="tpu_custom_call" | custom-call | tf_op jit(solution)/shard_map/sign_filter/pallas_call | solution.py:347
  67.0 1.5 %collective-permute-start.19 = (bf16[128,640]{1,0:T(8,128)(2,1)S(1)}, bf16[128,640]{1,0:T(8,128)(2,1)S(1)}, u32[]{:S(2)}, u32[]{:S(2)}) collective-permute-start(bf16[128,640]{1,0:T(8,128)(2,1)S(1)} %get-tuple-element.32.refs_7_), channel_id=1, source_target_pairs={{0,16},{4,20},{8,24},{12,28},{16,0},{20,4},{24,8},{28,12},{1,17},{... | collective-permute-start | bytes 491528 | tf_op jit(solution)/shard_map/ppermute | solution.py:359
  69.2 3.7 %collective-permute-done.12.refs_2_ = bf16[128,512]{1,0:T(8,128)(2,1)S(1)} collective-permute-done((bf16[128,512]{1,0:T(8,128)(2,1)S(1)}, bf16[128,512]{1,0:T(8,128)(2,1)S(1)}, u32[]{:S(2)}, u32[]{:S(2)}) %collective-permute-start.12) | collective-permute-done | bytes 131104 | tf_op jit(solution)/shard_map/ppermute | solution.py:359
  72.9 1.8 %collective-permute-done.19.refs_8_ = bf16[128,640]{1,0:T(8,128)(2,1)S(1)} collective-permute-done((bf16[128,640]{1,0:T(8,128)(2,1)S(1)}, bf16[128,640]{1,0:T(8,128)(2,1)S(1)}, u32[]{:S(2)}, u32[]{:S(2)}) %collective-permute-start.19) | collective-permute-done | bytes 163872 | tf_op jit(solution)/shard_map/ppermute | solution.py:359
  74.7 7.3 %sign_filter.5 = (f32[16,640]{1,0:T(8,128)S(1)}, f32[16,640]{1,0:T(8,128)S(1)}, f32[16,640]{1,0:T(8,128)S(1)}, f32[16,640]{1,0:T(8,128)S(1)}) custom-call(f32[128,256]{1,0:T(8,128)S(1)} %get-tuple-element.29.refs_0_, f32[128,128]{1,0:T(8,128)S(1)} %get-tuple-element.30.refs_1_, bf16[128,512]{1,0:T(8,128)(2,1)S(1)} %collective-permute-done.12.refs_2_, ...), custom_call_target="tpu_custom_call" | custom-call | tf_op jit(solution)/shard_map/sign_filter/pallas_call | solution.py:347
  82.7 0.9 %collective-permute-start.21 = (f32[16,640]{1,0:T(8,128)S(1)}, f32[16,640]{1,0:T(8,128)S(1)}, u32[]{:S(2)}, u32[]{:S(2)}) collective-permute-start(f32[16,640]{1,0:T(8,128)S(1)} %get-tuple-element.35), channel_id=1, source_target_pairs={{0,8},{4,12},{8,0},{12,4},{16,24},{20,28},{24,16},{28,20},{1,9},{5... | collective-permute-start | bytes 122888 | tf_op jit(solution)/shard_map/ppermute | solution.py:359
  83.6 1.0 %collective-permute-start.22 = (f32[16,640]{1,0:T(8,128)S(1)}, f32[16,640]{1,0:T(8,128)S(1)}, u32[]{:S(2)}, u32[]{:S(2)}) collective-permute-start(f32[16,640]{1,0:T(8,128)S(1)} %get-tuple-element.36), channel_id=1, source_target_pairs={{0,12},{4,8},{8,4},{12,0},{16,28},{20,24},{24,20},{28,16},{1,13},{... | collective-permute-start | bytes 122888 | tf_op jit(solution)/shard_map/ppermute | solution.py:359
  84.5 2.3 %collective-permute-done.21.refs_2_ = f32[16,640]{1,0:T(8,128)S(1)} collective-permute-done((f32[16,640]{1,0:T(8,128)S(1)}, f32[16,640]{1,0:T(8,128)S(1)}, u32[]{:S(2)}, u32[]{:S(2)}) %collective-permute-start.21) | collective-permute-done | bytes 40992 | tf_op jit(solution)/shard_map/ppermute | solution.py:359
  87.9 1.5 %join.1 = f32[16,2560]{1,0:T(8,128)} custom-call(s32[5]{0:T(128)} %copy-done.6, f32[16,640]{1,0:T(8,128)} %copy-done.4, f32[16,640]{1,0:T(8,128)} %copy-done.8, f32[16,640]{1,0:T(8,128)} %copy-done.9, f32[16,640]{1,0:T(8,128)} %copy-done.10), custom_call_target="tpu_custom_call" | custom-call | tf_op jit(solution)/shard_map/join/pallas_call | solution.py:378
  (55 shorter events, 8.7 us)
Async XLA Ops:
  0.0 14.1 %copy-start.3 = (s32[2560]{0:T(1024)S(1)}, s32[2560]{0:T(1024)}, u32[]{:S(2)}) copy-start(s32[2560]{0:T(1024)} %param.7) | copy-start | bytes 30724
  0.0 22.6 %copy-start.7 = (f32[256,128]{1,0:T(8,128)S(1)}, f32[256,128]{1,0:T(8,128)}, u32[]{:S(2)}) copy-start(f32[256,128]{1,0:T(8,128)} %param.9) | copy-start | bytes 393220
  1.1 13.1 %collective-permute-start = (bf16[80,2560]{1,0:T(8,128)(2,1)S(1)}, bf16[80,2560]{1,0:T(8,128)(2,1)S(1)}, u32[]{:S(2)}, u32[]{:S(2)}) collective-permute-start(bf16[80,2560]{1,0:T(8,128)(2,1)S(1)} %slice.9), channel_id=1, source_target_pairs={{0,4},{4,8},{8,12},{12,16},{16,20},{20,24},{24,28},{1,5},{5,9},{9,... | collective-permute-start | bytes 1228808 | tf_op jit(solution)/shard_map/ppermute | solution.py:393
  14.2 1.3 %copy-start = (f32[128,2560]{1,0:T(8,128)S(1)}, f32[128,2560]{1,0:T(8,128)}, u32[]{:S(2)}) copy-start(f32[128,2560]{1,0:T(8,128)} %get-tuple-element.24.refs_5_) | copy-start | bytes 3932164
  15.5 1.1 %copy-start.1 = (bf16[128,2560]{1,0:T(8,128)(2,1)S(1)}, bf16[128,2560]{1,0:T(8,128)(2,1)}, u32[]{:S(2)}) copy-start(bf16[128,2560]{1,0:T(8,128)(2,1)} %get-tuple-element.21.refs_0_) | copy-start | bytes 1966084
  16.6 0.9 %copy-start.2 = (bf16[256,208]{1,0:T(8,128)(2,1)S(1)}, bf16[256,208]{1,0:T(8,128)(2,1)}, u32[]{:S(2)}) copy-start(bf16[256,208]{1,0:T(8,128)(2,1)} %get-tuple-element.22.refs_3_) | copy-start | bytes 319492
  17.5 0.8 copy-start.5
  20.0 4.4 %collective-permute-start.1 = (bf16[128,2560]{1,0:T(8,128)(2,1)S(1)}, bf16[128,2560]{1,0:T(8,128)(2,1)S(1)}, u32[]{:S(2)}, u32[]{:S(2)}) collective-permute-start(bf16[128,2560]{1,0:T(8,128)(2,1)S(1)} %front.3.own.refs_6_), channel_id=1, source_target_pairs={{0,4},{4,0},{8,12},{12,8},{16,20},{20,16},{24,28},{28,24},{1,5},{5... | collective-permute-start | bytes 1966088 | tf_op jit(solution)/shard_map/ppermute | solution.py:359
  22.8 21.3 %collective-permute-start.6 = (bf16[128,2560]{1,0:T(8,128)(2,1)S(1)}, bf16[128,2560]{1,0:T(8,128)(2,1)S(1)}, u32[]{:S(2)}, u32[]{:S(2)}) collective-permute-start(bf16[128,2560]{1,0:T(8,128)(2,1)S(1)} %front.3.own.refs_6_), channel_id=1, source_target_pairs={{0,8},{4,12},{8,0},{12,4},{16,24},{20,28},{24,16},{28,20},{1,9},{5... | collective-permute-start | bytes 1966088 | tf_op jit(solution)/shard_map/ppermute | solution.py:359
  25.2 5.2 %collective-permute-start.2 = (bf16[272,128]{1,0:T(8,128)(2,1)S(1)}, bf16[272,128]{1,0:T(8,128)(2,1)S(1)}, u32[]{:S(2)}, u32[]{:S(2)}) collective-permute-start(bf16[272,128]{1,0:T(8,128)(2,1)S(1)} %pair_gram.1.refs_0_), channel_id=1, source_target_pairs={{0,1},{1,0},{2,3},{3,2},{4,5},{5,4},{6,7},{7,6},{8,9},{9,8},{10,11... | collective-permute-start | bytes 208904 | tf_op jit(solution)/shard_map/ppermute | solution.py:359
  26.8 7.9 %collective-permute-start.3 = (bf16[272,128]{1,0:T(8,128)(2,1)S(1)}, bf16[272,128]{1,0:T(8,128)(2,1)S(1)}, u32[]{:S(2)}, u32[]{:S(2)}) collective-permute-start(bf16[272,128]{1,0:T(8,128)(2,1)S(1)} %pair_gram.1.refs_0_), channel_id=1, source_target_pairs={{0,2},{1,3},{2,0},{3,1},{4,6},{5,7},{6,4},{7,5},{8,10},{9,11},{10,... | collective-permute-start | bytes 208904 | tf_op jit(solution)/shard_map/ppermute | solution.py:359
  29.4 6.2 %collective-permute-start.4 = (bf16[272,128]{1,0:T(8,128)(2,1)S(1)}, bf16[272,128]{1,0:T(8,128)(2,1)S(1)}, u32[]{:S(2)}, u32[]{:S(2)}) collective-permute-start(bf16[272,128]{1,0:T(8,128)(2,1)S(1)} %pair_gram.1.refs_0_), channel_id=1, source_target_pairs={{0,3},{1,2},{2,1},{3,0},{4,7},{5,6},{6,5},{7,4},{8,11},{9,10},{10,... | collective-permute-start | bytes 208904 | tf_op jit(solution)/shard_map/ppermute | solution.py:359
  41.9 8.3 %collective-permute-start.11 = (bf16[128,1280]{1,0:T(8,128)(2,1)S(1)}, bf16[128,1280]{1,0:T(8,128)(2,1)S(1)}, u32[]{:S(2)}, u32[]{:S(2)}) collective-permute-start(bf16[128,1280]{1,0:T(8,128)(2,1)S(1)} %get-tuple-element.28.refs_7_.own), channel_id=1, source_target_pairs={{0,8},{4,12},{8,0},{12,4},{16,24},{20,28},{24,16},{28,20},{1,9},{5... | collective-permute-start | bytes 983048 | tf_op jit(solution)/shard_map/ppermute | solution.py:359
  43.5 7.9 %collective-permute-start.13 = (bf16[128,1280]{1,0:T(8,128)(2,1)S(1)}, bf16[128,1280]{1,0:T(8,128)(2,1)S(1)}, u32[]{:S(2)}, u32[]{:S(2)}) collective-permute-start(bf16[128,1280]{1,0:T(8,128)(2,1)S(1)} %get-tuple-element.28.refs_7_.own), channel_id=1, source_target_pairs={{0,16},{4,20},{8,24},{12,28},{16,0},{20,4},{24,8},{28,12},{1,17},{... | collective-permute-start | bytes 983048 | tf_op jit(solution)/shard_map/ppermute | solution.py:359
  44.6 7.2 %collective-permute-start.9 = (bf16[256,128]{1,0:T(8,128)(2,1)S(1)}, bf16[256,128]{1,0:T(8,128)(2,1)S(1)}, u32[]{:S(2)}, u32[]{:S(2)}) collective-permute-start(bf16[256,128]{1,0:T(8,128)(2,1)S(1)} %ahead_gram.2), channel_id=1, source_target_pairs={{0,3},{1,2},{2,1},{3,0},{4,7},{5,6},{6,5},{7,4},{8,11},{9,10},{10,... | collective-permute-start | bytes 196616 | tf_op jit(solution)/shard_map/ppermute | solution.py:359
  46.7 5.8 %collective-permute-start.8 = (bf16[256,128]{1,0:T(8,128)(2,1)S(1)}, bf16[256,128]{1,0:T(8,128)(2,1)S(1)}, u32[]{:S(2)}, u32[]{:S(2)}) collective-permute-start(bf16[256,128]{1,0:T(8,128)(2,1)S(1)} %ahead_gram.2), channel_id=1, source_target_pairs={{0,2},{1,3},{2,0},{3,1},{4,6},{5,7},{6,4},{7,5},{8,10},{9,11},{10,... | collective-permute-start | bytes 196616 | tf_op jit(solution)/shard_map/ppermute | solution.py:359
  47.1 5.4 %collective-permute-start.7 = (bf16[256,128]{1,0:T(8,128)(2,1)S(1)}, bf16[256,128]{1,0:T(8,128)(2,1)S(1)}, u32[]{:S(2)}, u32[]{:S(2)}) collective-permute-start(bf16[256,128]{1,0:T(8,128)(2,1)S(1)} %ahead_gram.2), channel_id=1, source_target_pairs={{0,1},{1,0},{2,3},{3,2},{4,5},{5,4},{6,7},{7,6},{8,9},{9,8},{10,11... | collective-permute-start | bytes 196616 | tf_op jit(solution)/shard_map/ppermute | solution.py:359
  49.1 38.1 %copy-start.6 = (s32[5]{0:T(128)}, s32[5]{0:T(128)S(1)}, u32[]{:S(2)}) copy-start(s32[5]{0:T(128)S(1)} %stack.19.refs_6_.offsets) | copy-start | bytes 64
  51.8 2.8 %collective-permute-start.14 = (bf16[256,128]{1,0:T(8,128)(2,1)S(1)}, bf16[256,128]{1,0:T(8,128)(2,1)S(1)}, u32[]{:S(2)}, u32[]{:S(2)}) collective-permute-start(bf16[256,128]{1,0:T(8,128)(2,1)S(1)} %ahead_gram.3), channel_id=1, source_target_pairs={{0,4},{4,0},{8,12},{12,8},{16,20},{20,16},{24,28},{28,24},{1,5},{5... | collective-permute-start | bytes 196616 | tf_op jit(solution)/shard_map/ppermute | solution.py:359
  52.6 7.2 %collective-permute-start.10 = (bf16[256,128]{1,0:T(8,128)(2,1)S(1)}, bf16[256,128]{1,0:T(8,128)(2,1)S(1)}, u32[]{:S(2)}, u32[]{:S(2)}) collective-permute-start(bf16[256,128]{1,0:T(8,128)(2,1)S(1)} %add_convert_fusion.2.refs_3_), channel_id=1, source_target_pairs={{0,4},{4,0},{8,12},{12,8},{16,20},{20,16},{24,28},{28,24},{1,5},{5... | collective-permute-start | bytes 196616 | tf_op jit(solution)/shard_map/ppermute | solution.py:359
  52.6 7.2 %collective-permute-start.5 = (bf16[128,512]{1,0:T(8,128)(2,1)S(1)}, bf16[128,512]{1,0:T(8,128)(2,1)S(1)}, u32[]{:S(2)}, u32[]{:S(2)}) collective-permute-start(bf16[128,512]{1,0:T(8,128)(2,1)S(1)} %get-tuple-element.27), channel_id=1, source_target_pairs={{0,8},{4,12},{8,0},{12,4},{16,24},{20,28},{24,16},{28,20},{1,9},{5... | collective-permute-start | bytes 393224 | tf_op jit(solution)/shard_map/ppermute | solution.py:359
  54.6 13.9 %collective-permute-start.17 = (bf16[256,128]{1,0:T(8,128)(2,1)S(1)}, bf16[256,128]{1,0:T(8,128)(2,1)S(1)}, u32[]{:S(2)}, u32[]{:S(2)}) collective-permute-start(bf16[256,128]{1,0:T(8,128)(2,1)S(1)} %add_convert_fusion.1), channel_id=1, source_target_pairs={{0,3},{1,2},{2,1},{3,0},{4,7},{5,6},{6,5},{7,4},{8,11},{9,10},{10,... | collective-permute-start | bytes 196616 | tf_op jit(solution)/shard_map/ppermute | solution.py:359
  56.6 11.9 %collective-permute-start.16 = (bf16[256,128]{1,0:T(8,128)(2,1)S(1)}, bf16[256,128]{1,0:T(8,128)(2,1)S(1)}, u32[]{:S(2)}, u32[]{:S(2)}) collective-permute-start(bf16[256,128]{1,0:T(8,128)(2,1)S(1)} %add_convert_fusion.1), channel_id=1, source_target_pairs={{0,2},{1,3},{2,0},{3,1},{4,6},{5,7},{6,4},{7,5},{8,10},{9,11},{10,... | collective-permute-start | bytes 196616 | tf_op jit(solution)/shard_map/ppermute | solution.py:359
  57.0 11.5 %collective-permute-start.15 = (bf16[256,128]{1,0:T(8,128)(2,1)S(1)}, bf16[256,128]{1,0:T(8,128)(2,1)S(1)}, u32[]{:S(2)}, u32[]{:S(2)}) collective-permute-start(bf16[256,128]{1,0:T(8,128)(2,1)S(1)} %add_convert_fusion.1), channel_id=1, source_target_pairs={{0,1},{1,0},{2,3},{3,2},{4,5},{5,4},{6,7},{7,6},{8,9},{9,8},{10,11... | collective-permute-start | bytes 196616 | tf_op jit(solution)/shard_map/ppermute | solution.py:359
  66.4 6.5 %collective-permute-start.12 = (bf16[128,512]{1,0:T(8,128)(2,1)S(1)}, bf16[128,512]{1,0:T(8,128)(2,1)S(1)}, u32[]{:S(2)}, u32[]{:S(2)}) collective-permute-start(bf16[128,512]{1,0:T(8,128)(2,1)S(1)} %get-tuple-element.31), channel_id=1, source_target_pairs={{0,16},{4,20},{8,24},{12,28},{16,0},{20,4},{24,8},{28,12},{1,17},{... | collective-permute-start | bytes 393224 | tf_op jit(solution)/shard_map/ppermute | solution.py:359
  67.0 7.7 %collective-permute-start.19 = (bf16[128,640]{1,0:T(8,128)(2,1)S(1)}, bf16[128,640]{1,0:T(8,128)(2,1)S(1)}, u32[]{:S(2)}, u32[]{:S(2)}) collective-permute-start(bf16[128,640]{1,0:T(8,128)(2,1)S(1)} %get-tuple-element.32.refs_7_), channel_id=1, source_target_pairs={{0,16},{4,20},{8,24},{12,28},{16,0},{20,4},{24,8},{28,12},{1,17},{... | collective-permute-start | bytes 491528 | tf_op jit(solution)/shard_map/ppermute | solution.py:359
  68.6 6.2 %collective-permute-start.18 = (bf16[256,128]{1,0:T(8,128)(2,1)S(1)}, bf16[256,128]{1,0:T(8,128)(2,1)S(1)}, u32[]{:S(2)}, u32[]{:S(2)}) collective-permute-start(bf16[256,128]{1,0:T(8,128)(2,1)S(1)} %add_convert_fusion.refs_3_), channel_id=1, source_target_pairs={{0,8},{4,12},{8,0},{12,4},{16,24},{20,28},{24,16},{28,20},{1,9},{5... | collective-permute-start | bytes 196616 | tf_op jit(solution)/shard_map/ppermute | solution.py:359
  82.0 0.6 copy-start.4
  82.7 1.9 %collective-permute-start.20 = (f32[16,640]{1,0:T(8,128)S(1)}, f32[16,640]{1,0:T(8,128)S(1)}, u32[]{:S(2)}, u32[]{:S(2)}) collective-permute-start(f32[16,640]{1,0:T(8,128)S(1)} %get-tuple-element.34), channel_id=1, source_target_pairs={{0,4},{4,0},{8,12},{12,8},{16,20},{20,16},{24,28},{28,24},{1,5},{5... | collective-permute-start | bytes 122888 | tf_op jit(solution)/shard_map/ppermute | solution.py:359
  82.7 4.1 %collective-permute-start.21 = (f32[16,640]{1,0:T(8,128)S(1)}, f32[16,640]{1,0:T(8,128)S(1)}, u32[]{:S(2)}, u32[]{:S(2)}) collective-permute-start(f32[16,640]{1,0:T(8,128)S(1)} %get-tuple-element.35), channel_id=1, source_target_pairs={{0,8},{4,12},{8,0},{12,4},{16,24},{20,28},{24,16},{28,20},{1,9},{5... | collective-permute-start | bytes 122888 | tf_op jit(solution)/shard_map/ppermute | solution.py:359
  83.6 3.7 %collective-permute-start.22 = (f32[16,640]{1,0:T(8,128)S(1)}, f32[16,640]{1,0:T(8,128)S(1)}, u32[]{:S(2)}, u32[]{:S(2)}) collective-permute-start(f32[16,640]{1,0:T(8,128)S(1)} %get-tuple-element.36), channel_id=1, source_target_pairs={{0,12},{4,8},{8,4},{12,0},{16,28},{20,24},{24,20},{28,16},{1,13},{... | collective-permute-start | bytes 122888 | tf_op jit(solution)/shard_map/ppermute | solution.py:359
  84.5 2.7 %copy-start.8 = (f32[16,640]{1,0:T(8,128)}, f32[16,640]{1,0:T(8,128)S(1)}, u32[]{:S(2)}) copy-start(f32[16,640]{1,0:T(8,128)S(1)} %collective-permute-done.20.refs_1_) | copy-start | bytes 122884
  (2 other events, 1.2 us)

commit v4 on v3

--- a/solution.py
+++ b/solution.py
@@ -18,6 +18,7 @@
 F32 = jnp.float32
 BF16 = jnp.bfloat16
 ANY = pl.BlockSpec(memory_space=pl.ANY)
+HBM = pl.BlockSpec(memory_space=pltpu.HBM)
 SMEM = pl.BlockSpec(memory_space=pltpu.SMEM)
 VMEM = pl.BlockSpec(memory_space=pltpu.VMEM)
 PARAMS = pltpu.CompilerParams(vmem_limit_bytes=40 * 2**20)
@@ -66,13 +67,23 @@
 
 def front_kernel(first, last, *refs):
     if first == 0:
-        record, halo, lag, band, weights, begun, out, strain = refs
+        record, halo, lag, band, weights, begun, side, out, send, strain = refs
     else:
-        record, lag, taps, projector, out, band, head_weights, head, strain, weights = refs
+        record, lag_ref, taps_ref, projector_ref, out, band, head_weights, head = refs[:8]
+        strain, weights, lag, taps, projector, sems = refs[8:]
         halo = begun = None
 
         @pl.when(pl.program_id(0) == 0)
         def _():
+            sources, targets = (lag_ref, taps_ref, projector_ref), (lag, taps, projector)
+            copies = [
+                pltpu.make_async_copy(source, target, sems.at[i])
+                for i, (source, target) in enumerate(zip(sources, targets))
+            ]
+            for copy in copies:
+                copy.start()
+            for copy in copies:
+                copy.wait()
             turn = one_hot((TAPS, 256), lambda tap: TAPS - tap)
             line = dot(jnp.broadcast_to(taps[...], (8, TAPS)), turn)[0:1]
             line = jnp.broadcast_to(line, (BLOCK + GAUGE_MAX, 256))
@@ -82,44 +93,53 @@
             order = one_hot((BLOCK, BLOCK), lambda row: row // 8 + STEP * (row % 8))
             for block in range(projector.shape[0] // BLOCK):
                 part = slice(block * BLOCK, (block + 1) * BLOCK)
-                weights[part, :] = dot(order, projector[part, :]).astype(BF16)
-            head_weights[...] = weights[0:BLOCK, :]
+                weights[:, part] = dot(order, projector[part, :]).T.astype(BF16)
+            head_weights[...] = weights[:, 0:BLOCK]
 
     cols = record.shape[1]
     lane = min(128, cols)
     lanes = cols // lane
+    group = 256 if cols % 256 == 0 else lane
     total = None
     used = first * BLOCK
     if first > 0:
         head[...] = record[0:BLOCK, :]
     for block in range(first, last):
         start = block * BLOCK
-        if block == 0:
-            segment = jnp.concatenate([halo[...], record[0:BLOCK, :]], 0)
-        else:
-            segment = record[start - HALO : start + BLOCK, :]
-        result = dot(band[...], segment)
-        for c in range(lanes):
-            span = slice(c * lane, (c + 1) * lane)
-            shift = GAUGE_MAX - lag[pl.ds(pl.program_id(0) * lanes + c, 1), :]
-            wide = result[:, span]
-            picked = wide
-            length = 2 * BLOCK
-            for step in (8, 4, 2, 1):
-                length = BLOCK + 8 * (step - 1)
-                picked = jnp.where(
-                    (shift & step) != 0, picked[8 * step : 8 * step + length], picked[:length]
+        for g in range(0, cols, group):
+            if block == 0:
+                segment = jnp.concatenate([halo[:, g : g + group], record[0:BLOCK, g : g + group]], 0)
+            else:
+                segment = record[start - HALO : start + BLOCK, g : g + group]
+            result = dot(band[...], segment)
+            for c in range(0, group, lane):
+                line = pl.program_id(0) * lanes + (g + c) // lane
+                shift = GAUGE_MAX - lag[pl.ds(line, 1), :]
+                wide = result[:, c : c + lane]
+                picked = wide
+                for step in (8, 4, 2, 1):
+                    length = BLOCK + 8 * (step - 1)
+                    picked = jnp.where(
+                        (shift & step) != 0, picked[8 * step : 8 * step + length], picked[:length]
+                    )
+                strain[start : start + BLOCK, g + c : g + c + lane] = (wide[BLOCK:] - picked).astype(
+                    BF16
                 )
-            strain[span, start : start + BLOCK] = (wide[BLOCK:] - picked).T.astype(BF16)
         done = start + BLOCK
         if done % CHUNK == 0 or block == last - 1:
-            part = dot(strain[:, used:done], weights[used:done, :])
+            part = dot(weights[:, used:done], strain[used:done, :])
             total = part if total is None else total + part
             used = done
-    total = total.T
-    if begun is not None:
-        total = total + begun[...]
-    out[...] = total.astype(out.dtype)
+    if begun is None:
+        out[...] = total
+    else:
+        total = (total + begun[...]).astype(BF16)
+        out[...] = total
+        if send.shape[1] == cols:
+
+            @pl.when(pl.program_id(0) == side[0])
+            def _():
+                send[...] = total
 
 
 def front_call(blocks, args, in_specs, out_specs, out_shape, scratch, steps, grant):
@@ -129,13 +149,14 @@
         in_specs=in_specs,
         out_specs=out_specs,
         out_shape=out_shape,
-        scratch_shapes=[pltpu.VMEM(shape, BF16) for shape in scratch],
+        scratch_shapes=scratch,
         compiler_params=pltpu.CompilerParams(vmem_limit_bytes=grant * 2**20),
+        cost_estimate=cost(100 * (blocks[1] - blocks[0]) * BLOCK * BLOCK * args[0].shape[1] * 2),
         name="front",
     )(*args)
 
 
-def front(record, halo, lag, taps, projector):
+def front(record, halo, lag, taps, projector, side):
     rows, cols = record.shape
     rank = projector.shape[1]
     lag = lag.reshape(cols // 128, 128) if cols % 128 == 0 else lag[None, :]
@@ -145,23 +166,31 @@
     shapes = [
         jax.ShapeDtypeStruct((rank, cols), F32),
         jax.ShapeDtypeStruct((2 * BLOCK, BLOCK + HALO), BF16),
-        jax.ShapeDtypeStruct((BLOCK, rank), BF16),
+        jax.ShapeDtypeStruct((rank, BLOCK), BF16),
         jax.ShapeDtypeStruct((BLOCK, cols), BF16),
     ]
     begun, band, weights, head = front_call(
         (1, rows // BLOCK),
         (record, lag, taps, projector),
-        [columns(rows, tile), whole(lag), whole(taps), whole(projector)],
+        [columns(rows, tile), HBM, HBM, HBM],
         [columns(rank, tile), whole(shapes[1]), whole(shapes[2]), columns(BLOCK, tile)],
         shapes,
-        [(tile, rows), (rows, rank)],
+        [
+            pltpu.VMEM((rows, tile), BF16),
+            pltpu.VMEM((rank, rows), BF16),
+            pltpu.VMEM(lag.shape, lag.dtype),
+            pltpu.VMEM(taps.shape, BF16),
+            pltpu.VMEM(projector.shape, BF16),
+            pltpu.SemaphoreType.DMA((3,)),
+        ],
         cols // tile,
-        58,
-    )
-    tile = next((t for t in (1280, 640, 512, 256, 128) if cols % t == 0), cols)
+        50,
+    )
+    halves = cols % 256 == 0
+    tile = cols // 2 if halves else cols
     return front_call(
         (0, 1),
-        (head, halo, lag, band, weights, begun),
+        (head, halo, lag, band, weights, begun, side),
         [
             columns(BLOCK, tile),
             columns(HALO, tile),
@@ -169,10 +198,14 @@
             whole(band),
             whole(weights),
             columns(rank, tile),
+            SMEM,
         ],
-        columns(rank, tile),
-        jax.ShapeDtypeStruct((rank, cols), BF16),
-        [(tile, BLOCK)],
+        [columns(rank, tile), pl.BlockSpec((rank, tile if halves else 128), lambda i: (0, 0))],
+        [
+            jax.ShapeDtypeStruct((rank, cols), BF16),
+            jax.ShapeDtypeStruct((rank, tile if halves else 128), BF16),
+        ],
+        [pltpu.VMEM((BLOCK, tile), BF16)],
         cols // tile,
         32,
     )
@@ -213,21 +246,24 @@
     )(own, other)
 
 
-def ahead_kernel(own, sibling, partner, out):
+def ahead_kernel(own, sibling, partner, start, _, out):
     rank = own.shape[0]
     there = partner[...]
-    out[0:rank, :] = dot_nt(own[...], there).astype(out.dtype)
-    out[rank:, :] = dot_nt(sibling[...], there).astype(out.dtype)
-
-
-def ahead_gram(own, sibling, partner):
+    width = there.shape[1]
+    span = slice(None) if width == own.shape[1] else pl.ds(pl.multiple_of(start[0], 128), width)
+    out[0:rank, :] = dot_nt(own[:, span], there).astype(out.dtype)
+    out[rank:, :] = dot_nt(sibling[:, span], there).astype(out.dtype)
+
+
+def ahead_gram(own, sibling, partner, start, after):
     rank = own.shape[0]
     return pl.pallas_call(
         ahead_kernel,
+        in_specs=[VMEM, VMEM, VMEM, SMEM, ANY],
         out_shape=jax.ShapeDtypeStruct((2 * rank, rank), BF16),
         compiler_params=PARAMS,
         name="ahead_gram",
-    )(own, sibling, partner)
+    )(own, sibling, partner, start, after)
 
 
 def summed(parts):
@@ -258,7 +294,7 @@
     return square_of(aa, ab, bb), mean
 
 
-def later_gram(own_mix, own_level, packed, ahead, sibling_ahead):
+def later_gram(own_mix, own_level, packed, ahead, sibling_ahead, *other_half):
     rank = own_mix.shape[0]
     mine, theirs = ahead[...], sibling_ahead[...]
     cross = jnp.concatenate(
@@ -268,6 +304,11 @@
         ],
         0,
     )
+    if other_half:
+        first, second = (ref[...].astype(F32) for ref in other_half)
+        blocks = ((first[:rank], first[rank:]), (second[rank:], second[:rank]))
+        turned = [jnp.concatenate([block.T for block in row], 1) for row in blocks]
+        cross = (cross.astype(F32) + jnp.concatenate(turned, 0)).astype(BF16)
     high, low = split(own_mix[...])
     half = dot(high, cross) + dot(low, cross)
     high, low = split(half)
@@ -282,7 +323,7 @@
 
 def filter_kernel(count, first, last, *refs):
     grams, refs = refs[:count], refs[count:]
-    compress_t, offset, own, other, refs = *refs[:4], refs[4:]
+    compress_t, offset, own, other, _, refs = *refs[:5], refs[5:]
     if last:
         *sketch, pair, sems = refs
     else:
@@ -333,7 +374,11 @@
         packed[:, 3 * rank :] = low
 
 
-def filter_call(grams, compress_t, offset, own, other, width, first, last, pieces):
+def cost(flops, bytes_accessed=0):
+    return pl.CostEstimate(flops=int(flops), bytes_accessed=int(bytes_accessed), transcendentals=0)
+
+
+def filter_call(grams, compress_t, offset, own, other, before, width, first, last, pieces):
     rank = own.shape[0]
     rows = compress_t.shape[0]
     if last:
@@ -346,12 +391,13 @@
     args = [*grams, compress_t]
     return pl.pallas_call(
         functools.partial(filter_kernel, len(grams), first, last),
-        in_specs=[VMEM] * len(args) + [SMEM, ANY, ANY],
+        in_specs=[VMEM] * len(args) + [SMEM, ANY, ANY, ANY],
         out_shape=out,
         scratch_shapes=[pltpu.VMEM((2 * rank, width), BF16), pltpu.SemaphoreType.DMA((2,))],
         compiler_params=PARAMS,
+        cost_estimate=cost(50 * K_ITERS * (2 * rank) ** 3),
         name="sign_filter",
-    )(*args, offset, own, other)
+    )(*args, offset, own, other, before)
 
 
 def swap(value, axis, mask):
@@ -393,7 +439,10 @@
     halo = lax.ppermute(
         record[rows - HALO :], "tm", [(source, source + 1) for source in range(count - 1)]
     )
-    sketch = front(record, halo, gauge_lag, fir_taps[None, :], projector)
+    side = position // 2 % 2
+    sketch, half = front(
+        record, halo, gauge_lag, fir_taps[None, :], projector, jnp.reshape(1 - side, (1,)).astype(jnp.int32)
+    )
 
     widths = []
     width = cols
@@ -439,17 +488,30 @@
         else:
             mixing, level, packed = kept
             grams = [mixing, level, swap(packed, "tm", mask), *ahead]
-        if not last:
-            part = ahead_gram(sketch, other, swap(sketch, "tm", 2 * mask))
-            for bit in [b for b in narrowed if b < depth]:
-                part = (part.astype(F32) + swap(part, "tm", 2**bit).astype(F32)).astype(BF16)
-            parts = gather_parts(part, "chan")
-            total = sum(piece.astype(F32) for piece in parts).astype(BF16)
-            ahead = total, swap(total, "tm", mask)
         width = here if last else widths[depth]
-        sketch, *kept = filter_call(
-            grams, weights, offset, sketch, other, width, first, last, span
+        merge = lambda before: filter_call(
+            grams, weights, offset, sketch, other, before, width, first, last, span
         )
+        if last:
+            sketch, *kept = merge(grams[0])
+            continue
+        halves = first and cols % 256 == 0
+        partner = swap(half if halves else sketch, "tm", 2 * mask)
+        start = jnp.reshape(side * (here // 2), (1,)).astype(jnp.int32)
+        if first:
+            part = ahead_gram(sketch, other, partner, start, start)
+            merged, *kept = merge(part)
+        else:
+            merged, *kept = merge(grams[0])
+            part = ahead_gram(sketch, other, partner, start, kept[1])
+        for bit in [b for b in narrowed if b < depth]:
+            part = (part.astype(F32) + swap(part, "tm", 2**bit).astype(F32)).astype(BF16)
+        parts = gather_parts(part, "chan")
+        total = sum(piece.astype(F32) for piece in parts).astype(BF16)
+        ahead = [total, swap(total, "tm", mask)]
+        if halves:
+            ahead += [swap(total, "tm", 2 * mask), swap(total, "tm", 3 * mask)]
+        sketch = merged
     if span == 1:
         return sketch
     pieces = [sketch] + [

time: 89.8 us -> 93.3 us (1.039)
  waiting for transfers between devices: 16.5 us -> 19.9 us
  starting transfers between devices: 28.7 us -> 31.8 us
  Pallas kernels: 35.8 us -> 33.6 us
    ppermute x22 -> x24, waiting for transfers between devices: 16.5 us -> 19.9 us  [swap(): lax.ppermute(value, axis, [(source, source ^ mask) for source in range(co...]
    ppermute x22 -> x24, starting transfers between devices: 26.4 us -> 29.4 us  [swap(): lax.ppermute(value, axis, [(source, source ^ mask) for source in range(co...]
    pallas_call x2, Pallas kernels: 12.4 us -> 10.2 us  [front_call(): pl.pallas_call(functools.partial(front_kernel, *blocks), grid=(steps,), i...]
    unnamed x23 -> x25, local copies, waits for them, and re-layouts: 5.38 us -> 6.05 us
  transfers between devices with their start and end apart: 23 -> 25, of which waited for: 9 -> 9; matrix products, arithmetic and copies ran while one was open for 2% -> 0% of each run, Pallas kernels for 28% -> 25%
where the time goes in v4:
time: 93.3 us; the launch traced here: 92.9 us
  Pallas kernels  33.6 us (36%)
  starting transfers between devices  31.8 us (34%)
  waiting for transfers between devices  19.9 us (21%)
  local copies, waits for them, and re-layouts  7.17 us (8%)
    ppermute x24, starting transfers between devices, swap(): lax.ppermute(value, axis, [(source, source ^ mask) for source in range(co...  29.4 us
    pallas_call x3, Pallas kernels, filter_call(): pl.pallas_call(functools.partial(filter_kernel, len(grams), first, last),...  20.3 us
    ppermute x24, waiting for transfers between devices, swap(): lax.ppermute(value, axis, [(source, source ^ mask) for source in range(co...  19.9 us
    pallas_call x2, Pallas kernels, front_call(): pl.pallas_call(functools.partial(front_kernel, *blocks), grid=(steps,), i...  10.2 us
    unnamed x25, local copies, waits for them, and re-layouts  6.05 us
    ppermute x1, starting transfers between devices, on_device(): lax.ppermute(record[rows - HALO:], 'tm', [(source, source + 1) for source...  2.38 us
  transfers between devices with their start and end apart: 25, of which 9 were waited for; matrix products, arithmetic and copies ran while one was open for 0% of the time, Pallas kernels for 25%

profile of v4, /device:TPU:0, one launch (start us, length us, event | category | flops | bytes accessed | tf_op | source)
XLA Modules:
  0.0 92.9 jit_solution(2565391686452847661)
XLA Ops:
  0.0 1.0 %slice.9 = bf16[80,2560]{1,0:T(8,128)(2,1)S(1)} slice(bf16[1024,2560]{1,0:T(8,128)(2,1)} %refs_0_.1), slice={[944:1024], [0:2560]} | slice | bytes 819200 | tf_op jit(solution)/shard_map/slice | solution.py:440
  1.0 2.4 %collective-permute-start = (bf16[80,2560]{1,0:T(8,128)(2,1)S(1)}, bf16[80,2560]{1,0:T(8,128)(2,1)S(1)}, u32[]{:S(2)}, u32[]{:S(2)}) collective-permute-start(bf16[80,2560]{1,0:T(8,128)(2,1)S(1)} %slice.9), channel_id=1, source_target_pairs={{0,4},{4,8},{8,12},{12,16},{16,20},{20,24},{24,28},{1,5},{5,9},{9,... | collective-permute-start | bytes 1228808 | tf_op jit(solution)/shard_map/ppermute | solution.py:439
  3.4 0.9 %copy-done.2 = bf16[1024,128]{1,0:T(8,128)(2,1)S(1)} copy-done((bf16[1024,128]{1,0:T(8,128)(2,1)S(1)}, bf16[1024,128]{1,0:T(8,128)(2,1)}, u32[]{:S(2)}) %copy-start.2) | copy-done | bytes 262168
  5.7 8.8 %front.2 = (f32[128,2560]{1,0:T(8,128)S(1)}, bf16[256,208]{1,0:T(8,128)(2,1)S(1)}, bf16[128,128]{1,0:T(8,128)(2,1)S(1)}, bf16[128,2560]{1,0:T(8,128)(2,1)S(1)}) custom-call(bf16[1024,2560]{1,0:T(8,128)(2,1)} %refs_0_.1, s32[20,128]{1,0:T(8,128)S(1)} %bitcast.14, bf16[1,64]{1,0:T(2,128)(2,1)S(1)} %bitcast.16, bf16[1024,128]{1,0:T(8,128)(2,1)S(1)} %copy-done.2), custom_call_target="tpu_custom_call" | custom-call | flops 58720256000 | tf_op jit(solution)/shard_map/front/pallas_call | solution.py:146
  14.6 1.1 %copy-done.6 = f32[128,2560]{1,0:T(8,128)} copy-done((f32[128,2560]{1,0:T(8,128)}, f32[128,2560]{1,0:T(8,128)S(1)}, u32[]{:S(2)}) %copy-start.6) | copy-done | bytes 1310744
  15.7 1.3 %copy-done.7 = f32[128,2560]{1,0:T(8,128)S(1)} copy-done((f32[128,2560]{1,0:T(8,128)S(1)}, f32[128,2560]{1,0:T(8,128)}, u32[]{:S(2)}) %copy-start.7) | copy-done | bytes 1310744
  17.0 1.4 %front.3 = (bf16[128,2560]{1,0:T(8,128)(2,1)S(1)}, bf16[128,1280]{1,0:T(8,128)(2,1)S(1)}) custom-call(bf16[128,2560]{1,0:T(8,128)(2,1)S(1)} %get-tuple-element.23.refs_0_, bf16[80,2560]{1,0:T(8,128)(2,1)S(1)} %collective-permute-done.refs_1_, s32[20,128]{1,0:T(8,128)S(1)} %bitcast.15, bf16[256,208]{1,0:T(8,128)(2,1)S(1)} %get-tuple-element.24.refs_3_, ...), custom_call_target="tpu_custom_call" | custom-call | flops 8388608000 | tf_op jit(solution)/shard_map/front/pallas_call | solution.py:146
  18.4 2.6 %collective-permute-start.1 = (bf16[128,2560]{1,0:T(8,128)(2,1)S(1)}, bf16[128,2560]{1,0:T(8,128)(2,1)S(1)}, u32[]{:S(2)}, u32[]{:S(2)}) collective-permute-start(bf16[128,2560]{1,0:T(8,128)(2,1)S(1)} %get-tuple-element.27.own.refs_6_), channel_id=1, source_target_pairs={{0,4},{4,0},{8,12},{12,8},{16,20},{20,16},{24,28},{28,24},{1,5},{5... | collective-permute-start | bytes 1966088 | tf_op jit(solution)/shard_map/ppermute | solution.py:405
  21.2 1.6 %collective-permute-start.5 = (bf16[128,1280]{1,0:T(8,128)(2,1)S(1)}, bf16[128,1280]{1,0:T(8,128)(2,1)S(1)}, u32[]{:S(2)}, u32[]{:S(2)}) collective-permute-start(bf16[128,1280]{1,0:T(8,128)(2,1)S(1)} %get-tuple-element.28), channel_id=1, source_target_pairs={{0,8},{4,12},{8,0},{12,4},{16,24},{20,28},{24,16},{28,20},{1,9},{5... | collective-permute-start | bytes 983048 | tf_op jit(solution)/shard_map/ppermute | solution.py:405
  23.6 1.7 %collective-permute-start.2 = (bf16[272,128]{1,0:T(8,128)(2,1)S(1)}, bf16[272,128]{1,0:T(8,128)(2,1)S(1)}, u32[]{:S(2)}, u32[]{:S(2)}) collective-permute-start(bf16[272,128]{1,0:T(8,128)(2,1)S(1)} %pair_gram.1.refs_0_), channel_id=1, source_target_pairs={{0,1},{1,0},{2,3},{3,2},{4,5},{5,4},{6,7},{7,6},{8,9},{9,8},{10,11... | collective-permute-start | bytes 208904 | tf_op jit(solution)/shard_map/ppermute | solution.py:405
  25.3 2.6 %collective-permute-start.3 = (bf16[272,128]{1,0:T(8,128)(2,1)S(1)}, bf16[272,128]{1,0:T(8,128)(2,1)S(1)}, u32[]{:S(2)}, u32[]{:S(2)}) collective-permute-start(bf16[272,128]{1,0:T(8,128)(2,1)S(1)} %pair_gram.1.refs_0_), channel_id=1, source_target_pairs={{0,2},{1,3},{2,0},{3,1},{4,6},{5,7},{6,4},{7,5},{8,10},{9,11},{10,... | collective-permute-start | bytes 208904 | tf_op jit(solution)/shard_map/ppermute | solution.py:405
  28.1 2.7 %collective-permute-done.5.partner = bf16[128,1280]{1,0:T(8,128)(2,1)S(1)} collective-permute-done((bf16[128,1280]{1,0:T(8,128)(2,1)S(1)}, bf16[128,1280]{1,0:T(8,128)(2,1)S(1)}, u32[]{:S(2)}, u32[]{:S(2)}) %collective-permute-start.5) | collective-permute-done | bytes 327712 | tf_op jit(solution)/shard_map/ppermute | solution.py:405
  31.2 3.7 %collective-permute-start.9 = (bf16[256,128]{1,0:T(8,128)(2,1)S(1)}, bf16[256,128]{1,0:T(8,128)(2,1)S(1)}, u32[]{:S(2)}, u32[]{:S(2)}) collective-permute-start(bf16[256,128]{1,0:T(8,128)(2,1)S(1)} %ahead_gram.2.refs_8_), channel_id=1, source_target_pairs={{0,3},{1,2},{2,1},{3,0},{4,7},{5,6},{6,5},{7,4},{8,11},{9,10},{10,... | collective-permute-start | bytes 196616 | tf_op jit(solution)/shard_map/ppermute | solution.py:405
  35.7 6.3 %sign_filter.3 = (bf16[128,1280]{1,0:T(8,128)(2,1)S(1)}, f32[128,256]{1,0:T(8,128)S(1)}, f32[128,128]{1,0:T(8,128)S(1)}, bf16[128,512]{1,0:T(8,128)(2,1)S(1)}) custom-call(bf16[272,128]{1,0:T(8,128)(2,1)S(1)} %pair_gram.1.refs_0_, bf16[272,128]{1,0:T(8,128)(2,1)S(1)} %collective-permute-done.2.refs_1_, bf16[272,128]{1,0:T(8,128)(2,1)S(1)} %collective-permute-done.3.refs_2_, ...), custom_call_target="tpu_custom_call" | custom-call | flops 6710886400 | tf_op jit(solution)/shard_map/sign_filter/pallas_call | solution.py:392
  42.0 1.6 %collective-permute-start.13 = (bf16[128,1280]{1,0:T(8,128)(2,1)S(1)}, bf16[128,1280]{1,0:T(8,128)(2,1)S(1)}, u32[]{:S(2)}, u32[]{:S(2)}) collective-permute-start(bf16[128,1280]{1,0:T(8,128)(2,1)S(1)} %get-tuple-element.32.refs_9_.own), channel_id=1, source_target_pairs={{0,8},{4,12},{8,0},{12,4},{16,24},{20,28},{24,16},{28,20},{1,9},{5... | collective-permute-start | bytes 983048 | tf_op jit(solution)/shard_map/ppermute | solution.py:405
  44.3 1.6 %collective-permute-start.11 = (bf16[256,128]{1,0:T(8,128)(2,1)S(1)}, bf16[256,128]{1,0:T(8,128)(2,1)S(1)}, u32[]{:S(2)}, u32[]{:S(2)}) collective-permute-start(bf16[256,128]{1,0:T(8,128)(2,1)S(1)} %add_convert_fusion.2.refs_3_), channel_id=1, source_target_pairs={{0,8},{4,12},{8,0},{12,4},{16,24},{20,28},{24,16},{28,20},{1,9},{5... | collective-permute-start | bytes 196616 | tf_op jit(solution)/shard_map/ppermute | solution.py:405
  46.1 1.5 %collective-permute-start.15 = (bf16[128,1280]{1,0:T(8,128)(2,1)S(1)}, bf16[128,1280]{1,0:T(8,128)(2,1)S(1)}, u32[]{:S(2)}, u32[]{:S(2)}) collective-permute-start(bf16[128,1280]{1,0:T(8,128)(2,1)S(1)} %get-tuple-element.32.refs_9_.own), channel_id=1, source_target_pairs={{0,16},{4,20},{8,24},{12,28},{16,0},{20,4},{24,8},{28,12},{1,17},{... | collective-permute-start | bytes 983048 | tf_op jit(solution)/shard_map/ppermute | solution.py:405
  47.6 7.4 %collective-permute-done.11.refs_5_ = bf16[256,128]{1,0:T(8,128)(2,1)S(1)} collective-permute-done((bf16[256,128]{1,0:T(8,128)(2,1)S(1)}, bf16[256,128]{1,0:T(8,128)(2,1)S(1)}, u32[]{:S(2)}, u32[]{:S(2)}) %collective-permute-start.11) | collective-permute-done | bytes 65568 | tf_op jit(solution)/shard_map/ppermute | solution.py:405
  55.1 6.7 %sign_filter.4 = (bf16[128,640]{1,0:T(8,128)(2,1)S(1)}, f32[128,256]{1,0:T(8,128)S(1)}, f32[128,128]{1,0:T(8,128)S(1)}, bf16[128,512]{1,0:T(8,128)(2,1)S(1)}) custom-call(f32[128,256]{1,0:T(8,128)S(1)} %get-tuple-element.29.refs_0_.refs_11_, f32[128,128]{1,0:T(8,128)S(1)} %get-tuple-element.30.refs_1_, bf16[128,512]{1,0:T(8,128)(2,1)S(1)} %collective-permute-done.6.refs_2_, ...), custom_call_target="tpu_custom_call" | custom-call | flops 6710886400 | tf_op jit(solution)/shard_map/sign_filter/pallas_call | solution.py:392
  62.1 0.9 collective-permute-start.16
  63.9 3.5 %collective-permute-start.19 = (bf16[256,128]{1,0:T(8,128)(2,1)S(1)}, bf16[256,128]{1,0:T(8,128)(2,1)S(1)}, u32[]{:S(2)}, u32[]{:S(2)}) collective-permute-start(bf16[256,128]{1,0:T(8,128)(2,1)S(1)} %add_convert_fusion.1), channel_id=1, source_target_pairs={{0,3},{1,2},{2,1},{3,0},{4,7},{5,6},{6,5},{7,4},{8,11},{9,10},{10,... | collective-permute-start | bytes 196616 | tf_op jit(solution)/shard_map/ppermute | solution.py:405
  67.5 0.9 collective-permute-start.17
  68.4 1.5 %collective-permute-start.14 = (bf16[128,512]{1,0:T(8,128)(2,1)S(1)}, bf16[128,512]{1,0:T(8,128)(2,1)S(1)}, u32[]{:S(2)}, u32[]{:S(2)}) collective-permute-start(bf16[128,512]{1,0:T(8,128)(2,1)S(1)} %get-tuple-element.35), channel_id=1, source_target_pairs={{0,16},{4,20},{8,24},{12,28},{16,0},{20,4},{24,8},{28,12},{1,17},{... | collective-permute-start | bytes 393224 | tf_op jit(solution)/shard_map/ppermute | solution.py:405
  70.6 2.8 %collective-permute-done.18 = bf16[256,128]{1,0:T(8,128)(2,1)S(1)} collective-permute-done((bf16[256,128]{1,0:T(8,128)(2,1)S(1)}, bf16[256,128]{1,0:T(8,128)(2,1)S(1)}, u32[]{:S(2)}, u32[]{:S(2)}) %collective-permute-start.18) | collective-permute-done | bytes 65568 | tf_op jit(solution)/shard_map/ppermute | solution.py:405
  73.4 1.6 %collective-permute-start.20 = (bf16[256,128]{1,0:T(8,128)(2,1)S(1)}, bf16[256,128]{1,0:T(8,128)(2,1)S(1)}, u32[]{:S(2)}, u32[]{:S(2)}) collective-permute-start(bf16[256,128]{1,0:T(8,128)(2,1)S(1)} %add_convert_fusion.refs_3_), channel_id=1, source_target_pairs={{0,8},{4,12},{8,0},{12,4},{16,24},{20,28},{24,16},{28,20},{1,9},{5... | collective-permute-start | bytes 196616 | tf_op jit(solution)/shard_map/ppermute | solution.py:405
  75.0 1.8 %collective-permute-done.21.refs_8_ = bf16[128,640]{1,0:T(8,128)(2,1)S(1)} collective-permute-done((bf16[128,640]{1,0:T(8,128)(2,1)S(1)}, bf16[128,640]{1,0:T(8,128)(2,1)S(1)}, u32[]{:S(2)}, u32[]{:S(2)}) %collective-permute-start.21) | collective-permute-done | bytes 163872 | tf_op jit(solution)/shard_map/ppermute | solution.py:405
  76.8 0.9 %collective-permute-done.20.refs_4_ = bf16[256,128]{1,0:T(8,128)(2,1)S(1)} collective-permute-done((bf16[256,128]{1,0:T(8,128)(2,1)S(1)}, bf16[256,128]{1,0:T(8,128)(2,1)S(1)}, u32[]{:S(2)}, u32[]{:S(2)}) %collective-permute-start.20) | collective-permute-done | bytes 65568 | tf_op jit(solution)/shard_map/ppermute | solution.py:405
  77.8 7.3 %sign_filter.5 = (f32[16,640]{1,0:T(8,128)S(1)}, f32[16,640]{1,0:T(8,128)S(1)}, f32[16,640]{1,0:T(8,128)S(1)}, f32[16,640]{1,0:T(8,128)S(1)}) custom-call(f32[128,256]{1,0:T(8,128)S(1)} %get-tuple-element.33.refs_0_.refs_9_, f32[128,128]{1,0:T(8,128)S(1)} %get-tuple-element.34._.refs_1_, bf16[128,512]{1,0:T(8,128)(2,1)S(1)} %collective-permute-done.14.refs_2_, ...), custom_call_target="tpu_custom_call" | custom-call | flops 6710886400 | tf_op jit(solution)/shard_map/sign_filter/pallas_call | solution.py:392
  85.7 1.5 %collective-permute-start.23 = (f32[16,640]{1,0:T(8,128)S(1)}, f32[16,640]{1,0:T(8,128)S(1)}, u32[]{:S(2)}, u32[]{:S(2)}) collective-permute-start(f32[16,640]{1,0:T(8,128)S(1)} %get-tuple-element.39), channel_id=1, source_target_pairs={{0,8},{4,12},{8,0},{12,4},{16,24},{20,28},{24,16},{28,20},{1,9},{5... | collective-permute-start | bytes 122888 | tf_op jit(solution)/shard_map/ppermute | solution.py:405
  87.6 2.1 %collective-permute-done.23.refs_2_ = f32[16,640]{1,0:T(8,128)S(1)} collective-permute-done((f32[16,640]{1,0:T(8,128)S(1)}, f32[16,640]{1,0:T(8,128)S(1)}, u32[]{:S(2)}, u32[]{:S(2)}) %collective-permute-start.23) | collective-permute-done | bytes 40992 | tf_op jit(solution)/shard_map/ppermute | solution.py:405
  89.7 1.0 %collective-permute-done.24.refs_3_ = f32[16,640]{1,0:T(8,128)S(1)} collective-permute-done((f32[16,640]{1,0:T(8,128)S(1)}, f32[16,640]{1,0:T(8,128)S(1)}, u32[]{:S(2)}, u32[]{:S(2)}) %collective-permute-start.24) | collective-permute-done | bytes 40992 | tf_op jit(solution)/shard_map/ppermute | solution.py:405
  91.3 1.5 %join.1 = f32[16,2560]{1,0:T(8,128)} custom-call(s32[5]{0:T(128)} %copy-done.1, f32[16,640]{1,0:T(8,128)} %copy-done, f32[16,640]{1,0:T(8,128)} %copy-done.9, f32[16,640]{1,0:T(8,128)} %copy-done.10, f32[16,640]{1,0:T(8,128)} %copy-done.11), custom_call_target="tpu_custom_call" | custom-call | tf_op jit(solution)/shard_map/join/pallas_call | solution.py:424
  (61 shorter events, 8.3 us)
Async XLA Ops:
  1.0 14.6 %collective-permute-start = (bf16[80,2560]{1,0:T(8,128)(2,1)S(1)}, bf16[80,2560]{1,0:T(8,128)(2,1)S(1)}, u32[]{:S(2)}, u32[]{:S(2)}) collective-permute-start(bf16[80,2560]{1,0:T(8,128)(2,1)S(1)} %slice.9), channel_id=1, source_target_pairs={{0,4},{4,8},{8,12},{12,16},{16,20},{20,24},{24,28},{1,5},{5,9},{9,... | collective-permute-start | bytes 1228808 | tf_op jit(solution)/shard_map/ppermute | solution.py:439
  5.7 9.9 %copy-start.4 = (s32[2560]{0:T(1024)S(1)}, s32[2560]{0:T(1024)}, u32[]{:S(2)}) copy-start(s32[2560]{0:T(1024)} %param.7) | copy-start | bytes 30724
  14.6 1.1 %copy-start.6 = (f32[128,2560]{1,0:T(8,128)}, f32[128,2560]{1,0:T(8,128)S(1)}, u32[]{:S(2)}) copy-start(f32[128,2560]{1,0:T(8,128)S(1)} %get-tuple-element.26.refs_5_) | copy-start | bytes 3932164
  15.7 1.3 %copy-start.7 = (f32[128,2560]{1,0:T(8,128)S(1)}, f32[128,2560]{1,0:T(8,128)}, u32[]{:S(2)}) copy-start(f32[128,2560]{1,0:T(8,128)} %copy-done.6) | copy-start | bytes 3932164
  17.0 4.1 %copy-start.8 = (f32[256,128]{1,0:T(8,128)S(1)}, f32[256,128]{1,0:T(8,128)}, u32[]{:S(2)}) copy-start(f32[256,128]{1,0:T(8,128)} %param.9) | copy-start | bytes 393220
  18.4 4.4 %collective-permute-start.1 = (bf16[128,2560]{1,0:T(8,128)(2,1)S(1)}, bf16[128,2560]{1,0:T(8,128)(2,1)S(1)}, u32[]{:S(2)}, u32[]{:S(2)}) collective-permute-start(bf16[128,2560]{1,0:T(8,128)(2,1)S(1)} %get-tuple-element.27.own.refs_6_), channel_id=1, source_target_pairs={{0,4},{4,0},{8,12},{12,8},{16,20},{20,16},{24,28},{28,24},{1,5},{5... | collective-permute-start | bytes 1966088 | tf_op jit(solution)/shard_map/ppermute | solution.py:405
  21.2 9.7 %collective-permute-start.5 = (bf16[128,1280]{1,0:T(8,128)(2,1)S(1)}, bf16[128,1280]{1,0:T(8,128)(2,1)S(1)}, u32[]{:S(2)}, u32[]{:S(2)}) collective-permute-start(bf16[128,1280]{1,0:T(8,128)(2,1)S(1)} %get-tuple-element.28), channel_id=1, source_target_pairs={{0,8},{4,12},{8,0},{12,4},{16,24},{20,28},{24,16},{28,20},{1,9},{5... | collective-permute-start | bytes 983048 | tf_op jit(solution)/shard_map/ppermute | solution.py:405
  23.6 11.3 %collective-permute-start.2 = (bf16[272,128]{1,0:T(8,128)(2,1)S(1)}, bf16[272,128]{1,0:T(8,128)(2,1)S(1)}, u32[]{:S(2)}, u32[]{:S(2)}) collective-permute-start(bf16[272,128]{1,0:T(8,128)(2,1)S(1)} %pair_gram.1.refs_0_), channel_id=1, source_target_pairs={{0,1},{1,0},{2,3},{3,2},{4,5},{5,4},{6,7},{7,6},{8,9},{9,8},{10,11... | collective-permute-start | bytes 208904 | tf_op jit(solution)/shard_map/ppermute | solution.py:405
  25.3 10.4 %collective-permute-start.3 = (bf16[272,128]{1,0:T(8,128)(2,1)S(1)}, bf16[272,128]{1,0:T(8,128)(2,1)S(1)}, u32[]{:S(2)}, u32[]{:S(2)}) collective-permute-start(bf16[272,128]{1,0:T(8,128)(2,1)S(1)} %pair_gram.1.refs_0_), channel_id=1, source_target_pairs={{0,2},{1,3},{2,0},{3,1},{4,6},{5,7},{6,4},{7,5},{8,10},{9,11},{10,... | collective-permute-start | bytes 208904 | tf_op jit(solution)/shard_map/ppermute | solution.py:405
  27.9 7.8 %collective-permute-start.4 = (bf16[272,128]{1,0:T(8,128)(2,1)S(1)}, bf16[272,128]{1,0:T(8,128)(2,1)S(1)}, u32[]{:S(2)}, u32[]{:S(2)}) collective-permute-start(bf16[272,128]{1,0:T(8,128)(2,1)S(1)} %pair_gram.1.refs_0_), channel_id=1, source_target_pairs={{0,3},{1,2},{2,1},{3,0},{4,7},{5,6},{6,5},{7,4},{8,11},{9,10},{10,... | collective-permute-start | bytes 208904 | tf_op jit(solution)/shard_map/ppermute | solution.py:405
  31.2 12.9 %collective-permute-start.9 = (bf16[256,128]{1,0:T(8,128)(2,1)S(1)}, bf16[256,128]{1,0:T(8,128)(2,1)S(1)}, u32[]{:S(2)}, u32[]{:S(2)}) collective-permute-start(bf16[256,128]{1,0:T(8,128)(2,1)S(1)} %ahead_gram.2.refs_8_), channel_id=1, source_target_pairs={{0,3},{1,2},{2,1},{3,0},{4,7},{5,6},{6,5},{7,4},{8,11},{9,10},{10,... | collective-permute-start | bytes 196616 | tf_op jit(solution)/shard_map/ppermute | solution.py:405
  34.9 9.2 %collective-permute-start.8 = (bf16[256,128]{1,0:T(8,128)(2,1)S(1)}, bf16[256,128]{1,0:T(8,128)(2,1)S(1)}, u32[]{:S(2)}, u32[]{:S(2)}) collective-permute-start(bf16[256,128]{1,0:T(8,128)(2,1)S(1)} %ahead_gram.2.refs_8_), channel_id=1, source_target_pairs={{0,2},{1,3},{2,0},{3,1},{4,6},{5,7},{6,4},{7,5},{8,10},{9,11},{10,... | collective-permute-start | bytes 196616 | tf_op jit(solution)/shard_map/ppermute | solution.py:405
  34.9 9.2 %collective-permute-start.7 = (bf16[256,128]{1,0:T(8,128)(2,1)S(1)}, bf16[256,128]{1,0:T(8,128)(2,1)S(1)}, u32[]{:S(2)}, u32[]{:S(2)}) collective-permute-start(bf16[256,128]{1,0:T(8,128)(2,1)S(1)} %ahead_gram.2.refs_8_), channel_id=1, source_target_pairs={{0,1},{1,0},{2,3},{3,2},{4,5},{5,4},{6,7},{7,6},{8,9},{9,8},{10,11... | collective-permute-start | bytes 196616 | tf_op jit(solution)/shard_map/ppermute | solution.py:405
  42.0 13.1 %collective-permute-start.13 = (bf16[128,1280]{1,0:T(8,128)(2,1)S(1)}, bf16[128,1280]{1,0:T(8,128)(2,1)S(1)}, u32[]{:S(2)}, u32[]{:S(2)}) collective-permute-start(bf16[128,1280]{1,0:T(8,128)(2,1)S(1)} %get-tuple-element.32.refs_9_.own), channel_id=1, source_target_pairs={{0,8},{4,12},{8,0},{12,4},{16,24},{20,28},{24,16},{28,20},{1,9},{5... | collective-permute-start | bytes 983048 | tf_op jit(solution)/shard_map/ppermute | solution.py:405
  43.6 11.5 %collective-permute-start.6 = (bf16[128,512]{1,0:T(8,128)(2,1)S(1)}, bf16[128,512]{1,0:T(8,128)(2,1)S(1)}, u32[]{:S(2)}, u32[]{:S(2)}) collective-permute-start(bf16[128,512]{1,0:T(8,128)(2,1)S(1)} %get-tuple-element.31), channel_id=1, source_target_pairs={{0,8},{4,12},{8,0},{12,4},{16,24},{20,28},{24,16},{28,20},{1,9},{5... | collective-permute-start | bytes 393224 | tf_op jit(solution)/shard_map/ppermute | solution.py:405
  44.2 1.9 %collective-permute-start.10 = (bf16[256,128]{1,0:T(8,128)(2,1)S(1)}, bf16[256,128]{1,0:T(8,128)(2,1)S(1)}, u32[]{:S(2)}, u32[]{:S(2)}) collective-permute-start(bf16[256,128]{1,0:T(8,128)(2,1)S(1)} %add_convert_fusion.2.refs_3_), channel_id=1, source_target_pairs={{0,4},{4,0},{8,12},{12,8},{16,20},{20,16},{24,28},{28,24},{1,5},{5... | collective-permute-start | bytes 196616 | tf_op jit(solution)/shard_map/ppermute | solution.py:405
  44.3 10.8 %collective-permute-start.11 = (bf16[256,128]{1,0:T(8,128)(2,1)S(1)}, bf16[256,128]{1,0:T(8,128)(2,1)S(1)}, u32[]{:S(2)}, u32[]{:S(2)}) collective-permute-start(bf16[256,128]{1,0:T(8,128)(2,1)S(1)} %add_convert_fusion.2.refs_3_), channel_id=1, source_target_pairs={{0,8},{4,12},{8,0},{12,4},{16,24},{20,28},{24,16},{28,20},{1,9},{5... | collective-permute-start | bytes 196616 | tf_op jit(solution)/shard_map/ppermute | solution.py:405
  45.8 9.3 %collective-permute-start.12 = (bf16[256,128]{1,0:T(8,128)(2,1)S(1)}, bf16[256,128]{1,0:T(8,128)(2,1)S(1)}, u32[]{:S(2)}, u32[]{:S(2)}) collective-permute-start(bf16[256,128]{1,0:T(8,128)(2,1)S(1)} %add_convert_fusion.2.refs_3_), channel_id=1, source_target_pairs={{0,12},{4,8},{8,4},{12,0},{16,28},{20,24},{24,20},{28,16},{1,13},{... | collective-permute-start | bytes 196616 | tf_op jit(solution)/shard_map/ppermute | solution.py:405
  46.1 15.7 %collective-permute-start.15 = (bf16[128,1280]{1,0:T(8,128)(2,1)S(1)}, bf16[128,1280]{1,0:T(8,128)(2,1)S(1)}, u32[]{:S(2)}, u32[]{:S(2)}) collective-permute-start(bf16[128,1280]{1,0:T(8,128)(2,1)S(1)} %get-tuple-element.32.refs_9_.own), channel_id=1, source_target_pairs={{0,16},{4,20},{8,24},{12,28},{16,0},{20,4},{24,8},{28,12},{1,17},{... | collective-permute-start | bytes 983048 | tf_op jit(solution)/shard_map/ppermute | solution.py:405
  62.1 1.8 %collective-permute-start.16 = (bf16[256,128]{1,0:T(8,128)(2,1)S(1)}, bf16[256,128]{1,0:T(8,128)(2,1)S(1)}, u32[]{:S(2)}, u32[]{:S(2)}) collective-permute-start(bf16[256,128]{1,0:T(8,128)(2,1)S(1)} %ahead_gram.3), channel_id=1, source_target_pairs={{0,4},{4,0},{8,12},{12,8},{16,20},{20,16},{24,28},{28,24},{1,5},{5... | collective-permute-start | bytes 196616 | tf_op jit(solution)/shard_map/ppermute | solution.py:405
  63.1 22.0 %copy-start.1 = (s32[5]{0:T(128)}, s32[5]{0:T(128)S(1)}, u32[]{:S(2)}) copy-start(s32[5]{0:T(128)S(1)} %stack.19.refs_6_.offsets) | copy-start | bytes 64
  63.9 6.7 %collective-permute-start.19 = (bf16[256,128]{1,0:T(8,128)(2,1)S(1)}, bf16[256,128]{1,0:T(8,128)(2,1)S(1)}, u32[]{:S(2)}, u32[]{:S(2)}) collective-permute-start(bf16[256,128]{1,0:T(8,128)(2,1)S(1)} %add_convert_fusion.1), channel_id=1, source_target_pairs={{0,3},{1,2},{2,1},{3,0},{4,7},{5,6},{6,5},{7,4},{8,11},{9,10},{10,... | collective-permute-start | bytes 196616 | tf_op jit(solution)/shard_map/ppermute | solution.py:405
  67.5 5.9 %collective-permute-start.18 = (bf16[256,128]{1,0:T(8,128)(2,1)S(1)}, bf16[256,128]{1,0:T(8,128)(2,1)S(1)}, u32[]{:S(2)}, u32[]{:S(2)}) collective-permute-start(bf16[256,128]{1,0:T(8,128)(2,1)S(1)} %add_convert_fusion.1), channel_id=1, source_target_pairs={{0,2},{1,3},{2,0},{3,1},{4,6},{5,7},{6,4},{7,5},{8,10},{9,11},{10,... | collective-permute-start | bytes 196616 | tf_op jit(solution)/shard_map/ppermute | solution.py:405
  67.5 5.9 %collective-permute-start.17 = (bf16[256,128]{1,0:T(8,128)(2,1)S(1)}, bf16[256,128]{1,0:T(8,128)(2,1)S(1)}, u32[]{:S(2)}, u32[]{:S(2)}) collective-permute-start(bf16[256,128]{1,0:T(8,128)(2,1)S(1)} %add_convert_fusion.1), channel_id=1, source_target_pairs={{0,1},{1,0},{2,3},{3,2},{4,5},{5,4},{6,7},{7,6},{8,9},{9,8},{10,11... | collective-permute-start | bytes 196616 | tf_op jit(solution)/shard_map/ppermute | solution.py:405
  68.4 6.6 %collective-permute-start.14 = (bf16[128,512]{1,0:T(8,128)(2,1)S(1)}, bf16[128,512]{1,0:T(8,128)(2,1)S(1)}, u32[]{:S(2)}, u32[]{:S(2)}) collective-permute-start(bf16[128,512]{1,0:T(8,128)(2,1)S(1)} %get-tuple-element.35), channel_id=1, source_target_pairs={{0,16},{4,20},{8,24},{12,28},{16,0},{20,4},{24,8},{28,12},{1,17},{... | collective-permute-start | bytes 393224 | tf_op jit(solution)/shard_map/ppermute | solution.py:405
  69.9 6.9 %collective-permute-start.21 = (bf16[128,640]{1,0:T(8,128)(2,1)S(1)}, bf16[128,640]{1,0:T(8,128)(2,1)S(1)}, u32[]{:S(2)}, u32[]{:S(2)}) collective-permute-start(bf16[128,640]{1,0:T(8,128)(2,1)S(1)} %get-tuple-element.36.refs_7_), channel_id=1, source_target_pairs={{0,16},{4,20},{8,24},{12,28},{16,0},{20,4},{24,8},{28,12},{1,17},{... | collective-permute-start | bytes 491528 | tf_op jit(solution)/shard_map/ppermute | solution.py:405
  73.4 4.3 %collective-permute-start.20 = (bf16[256,128]{1,0:T(8,128)(2,1)S(1)}, bf16[256,128]{1,0:T(8,128)(2,1)S(1)}, u32[]{:S(2)}, u32[]{:S(2)}) collective-permute-start(bf16[256,128]{1,0:T(8,128)(2,1)S(1)} %add_convert_fusion.refs_3_), channel_id=1, source_target_pairs={{0,8},{4,12},{8,0},{12,4},{16,24},{20,28},{24,16},{28,20},{1,9},{5... | collective-permute-start | bytes 196616 | tf_op jit(solution)/shard_map/ppermute | solution.py:405
  85.7 1.9 %collective-permute-start.22 = (f32[16,640]{1,0:T(8,128)S(1)}, f32[16,640]{1,0:T(8,128)S(1)}, u32[]{:S(2)}, u32[]{:S(2)}) collective-permute-start(f32[16,640]{1,0:T(8,128)S(1)} %get-tuple-element.38), channel_id=1, source_target_pairs={{0,4},{4,0},{8,12},{12,8},{16,20},{20,16},{24,28},{28,24},{1,5},{5... | collective-permute-start | bytes 122888 | tf_op jit(solution)/shard_map/ppermute | solution.py:405
  85.7 4.0 %collective-permute-start.23 = (f32[16,640]{1,0:T(8,128)S(1)}, f32[16,640]{1,0:T(8,128)S(1)}, u32[]{:S(2)}, u32[]{:S(2)}) collective-permute-start(f32[16,640]{1,0:T(8,128)S(1)} %get-tuple-element.39), channel_id=1, source_target_pairs={{0,8},{4,12},{8,0},{12,4},{16,24},{20,28},{24,16},{28,20},{1,9},{5... | collective-permute-start | bytes 122888 | tf_op jit(solution)/shard_map/ppermute | solution.py:405
  87.2 3.5 %collective-permute-start.24 = (f32[16,640]{1,0:T(8,128)S(1)}, f32[16,640]{1,0:T(8,128)S(1)}, u32[]{:S(2)}, u32[]{:S(2)}) collective-permute-start(f32[16,640]{1,0:T(8,128)S(1)} %get-tuple-element.40), channel_id=1, source_target_pairs={{0,12},{4,8},{8,4},{12,0},{16,28},{20,24},{24,20},{28,16},{1,13},{... | collective-permute-start | bytes 122888 | tf_op jit(solution)/shard_map/ppermute | solution.py:405
  87.6 3.2 %copy-start.9 = (f32[16,640]{1,0:T(8,128)}, f32[16,640]{1,0:T(8,128)S(1)}, u32[]{:S(2)}) copy-start(f32[16,640]{1,0:T(8,128)S(1)} %collective-permute-done.22.refs_1_) | copy-start | bytes 122884
  89.7 1.0 %copy-start.10 = (f32[16,640]{1,0:T(8,128)}, f32[16,640]{1,0:T(8,128)S(1)}, u32[]{:S(2)}) copy-start(f32[16,640]{1,0:T(8,128)S(1)} %collective-permute-done.23.refs_2_) | copy-start | bytes 122884
  (5 other events, 3.6 us)

commit v5 on v4

--- a/solution.py
+++ b/solution.py
@@ -184,7 +184,7 @@
             pltpu.SemaphoreType.DMA((3,)),
         ],
         cols // tile,
-        50,
+        48,
     )
     halves = cols % 256 == 0
     tile = cols // 2 if halves else cols
@@ -321,15 +321,14 @@
     return gram - jnp.where(diag, mean, 0.0), mean
 
 
-def filter_kernel(count, first, last, *refs):
+def filter_kernel(count, first, last, quarters, *refs):
     grams, refs = refs[:count], refs[count:]
-    compress_t, offset, own, other, _, refs = *refs[:5], refs[5:]
-    if last:
-        *sketch, pair, sems = refs
-    else:
-        sketch, mix_out, level, packed, pair, sems = refs
+    compress_t, places, own, other, _, refs = *refs[:5], refs[5:]
+    *out, pair, sems = refs
+    if not last:
+        *out, mix_out, level, packed = out
     rank, width = own.shape[0], pair.shape[1]
-    start = pl.multiple_of(offset[0], 128) if width % 128 == 0 else 0
+    start = pl.multiple_of(places[0], 128) if width < own.shape[1] else 0
     copies = [
         pltpu.make_async_copy(
             source.at[:, pl.ds(start, width)] if width < own.shape[1] else source,
@@ -354,16 +353,31 @@
     high, low = split(mixing)
     both = jnp.concatenate([high, low], 0)
     rows = mixing.shape[0]
-    tile = next((t for t in (640, 512, 256, 128) if width % t == 0), width)
-    for c in range(0, width, tile):
-        wide = dot(both, pair[:, c : c + tile])
-        wide = wide[:rows] + wide[rows:]
-        if last:
-            share = rows // len(sketch)
-            for i, piece in enumerate(sketch):
-                piece[:, c : c + tile] = wide[i * share : (i + 1) * share]
-        else:
-            sketch[:, c : c + tile] = wide.astype(BF16)
+
+    def mixed(span):
+        wide = dot(both, pair[:, span])
+        return wide[:rows] + wide[rows:]
+
+    if quarters:
+        for half in range(2):
+            part = mixed(slice(half * width // 2, (half + 1) * width // 2)).astype(BF16)
+            for i, place in enumerate((1, 2)):
+                mine, theirs = out[2 * i], out[2 * i + 1]
+
+                @pl.when(places[place] == half)
+                def _():
+                    mine[...] = part
+
+                @pl.when(places[place] != half)
+                def _():
+                    theirs[...] = part
+    else:
+        tile = next((t for t in (640, 512, 256, 128) if width % t == 0), width)
+        for c in range(0, width, tile):
+            part = mixed(slice(c, c + tile))
+            share = rows // len(out)
+            for i, piece in enumerate(out):
+                piece[:, c : c + tile] = part[i * share : (i + 1) * share].astype(piece.dtype)
     if not last:
         block = dot3_nt(dot3(mixing, gram + mean * eye), mixing)
         mix_out[...] = mixing
@@ -378,26 +392,28 @@
     return pl.CostEstimate(flops=int(flops), bytes_accessed=int(bytes_accessed), transcendentals=0)
 
 
-def filter_call(grams, compress_t, offset, own, other, before, width, first, last, pieces):
+def filter_call(grams, compress_t, places, own, other, before, width, first, last, pieces, quarters):
     rank = own.shape[0]
     rows = compress_t.shape[0]
     if last:
         out = [jax.ShapeDtypeStruct((rows // pieces, width), F32)] * pieces
     else:
-        out = [jax.ShapeDtypeStruct((rows, width), BF16)]
+        out = [jax.ShapeDtypeStruct((rank, width // 2), BF16)] * 4
+        if not quarters:
+            out = [jax.ShapeDtypeStruct((rank, width), BF16)]
         out.append(jax.ShapeDtypeStruct((rank, 2 * rank), F32))
         out.append(jax.ShapeDtypeStruct((rank, rank), F32))
         out.append(jax.ShapeDtypeStruct((rank, 4 * rank), BF16))
     args = [*grams, compress_t]
     return pl.pallas_call(
-        functools.partial(filter_kernel, len(grams), first, last),
+        functools.partial(filter_kernel, len(grams), first, last, quarters),
         in_specs=[VMEM] * len(args) + [SMEM, ANY, ANY, ANY],
         out_shape=out,
         scratch_shapes=[pltpu.VMEM((2 * rank, width), BF16), pltpu.SemaphoreType.DMA((2,))],
         compiler_params=PARAMS,
         cost_estimate=cost(50 * K_ITERS * (2 * rank) ** 3),
         name="sign_filter",
-    )(*args, offset, own, other, before)
+    )(*args, places, own, other, before)
 
 
 def swap(value, axis, mask):
@@ -444,13 +460,10 @@
         record, halo, gauge_lag, fir_taps[None, :], projector, jnp.reshape(1 - side, (1,)).astype(jnp.int32)
     )
 
-    widths = []
-    width = cols
+    widths = [cols]
     for depth in range(1, depths):
-        if width % 256 == 0:
-            width //= 2
-        widths.append(width)
-    narrowed = [depth for depth in range(depths - 1) if widths[depth] < ([cols] + widths)[depth]]
+        widths.append(widths[-1] // 2 if widths[-1] % 256 == 0 else widths[-1])
+    narrowed = [depth for depth in range(depths - 1) if widths[depth + 1] < widths[depth]]
     assert narrowed == list(range(len(narrowed)))
     span = 2 ** len(narrowed)
 
@@ -460,12 +473,16 @@
     compress_t = compress.T
     flipped = jnp.concatenate([compress_t[:, rank:], compress_t[:, :rank]], 1)
 
-    places = [position * 0]
+    def scalars(*values):
+        return jnp.stack([position * 0 + value for value in values]).astype(jnp.int32)
+
+    joined = [0]
     for part in range(span):
         source = position ^ part
-        places.append(sum([bit_of(source, bit) * (cols >> (bit + 1)) for bit in narrowed], position * 0))
-    places = jnp.stack(places).astype(jnp.int32)
+        joined.append(sum([bit_of(source, bit) * (cols >> (bit + 1)) for bit in narrowed], 0))
+    joined = scalars(*joined)
     kept = ahead = None
+    keep, send, given = sketch, half if 0 in narrowed else sketch, sketch
     for depth in range(depths):
         first, last = depth == 0, depth == depths - 1
         mask = 2**depth
@@ -478,46 +495,56 @@
                 ],
                 0,
             )
-        here = sketch.shape[1]
-        narrow = not last and widths[depth] < here
-        offset = bit_of(position, depth) * (here // 2) if narrow else jnp.int32(0)
-        offset = places if last else jnp.reshape(offset, (1,)).astype(jnp.int32)
-        other = swap(sketch, "tm", mask)
+        other = swap(given, "tm", mask)
         if first:
             grams = gather_parts(pair_gram(sketch, other), "chan")
         else:
             mixing, level, packed = kept
             grams = [mixing, level, swap(packed, "tm", mask), *ahead]
-        width = here if last else widths[depth]
-        merge = lambda before: filter_call(
-            grams, weights, offset, sketch, other, before, width, first, last, span
-        )
+        here = widths[depth]
         if last:
-            sketch, *kept = merge(grams[0])
+            out = filter_call(
+                grams, weights, joined, sketch, other, grams[0], here, first, last, span, False
+            )
+            sketch, *kept = out
             continue
-        halves = first and cols % 256 == 0
-        partner = swap(half if halves else sketch, "tm", 2 * mask)
-        start = jnp.reshape(side * (here // 2), (1,)).astype(jnp.int32)
+        ahead_bit = bit_of(position, depth + 1)
+        halved = depth in narrowed
+        sibling = other if first else swap(keep, "tm", mask)
+        start = scalars(ahead_bit * (here // 2))
         if first:
-            part = ahead_gram(sketch, other, partner, start, start)
-            merged, *kept = merge(part)
+            part = ahead_gram(sketch, sibling, swap(send, "tm", 2 * mask), start, start)
         else:
-            merged, *kept = merge(grams[0])
-            part = ahead_gram(sketch, other, partner, start, kept[1])
+            part = ahead_gram(keep, sibling, swap(send, "tm", 2 * mask), start, ahead[0])
         for bit in [b for b in narrowed if b < depth]:
             part = (part.astype(F32) + swap(part, "tm", 2**bit).astype(F32)).astype(BF16)
+        quarters = depth + 1 in narrowed
+        places = scalars(
+            bit_of(position, depth) * (here // 2) if halved and first else 0,
+            bit_of(position, depth + 1),
+            bit_of(position, min(depth + 2, depths - 1)),
+        )
+        width = widths[depth + 1]
+        out = filter_call(
+            grams, weights, places, sketch, other, part, width, first, last, span, quarters
+        )
         parts = gather_parts(part, "chan")
         total = sum(piece.astype(F32) for piece in parts).astype(BF16)
         ahead = [total, swap(total, "tm", mask)]
-        if halves:
+        if halved:
             ahead += [swap(total, "tm", 2 * mask), swap(total, "tm", 3 * mask)]
-        sketch = merged
+        *out, mixing, level, packed = out
+        kept = mixing, level, packed
+        if quarters:
+            sketch, given, keep, send = out
+        else:
+            sketch = given = keep = send = out[0]
     if span == 1:
         return sketch
     pieces = [sketch] + [
         swap(piece, "tm", part) for part, piece in enumerate(kept, 1)
     ]
-    return join(places, pieces)
+    return join(joined, pieces)
 
 
 def solution(mesh):

time: 93.3 us -> 95.8 us (1.027)
  starting transfers between devices: 31.8 us -> 34.6 us
  Pallas kernels: 33.6 us -> 35.6 us
  local copies, waits for them, and re-layouts: 7.17 us -> 5.67 us
  waiting for transfers between devices: 19.9 us -> 18.9 us
    ppermute x24 -> x27, starting transfers between devices: 29.4 us -> 32.2 us  [swap(): lax.ppermute(value, axis, [(source, source ^ mask) for source in range(co...]
    pallas_call x3, Pallas kernels: 20.3 us -> 22.4 us  [filter_call(): pl.pallas_call(functools.partial(filter_kernel, len(grams), first, last,...]
    unnamed x25 -> x19, local copies, waits for them, and re-layouts: 6.05 us -> 4.54 us
    ppermute x24 -> x27, waiting for transfers between devices: 19.9 us -> 18.9 us  [swap(): lax.ppermute(value, axis, [(source, source ^ mask) for source in range(co...]
  transfers between devices with their start and end apart: 25 -> 28, of which waited for: 9 -> 8; matrix products, arithmetic and copies ran while one was open for 0% -> 1% of each run, Pallas kernels for 25% -> 26%
where the time goes in v5:
time: 95.8 us; the launch traced here: 95.4 us
  Pallas kernels  35.6 us (37%)
  starting transfers between devices  34.6 us (36%)
  waiting for transfers between devices  18.9 us (20%)
  local copies, waits for them, and re-layouts  5.67 us (6%)
    ppermute x27, starting transfers between devices, swap(): lax.ppermute(value, axis, [(source, source ^ mask) for source in range(co...  32.2 us
    pallas_call x3, Pallas kernels, filter_call(): pl.pallas_call(functools.partial(filter_kernel, len(grams), first, last,...  22.4 us
    ppermute x27, waiting for transfers between devices, swap(): lax.ppermute(value, axis, [(source, source ^ mask) for source in range(co...  18.9 us
    pallas_call x2, Pallas kernels, front_call(): pl.pallas_call(functools.partial(front_kernel, *blocks), grid=(steps,), i...  10.3 us
    unnamed x19, local copies, waits for them, and re-layouts  4.54 us
    ppermute x1, starting transfers between devices, on_device(): lax.ppermute(record[rows - HALO:], 'tm', [(source, source + 1) for source...  2.38 us
  transfers between devices with their start and end apart: 28, of which 8 were waited for; matrix products, arithmetic and copies ran while one was open for 1% of the time, Pallas kernels for 26%

profile of v5, /device:TPU:0, one launch (start us, length us, event | category | flops | bytes accessed | tf_op | source)
XLA Modules:
  0.0 95.4 jit_solution(1653991811560785791)
XLA Ops:
  0.0 1.0 %slice.9 = bf16[80,2560]{1,0:T(8,128)(2,1)S(1)} slice(bf16[1024,2560]{1,0:T(8,128)(2,1)} %refs_0_.1), slice={[944:1024], [0:2560]} | slice | bytes 819200 | tf_op jit(solution)/shard_map/slice | solution.py:456
  1.0 2.4 %collective-permute-start = (bf16[80,2560]{1,0:T(8,128)(2,1)S(1)}, bf16[80,2560]{1,0:T(8,128)(2,1)S(1)}, u32[]{:S(2)}, u32[]{:S(2)}) collective-permute-start(bf16[80,2560]{1,0:T(8,128)(2,1)S(1)} %slice.9), channel_id=1, source_target_pairs={{0,4},{4,8},{8,12},{12,16},{16,20},{20,24},{24,28},{1,5},{5,9},{9,... | collective-permute-start | bytes 1228808 | tf_op jit(solution)/shard_map/ppermute | solution.py:455
  3.4 0.9 copy-done.2
  5.7 8.8 %front.2 = (f32[128,2560]{1,0:T(8,128)S(1)}, bf16[256,208]{1,0:T(8,128)(2,1)S(1)}, bf16[128,128]{1,0:T(8,128)(2,1)S(1)}, bf16[128,2560]{1,0:T(8,128)(2,1)S(1)}) custom-call(bf16[1024,2560]{1,0:T(8,128)(2,1)} %refs_0_.1, s32[20,128]{1,0:T(8,128)S(1)} %bitcast.16, bf16[1,64]{1,0:T(2,128)(2,1)S(1)} %bitcast.18, bf16[1024,128]{1,0:T(8,128)(2,1)S(1)} %copy-done.2), custom_call_target="tpu_custom_call" | custom-call | flops 58720256000 | tf_op jit(solution)/shard_map/front/pallas_call | solution.py:146
  14.6 1.4 %front.3 = (bf16[128,2560]{1,0:T(8,128)(2,1)S(1)}, bf16[128,1280]{1,0:T(8,128)(2,1)S(1)}) custom-call(bf16[128,2560]{1,0:T(8,128)(2,1)S(1)} %get-tuple-element.26.refs_0_, bf16[80,2560]{1,0:T(8,128)(2,1)S(1)} %collective-permute-done.refs_1_, s32[20,128]{1,0:T(8,128)S(1)} %bitcast.17, bf16[256,208]{1,0:T(8,128)(2,1)S(1)} %get-tuple-element.27.refs_3_, ...), custom_call_target="tpu_custom_call" | custom-call | flops 8388608000 | tf_op jit(solution)/shard_map/front/pallas_call | solution.py:146
  16.1 2.6 %collective-permute-start.1 = (bf16[128,2560]{1,0:T(8,128)(2,1)S(1)}, bf16[128,2560]{1,0:T(8,128)(2,1)S(1)}, u32[]{:S(2)}, u32[]{:S(2)}) collective-permute-start(bf16[128,2560]{1,0:T(8,128)(2,1)S(1)} %get-tuple-element.30.own.refs_6_), channel_id=1, source_target_pairs={{0,4},{4,0},{8,12},{12,8},{16,20},{20,16},{24,28},{28,24},{1,5},{5... | collective-permute-start | bytes 1966088 | tf_op jit(solution)/shard_map/ppermute | solution.py:421
  18.7 1.0 %copy.6 = f32[256,128]{0,1:T(8,128)S(1)} copy(f32[256,128]{1,0:T(8,128)} %param.9) | data formatting | bytes 262144 | tf_op args[4]
  19.8 1.6 %collective-permute-start.5 = (bf16[128,1280]{1,0:T(8,128)(2,1)S(1)}, bf16[128,1280]{1,0:T(8,128)(2,1)S(1)}, u32[]{:S(2)}, u32[]{:S(2)}) collective-permute-start(bf16[128,1280]{1,0:T(8,128)(2,1)S(1)} %get-tuple-element.31), channel_id=1, source_target_pairs={{0,8},{4,12},{8,0},{12,4},{16,24},{20,28},{24,16},{28,20},{1,9},{5... | collective-permute-start | bytes 983048 | tf_op jit(solution)/shard_map/ppermute | solution.py:421
  22.4 1.6 %collective-permute-start.2 = (bf16[272,128]{1,0:T(8,128)(2,1)S(1)}, bf16[272,128]{1,0:T(8,128)(2,1)S(1)}, u32[]{:S(2)}, u32[]{:S(2)}) collective-permute-start(bf16[272,128]{1,0:T(8,128)(2,1)S(1)} %pair_gram.1.refs_0_), channel_id=1, source_target_pairs={{0,1},{1,0},{2,3},{3,2},{4,5},{5,4},{6,7},{7,6},{8,9},{9,8},{10,11... | collective-permute-start | bytes 208904 | tf_op jit(solution)/shard_map/ppermute | solution.py:421
  24.1 2.6 %collective-permute-start.3 = (bf16[272,128]{1,0:T(8,128)(2,1)S(1)}, bf16[272,128]{1,0:T(8,128)(2,1)S(1)}, u32[]{:S(2)}, u32[]{:S(2)}) collective-permute-start(bf16[272,128]{1,0:T(8,128)(2,1)S(1)} %pair_gram.1.refs_0_), channel_id=1, source_target_pairs={{0,2},{1,3},{2,0},{3,1},{4,6},{5,7},{6,4},{7,5},{8,10},{9,11},{10,... | collective-permute-start | bytes 208904 | tf_op jit(solution)/shard_map/ppermute | solution.py:421
  27.0 2.5 %collective-permute-done.5.partner = bf16[128,1280]{1,0:T(8,128)(2,1)S(1)} collective-permute-done((bf16[128,1280]{1,0:T(8,128)(2,1)S(1)}, bf16[128,1280]{1,0:T(8,128)(2,1)S(1)}, u32[]{:S(2)}, u32[]{:S(2)}) %collective-permute-start.5) | collective-permute-done | bytes 327712 | tf_op jit(solution)/shard_map/ppermute | solution.py:421
  29.8 3.7 %collective-permute-start.9 = (bf16[256,128]{1,0:T(8,128)(2,1)S(1)}, bf16[256,128]{1,0:T(8,128)(2,1)S(1)}, u32[]{:S(2)}, u32[]{:S(2)}) collective-permute-start(bf16[256,128]{1,0:T(8,128)(2,1)S(1)} %ahead_gram.2.refs_8_), channel_id=1, source_target_pairs={{0,3},{1,2},{2,1},{3,0},{4,7},{5,6},{6,5},{7,4},{8,11},{9,10},{10,... | collective-permute-start | bytes 196616 | tf_op jit(solution)/shard_map/ppermute | solution.py:421
  34.3 7.6 %sign_filter.3 = (bf16[128,640]{1,0:T(8,128)(2,1)S(1)}, bf16[128,640]{1,0:T(8,128)(2,1)S(1)}, bf16[128,640]{1,0:T(8,128)(2,1)S(1)}, bf16[128,640]{1,0:T(8,128)(2...) custom-call(bf16[272,128]{1,0:T(8,128)(2,1)S(1)} %pair_gram.1.refs_0_, ...), custom_call_target="tpu_custom_call" | custom-call | flops 6710886400 | tf_op jit(solution)/shard_map/sign_filter/pallas_call | solution.py:408
  41.9 1.5 %collective-permute-start.14 = (bf16[128,640]{1,0:T(8,128)(2,1)S(1)}, bf16[128,640]{1,0:T(8,128)(2,1)S(1)}, u32[]{:S(2)}, u32[]{:S(2)}) collective-permute-start(bf16[128,640]{1,0:T(8,128)(2,1)S(1)} %get-tuple-element.37.own), channel_id=1, source_target_pairs={{0,8},{4,12},{8,0},{12,4},{16,24},{20,28},{24,16},{28,20},{1,9},{5... | collective-permute-start | bytes 491528 | tf_op jit(solution)/shard_map/ppermute | solution.py:421
  43.9 3.4 %collective-permute-done.14.sibling = bf16[128,640]{1,0:T(8,128)(2,1)S(1)} collective-permute-done((bf16[128,640]{1,0:T(8,128)(2,1)S(1)}, bf16[128,640]{1,0:T(8,128)(2,1)S(1)}, u32[]{:S(2)}, u32[]{:S(2)}) %collective-permute-start.14) | collective-permute-done | bytes 163872 | tf_op jit(solution)/shard_map/ppermute | solution.py:421
  47.3 1.5 %collective-permute-done.15.partner = bf16[128,640]{1,0:T(8,128)(2,1)S(1)} collective-permute-done((bf16[128,640]{1,0:T(8,128)(2,1)S(1)}, bf16[128,640]{1,0:T(8,128)(2,1)S(1)}, u32[]{:S(2)}, u32[]{:S(2)}) %collective-permute-start.15) | collective-permute-done | bytes 163872 | tf_op jit(solution)/shard_map/ppermute | solution.py:421
  50.2 0.9 collective-permute-start.12
  51.7 1.4 %collective-permute-start.13 = (bf16[128,640]{1,0:T(8,128)(2,1)S(1)}, bf16[128,640]{1,0:T(8,128)(2,1)S(1)}, u32[]{:S(2)}, u32[]{:S(2)}) collective-permute-start(bf16[128,640]{1,0:T(8,128)(2,1)S(1)} %get-tuple-element.36), channel_id=1, source_target_pairs={{0,8},{4,12},{8,0},{12,4},{16,24},{20,28},{24,16},{28,20},{1,9},{5... | collective-permute-start | bytes 491528 | tf_op jit(solution)/shard_map/ppermute | solution.py:421
  53.2 3.7 %collective-permute-start.20 = (bf16[256,128]{1,0:T(8,128)(2,1)S(1)}, bf16[256,128]{1,0:T(8,128)(2,1)S(1)}, u32[]{:S(2)}, u32[]{:S(2)}) collective-permute-start(bf16[256,128]{1,0:T(8,128)(2,1)S(1)} %add_convert_fusion.1.refs_11_), channel_id=1, source_target_pairs={{0,3},{1,2},{2,1},{3,0},{4,7},{5,6},{6,5},{7,4},{8,11},{9,10},{10,... | collective-permute-start | bytes 196616 | tf_op jit(solution)/shard_map/ppermute | solution.py:421
  56.8 2.0 %collective-permute-start.18 = (bf16[256,128]{1,0:T(8,128)(2,1)S(1)}, bf16[256,128]{1,0:T(8,128)(2,1)S(1)}, u32[]{:S(2)}, u32[]{:S(2)}) collective-permute-start(bf16[256,128]{1,0:T(8,128)(2,1)S(1)} %add_convert_fusion.1.refs_11_), channel_id=1, source_target_pairs={{0,1},{1,0},{2,3},{3,2},{4,5},{5,4},{6,7},{7,6},{8,9},{9,8},{10,11... | collective-permute-start | bytes 196616 | tf_op jit(solution)/shard_map/ppermute | solution.py:421
  58.8 2.8 %collective-permute-done.13.refs_10_ = bf16[128,640]{1,0:T(8,128)(2,1)S(1)} collective-permute-done((bf16[128,640]{1,0:T(8,128)(2,1)S(1)}, bf16[128,640]{1,0:T(8,128)(2,1)S(1)}, u32[]{:S(2)}, u32[]{:S(2)}) %collective-permute-start.13) | collective-permute-done | bytes 163872 | tf_op jit(solution)/shard_map/ppermute | solution.py:421
  61.6 7.6 %sign_filter.4 = (bf16[128,640]{1,0:T(8,128)(2,1)S(1)}, f32[128,256]{1,0:T(8,128)S(1)}, f32[128,128]{1,0:T(8,128)S(1)}, bf16[128,512]{1,0:T(8,128)(2,1)S(1)}) custom-call(f32[128,256]{1,0:T(8,128)S(1)} %get-tuple-element.32.refs_0_, f32[128,128]{1,0:T(8,128)S(1)} %get-tuple-element.33.refs_1_, bf16[128,512]{1,0:T(8,128)(2,1)S(1)} %collective-permute-done.6.refs_2_, ...), custom_call_target="tpu_custom_call" | custom-call | flops 6710886400 | tf_op jit(solution)/shard_map/sign_filter/pallas_call | solution.py:408
  70.1 1.2 %collective-permute-start.24 = (bf16[128,640]{1,0:T(8,128)(2,1)S(1)}, bf16[128,640]{1,0:T(8,128)(2,1)S(1)}, u32[]{:S(2)}, u32[]{:S(2)}) collective-permute-start(bf16[128,640]{1,0:T(8,128)(2,1)S(1)} %get-tuple-element.42.refs_9_), channel_id=1, source_target_pairs={{0,16},{4,20},{8,24},{12,28},{16,0},{20,4},{24,8},{28,12},{1,17},{... | collective-permute-start | bytes 491528 | tf_op jit(solution)/shard_map/ppermute | solution.py:421
  72.2 1.2 %collective-permute-start.22 = (bf16[256,128]{1,0:T(8,128)(2,1)S(1)}, bf16[256,128]{1,0:T(8,128)(2,1)S(1)}, u32[]{:S(2)}, u32[]{:S(2)}) collective-permute-start(bf16[256,128]{1,0:T(8,128)(2,1)S(1)} %add_convert_fusion.refs_3_), channel_id=1, source_target_pairs={{0,16},{4,20},{8,24},{12,28},{16,0},{20,4},{24,8},{28,12},{1,17},{... | collective-permute-start | bytes 196616 | tf_op jit(solution)/shard_map/ppermute | solution.py:421
  73.3 1.6 %collective-permute-start.23 = (bf16[256,128]{1,0:T(8,128)(2,1)S(1)}, bf16[256,128]{1,0:T(8,128)(2,1)S(1)}, u32[]{:S(2)}, u32[]{:S(2)}) collective-permute-start(bf16[256,128]{1,0:T(8,128)(2,1)S(1)} %add_convert_fusion.refs_3_), channel_id=1, source_target_pairs={{0,24},{4,28},{8,16},{12,20},{16,8},{20,12},{24,0},{28,4},{1,25},{... | collective-permute-start | bytes 196616 | tf_op jit(solution)/shard_map/ppermute | solution.py:421
  74.9 1.5 %collective-permute-done.17.refs_2_ = bf16[128,512]{1,0:T(8,128)(2,1)S(1)} collective-permute-done((bf16[128,512]{1,0:T(8,128)(2,1)S(1)}, bf16[128,512]{1,0:T(8,128)(2,1)S(1)}, u32[]{:S(2)}, u32[]{:S(2)}) %collective-permute-start.17) | collective-permute-done | bytes 131104 | tf_op jit(solution)/shard_map/ppermute | solution.py:421
  76.4 4.0 %collective-permute-done.22.refs_5_ = bf16[256,128]{1,0:T(8,128)(2,1)S(1)} collective-permute-done((bf16[256,128]{1,0:T(8,128)(2,1)S(1)}, bf16[256,128]{1,0:T(8,128)(2,1)S(1)}, u32[]{:S(2)}, u32[]{:S(2)}) %collective-permute-start.22) | collective-permute-done | bytes 65568 | tf_op jit(solution)/shard_map/ppermute | solution.py:421
  80.4 7.2 %sign_filter.5 = (f32[16,640]{1,0:T(8,128)S(1)}, f32[16,640]{1,0:T(8,128)S(1)}, f32[16,640]{1,0:T(8,128)S(1)}, f32[16,640]{1,0:T(8,128)S(1)}) custom-call(f32[128,256]{1,0:T(8,128)S(1)} %get-tuple-element.39.refs_0_.refs_11_, f32[128,128]{1,0:T(8,128)S(1)} %get-tuple-element.40.refs_1_, bf16[128,512]{1,0:T(8,128)(2,1)S(1)} %collective-permute-done.17.refs_2_, ...), custom_call_target="tpu_custom_call" | custom-call | flops 6710886400 | tf_op jit(solution)/shard_map/sign_filter/pallas_call | solution.py:408
  88.2 1.5 %collective-permute-start.26 = (f32[16,640]{1,0:T(8,128)S(1)}, f32[16,640]{1,0:T(8,128)S(1)}, u32[]{:S(2)}, u32[]{:S(2)}) collective-permute-start(f32[16,640]{1,0:T(8,128)S(1)} %get-tuple-element.45), channel_id=1, source_target_pairs={{0,8},{4,12},{8,0},{12,4},{16,24},{20,28},{24,16},{28,20},{1,9},{5... | collective-permute-start | bytes 122888 | tf_op jit(solution)/shard_map/ppermute | solution.py:421
  90.1 2.1 %collective-permute-done.26.refs_2_ = f32[16,640]{1,0:T(8,128)S(1)} collective-permute-done((f32[16,640]{1,0:T(8,128)S(1)}, f32[16,640]{1,0:T(8,128)S(1)}, u32[]{:S(2)}, u32[]{:S(2)}) %collective-permute-start.26) | collective-permute-done | bytes 40992 | tf_op jit(solution)/shard_map/ppermute | solution.py:421
  92.3 1.0 %collective-permute-done.27.refs_3_ = f32[16,640]{1,0:T(8,128)S(1)} collective-permute-done((f32[16,640]{1,0:T(8,128)S(1)}, f32[16,640]{1,0:T(8,128)S(1)}, u32[]{:S(2)}, u32[]{:S(2)}) %collective-permute-start.27) | collective-permute-done | bytes 40992 | tf_op jit(solution)/shard_map/ppermute | solution.py:421
  93.9 1.5 %join.1 = f32[16,2560]{1,0:T(8,128)} custom-call(s32[5]{0:T(128)} %copy-done.1, f32[16,640]{1,0:T(8,128)} %copy-done, f32[16,640]{1,0:T(8,128)} %copy-done.6, f32[16,640]{1,0:T(8,128)} %copy-done.7, f32[16,640]{1,0:T(8,128)} %copy-done.8), custom_call_target="tpu_custom_call" | custom-call | tf_op jit(solution)/shard_map/join/pallas_call | solution.py:440
  (63 shorter events, 9.6 us)
Async XLA Ops:
  1.0 13.6 %collective-permute-start = (bf16[80,2560]{1,0:T(8,128)(2,1)S(1)}, bf16[80,2560]{1,0:T(8,128)(2,1)S(1)}, u32[]{:S(2)}, u32[]{:S(2)}) collective-permute-start(bf16[80,2560]{1,0:T(8,128)(2,1)S(1)} %slice.9), channel_id=1, source_target_pairs={{0,4},{4,8},{8,12},{12,16},{16,20},{20,24},{24,28},{1,5},{5,9},{9,... | collective-permute-start | bytes 1228808 | tf_op jit(solution)/shard_map/ppermute | solution.py:455
  5.7 8.9 %copy-start.4 = (s32[2560]{0:T(1024)S(1)}, s32[2560]{0:T(1024)}, u32[]{:S(2)}) copy-start(s32[2560]{0:T(1024)} %param.7) | copy-start | bytes 30724
  16.1 5.5 %collective-permute-start.1 = (bf16[128,2560]{1,0:T(8,128)(2,1)S(1)}, bf16[128,2560]{1,0:T(8,128)(2,1)S(1)}, u32[]{:S(2)}, u32[]{:S(2)}) collective-permute-start(bf16[128,2560]{1,0:T(8,128)(2,1)S(1)} %get-tuple-element.30.own.refs_6_), channel_id=1, source_target_pairs={{0,4},{4,0},{8,12},{12,8},{16,20},{20,16},{24,28},{28,24},{1,5},{5... | collective-permute-start | bytes 1966088 | tf_op jit(solution)/shard_map/ppermute | solution.py:421
  19.8 9.7 %collective-permute-start.5 = (bf16[128,1280]{1,0:T(8,128)(2,1)S(1)}, bf16[128,1280]{1,0:T(8,128)(2,1)S(1)}, u32[]{:S(2)}, u32[]{:S(2)}) collective-permute-start(bf16[128,1280]{1,0:T(8,128)(2,1)S(1)} %get-tuple-element.31), channel_id=1, source_target_pairs={{0,8},{4,12},{8,0},{12,4},{16,24},{20,28},{24,16},{28,20},{1,9},{5... | collective-permute-start | bytes 983048 | tf_op jit(solution)/shard_map/ppermute | solution.py:421
  21.6 58.8 %copy-start.1 = (s32[5]{0:T(128)}, s32[5]{0:T(128)S(1)}, u32[]{:S(2)}) copy-start(s32[5]{0:T(128)S(1)} %stack.42.refs_8_.offsets) | copy-start | bytes 64
  22.4 11.1 %collective-permute-start.2 = (bf16[272,128]{1,0:T(8,128)(2,1)S(1)}, bf16[272,128]{1,0:T(8,128)(2,1)S(1)}, u32[]{:S(2)}, u32[]{:S(2)}) collective-permute-start(bf16[272,128]{1,0:T(8,128)(2,1)S(1)} %pair_gram.1.refs_0_), channel_id=1, source_target_pairs={{0,1},{1,0},{2,3},{3,2},{4,5},{5,4},{6,7},{7,6},{8,9},{9,8},{10,11... | collective-permute-start | bytes 208904 | tf_op jit(solution)/shard_map/ppermute | solution.py:421
  24.1 10.2 %collective-permute-start.3 = (bf16[272,128]{1,0:T(8,128)(2,1)S(1)}, bf16[272,128]{1,0:T(8,128)(2,1)S(1)}, u32[]{:S(2)}, u32[]{:S(2)}) collective-permute-start(bf16[272,128]{1,0:T(8,128)(2,1)S(1)} %pair_gram.1.refs_0_), channel_id=1, source_target_pairs={{0,2},{1,3},{2,0},{3,1},{4,6},{5,7},{6,4},{7,5},{8,10},{9,11},{10,... | collective-permute-start | bytes 208904 | tf_op jit(solution)/shard_map/ppermute | solution.py:421
  26.7 7.6 %collective-permute-start.4 = (bf16[272,128]{1,0:T(8,128)(2,1)S(1)}, bf16[272,128]{1,0:T(8,128)(2,1)S(1)}, u32[]{:S(2)}, u32[]{:S(2)}) collective-permute-start(bf16[272,128]{1,0:T(8,128)(2,1)S(1)} %pair_gram.1.refs_0_), channel_id=1, source_target_pairs={{0,3},{1,2},{2,1},{3,0},{4,7},{5,6},{6,5},{7,4},{8,11},{9,10},{10,... | collective-permute-start | bytes 208904 | tf_op jit(solution)/shard_map/ppermute | solution.py:421
  29.8 14.0 %collective-permute-start.9 = (bf16[256,128]{1,0:T(8,128)(2,1)S(1)}, bf16[256,128]{1,0:T(8,128)(2,1)S(1)}, u32[]{:S(2)}, u32[]{:S(2)}) collective-permute-start(bf16[256,128]{1,0:T(8,128)(2,1)S(1)} %ahead_gram.2.refs_8_), channel_id=1, source_target_pairs={{0,3},{1,2},{2,1},{3,0},{4,7},{5,6},{6,5},{7,4},{8,11},{9,10},{10,... | collective-permute-start | bytes 196616 | tf_op jit(solution)/shard_map/ppermute | solution.py:421
  33.5 10.3 %collective-permute-start.8 = (bf16[256,128]{1,0:T(8,128)(2,1)S(1)}, bf16[256,128]{1,0:T(8,128)(2,1)S(1)}, u32[]{:S(2)}, u32[]{:S(2)}) collective-permute-start(bf16[256,128]{1,0:T(8,128)(2,1)S(1)} %ahead_gram.2.refs_8_), channel_id=1, source_target_pairs={{0,2},{1,3},{2,0},{3,1},{4,6},{5,7},{6,4},{7,5},{8,10},{9,11},{10,... | collective-permute-start | bytes 196616 | tf_op jit(solution)/shard_map/ppermute | solution.py:421
  33.5 10.3 %collective-permute-start.7 = (bf16[256,128]{1,0:T(8,128)(2,1)S(1)}, bf16[256,128]{1,0:T(8,128)(2,1)S(1)}, u32[]{:S(2)}, u32[]{:S(2)}) collective-permute-start(bf16[256,128]{1,0:T(8,128)(2,1)S(1)} %ahead_gram.2.refs_8_), channel_id=1, source_target_pairs={{0,1},{1,0},{2,3},{3,2},{4,5},{5,4},{6,7},{7,6},{8,9},{9,8},{10,11... | collective-permute-start | bytes 196616 | tf_op jit(solution)/shard_map/ppermute | solution.py:421
  41.9 5.4 %collective-permute-start.14 = (bf16[128,640]{1,0:T(8,128)(2,1)S(1)}, bf16[128,640]{1,0:T(8,128)(2,1)S(1)}, u32[]{:S(2)}, u32[]{:S(2)}) collective-permute-start(bf16[128,640]{1,0:T(8,128)(2,1)S(1)} %get-tuple-element.37.own), channel_id=1, source_target_pairs={{0,8},{4,12},{8,0},{12,4},{16,24},{20,28},{24,16},{28,20},{1,9},{5... | collective-permute-start | bytes 491528 | tf_op jit(solution)/shard_map/ppermute | solution.py:421
  43.4 5.3 %collective-permute-start.15 = (bf16[128,640]{1,0:T(8,128)(2,1)S(1)}, bf16[128,640]{1,0:T(8,128)(2,1)S(1)}, u32[]{:S(2)}, u32[]{:S(2)}) collective-permute-start(bf16[128,640]{1,0:T(8,128)(2,1)S(1)} %get-tuple-element.38), channel_id=1, source_target_pairs={{0,16},{4,20},{8,24},{12,28},{16,0},{20,4},{24,8},{28,12},{1,17},{... | collective-permute-start | bytes 491528 | tf_op jit(solution)/shard_map/ppermute | solution.py:421
  49.0 2.7 %collective-permute-start.16 = (bf16[256,128]{1,0:T(8,128)(2,1)S(1)}, bf16[256,128]{1,0:T(8,128)(2,1)S(1)}, u32[]{:S(2)}, u32[]{:S(2)}) collective-permute-start(bf16[256,128]{1,0:T(8,128)(2,1)S(1)} %ahead_gram.3), channel_id=1, source_target_pairs={{0,4},{4,0},{8,12},{12,8},{16,20},{20,16},{24,28},{28,24},{1,5},{5... | collective-permute-start | bytes 196616 | tf_op jit(solution)/shard_map/ppermute | solution.py:421
  49.2 4.0 %collective-permute-start.10 = (bf16[256,128]{1,0:T(8,128)(2,1)S(1)}, bf16[256,128]{1,0:T(8,128)(2,1)S(1)}, u32[]{:S(2)}, u32[]{:S(2)}) collective-permute-start(bf16[256,128]{1,0:T(8,128)(2,1)S(1)} %add_convert_fusion.2._.refs_3_), channel_id=1, source_target_pairs={{0,4},{4,0},{8,12},{12,8},{16,20},{20,16},{24,28},{28,24},{1,5},{5... | collective-permute-start | bytes 196616 | tf_op jit(solution)/shard_map/ppermute | solution.py:421
  49.7 7.2 %collective-permute-start.11 = (bf16[256,128]{1,0:T(8,128)(2,1)S(1)}, bf16[256,128]{1,0:T(8,128)(2,1)S(1)}, u32[]{:S(2)}, u32[]{:S(2)}) collective-permute-start(bf16[256,128]{1,0:T(8,128)(2,1)S(1)} %add_convert_fusion.2._.refs_3_), channel_id=1, source_target_pairs={{0,8},{4,12},{8,0},{12,4},{16,24},{20,28},{24,16},{28,20},{1,9},{5... | collective-permute-start | bytes 196616 | tf_op jit(solution)/shard_map/ppermute | solution.py:421
  50.2 6.6 %collective-permute-start.12 = (bf16[256,128]{1,0:T(8,128)(2,1)S(1)}, bf16[256,128]{1,0:T(8,128)(2,1)S(1)}, u32[]{:S(2)}, u32[]{:S(2)}) collective-permute-start(bf16[256,128]{1,0:T(8,128)(2,1)S(1)} %add_convert_fusion.2._.refs_3_), channel_id=1, source_target_pairs={{0,12},{4,8},{8,4},{12,0},{16,28},{20,24},{24,20},{28,16},{1,13},{... | collective-permute-start | bytes 196616 | tf_op jit(solution)/shard_map/ppermute | solution.py:421
  51.1 7.7 %collective-permute-start.6 = (bf16[128,512]{1,0:T(8,128)(2,1)S(1)}, bf16[128,512]{1,0:T(8,128)(2,1)S(1)}, u32[]{:S(2)}, u32[]{:S(2)}) collective-permute-start(bf16[128,512]{1,0:T(8,128)(2,1)S(1)} %get-tuple-element.34), channel_id=1, source_target_pairs={{0,8},{4,12},{8,0},{12,4},{16,24},{20,28},{24,16},{28,20},{1,9},{5... | collective-permute-start | bytes 393224 | tf_op jit(solution)/shard_map/ppermute | solution.py:421
  51.7 9.9 %collective-permute-start.13 = (bf16[128,640]{1,0:T(8,128)(2,1)S(1)}, bf16[128,640]{1,0:T(8,128)(2,1)S(1)}, u32[]{:S(2)}, u32[]{:S(2)}) collective-permute-start(bf16[128,640]{1,0:T(8,128)(2,1)S(1)} %get-tuple-element.36), channel_id=1, source_target_pairs={{0,8},{4,12},{8,0},{12,4},{16,24},{20,28},{24,16},{28,20},{1,9},{5... | collective-permute-start | bytes 491528 | tf_op jit(solution)/shard_map/ppermute | solution.py:421
  53.2 18.2 %collective-permute-start.20 = (bf16[256,128]{1,0:T(8,128)(2,1)S(1)}, bf16[256,128]{1,0:T(8,128)(2,1)S(1)}, u32[]{:S(2)}, u32[]{:S(2)}) collective-permute-start(bf16[256,128]{1,0:T(8,128)(2,1)S(1)} %add_convert_fusion.1.refs_11_), channel_id=1, source_target_pairs={{0,3},{1,2},{2,1},{3,0},{4,7},{5,6},{6,5},{7,4},{8,11},{9,10},{10,... | collective-permute-start | bytes 196616 | tf_op jit(solution)/shard_map/ppermute | solution.py:421
  56.8 14.5 %collective-permute-start.19 = (bf16[256,128]{1,0:T(8,128)(2,1)S(1)}, bf16[256,128]{1,0:T(8,128)(2,1)S(1)}, u32[]{:S(2)}, u32[]{:S(2)}) collective-permute-start(bf16[256,128]{1,0:T(8,128)(2,1)S(1)} %add_convert_fusion.1.refs_11_), channel_id=1, source_target_pairs={{0,2},{1,3},{2,0},{3,1},{4,6},{5,7},{6,4},{7,5},{8,10},{9,11},{10,... | collective-permute-start | bytes 196616 | tf_op jit(solution)/shard_map/ppermute | solution.py:421
  56.8 14.5 %collective-permute-start.18 = (bf16[256,128]{1,0:T(8,128)(2,1)S(1)}, bf16[256,128]{1,0:T(8,128)(2,1)S(1)}, u32[]{:S(2)}, u32[]{:S(2)}) collective-permute-start(bf16[256,128]{1,0:T(8,128)(2,1)S(1)} %add_convert_fusion.1.refs_11_), channel_id=1, source_target_pairs={{0,1},{1,0},{2,3},{3,2},{4,5},{5,4},{6,7},{7,6},{8,9},{9,8},{10,11... | collective-permute-start | bytes 196616 | tf_op jit(solution)/shard_map/ppermute | solution.py:421
  69.2 7.2 %collective-permute-start.17 = (bf16[128,512]{1,0:T(8,128)(2,1)S(1)}, bf16[128,512]{1,0:T(8,128)(2,1)S(1)}, u32[]{:S(2)}, u32[]{:S(2)}) collective-permute-start(bf16[128,512]{1,0:T(8,128)(2,1)S(1)} %get-tuple-element.41), channel_id=1, source_target_pairs={{0,16},{4,20},{8,24},{12,28},{16,0},{20,4},{24,8},{28,12},{1,17},{... | collective-permute-start | bytes 393224 | tf_op jit(solution)/shard_map/ppermute | solution.py:421
  70.1 10.3 %collective-permute-start.24 = (bf16[128,640]{1,0:T(8,128)(2,1)S(1)}, bf16[128,640]{1,0:T(8,128)(2,1)S(1)}, u32[]{:S(2)}, u32[]{:S(2)}) collective-permute-start(bf16[128,640]{1,0:T(8,128)(2,1)S(1)} %get-tuple-element.42.refs_9_), channel_id=1, source_target_pairs={{0,16},{4,20},{8,24},{12,28},{16,0},{20,4},{24,8},{28,12},{1,17},{... | collective-permute-start | bytes 491528 | tf_op jit(solution)/shard_map/ppermute | solution.py:421
  71.4 5.1 %collective-permute-start.21 = (bf16[256,128]{1,0:T(8,128)(2,1)S(1)}, bf16[256,128]{1,0:T(8,128)(2,1)S(1)}, u32[]{:S(2)}, u32[]{:S(2)}) collective-permute-start(bf16[256,128]{1,0:T(8,128)(2,1)S(1)} %add_convert_fusion.refs_3_), channel_id=1, source_target_pairs={{0,8},{4,12},{8,0},{12,4},{16,24},{20,28},{24,16},{28,20},{1,9},{5... | collective-permute-start | bytes 196616 | tf_op jit(solution)/shard_map/ppermute | solution.py:421
  72.2 8.2 %collective-permute-start.22 = (bf16[256,128]{1,0:T(8,128)(2,1)S(1)}, bf16[256,128]{1,0:T(8,128)(2,1)S(1)}, u32[]{:S(2)}, u32[]{:S(2)}) collective-permute-start(bf16[256,128]{1,0:T(8,128)(2,1)S(1)} %add_convert_fusion.refs_3_), channel_id=1, source_target_pairs={{0,16},{4,20},{8,24},{12,28},{16,0},{20,4},{24,8},{28,12},{1,17},{... | collective-permute-start | bytes 196616 | tf_op jit(solution)/shard_map/ppermute | solution.py:421
  73.3 7.1 %collective-permute-start.23 = (bf16[256,128]{1,0:T(8,128)(2,1)S(1)}, bf16[256,128]{1,0:T(8,128)(2,1)S(1)}, u32[]{:S(2)}, u32[]{:S(2)}) collective-permute-start(bf16[256,128]{1,0:T(8,128)(2,1)S(1)} %add_convert_fusion.refs_3_), channel_id=1, source_target_pairs={{0,24},{4,28},{8,16},{12,20},{16,8},{20,12},{24,0},{28,4},{1,25},{... | collective-permute-start | bytes 196616 | tf_op jit(solution)/shard_map/ppermute | solution.py:421
  88.2 1.9 %collective-permute-start.25 = (f32[16,640]{1,0:T(8,128)S(1)}, f32[16,640]{1,0:T(8,128)S(1)}, u32[]{:S(2)}, u32[]{:S(2)}) collective-permute-start(f32[16,640]{1,0:T(8,128)S(1)} %get-tuple-element.44), channel_id=1, source_target_pairs={{0,4},{4,0},{8,12},{12,8},{16,20},{20,16},{24,28},{28,24},{1,5},{5... | collective-permute-start | bytes 122888 | tf_op jit(solution)/shard_map/ppermute | solution.py:421
  88.2 4.0 %collective-permute-start.26 = (f32[16,640]{1,0:T(8,128)S(1)}, f32[16,640]{1,0:T(8,128)S(1)}, u32[]{:S(2)}, u32[]{:S(2)}) collective-permute-start(f32[16,640]{1,0:T(8,128)S(1)} %get-tuple-element.45), channel_id=1, source_target_pairs={{0,8},{4,12},{8,0},{12,4},{16,24},{20,28},{24,16},{28,20},{1,9},{5... | collective-permute-start | bytes 122888 | tf_op jit(solution)/shard_map/ppermute | solution.py:421
  89.7 3.5 %collective-permute-start.27 = (f32[16,640]{1,0:T(8,128)S(1)}, f32[16,640]{1,0:T(8,128)S(1)}, u32[]{:S(2)}, u32[]{:S(2)}) collective-permute-start(f32[16,640]{1,0:T(8,128)S(1)} %get-tuple-element.46), channel_id=1, source_target_pairs={{0,12},{4,8},{8,4},{12,0},{16,28},{20,24},{24,20},{28,16},{1,13},{... | collective-permute-start | bytes 122888 | tf_op jit(solution)/shard_map/ppermute | solution.py:421
  90.1 3.2 %copy-start.6 = (f32[16,640]{1,0:T(8,128)}, f32[16,640]{1,0:T(8,128)S(1)}, u32[]{:S(2)}) copy-start(f32[16,640]{1,0:T(8,128)S(1)} %collective-permute-done.25.refs_1_) | copy-start | bytes 122884
  92.2 1.0 %copy-start.7 = (f32[16,640]{1,0:T(8,128)}, f32[16,640]{1,0:T(8,128)S(1)}, u32[]{:S(2)}) copy-start(f32[16,640]{1,0:T(8,128)S(1)} %collective-permute-done.26.refs_2_) | copy-start | bytes 122884
  (5 other events, 3.6 us)

commit v6 on v4

--- a/solution.py
+++ b/solution.py
@@ -67,7 +67,7 @@
 
 def front_kernel(first, last, *refs):
     if first == 0:
-        record, halo, lag, band, weights, begun, side, out, send, strain = refs
+        record, halo, lag, band, weights, begun, out, strain = refs
     else:
         record, lag_ref, taps_ref, projector_ref, out, band, head_weights, head = refs[:8]
         strain, weights, lag, taps, projector, sems = refs[8:]
@@ -133,13 +133,7 @@
     if begun is None:
         out[...] = total
     else:
-        total = (total + begun[...]).astype(BF16)
-        out[...] = total
-        if send.shape[1] == cols:
-
-            @pl.when(pl.program_id(0) == side[0])
-            def _():
-                send[...] = total
+        out[...] = (total + begun[...]).astype(BF16)
 
 
 def front_call(blocks, args, in_specs, out_specs, out_shape, scratch, steps, grant):
@@ -151,12 +145,11 @@
         out_shape=out_shape,
         scratch_shapes=scratch,
         compiler_params=pltpu.CompilerParams(vmem_limit_bytes=grant * 2**20),
-        cost_estimate=cost(100 * (blocks[1] - blocks[0]) * BLOCK * BLOCK * args[0].shape[1] * 2),
         name="front",
     )(*args)
 
 
-def front(record, halo, lag, taps, projector, side):
+def front(record, halo, lag, taps, projector):
     rows, cols = record.shape
     rank = projector.shape[1]
     lag = lag.reshape(cols // 128, 128) if cols % 128 == 0 else lag[None, :]
@@ -184,13 +177,12 @@
             pltpu.SemaphoreType.DMA((3,)),
         ],
         cols // tile,
-        50,
-    )
-    halves = cols % 256 == 0
-    tile = cols // 2 if halves else cols
+        48,
+    )
+    tile = cols // 2 if cols % 256 == 0 else cols
     return front_call(
         (0, 1),
-        (head, halo, lag, band, weights, begun, side),
+        (head, halo, lag, band, weights, begun),
         [
             columns(BLOCK, tile),
             columns(HALO, tile),
@@ -198,13 +190,9 @@
             whole(band),
             whole(weights),
             columns(rank, tile),
-            SMEM,
         ],
-        [columns(rank, tile), pl.BlockSpec((rank, tile if halves else 128), lambda i: (0, 0))],
-        [
-            jax.ShapeDtypeStruct((rank, cols), BF16),
-            jax.ShapeDtypeStruct((rank, tile if halves else 128), BF16),
-        ],
+        columns(rank, tile),
+        jax.ShapeDtypeStruct((rank, cols), BF16),
         [pltpu.VMEM((BLOCK, tile), BF16)],
         cols // tile,
         32,
@@ -246,24 +234,21 @@
     )(own, other)
 
 
-def ahead_kernel(own, sibling, partner, start, _, out):
+def ahead_kernel(width, own, sibling, partner, out):
     rank = own.shape[0]
-    there = partner[...]
-    width = there.shape[1]
-    span = slice(None) if width == own.shape[1] else pl.ds(pl.multiple_of(start[0], 128), width)
-    out[0:rank, :] = dot_nt(own[:, span], there).astype(out.dtype)
-    out[rank:, :] = dot_nt(sibling[:, span], there).astype(out.dtype)
-
-
-def ahead_gram(own, sibling, partner, start, after):
+    there = partner[:, :width]
+    out[0:rank, :] = dot_nt(own[:, :width], there).astype(out.dtype)
+    out[rank:, :] = dot_nt(sibling[:, :width], there).astype(out.dtype)
+
+
+def ahead_gram(own, sibling, partner, width):
     rank = own.shape[0]
     return pl.pallas_call(
-        ahead_kernel,
-        in_specs=[VMEM, VMEM, VMEM, SMEM, ANY],
+        functools.partial(ahead_kernel, width),
         out_shape=jax.ShapeDtypeStruct((2 * rank, rank), BF16),
         compiler_params=PARAMS,
         name="ahead_gram",
-    )(own, sibling, partner, start, after)
+    )(own, sibling, partner)
 
 
 def summed(parts):
@@ -294,7 +279,7 @@
     return square_of(aa, ab, bb), mean
 
 
-def later_gram(own_mix, own_level, packed, ahead, sibling_ahead, *other_half):
+def later_gram(own_mix, own_level, ahead, sibling_ahead, other):
     rank = own_mix.shape[0]
     mine, theirs = ahead[...], sibling_ahead[...]
     cross = jnp.concatenate(
@@ -304,51 +289,67 @@
         ],
         0,
     )
-    if other_half:
-        first, second = (ref[...].astype(F32) for ref in other_half)
-        blocks = ((first[:rank], first[rank:]), (second[rank:], second[:rank]))
-        turned = [jnp.concatenate([block.T for block in row], 1) for row in blocks]
-        cross = (cross.astype(F32) + jnp.concatenate(turned, 0)).astype(BF16)
     high, low = split(own_mix[...])
     half = dot(high, cross) + dot(low, cross)
     high, low = split(half)
-    other_mix = packed[:, : 2 * rank]
+    place = other.shape[1] - 4 * rank
+    other_mix = other[:, place : place + 2 * rank]
     ab = dot_nt(high, other_mix) + dot_nt(low, other_mix)
-    other_level = packed[:, 2 * rank : 3 * rank].astype(F32) + packed[:, 3 * rank :].astype(F32)
+    place += 2 * rank
+    other_level = other[:, place : place + rank].astype(F32) + other[:, place + rank :].astype(F32)
     gram = square_of(own_level[...], ab, other_level)
     diag = eye_mask(gram.shape[0])
     mean = jnp.sum(jnp.where(diag, gram, 0.0), axis=(0, 1), keepdims=True) / gram.shape[0]
     return gram - jnp.where(diag, mean, 0.0), mean
 
 
-def filter_kernel(count, first, last, *refs):
+def filter_kernel(count, first, last, used, *refs):
     grams, refs = refs[:count], refs[count:]
-    compress_t, offset, own, other, _, refs = *refs[:5], refs[5:]
-    if last:
-        *sketch, pair, sems = refs
+    compress, places, own, other, refs = *refs[:4], refs[4:]
+    *out, pair, turned, sems = refs
+    if not last:
+        *sketch, packed, mix_out, level = out
+        place = packed.shape[1] - 4 * own.shape[0]
+        sketch = sketch[0] if sketch else packed
+    rank, width = own.shape[0], pair.shape[1]
+    if width < used:
+        span = pl.ds(pl.multiple_of(places[0], 128), width)
     else:
-        sketch, mix_out, level, packed, pair, sems = refs
-    rank, width = own.shape[0], pair.shape[1]
-    start = pl.multiple_of(offset[0], 128) if width % 128 == 0 else 0
+        span = slice(0, width)
     copies = [
-        pltpu.make_async_copy(
-            source.at[:, pl.ds(start, width)] if width < own.shape[1] else source,
-            pair.at[slice(i * rank, (i + 1) * rank)],
-            sems.at[i],
-        )
+        pltpu.make_async_copy(source.at[:, span], pair.at[slice(i * rank, (i + 1) * rank)], sems.at[i])
         for i, source in enumerate((own, other))
     ]
     for copy in copies:
         copy.start()
+    flip = places[1]
+    for i in range(2):
+        half = compress[pl.ds(pl.multiple_of((flip + i) % 2 * rank, 128), rank), :]
+        turned[:, i * rank : (i + 1) * rank] = half.T
+    if last:
+        share = out[0].shape[0]
+        compress_t = jnp.concatenate(
+            [
+                turned[pl.ds(pl.multiple_of(places[2 + i] * share, 8), share), :]
+                for i in range(len(out))
+            ],
+            0,
+        )
+    else:
+        compress_t = turned[...]
     gram, mean = first_gram(grams) if first else later_gram(*grams)
     size = gram.shape[0]
     eye = jnp.where(eye_mask(size), 1.0, 0.0)
     z = gram * lax.rsqrt(jnp.sum(gram * gram, axis=(0, 1), keepdims=True) + 1e-6)
-    for _ in range(K_ITERS):
+    for step in range(K_ITERS):
         zh, zl = split(z)
         square = dot3_split(zh, zl, zh, zl)
-        z = dot3_split(zh, zl, *split(1.5 * eye - 0.5 * square))
-    mixing = dot3(compress_t[...], 0.5 * (eye + z))
+        factor = split(1.5 * eye - 0.5 * square)
+        if step < K_ITERS - 1:
+            z = dot3_split(zh, zl, *factor)
+        else:
+            turn = dot3_split(*split(compress_t), zh, zl)
+            mixing = 0.5 * (compress_t + dot3_split(*split(turn), *factor))
     for copy in copies:
         copy.wait()
     high, low = split(mixing)
@@ -356,48 +357,48 @@
     rows = mixing.shape[0]
     tile = next((t for t in (640, 512, 256, 128) if width % t == 0), width)
     for c in range(0, width, tile):
-        wide = dot(both, pair[:, c : c + tile])
-        wide = wide[:rows] + wide[rows:]
+        part = dot(both, pair[:, c : c + tile])
+        part = part[:rows] + part[rows:]
         if last:
-            share = rows // len(sketch)
-            for i, piece in enumerate(sketch):
-                piece[:, c : c + tile] = wide[i * share : (i + 1) * share]
+            for i, piece in enumerate(out):
+                piece[:, c : c + tile] = part[i * share : (i + 1) * share]
         else:
-            sketch[:, c : c + tile] = wide.astype(BF16)
+            sketch[:, c : c + tile] = part.astype(BF16)
     if not last:
         block = dot3_nt(dot3(mixing, gram + mean * eye), mixing)
         mix_out[...] = mixing
         level[...] = block
-        packed[:, : 2 * rank] = high
+        packed[:, place : place + 2 * rank] = high
         high, low = split(block)
-        packed[:, 2 * rank : 3 * rank] = high
-        packed[:, 3 * rank :] = low
-
-
-def cost(flops, bytes_accessed=0):
-    return pl.CostEstimate(flops=int(flops), bytes_accessed=int(bytes_accessed), transcendentals=0)
-
-
-def filter_call(grams, compress_t, offset, own, other, before, width, first, last, pieces):
+        packed[:, place + 2 * rank : place + 3 * rank] = high
+        packed[:, place + 3 * rank :] = low
+
+
+def filter_call(grams, compress, places, own, other, used, width, first, last, pieces, joint):
     rank = own.shape[0]
-    rows = compress_t.shape[0]
     if last:
-        out = [jax.ShapeDtypeStruct((rows // pieces, width), F32)] * pieces
+        share = rank // lax.axis_size("tm")
+        out = [jax.ShapeDtypeStruct((share, width), F32)] * pieces
     else:
-        out = [jax.ShapeDtypeStruct((rows, width), BF16)]
-        out.append(jax.ShapeDtypeStruct((rank, 2 * rank), F32))
-        out.append(jax.ShapeDtypeStruct((rank, rank), F32))
-        out.append(jax.ShapeDtypeStruct((rank, 4 * rank), BF16))
-    args = [*grams, compress_t]
+        out = [] if joint else [jax.ShapeDtypeStruct((rank, width), BF16)]
+        out += [
+            jax.ShapeDtypeStruct((rank, width * joint + 4 * rank), BF16),
+            jax.ShapeDtypeStruct((rank, 2 * rank), F32),
+            jax.ShapeDtypeStruct((rank, rank), F32),
+        ]
+    args = [*grams, compress]
     return pl.pallas_call(
-        functools.partial(filter_kernel, len(grams), first, last),
-        in_specs=[VMEM] * len(args) + [SMEM, ANY, ANY, ANY],
+        functools.partial(filter_kernel, len(grams), first, last, used),
+        in_specs=[VMEM] * len(args) + [SMEM, ANY, ANY],
         out_shape=out,
-        scratch_shapes=[pltpu.VMEM((2 * rank, width), BF16), pltpu.SemaphoreType.DMA((2,))],
+        scratch_shapes=[
+            pltpu.VMEM((2 * rank, width), BF16),
+            pltpu.VMEM((rank, 2 * rank), F32),
+            pltpu.SemaphoreType.DMA((2,)),
+        ],
         compiler_params=PARAMS,
-        cost_estimate=cost(50 * K_ITERS * (2 * rank) ** 3),
         name="sign_filter",
-    )(*args, offset, own, other, before)
+    )(*args, places, own, other)
 
 
 def swap(value, axis, mask):
@@ -439,85 +440,65 @@
     halo = lax.ppermute(
         record[rows - HALO :], "tm", [(source, source + 1) for source in range(count - 1)]
     )
-    side = position // 2 % 2
-    sketch, half = front(
-        record, halo, gauge_lag, fir_taps[None, :], projector, jnp.reshape(1 - side, (1,)).astype(jnp.int32)
-    )
-
-    widths = []
-    width = cols
+    sketch = front(record, halo, gauge_lag, fir_taps[None, :], projector)
+
+    widths = [cols]
     for depth in range(1, depths):
-        if width % 256 == 0:
-            width //= 2
-        widths.append(width)
-    narrowed = [depth for depth in range(depths - 1) if widths[depth] < ([cols] + widths)[depth]]
+        widths.append(widths[-1] // 2 if widths[-1] % 256 == 0 else widths[-1])
+    narrowed = [depth for depth in range(depths - 1) if widths[depth + 1] < widths[depth]]
     assert narrowed == list(range(len(narrowed)))
     span = 2 ** len(narrowed)
 
     def bit_of(where, bit):
         return where // 2**bit % 2
 
-    compress_t = compress.T
-    flipped = jnp.concatenate([compress_t[:, rank:], compress_t[:, :rank]], 1)
-
-    places = [position * 0]
+    def scalars(*values):
+        return jnp.stack([position * 0 + value for value in values]).astype(jnp.int32)
+
+    joined = [0]
     for part in range(span):
         source = position ^ part
-        places.append(sum([bit_of(source, bit) * (cols >> (bit + 1)) for bit in narrowed], position * 0))
-    places = jnp.stack(places).astype(jnp.int32)
+        joined.append(sum([bit_of(source, bit) * (cols >> (bit + 1)) for bit in narrowed], 0))
+    joined = scalars(*joined)
     kept = ahead = None
     for depth in range(depths):
         first, last = depth == 0, depth == depths - 1
         mask = 2**depth
-        weights = jnp.where(bit_of(position, depth) == 0, compress_t, flipped)
-        if last:
-            weights = jnp.concatenate(
-                [
-                    lax.dynamic_slice_in_dim(weights, (position ^ part) * share, share, 0)
-                    for part in range(span)
-                ],
-                0,
-            )
-        here = sketch.shape[1]
-        narrow = not last and widths[depth] < here
-        offset = bit_of(position, depth) * (here // 2) if narrow else jnp.int32(0)
-        offset = places if last else jnp.reshape(offset, (1,)).astype(jnp.int32)
+        here = widths[depth]
         other = swap(sketch, "tm", mask)
         if first:
             grams = gather_parts(pair_gram(sketch, other), "chan")
         else:
-            mixing, level, packed = kept
-            grams = [mixing, level, swap(packed, "tm", mask), *ahead]
-        width = here if last else widths[depth]
-        merge = lambda before: filter_call(
-            grams, weights, offset, sketch, other, before, width, first, last, span
+            grams = [*kept, *ahead, other if packed is None else swap(packed, "tm", mask)]
+        flip = bit_of(position, depth)
+        if last:
+            order = [position ^ part for part in range(span)]
+            places = scalars(0, flip, *order)
+            sketch, *kept = filter_call(
+                grams, compress, places, sketch, other, here, here, first, last, span, False
+            )
+            continue
+        width = widths[depth + 1]
+        places = scalars(flip * (here // 2) if width < here else 0, flip)
+        joint = depth + 1 == depths - 1
+        sent = sketch if sketch.shape[1] == here else sketch[:, :here]
+        part = ahead_gram(sketch, other, swap(sent, "tm", 2 * mask), here)
+        out = filter_call(
+            grams, compress, places, sketch, other, here, width, first, last, span, joint
         )
-        if last:
-            sketch, *kept = merge(grams[0])
-            continue
-        halves = first and cols % 256 == 0
-        partner = swap(half if halves else sketch, "tm", 2 * mask)
-        start = jnp.reshape(side * (here // 2), (1,)).astype(jnp.int32)
-        if first:
-            part = ahead_gram(sketch, other, partner, start, start)
-            merged, *kept = merge(part)
-        else:
-            merged, *kept = merge(grams[0])
-            part = ahead_gram(sketch, other, partner, start, kept[1])
         for bit in [b for b in narrowed if b < depth]:
             part = (part.astype(F32) + swap(part, "tm", 2**bit).astype(F32)).astype(BF16)
         parts = gather_parts(part, "chan")
         total = sum(piece.astype(F32) for piece in parts).astype(BF16)
         ahead = [total, swap(total, "tm", mask)]
-        if halves:
-            ahead += [swap(total, "tm", 2 * mask), swap(total, "tm", 3 * mask)]
-        sketch = merged
+        sketch, *kept = out
+        packed = None if joint else kept.pop(0)
     if span == 1:
         return sketch
     pieces = [sketch] + [
         swap(piece, "tm", part) for part, piece in enumerate(kept, 1)
     ]
-    return join(places, pieces)
+    return join(joined, pieces)
 
 
 def solution(mesh):

time: 93.3 us -> 85.2 us (0.913)
  starting transfers between devices: 31.8 us -> 27.5 us
  local copies, waits for them, and re-layouts: 7.17 us -> 5.32 us
  waiting for transfers between devices: 19.9 us -> 18.2 us
    ppermute x24 -> x21, starting transfers between devices: 29.4 us -> 25 us  [swap(): lax.ppermute(value, axis, [(source, source ^ mask) for source in range(co...]
    unnamed x25 -> x16, local copies, waits for them, and re-layouts: 6.05 us -> 3.55 us
    ppermute x24 -> x21, waiting for transfers between devices: 19.9 us -> 18.2 us  [swap(): lax.ppermute(value, axis, [(source, source ^ mask) for source in range(co...]
  transfers between devices with their start and end apart: 25 -> 22, of which waited for: 9 -> 9; matrix products, arithmetic and copies ran while one was open for 0% -> 1% of each run, Pallas kernels for 25% -> 28%
where the time goes in v6:
time: 85.2 us; the launch traced here: 84.9 us
  Pallas kernels  33.4 us (39%)
  starting transfers between devices  27.5 us (32%)
  waiting for transfers between devices  18.2 us (21%)
  local copies, waits for them, and re-layouts  5.32 us (6%)
    ppermute x21, starting transfers between devices, swap(): lax.ppermute(value, axis, [(source, source ^ mask) for source in range(co...  25 us
    pallas_call x3, Pallas kernels, filter_call(): pl.pallas_call(functools.partial(filter_kernel, len(grams), first, last,...  20 us
    ppermute x21, waiting for transfers between devices, swap(): lax.ppermute(value, axis, [(source, source ^ mask) for source in range(co...  18.2 us
    pallas_call x2, Pallas kernels, front_call(): pl.pallas_call(functools.partial(front_kernel, *blocks), grid=(steps,), i...  10.2 us
    unnamed x16, local copies, waits for them, and re-layouts  3.55 us
    ppermute x1, starting transfers between devices, on_device(): lax.ppermute(record[rows - HALO:], 'tm', [(source, source + 1) for source...  2.51 us
  transfers between devices with their start and end apart: 22, of which 9 were waited for; matrix products, arithmetic and copies ran while one was open for 1% of the time, Pallas kernels for 28%

profile of v6, /device:TPU:0, one launch (start us, length us, event | category | flops | bytes accessed | tf_op | source)
XLA Modules:
  0.0 84.9 jit_solution(14396072283623118540)
XLA Ops:
  0.0 1.0 %slice.3 = bf16[80,2560]{1,0:T(8,128)(2,1)S(1)} slice(bf16[1024,2560]{1,0:T(8,128)(2,1)} %refs_0_.1), slice={[944:1024], [0:2560]} | slice | bytes 819200 | tf_op jit(solution)/shard_map/slice | solution.py:441
  1.0 2.5 %collective-permute-start = (bf16[80,2560]{1,0:T(8,128)(2,1)S(1)}, bf16[80,2560]{1,0:T(8,128)(2,1)S(1)}, u32[]{:S(2)}, u32[]{:S(2)}) collective-permute-start(bf16[80,2560]{1,0:T(8,128)(2,1)S(1)} %slice.3), channel_id=1, source_target_pairs={{0,4},{4,8},{8,12},{12,16},{16,20},{20,24},{24,28},{1,5},{5,9},{9,... | collective-permute-start | bytes 1228808 | tf_op jit(solution)/shard_map/ppermute | solution.py:440
  3.6 0.9 %copy-done.1 = bf16[1024,128]{1,0:T(8,128)(2,1)S(1)} copy-done((bf16[1024,128]{1,0:T(8,128)(2,1)S(1)}, bf16[1024,128]{1,0:T(8,128)(2,1)}, u32[]{:S(2)}) %copy-start.1) | copy-done | bytes 262168
  4.5 0.7 copy-done.2
  5.9 8.8 %front.2 = (f32[128,2560]{1,0:T(8,128)S(1)}, bf16[256,208]{1,0:T(8,128)(2,1)S(1)}, bf16[128,128]{1,0:T(8,128)(2,1)S(1)}, bf16[128,2560]{1,0:T(8,128)(2,1)S(1)}) custom-call(bf16[1024,2560]{1,0:T(8,128)(2,1)} %refs_0_.1, s32[20,128]{1,0:T(8,128)S(1)} %bitcast.15, bf16[1,64]{1,0:T(2,128)(2,1)S(1)} %bitcast.17, bf16[1024,128]{1,0:T(8,128)(2,1)S(1)} %copy-done.1), custom_call_target="tpu_custom_call" | custom-call | tf_op jit(solution)/shard_map/front/pallas_call | solution.py:140
  14.7 1.4 %front.3.own.refs_6_ = bf16[128,2560]{1,0:T(8,128)(2,1)S(1)} custom-call(bf16[128,2560]{1,0:T(8,128)(2,1)S(1)} %get-tuple-element.20.refs_0_, bf16[80,2560]{1,0:T(8,128)(2,1)S(1)} %collective-permute-done.refs_1_, s32[20,128]{1,0:T(8,128)S(1)} %bitcast.16, bf16[256,208]{1,0:T(8,128)(2,1)S(1)} %get-tuple-element.21.refs_3_, ...), custom_call_target="tpu_custom_call" | custom-call | tf_op jit(solution)/shard_map/front/pallas_call | solution.py:140
  16.1 2.6 %collective-permute-start.1 = (bf16[128,2560]{1,0:T(8,128)(2,1)S(1)}, bf16[128,2560]{1,0:T(8,128)(2,1)S(1)}, u32[]{:S(2)}, u32[]{:S(2)}) collective-permute-start(bf16[128,2560]{1,0:T(8,128)(2,1)S(1)} %front.3.own.refs_6_), channel_id=1, source_target_pairs={{0,4},{4,0},{8,12},{12,8},{16,20},{20,16},{24,28},{28,24},{1,5},{5... | collective-permute-start | bytes 1966088 | tf_op jit(solution)/shard_map/ppermute | solution.py:406
  18.7 1.5 %collective-permute-start.5 = (bf16[128,2560]{1,0:T(8,128)(2,1)S(1)}, bf16[128,2560]{1,0:T(8,128)(2,1)S(1)}, u32[]{:S(2)}, u32[]{:S(2)}) collective-permute-start(bf16[128,2560]{1,0:T(8,128)(2,1)S(1)} %front.3.own.refs_6_), channel_id=1, source_target_pairs={{0,8},{4,12},{8,0},{12,4},{16,24},{20,28},{24,16},{28,20},{1,9},{5... | collective-permute-start | bytes 1966088 | tf_op jit(solution)/shard_map/ppermute | solution.py:406
  20.5 0.8 pair_gram.1.refs_0_
  21.3 3.7 %collective-permute-start.4 = (bf16[272,128]{1,0:T(8,128)(2,1)S(1)}, bf16[272,128]{1,0:T(8,128)(2,1)S(1)}, u32[]{:S(2)}, u32[]{:S(2)}) collective-permute-start(bf16[272,128]{1,0:T(8,128)(2,1)S(1)} %pair_gram.1.refs_0_), channel_id=1, source_target_pairs={{0,3},{1,2},{2,1},{3,0},{4,7},{5,6},{6,5},{7,4},{8,11},{9,10},{10,... | collective-permute-start | bytes 208904 | tf_op jit(solution)/shard_map/ppermute | solution.py:406
  25.0 0.8 collective-permute-start.2
  25.8 2.2 %collective-permute-done.4.refs_3_ = bf16[272,128]{1,0:T(8,128)(2,1)S(1)} collective-permute-done((bf16[272,128]{1,0:T(8,128)(2,1)S(1)}, bf16[272,128]{1,0:T(8,128)(2,1)S(1)}, u32[]{:S(2)}, u32[]{:S(2)}) %collective-permute-start.4) | collective-permute-done | bytes 69664 | tf_op jit(solution)/shard_map/ppermute | solution.py:406
  28.0 3.3 %collective-permute-done.3.refs_2_ = bf16[272,128]{1,0:T(8,128)(2,1)S(1)} collective-permute-done((bf16[272,128]{1,0:T(8,128)(2,1)S(1)}, bf16[272,128]{1,0:T(8,128)(2,1)S(1)}, u32[]{:S(2)}, u32[]{:S(2)}) %collective-permute-start.3) | collective-permute-done | bytes 69664 | tf_op jit(solution)/shard_map/ppermute | solution.py:406
  31.3 6.7 %sign_filter.3 = (bf16[128,1280]{1,0:T(8,128)(2,1)S(1)}, bf16[128,512]{1,0:T(8,128)(2,1)S(1)}, f32[128,256]{1,0:T(8,128)S(1)}, f32[128,128]{1,0:T(8,128)S(1)}) custom-call(bf16[272,128]{1,0:T(8,128)(2,1)S(1)} %pair_gram.1.refs_0_, bf16[272,128]{1,0:T(8,128)(2,1)S(1)} %collective-permute-done.2.refs_1_, bf16[272,128]{1,0:T(8,128)(2,1)S(1)} %collective-permute-done.3.refs_2_, ...), custom_call_target="tpu_custom_call" | custom-call | tf_op jit(solution)/shard_map/sign_filter/pallas_call | solution.py:390
  38.0 1.6 %collective-permute-start.12 = (bf16[128,1280]{1,0:T(8,128)(2,1)S(1)}, bf16[128,1280]{1,0:T(8,128)(2,1)S(1)}, u32[]{:S(2)}, u32[]{:S(2)}) collective-permute-start(bf16[128,1280]{1,0:T(8,128)(2,1)S(1)} %get-tuple-element.27.refs_7_.own), channel_id=1, source_target_pairs={{0,16},{4,20},{8,24},{12,28},{16,0},{20,4},{24,8},{28,12},{1,17},{... | collective-permute-start | bytes 983048 | tf_op jit(solution)/shard_map/ppermute | solution.py:406
  40.2 2.6 %collective-permute-start.8 = (bf16[256,128]{1,0:T(8,128)(2,1)S(1)}, bf16[256,128]{1,0:T(8,128)(2,1)S(1)}, u32[]{:S(2)}, u32[]{:S(2)}) collective-permute-start(bf16[256,128]{1,0:T(8,128)(2,1)S(1)} %ahead_gram.2), channel_id=1, source_target_pairs={{0,3},{1,2},{2,1},{3,0},{4,7},{5,6},{6,5},{7,4},{8,11},{9,10},{10,... | collective-permute-start | bytes 196616 | tf_op jit(solution)/shard_map/ppermute | solution.py:406
  42.8 1.9 %collective-permute-start.6 = (bf16[256,128]{1,0:T(8,128)(2,1)S(1)}, bf16[256,128]{1,0:T(8,128)(2,1)S(1)}, u32[]{:S(2)}, u32[]{:S(2)}) collective-permute-start(bf16[256,128]{1,0:T(8,128)(2,1)S(1)} %ahead_gram.2), channel_id=1, source_target_pairs={{0,1},{1,0},{2,3},{3,2},{4,5},{5,4},{6,7},{7,6},{8,9},{9,8},{10,11... | collective-permute-start | bytes 196616 | tf_op jit(solution)/shard_map/ppermute | solution.py:406
  44.7 2.6 %collective-permute-done.12.partner = bf16[128,1280]{1,0:T(8,128)(2,1)S(1)} collective-permute-done((bf16[128,1280]{1,0:T(8,128)(2,1)S(1)}, bf16[128,1280]{1,0:T(8,128)(2,1)S(1)}, u32[]{:S(2)}, u32[]{:S(2)}) %collective-permute-start.12) | collective-permute-done | bytes 327712 | tf_op jit(solution)/shard_map/ppermute | solution.py:406
  47.2 1.2 %collective-permute-done.11.refs_8_.sibling = bf16[128,1280]{1,0:T(8,128)(2,1)S(1)} collective-permute-done((bf16[128,1280]{1,0:T(8,128)(2,1)S(1)}, bf16[128,1280]{1,0:T(8,128)(2,1)S(1)}, u32[]{:S(2)}, u32[]{:S(2)}) %collective-permute-start.11) | collective-permute-done | bytes 327712 | tf_op jit(solution)/shard_map/ppermute | solution.py:406
  49.5 1.2 %collective-permute-start.10 = (bf16[128,512]{1,0:T(8,128)(2,1)S(1)}, bf16[128,512]{1,0:T(8,128)(2,1)S(1)}, u32[]{:S(2)}, u32[]{:S(2)}) collective-permute-start(bf16[128,512]{1,0:T(8,128)(2,1)S(1)} %get-tuple-element.26), channel_id=1, source_target_pairs={{0,8},{4,12},{8,0},{12,4},{16,24},{20,28},{24,16},{28,20},{1,9},{5... | collective-permute-start | bytes 393224 | tf_op jit(solution)/shard_map/ppermute | solution.py:406
  50.7 2.2 %collective-permute-start.16 = (bf16[256,128]{1,0:T(8,128)(2,1)S(1)}, bf16[256,128]{1,0:T(8,128)(2,1)S(1)}, u32[]{:S(2)}, u32[]{:S(2)}) collective-permute-start(bf16[256,128]{1,0:T(8,128)(2,1)S(1)} %add_convert_fusion.1), channel_id=1, source_target_pairs={{0,3},{1,2},{2,1},{3,0},{4,7},{5,6},{6,5},{7,4},{8,11},{9,10},{10,... | collective-permute-start | bytes 196616 | tf_op jit(solution)/shard_map/ppermute | solution.py:406
  52.9 2.2 %collective-permute-start.14 = (bf16[256,128]{1,0:T(8,128)(2,1)S(1)}, bf16[256,128]{1,0:T(8,128)(2,1)S(1)}, u32[]{:S(2)}, u32[]{:S(2)}) collective-permute-start(bf16[256,128]{1,0:T(8,128)(2,1)S(1)} %add_convert_fusion.1), channel_id=1, source_target_pairs={{0,1},{1,0},{2,3},{3,2},{4,5},{5,4},{6,7},{7,6},{8,9},{9,8},{10,11... | collective-permute-start | bytes 196616 | tf_op jit(solution)/shard_map/ppermute | solution.py:406
  55.2 6.8 %sign_filter.4 = (bf16[128,1152]{1,0:T(8,128)(2,1)S(1)}, f32[128,256]{1,0:T(8,128)S(1)}, f32[128,128]{1,0:T(8,128)S(1)}) custom-call(f32[128,256]{1,0:T(8,128)S(1)} %get-tuple-element.24.refs_0_, f32[128,128]{1,0:T(8,128)S(1)} %get-tuple-element.25.refs_1_, bf16[256,128]{1,0:T(8,128)(2,1)S(1)} %add_convert_fusion.2.refs_2_, ...), custom_call_target="tpu_custom_call" | custom-call | tf_op jit(solution)/shard_map/sign_filter/pallas_call | solution.py:390
  62.0 1.3 %collective-permute-start.18 = (bf16[128,1152]{1,0:T(8,128)(2,1)S(1)}, bf16[128,1152]{1,0:T(8,128)(2,1)S(1)}, u32[]{:S(2)}, u32[]{:S(2)}) collective-permute-start(bf16[128,1152]{1,0:T(8,128)(2,1)S(1)} %get-tuple-element.30.refs_7_), channel_id=1, source_target_pairs={{0,16},{4,20},{8,24},{12,28},{16,0},{20,4},{24,8},{28,12},{1,17},{... | collective-permute-start | bytes 884744 | tf_op jit(solution)/shard_map/ppermute | solution.py:406
  63.4 0.8 collective-permute-start.17
  64.3 3.4 %collective-permute-done.17.refs_3_ = bf16[256,128]{1,0:T(8,128)(2,1)S(1)} collective-permute-done((bf16[256,128]{1,0:T(8,128)(2,1)S(1)}, bf16[256,128]{1,0:T(8,128)(2,1)S(1)}, u32[]{:S(2)}, u32[]{:S(2)}) %collective-permute-start.17) | collective-permute-done | bytes 65568 | tf_op jit(solution)/shard_map/ppermute | solution.py:406
  67.7 2.6 %collective-permute-done.18.refs_4_.refs_8_ = bf16[128,1152]{1,0:T(8,128)(2,1)S(1)} collective-permute-done((bf16[128,1152]{1,0:T(8,128)(2,1)S(1)}, bf16[128,1152]{1,0:T(8,128)(2,1)S(1)}, u32[]{:S(2)}, u32[]{:S(2)}) %collective-permute-start.18) | collective-permute-done | bytes 294944 | tf_op jit(solution)/shard_map/ppermute | solution.py:406
  70.3 6.6 %sign_filter.5 = (f32[16,640]{1,0:T(8,128)S(1)}, f32[16,640]{1,0:T(8,128)S(1)}, f32[16,640]{1,0:T(8,128)S(1)}, f32[16,640]{1,0:T(8,128)S(1)}) custom-call(f32[128,256]{1,0:T(8,128)S(1)} %get-tuple-element.28.refs_0_, f32[128,128]{1,0:T(8,128)S(1)} %get-tuple-element.29.refs_1_, bf16[256,128]{1,0:T(8,128)(2,1)S(1)} %add_convert_fusion.refs_2_, ...), custom_call_target="tpu_custom_call" | custom-call | tf_op jit(solution)/shard_map/sign_filter/pallas_call | solution.py:390
  77.5 1.6 %collective-permute-start.20 = (f32[16,640]{1,0:T(8,128)S(1)}, f32[16,640]{1,0:T(8,128)S(1)}, u32[]{:S(2)}, u32[]{:S(2)}) collective-permute-start(f32[16,640]{1,0:T(8,128)S(1)} %get-tuple-element.33), channel_id=1, source_target_pairs={{0,8},{4,12},{8,0},{12,4},{16,24},{20,28},{24,16},{28,20},{1,9},{5... | collective-permute-start | bytes 122888 | tf_op jit(solution)/shard_map/ppermute | solution.py:406
  80.1 1.5 %collective-permute-done.20.refs_2_ = f32[16,640]{1,0:T(8,128)S(1)} collective-permute-done((f32[16,640]{1,0:T(8,128)S(1)}, f32[16,640]{1,0:T(8,128)S(1)}, u32[]{:S(2)}, u32[]{:S(2)}) %collective-permute-start.20) | collective-permute-done | bytes 40992 | tf_op jit(solution)/shard_map/ppermute | solution.py:406
  81.5 1.2 %collective-permute-done.21.refs_3_ = f32[16,640]{1,0:T(8,128)S(1)} collective-permute-done((f32[16,640]{1,0:T(8,128)S(1)}, f32[16,640]{1,0:T(8,128)S(1)}, u32[]{:S(2)}, u32[]{:S(2)}) %collective-permute-start.21) | collective-permute-done | bytes 40992 | tf_op jit(solution)/shard_map/ppermute | solution.py:406
  83.3 1.5 %join.1 = f32[16,2560]{1,0:T(8,128)} custom-call(s32[5]{0:T(128)} %stack.55.offsets, f32[16,640]{1,0:T(8,128)} %copy-done.3, f32[16,640]{1,0:T(8,128)} %copy-done.5, f32[16,640]{1,0:T(8,128)} %copy-done.6, f32[16,640]{1,0:T(8,128)} %copy-done.7), custom_call_target="tpu_custom_call" | custom-call | tf_op jit(solution)/shard_map/join/pallas_call | solution.py:425
  (45 shorter events, 5.0 us)
Async XLA Ops:
  1.0 30.3 %copy-start = (f32[256,128]{1,0:T(8,128)S(1)}, f32[256,128]{1,0:T(8,128)}, u32[]{:S(2)}) copy-start(f32[256,128]{1,0:T(8,128)} %refs_5_.3) | copy-start | bytes 393220
  1.0 13.7 %collective-permute-start = (bf16[80,2560]{1,0:T(8,128)(2,1)S(1)}, bf16[80,2560]{1,0:T(8,128)(2,1)S(1)}, u32[]{:S(2)}, u32[]{:S(2)}) collective-permute-start(bf16[80,2560]{1,0:T(8,128)(2,1)S(1)} %slice.3), channel_id=1, source_target_pairs={{0,4},{4,8},{8,12},{12,16},{16,20},{20,24},{24,28},{1,5},{5,9},{9,... | collective-permute-start | bytes 1228808 | tf_op jit(solution)/shard_map/ppermute | solution.py:440
  3.6 1.0 %copy-start.1 = (bf16[1024,128]{1,0:T(8,128)(2,1)S(1)}, bf16[1024,128]{1,0:T(8,128)(2,1)}, u32[]{:S(2)}) copy-start(bf16[1024,128]{1,0:T(8,128)(2,1)} %refs_3_.1) | copy-start | bytes 786436
  4.5 0.7 copy-start.2
  5.2 0.7 copy-start.4
  16.1 4.4 %collective-permute-start.1 = (bf16[128,2560]{1,0:T(8,128)(2,1)S(1)}, bf16[128,2560]{1,0:T(8,128)(2,1)S(1)}, u32[]{:S(2)}, u32[]{:S(2)}) collective-permute-start(bf16[128,2560]{1,0:T(8,128)(2,1)S(1)} %front.3.own.refs_6_), channel_id=1, source_target_pairs={{0,4},{4,0},{8,12},{12,8},{16,20},{20,16},{24,28},{28,24},{1,5},{5... | collective-permute-start | bytes 1966088 | tf_op jit(solution)/shard_map/ppermute | solution.py:406
  18.7 21.0 %collective-permute-start.5 = (bf16[128,2560]{1,0:T(8,128)(2,1)S(1)}, bf16[128,2560]{1,0:T(8,128)(2,1)S(1)}, u32[]{:S(2)}, u32[]{:S(2)}) collective-permute-start(bf16[128,2560]{1,0:T(8,128)(2,1)S(1)} %front.3.own.refs_6_), channel_id=1, source_target_pairs={{0,8},{4,12},{8,0},{12,4},{16,24},{20,28},{24,16},{28,20},{1,9},{5... | collective-permute-start | bytes 1966088 | tf_op jit(solution)/shard_map/ppermute | solution.py:406
  21.3 6.7 %collective-permute-start.4 = (bf16[272,128]{1,0:T(8,128)(2,1)S(1)}, bf16[272,128]{1,0:T(8,128)(2,1)S(1)}, u32[]{:S(2)}, u32[]{:S(2)}) collective-permute-start(bf16[272,128]{1,0:T(8,128)(2,1)S(1)} %pair_gram.1.refs_0_), channel_id=1, source_target_pairs={{0,3},{1,2},{2,1},{3,0},{4,7},{5,6},{6,5},{7,4},{8,11},{9,10},{10,... | collective-permute-start | bytes 208904 | tf_op jit(solution)/shard_map/ppermute | solution.py:406
  25.0 6.3 %collective-permute-start.3 = (bf16[272,128]{1,0:T(8,128)(2,1)S(1)}, bf16[272,128]{1,0:T(8,128)(2,1)S(1)}, u32[]{:S(2)}, u32[]{:S(2)}) collective-permute-start(bf16[272,128]{1,0:T(8,128)(2,1)S(1)} %pair_gram.1.refs_0_), channel_id=1, source_target_pairs={{0,2},{1,3},{2,0},{3,1},{4,6},{5,7},{6,4},{7,5},{8,10},{9,11},{10,... | collective-permute-start | bytes 208904 | tf_op jit(solution)/shard_map/ppermute | solution.py:406
  25.0 6.3 %collective-permute-start.2 = (bf16[272,128]{1,0:T(8,128)(2,1)S(1)}, bf16[272,128]{1,0:T(8,128)(2,1)S(1)}, u32[]{:S(2)}, u32[]{:S(2)}) collective-permute-start(bf16[272,128]{1,0:T(8,128)(2,1)S(1)} %pair_gram.1.refs_0_), channel_id=1, source_target_pairs={{0,1},{1,0},{2,3},{3,2},{4,5},{5,4},{6,7},{7,6},{8,9},{9,8},{10,11... | collective-permute-start | bytes 208904 | tf_op jit(solution)/shard_map/ppermute | solution.py:406
  38.0 9.2 %collective-permute-start.12 = (bf16[128,1280]{1,0:T(8,128)(2,1)S(1)}, bf16[128,1280]{1,0:T(8,128)(2,1)S(1)}, u32[]{:S(2)}, u32[]{:S(2)}) collective-permute-start(bf16[128,1280]{1,0:T(8,128)(2,1)S(1)} %get-tuple-element.27.refs_7_.own), channel_id=1, source_target_pairs={{0,16},{4,20},{8,24},{12,28},{16,0},{20,4},{24,8},{28,12},{1,17},{... | collective-permute-start | bytes 983048 | tf_op jit(solution)/shard_map/ppermute | solution.py:406
  39.5 8.9 %collective-permute-start.11 = (bf16[128,1280]{1,0:T(8,128)(2,1)S(1)}, bf16[128,1280]{1,0:T(8,128)(2,1)S(1)}, u32[]{:S(2)}, u32[]{:S(2)}) collective-permute-start(bf16[128,1280]{1,0:T(8,128)(2,1)S(1)} %get-tuple-element.27.refs_7_.own), channel_id=1, source_target_pairs={{0,8},{4,12},{8,0},{12,4},{16,24},{20,28},{24,16},{28,20},{1,9},{5... | collective-permute-start | bytes 983048 | tf_op jit(solution)/shard_map/ppermute | solution.py:406
  40.2 8.7 %collective-permute-start.8 = (bf16[256,128]{1,0:T(8,128)(2,1)S(1)}, bf16[256,128]{1,0:T(8,128)(2,1)S(1)}, u32[]{:S(2)}, u32[]{:S(2)}) collective-permute-start(bf16[256,128]{1,0:T(8,128)(2,1)S(1)} %ahead_gram.2), channel_id=1, source_target_pairs={{0,3},{1,2},{2,1},{3,0},{4,7},{5,6},{6,5},{7,4},{8,11},{9,10},{10,... | collective-permute-start | bytes 196616 | tf_op jit(solution)/shard_map/ppermute | solution.py:406
  42.8 6.1 %collective-permute-start.7 = (bf16[256,128]{1,0:T(8,128)(2,1)S(1)}, bf16[256,128]{1,0:T(8,128)(2,1)S(1)}, u32[]{:S(2)}, u32[]{:S(2)}) collective-permute-start(bf16[256,128]{1,0:T(8,128)(2,1)S(1)} %ahead_gram.2), channel_id=1, source_target_pairs={{0,2},{1,3},{2,0},{3,1},{4,6},{5,7},{6,4},{7,5},{8,10},{9,11},{10,... | collective-permute-start | bytes 196616 | tf_op jit(solution)/shard_map/ppermute | solution.py:406
  42.8 6.1 %collective-permute-start.6 = (bf16[256,128]{1,0:T(8,128)(2,1)S(1)}, bf16[256,128]{1,0:T(8,128)(2,1)S(1)}, u32[]{:S(2)}, u32[]{:S(2)}) collective-permute-start(bf16[256,128]{1,0:T(8,128)(2,1)S(1)} %ahead_gram.2), channel_id=1, source_target_pairs={{0,1},{1,0},{2,3},{3,2},{4,5},{5,4},{6,7},{7,6},{8,9},{9,8},{10,11... | collective-permute-start | bytes 196616 | tf_op jit(solution)/shard_map/ppermute | solution.py:406
  48.8 1.9 %collective-permute-start.13 = (bf16[256,128]{1,0:T(8,128)(2,1)S(1)}, bf16[256,128]{1,0:T(8,128)(2,1)S(1)}, u32[]{:S(2)}, u32[]{:S(2)}) collective-permute-start(bf16[256,128]{1,0:T(8,128)(2,1)S(1)} %ahead_gram.3), channel_id=1, source_target_pairs={{0,4},{4,0},{8,12},{12,8},{16,20},{20,16},{24,28},{28,24},{1,5},{5... | collective-permute-start | bytes 196616 | tf_op jit(solution)/shard_map/ppermute | solution.py:406
  48.9 6.3 %collective-permute-start.9 = (bf16[256,128]{1,0:T(8,128)(2,1)S(1)}, bf16[256,128]{1,0:T(8,128)(2,1)S(1)}, u32[]{:S(2)}, u32[]{:S(2)}) collective-permute-start(bf16[256,128]{1,0:T(8,128)(2,1)S(1)} %add_convert_fusion.2.refs_2_), channel_id=1, source_target_pairs={{0,4},{4,0},{8,12},{12,8},{16,20},{20,16},{24,28},{28,24},{1,5},{5... | collective-permute-start | bytes 196616 | tf_op jit(solution)/shard_map/ppermute | solution.py:406
  49.5 5.7 %collective-permute-start.10 = (bf16[128,512]{1,0:T(8,128)(2,1)S(1)}, bf16[128,512]{1,0:T(8,128)(2,1)S(1)}, u32[]{:S(2)}, u32[]{:S(2)}) collective-permute-start(bf16[128,512]{1,0:T(8,128)(2,1)S(1)} %get-tuple-element.26), channel_id=1, source_target_pairs={{0,8},{4,12},{8,0},{12,4},{16,24},{20,28},{24,16},{28,20},{1,9},{5... | collective-permute-start | bytes 393224 | tf_op jit(solution)/shard_map/ppermute | solution.py:406
  50.7 12.6 %collective-permute-start.16 = (bf16[256,128]{1,0:T(8,128)(2,1)S(1)}, bf16[256,128]{1,0:T(8,128)(2,1)S(1)}, u32[]{:S(2)}, u32[]{:S(2)}) collective-permute-start(bf16[256,128]{1,0:T(8,128)(2,1)S(1)} %add_convert_fusion.1), channel_id=1, source_target_pairs={{0,3},{1,2},{2,1},{3,0},{4,7},{5,6},{6,5},{7,4},{8,11},{9,10},{10,... | collective-permute-start | bytes 196616 | tf_op jit(solution)/shard_map/ppermute | solution.py:406
  52.9 10.4 %collective-permute-start.15 = (bf16[256,128]{1,0:T(8,128)(2,1)S(1)}, bf16[256,128]{1,0:T(8,128)(2,1)S(1)}, u32[]{:S(2)}, u32[]{:S(2)}) collective-permute-start(bf16[256,128]{1,0:T(8,128)(2,1)S(1)} %add_convert_fusion.1), channel_id=1, source_target_pairs={{0,2},{1,3},{2,0},{3,1},{4,6},{5,7},{6,4},{7,5},{8,10},{9,11},{10,... | collective-permute-start | bytes 196616 | tf_op jit(solution)/shard_map/ppermute | solution.py:406
  52.9 10.4 %collective-permute-start.14 = (bf16[256,128]{1,0:T(8,128)(2,1)S(1)}, bf16[256,128]{1,0:T(8,128)(2,1)S(1)}, u32[]{:S(2)}, u32[]{:S(2)}) collective-permute-start(bf16[256,128]{1,0:T(8,128)(2,1)S(1)} %add_convert_fusion.1), channel_id=1, source_target_pairs={{0,1},{1,0},{2,3},{3,2},{4,5},{5,4},{6,7},{7,6},{8,9},{9,8},{10,11... | collective-permute-start | bytes 196616 | tf_op jit(solution)/shard_map/ppermute | solution.py:406
  62.0 8.3 %collective-permute-start.18 = (bf16[128,1152]{1,0:T(8,128)(2,1)S(1)}, bf16[128,1152]{1,0:T(8,128)(2,1)S(1)}, u32[]{:S(2)}, u32[]{:S(2)}) collective-permute-start(bf16[128,1152]{1,0:T(8,128)(2,1)S(1)} %get-tuple-element.30.refs_7_), channel_id=1, source_target_pairs={{0,16},{4,20},{8,24},{12,28},{16,0},{20,4},{24,8},{28,12},{1,17},{... | collective-permute-start | bytes 884744 | tf_op jit(solution)/shard_map/ppermute | solution.py:406
  63.4 4.3 %collective-permute-start.17 = (bf16[256,128]{1,0:T(8,128)(2,1)S(1)}, bf16[256,128]{1,0:T(8,128)(2,1)S(1)}, u32[]{:S(2)}, u32[]{:S(2)}) collective-permute-start(bf16[256,128]{1,0:T(8,128)(2,1)S(1)} %add_convert_fusion.refs_2_), channel_id=1, source_target_pairs={{0,8},{4,12},{8,0},{12,4},{16,24},{20,28},{24,16},{28,20},{1,9},{5... | collective-permute-start | bytes 196616 | tf_op jit(solution)/shard_map/ppermute | solution.py:406
  76.9 0.6 copy-start.3
  77.5 2.5 %collective-permute-start.19 = (f32[16,640]{1,0:T(8,128)S(1)}, f32[16,640]{1,0:T(8,128)S(1)}, u32[]{:S(2)}, u32[]{:S(2)}) collective-permute-start(f32[16,640]{1,0:T(8,128)S(1)} %get-tuple-element.32), channel_id=1, source_target_pairs={{0,4},{4,0},{8,12},{12,8},{16,20},{20,16},{24,28},{28,24},{1,5},{5... | collective-permute-start | bytes 122888 | tf_op jit(solution)/shard_map/ppermute | solution.py:406
  77.5 4.0 %collective-permute-start.20 = (f32[16,640]{1,0:T(8,128)S(1)}, f32[16,640]{1,0:T(8,128)S(1)}, u32[]{:S(2)}, u32[]{:S(2)}) collective-permute-start(f32[16,640]{1,0:T(8,128)S(1)} %get-tuple-element.33), channel_id=1, source_target_pairs={{0,8},{4,12},{8,0},{12,4},{16,24},{20,28},{24,16},{28,20},{1,9},{5... | collective-permute-start | bytes 122888 | tf_op jit(solution)/shard_map/ppermute | solution.py:406
  79.2 3.5 %collective-permute-start.21 = (f32[16,640]{1,0:T(8,128)S(1)}, f32[16,640]{1,0:T(8,128)S(1)}, u32[]{:S(2)}, u32[]{:S(2)}) collective-permute-start(f32[16,640]{1,0:T(8,128)S(1)} %get-tuple-element.34), channel_id=1, source_target_pairs={{0,12},{4,8},{8,4},{12,0},{16,28},{20,24},{24,20},{28,16},{1,13},{... | collective-permute-start | bytes 122888 | tf_op jit(solution)/shard_map/ppermute | solution.py:406
  80.1 2.6 %copy-start.5 = (f32[16,640]{1,0:T(8,128)}, f32[16,640]{1,0:T(8,128)S(1)}, u32[]{:S(2)}) copy-start(f32[16,640]{1,0:T(8,128)S(1)} %collective-permute-done.19.refs_1_) | copy-start | bytes 122884
  81.5 1.2 %copy-start.6 = (f32[16,640]{1,0:T(8,128)}, f32[16,640]{1,0:T(8,128)S(1)}, u32[]{:S(2)}) copy-start(f32[16,640]{1,0:T(8,128)S(1)} %collective-permute-done.20.refs_2_) | copy-start | bytes 122884
  82.7 0.6 copy-start.7

commit v7 on v6

--- a/solution.py
+++ b/solution.py
@@ -86,11 +86,10 @@
                 copy.wait()
             turn = one_hot((TAPS, 256), lambda tap: TAPS - tap)
             line = dot(jnp.broadcast_to(taps[...], (8, TAPS)), turn)[0:1]
-            line = jnp.broadcast_to(line, (BLOCK + GAUGE_MAX, 256))
-            rolled = pltpu.roll(line, 0, 1, stride=1, stride_axis=0)[:, : BLOCK + HALO]
-            order = one_hot((2 * BLOCK, BLOCK + GAUGE_MAX), lambda row: row // 8 + STEP * (row % 8))
+            line = jnp.broadcast_to(line, (BLOCK, 256))
+            rolled = pltpu.roll(line, 0, 1, stride=1, stride_axis=0)[:, : BLOCK + TAPS]
+            order = one_hot((BLOCK, BLOCK), lambda row: row // 8 + STEP * (row % 8))
             band[...] = dot(order, rolled.astype(BF16)).astype(BF16)
-            order = one_hot((BLOCK, BLOCK), lambda row: row // 8 + STEP * (row % 8))
             for block in range(projector.shape[0] // BLOCK):
                 part = slice(block * BLOCK, (block + 1) * BLOCK)
                 weights[:, part] = dot(order, projector[part, :]).T.astype(BF16)
@@ -104,27 +103,43 @@
     used = first * BLOCK
     if first > 0:
         head[...] = record[0:BLOCK, :]
+    top = lax.broadcasted_iota(jnp.int32, (STEP, 8, lane), 1) == 0
+
+    def later(rows):
+        return pltpu.roll(rows.reshape(STEP, 8, lane), 1, 1)
+
+    before = {}
+    for g in range(0, cols, group):
+        if first == 0:
+            result = dot(band[:, BLOCK + TAPS - HALO :], halo[:, g : g + group])
+        else:
+            result = dot(band[:, TAPS:], record[(first - 1) * BLOCK : first * BLOCK, g : g + group])
+        for c in range(0, group, lane):
+            before[g + c] = later(result[:, c : c + lane])
     for block in range(first, last):
         start = block * BLOCK
         for g in range(0, cols, group):
             if block == 0:
-                segment = jnp.concatenate([halo[:, g : g + group], record[0:BLOCK, g : g + group]], 0)
+                segment = jnp.concatenate(
+                    [halo[HALO - TAPS :, g : g + group], record[0:BLOCK, g : g + group]], 0
+                )
             else:
-                segment = record[start - HALO : start + BLOCK, g : g + group]
+                segment = record[start - TAPS : start + BLOCK, g : g + group]
             result = dot(band[...], segment)
             for c in range(0, group, lane):
                 line = pl.program_id(0) * lanes + (g + c) // lane
                 shift = GAUGE_MAX - lag[pl.ds(line, 1), :]
-                wide = result[:, c : c + lane]
-                picked = wide
+                here = result[:, c : c + lane]
+                moved = later(here)
+                early = jnp.where(top, before[g + c], moved).reshape(BLOCK, lane)
+                before[g + c] = moved
+                picked = jnp.concatenate([early, here], 0)
                 for step in (8, 4, 2, 1):
                     length = BLOCK + 8 * (step - 1)
                     picked = jnp.where(
                         (shift & step) != 0, picked[8 * step : 8 * step + length], picked[:length]
                     )
-                strain[start : start + BLOCK, g + c : g + c + lane] = (wide[BLOCK:] - picked).astype(
-                    BF16
-                )
+                strain[start : start + BLOCK, g + c : g + c + lane] = (here - picked).astype(BF16)
         done = start + BLOCK
         if done % CHUNK == 0 or block == last - 1:
             part = dot(weights[:, used:done], strain[used:done, :])
@@ -158,7 +173,7 @@
     tile = next((t for t in (512, 640, 256, 128) if cols % t == 0), cols)
     shapes = [
         jax.ShapeDtypeStruct((rank, cols), F32),
-        jax.ShapeDtypeStruct((2 * BLOCK, BLOCK + HALO), BF16),
+        jax.ShapeDtypeStruct((BLOCK, BLOCK + TAPS), BF16),
         jax.ShapeDtypeStruct((rank, BLOCK), BF16),
         jax.ShapeDtypeStruct((BLOCK, cols), BF16),
     ]
@@ -303,7 +318,7 @@
     return gram - jnp.where(diag, mean, 0.0), mean
 
 
-def filter_kernel(count, first, last, used, *refs):
+def filter_kernel(count, first, last, used, base, *refs):
     grams, refs = refs[:count], refs[count:]
     compress, places, own, other, refs = *refs[:4], refs[4:]
     *out, pair, turned, sems = refs
@@ -313,7 +328,7 @@
         sketch = sketch[0] if sketch else packed
     rank, width = own.shape[0], pair.shape[1]
     if width < used:
-        span = pl.ds(pl.multiple_of(places[0], 128), width)
+        span = pl.ds(pl.multiple_of(places[base], 128), width)
     else:
         span = slice(0, width)
     copies = [
@@ -322,7 +337,7 @@
     ]
     for copy in copies:
         copy.start()
-    flip = places[1]
+    flip = places[base + 1]
     for i in range(2):
         half = compress[pl.ds(pl.multiple_of((flip + i) % 2 * rank, 128), rank), :]
         turned[:, i * rank : (i + 1) * rank] = half.T
@@ -330,7 +345,7 @@
         share = out[0].shape[0]
         compress_t = jnp.concatenate(
             [
-                turned[pl.ds(pl.multiple_of(places[2 + i] * share, 8), share), :]
+                turned[pl.ds(pl.multiple_of(places[base + 2 + i] * share, 8), share), :]
                 for i in range(len(out))
             ],
             0,
@@ -374,7 +389,7 @@
         packed[:, place + 3 * rank :] = low
 
 
-def filter_call(grams, compress, places, own, other, used, width, first, last, pieces, joint):
+def filter_call(grams, compress, places, base, own, other, used, width, first, last, pieces, joint):
     rank = own.shape[0]
     if last:
         share = rank // lax.axis_size("tm")
@@ -388,7 +403,7 @@
         ]
     args = [*grams, compress]
     return pl.pallas_call(
-        functools.partial(filter_kernel, len(grams), first, last, used),
+        functools.partial(filter_kernel, len(grams), first, last, used, base),
         in_specs=[VMEM] * len(args) + [SMEM, ANY, ANY],
         out_shape=out,
         scratch_shapes=[
@@ -413,21 +428,22 @@
     return [value] + [swap(value, axis, mask) for mask in range(1, count)]
 
 
-def join_kernel(offsets, *refs):
+def join_kernel(base, places, *refs):
     out = refs[-1]
     width = refs[0].shape[1]
-    for i, piece in enumerate(refs[:-1], 1):
-        out[:, pl.ds(pl.multiple_of(offsets[i], 128), width)] = piece[...]
-
-
-def join(offsets, pieces):
+    for i, piece in enumerate(refs[:-1]):
+        out[:, pl.ds(pl.multiple_of(places[base + i], 128), width)] = piece[...]
+
+
+def join(places, base, pieces):
     share, width = pieces[0].shape
     return pl.pallas_call(
-        join_kernel,
+        functools.partial(join_kernel, base),
         in_specs=[SMEM] + [VMEM] * len(pieces),
         out_shape=jax.ShapeDtypeStruct((share, width * len(pieces)), F32),
+        compiler_params=pltpu.CompilerParams(vmem_limit_bytes=16 * 2**20),
         name="join",
-    )(offsets, *pieces)
+    )(places, *pieces)
 
 
 def on_device(record, fir_taps, gauge_lag, projector, compress):
@@ -452,14 +468,16 @@
     def bit_of(where, bit):
         return where // 2**bit % 2
 
-    def scalars(*values):
-        return jnp.stack([position * 0 + value for value in values]).astype(jnp.int32)
-
-    joined = [0]
+    places = []
+    for depth in range(depths):
+        half = widths[depth] // 2 if depth in narrowed else 0
+        flip = bit_of(position, depth)
+        places += [flip * half, flip]
+    places += [position ^ part for part in range(span)]
+    joined = len(places)
     for part in range(span):
-        source = position ^ part
-        joined.append(sum([bit_of(source, bit) * (cols >> (bit + 1)) for bit in narrowed], 0))
-    joined = scalars(*joined)
+        places.append(sum([bit_of(position ^ part, bit) * (cols >> (bit + 1)) for bit in narrowed], 0))
+    places = jnp.stack([position * 0 + place for place in places]).astype(jnp.int32)
     kept = ahead = None
     for depth in range(depths):
         first, last = depth == 0, depth == depths - 1
@@ -470,21 +488,17 @@
             grams = gather_parts(pair_gram(sketch, other), "chan")
         else:
             grams = [*kept, *ahead, other if packed is None else swap(packed, "tm", mask)]
-        flip = bit_of(position, depth)
         if last:
-            order = [position ^ part for part in range(span)]
-            places = scalars(0, flip, *order)
             sketch, *kept = filter_call(
-                grams, compress, places, sketch, other, here, here, first, last, span, False
+                grams, compress, places, 2 * depth, sketch, other, here, here, first, last, span, False
             )
             continue
         width = widths[depth + 1]
-        places = scalars(flip * (here // 2) if width < here else 0, flip)
         joint = depth + 1 == depths - 1
         sent = sketch if sketch.shape[1] == here else sketch[:, :here]
         part = ahead_gram(sketch, other, swap(sent, "tm", 2 * mask), here)
         out = filter_call(
-            grams, compress, places, sketch, other, here, width, first, last, span, joint
+            grams, compress, places, 2 * depth, sketch, other, here, width, first, last, span, joint
         )
         for bit in [b for b in narrowed if b < depth]:
             part = (part.astype(F32) + swap(part, "tm", 2**bit).astype(F32)).astype(BF16)
@@ -498,7 +512,7 @@
     pieces = [sketch] + [
         swap(piece, "tm", part) for part, piece in enumerate(kept, 1)
     ]
-    return join(joined, pieces)
+    return join(places, joined, pieces)
 
 
 def solution(mesh):

time: 85.2 us -> 85.4 us (level)
  local copies, waits for them, and re-layouts: 5.32 us -> 3.43 us
  Pallas kernels: 33.4 us -> 34.7 us
  waiting for transfers between devices: 18.2 us -> 19.1 us
    pallas_call x2, Pallas kernels: 10.2 us -> 11.8 us  [front_call(): pl.pallas_call(functools.partial(front_kernel, *blocks), grid=(steps,), i...]
    unnamed x16 -> x8, local copies, waits for them, and re-layouts: 3.55 us -> 2.31 us
    ppermute x21, waiting for transfers between devices: 18.2 us -> 19.1 us  [swap(): lax.ppermute(value, axis, [(source, source ^ mask) for source in range(co...]
  transfers between devices with their start and end apart: 22 -> 22, of which waited for: 9 -> 9; matrix products, arithmetic and copies ran while one was open for 1% -> 0% of each run, Pallas kernels for 28% -> 30%
where the time goes in v7:
time: 85.4 us; the launch traced here: 85.1 us
  Pallas kernels  34.7 us (41%)
  starting transfers between devices  27.6 us (32%)
  waiting for transfers between devices  19.1 us (22%)
  local copies, waits for them, and re-layouts  3.43 us (4%)
    ppermute x21, starting transfers between devices, swap(): lax.ppermute(value, axis, [(source, source ^ mask) for source in range(co...  25 us
    pallas_call x3, Pallas kernels, filter_call(): pl.pallas_call(functools.partial(filter_kernel, len(grams), first, last,...  20 us
    ppermute x21, waiting for transfers between devices, swap(): lax.ppermute(value, axis, [(source, source ^ mask) for source in range(co...  19.1 us
    pallas_call x2, Pallas kernels, front_call(): pl.pallas_call(functools.partial(front_kernel, *blocks), grid=(steps,), i...  11.8 us
    ppermute x1, starting transfers between devices, on_device(): lax.ppermute(record[rows - HALO:], 'tm', [(source, source + 1) for source...  2.51 us
    unnamed x8, local copies, waits for them, and re-layouts  2.31 us
  transfers between devices with their start and end apart: 22, of which 9 were waited for; matrix products, arithmetic and copies ran while one was open for 0% of the time, Pallas kernels for 30%

profile of v7, /device:TPU:0, one launch (start us, length us, event | category | flops | bytes accessed | tf_op | source)
XLA Modules:
  0.0 85.1 jit_solution(4441497543774936840)
XLA Ops:
  0.0 1.0 %slice.3 = bf16[80,2560]{1,0:T(8,128)(2,1)S(1)} slice(bf16[1024,2560]{1,0:T(8,128)(2,1)} %refs_0_.1), slice={[944:1024], [0:2560]} | slice | bytes 819200 | tf_op jit(solution)/shard_map/slice | solution.py:457
  1.0 2.5 %collective-permute-start = (bf16[80,2560]{1,0:T(8,128)(2,1)S(1)}, bf16[80,2560]{1,0:T(8,128)(2,1)S(1)}, u32[]{:S(2)}, u32[]{:S(2)}) collective-permute-start(bf16[80,2560]{1,0:T(8,128)(2,1)S(1)} %slice.3), channel_id=1, source_target_pairs={{0,4},{4,8},{8,12},{12,16},{16,20},{20,24},{24,28},{1,5},{5,9},{9,... | collective-permute-start | bytes 1228808 | tf_op jit(solution)/shard_map/ppermute | solution.py:456
  3.6 0.9 %copy-done.1 = bf16[1024,128]{1,0:T(8,128)(2,1)S(1)} copy-done((bf16[1024,128]{1,0:T(8,128)(2,1)S(1)}, bf16[1024,128]{1,0:T(8,128)(2,1)}, u32[]{:S(2)}) %copy-start.1) | copy-done | bytes 262168
  4.5 0.7 copy-done.2
  5.9 10.1 %front.2 = (f32[128,2560]{1,0:T(8,128)S(1)}, bf16[128,192]{1,0:T(8,128)(2,1)S(1)}, bf16[128,128]{1,0:T(8,128)(2,1)S(1)}, bf16[128,2560]{1,0:T(8,128)(2,1)S(1)}) custom-call(bf16[1024,2560]{1,0:T(8,128)(2,1)} %refs_0_.1, s32[20,128]{1,0:T(8,128)S(1)} %bitcast.15, bf16[1,64]{1,0:T(2,128)(2,1)S(1)} %bitcast.17, bf16[1024,128]{1,0:T(8,128)(2,1)S(1)} %copy-done.1), custom_call_target="tpu_custom_call" | custom-call | tf_op jit(solution)/shard_map/front/pallas_call | solution.py:155
  16.0 1.8 %front.3.own.refs_6_ = bf16[128,2560]{1,0:T(8,128)(2,1)S(1)} custom-call(bf16[128,2560]{1,0:T(8,128)(2,1)S(1)} %get-tuple-element.20.refs_0_, bf16[80,2560]{1,0:T(8,128)(2,1)S(1)} %collective-permute-done.refs_1_, s32[20,128]{1,0:T(8,128)S(1)} %bitcast.16, bf16[128,192]{1,0:T(8,128)(2,1)S(1)} %get-tuple-element.21.refs_3_, ...), custom_call_target="tpu_custom_call" | custom-call | tf_op jit(solution)/shard_map/front/pallas_call | solution.py:155
  17.7 2.7 %collective-permute-start.1 = (bf16[128,2560]{1,0:T(8,128)(2,1)S(1)}, bf16[128,2560]{1,0:T(8,128)(2,1)S(1)}, u32[]{:S(2)}, u32[]{:S(2)}) collective-permute-start(bf16[128,2560]{1,0:T(8,128)(2,1)S(1)} %front.3.own.refs_6_), channel_id=1, source_target_pairs={{0,4},{4,0},{8,12},{12,8},{16,20},{20,16},{24,28},{28,24},{1,5},{5... | collective-permute-start | bytes 1966088 | tf_op jit(solution)/shard_map/ppermute | solution.py:421
  20.4 1.5 %collective-permute-start.5 = (bf16[128,2560]{1,0:T(8,128)(2,1)S(1)}, bf16[128,2560]{1,0:T(8,128)(2,1)S(1)}, u32[]{:S(2)}, u32[]{:S(2)}) collective-permute-start(bf16[128,2560]{1,0:T(8,128)(2,1)S(1)} %front.3.own.refs_6_), channel_id=1, source_target_pairs={{0,8},{4,12},{8,0},{12,4},{16,24},{20,28},{24,16},{28,20},{1,9},{5... | collective-permute-start | bytes 1966088 | tf_op jit(solution)/shard_map/ppermute | solution.py:421
  22.1 0.8 pair_gram.1.refs_0_
  23.0 3.7 %collective-permute-start.4 = (bf16[272,128]{1,0:T(8,128)(2,1)S(1)}, bf16[272,128]{1,0:T(8,128)(2,1)S(1)}, u32[]{:S(2)}, u32[]{:S(2)}) collective-permute-start(bf16[272,128]{1,0:T(8,128)(2,1)S(1)} %pair_gram.1.refs_0_), channel_id=1, source_target_pairs={{0,3},{1,2},{2,1},{3,0},{4,7},{5,6},{6,5},{7,4},{8,11},{9,10},{10,... | collective-permute-start | bytes 208904 | tf_op jit(solution)/shard_map/ppermute | solution.py:421
  26.6 0.8 collective-permute-start.2
  27.5 2.1 %collective-permute-done.4.refs_3_ = bf16[272,128]{1,0:T(8,128)(2,1)S(1)} collective-permute-done((bf16[272,128]{1,0:T(8,128)(2,1)S(1)}, bf16[272,128]{1,0:T(8,128)(2,1)S(1)}, u32[]{:S(2)}, u32[]{:S(2)}) %collective-permute-start.4) | collective-permute-done | bytes 69664 | tf_op jit(solution)/shard_map/ppermute | solution.py:421
  29.7 3.3 %collective-permute-done.3.refs_2_ = bf16[272,128]{1,0:T(8,128)(2,1)S(1)} collective-permute-done((bf16[272,128]{1,0:T(8,128)(2,1)S(1)}, bf16[272,128]{1,0:T(8,128)(2,1)S(1)}, u32[]{:S(2)}, u32[]{:S(2)}) %collective-permute-start.3) | collective-permute-done | bytes 69664 | tf_op jit(solution)/shard_map/ppermute | solution.py:421
  33.0 6.7 %sign_filter.3 = (bf16[128,1280]{1,0:T(8,128)(2,1)S(1)}, bf16[128,512]{1,0:T(8,128)(2,1)S(1)}, f32[128,256]{1,0:T(8,128)S(1)}, f32[128,128]{1,0:T(8,128)S(1)}) custom-call(bf16[272,128]{1,0:T(8,128)(2,1)S(1)} %pair_gram.1.refs_0_, bf16[272,128]{1,0:T(8,128)(2,1)S(1)} %collective-permute-done.2.refs_1_, bf16[272,128]{1,0:T(8,128)(2,1)S(1)} %collective-permute-done.3.refs_2_, ...), custom_call_target="tpu_custom_call" | custom-call | tf_op jit(solution)/shard_map/sign_filter/pallas_call | solution.py:405
  39.6 1.6 %collective-permute-start.12 = (bf16[128,1280]{1,0:T(8,128)(2,1)S(1)}, bf16[128,1280]{1,0:T(8,128)(2,1)S(1)}, u32[]{:S(2)}, u32[]{:S(2)}) collective-permute-start(bf16[128,1280]{1,0:T(8,128)(2,1)S(1)} %get-tuple-element.27.refs_7_.own), channel_id=1, source_target_pairs={{0,16},{4,20},{8,24},{12,28},{16,0},{20,4},{24,8},{28,12},{1,17},{... | collective-permute-start | bytes 983048 | tf_op jit(solution)/shard_map/ppermute | solution.py:421
  41.8 2.6 %collective-permute-start.8 = (bf16[256,128]{1,0:T(8,128)(2,1)S(1)}, bf16[256,128]{1,0:T(8,128)(2,1)S(1)}, u32[]{:S(2)}, u32[]{:S(2)}) collective-permute-start(bf16[256,128]{1,0:T(8,128)(2,1)S(1)} %ahead_gram.2), channel_id=1, source_target_pairs={{0,3},{1,2},{2,1},{3,0},{4,7},{5,6},{6,5},{7,4},{8,11},{9,10},{10,... | collective-permute-start | bytes 196616 | tf_op jit(solution)/shard_map/ppermute | solution.py:421
  44.4 1.8 %collective-permute-start.6 = (bf16[256,128]{1,0:T(8,128)(2,1)S(1)}, bf16[256,128]{1,0:T(8,128)(2,1)S(1)}, u32[]{:S(2)}, u32[]{:S(2)}) collective-permute-start(bf16[256,128]{1,0:T(8,128)(2,1)S(1)} %ahead_gram.2), channel_id=1, source_target_pairs={{0,1},{1,0},{2,3},{3,2},{4,5},{5,4},{6,7},{7,6},{8,9},{9,8},{10,11... | collective-permute-start | bytes 196616 | tf_op jit(solution)/shard_map/ppermute | solution.py:421
  46.3 2.6 %collective-permute-done.12.partner = bf16[128,1280]{1,0:T(8,128)(2,1)S(1)} collective-permute-done((bf16[128,1280]{1,0:T(8,128)(2,1)S(1)}, bf16[128,1280]{1,0:T(8,128)(2,1)S(1)}, u32[]{:S(2)}, u32[]{:S(2)}) %collective-permute-start.12) | collective-permute-done | bytes 327712 | tf_op jit(solution)/shard_map/ppermute | solution.py:421
  48.9 1.2 %collective-permute-done.11.refs_8_.sibling = bf16[128,1280]{1,0:T(8,128)(2,1)S(1)} collective-permute-done((bf16[128,1280]{1,0:T(8,128)(2,1)S(1)}, bf16[128,1280]{1,0:T(8,128)(2,1)S(1)}, u32[]{:S(2)}, u32[]{:S(2)}) %collective-permute-start.11) | collective-permute-done | bytes 327712 | tf_op jit(solution)/shard_map/ppermute | solution.py:421
  51.1 1.2 %collective-permute-start.10 = (bf16[128,512]{1,0:T(8,128)(2,1)S(1)}, bf16[128,512]{1,0:T(8,128)(2,1)S(1)}, u32[]{:S(2)}, u32[]{:S(2)}) collective-permute-start(bf16[128,512]{1,0:T(8,128)(2,1)S(1)} %get-tuple-element.26), channel_id=1, source_target_pairs={{0,8},{4,12},{8,0},{12,4},{16,24},{20,28},{24,16},{28,20},{1,9},{5... | collective-permute-start | bytes 393224 | tf_op jit(solution)/shard_map/ppermute | solution.py:421
  52.3 2.2 %collective-permute-start.16 = (bf16[256,128]{1,0:T(8,128)(2,1)S(1)}, bf16[256,128]{1,0:T(8,128)(2,1)S(1)}, u32[]{:S(2)}, u32[]{:S(2)}) collective-permute-start(bf16[256,128]{1,0:T(8,128)(2,1)S(1)} %add_convert_fusion.1), channel_id=1, source_target_pairs={{0,3},{1,2},{2,1},{3,0},{4,7},{5,6},{6,5},{7,4},{8,11},{9,10},{10,... | collective-permute-start | bytes 196616 | tf_op jit(solution)/shard_map/ppermute | solution.py:421
  54.6 2.2 %collective-permute-start.14 = (bf16[256,128]{1,0:T(8,128)(2,1)S(1)}, bf16[256,128]{1,0:T(8,128)(2,1)S(1)}, u32[]{:S(2)}, u32[]{:S(2)}) collective-permute-start(bf16[256,128]{1,0:T(8,128)(2,1)S(1)} %add_convert_fusion.1), channel_id=1, source_target_pairs={{0,1},{1,0},{2,3},{3,2},{4,5},{5,4},{6,7},{7,6},{8,9},{9,8},{10,11... | collective-permute-start | bytes 196616 | tf_op jit(solution)/shard_map/ppermute | solution.py:421
  56.8 6.8 %sign_filter.4 = (bf16[128,1152]{1,0:T(8,128)(2,1)S(1)}, f32[128,256]{1,0:T(8,128)S(1)}, f32[128,128]{1,0:T(8,128)S(1)}) custom-call(f32[128,256]{1,0:T(8,128)S(1)} %get-tuple-element.24.refs_0_, f32[128,128]{1,0:T(8,128)S(1)} %get-tuple-element.25.refs_1_, bf16[256,128]{1,0:T(8,128)(2,1)S(1)} %add_convert_fusion.2.refs_2_, ...), custom_call_target="tpu_custom_call" | custom-call | tf_op jit(solution)/shard_map/sign_filter/pallas_call | solution.py:405
  63.6 1.4 %collective-permute-start.18 = (bf16[128,1152]{1,0:T(8,128)(2,1)S(1)}, bf16[128,1152]{1,0:T(8,128)(2,1)S(1)}, u32[]{:S(2)}, u32[]{:S(2)}) collective-permute-start(bf16[128,1152]{1,0:T(8,128)(2,1)S(1)} %get-tuple-element.30.refs_7_), channel_id=1, source_target_pairs={{0,16},{4,20},{8,24},{12,28},{16,0},{20,4},{24,8},{28,12},{1,17},{... | collective-permute-start | bytes 884744 | tf_op jit(solution)/shard_map/ppermute | solution.py:421
  65.0 0.7 collective-permute-start.17
  65.8 3.6 %collective-permute-done.17.refs_3_ = bf16[256,128]{1,0:T(8,128)(2,1)S(1)} collective-permute-done((bf16[256,128]{1,0:T(8,128)(2,1)S(1)}, bf16[256,128]{1,0:T(8,128)(2,1)S(1)}, u32[]{:S(2)}, u32[]{:S(2)}) %collective-permute-start.17) | collective-permute-done | bytes 65568 | tf_op jit(solution)/shard_map/ppermute | solution.py:421
  69.4 2.5 %collective-permute-done.18.refs_4_.refs_8_ = bf16[128,1152]{1,0:T(8,128)(2,1)S(1)} collective-permute-done((bf16[128,1152]{1,0:T(8,128)(2,1)S(1)}, bf16[128,1152]{1,0:T(8,128)(2,1)S(1)}, u32[]{:S(2)}, u32[]{:S(2)}) %collective-permute-start.18) | collective-permute-done | bytes 294944 | tf_op jit(solution)/shard_map/ppermute | solution.py:421
  71.9 6.6 %sign_filter.5 = (f32[16,640]{1,0:T(8,128)S(1)}, f32[16,640]{1,0:T(8,128)S(1)}, f32[16,640]{1,0:T(8,128)S(1)}, f32[16,640]{1,0:T(8,128)S(1)}) custom-call(f32[128,256]{1,0:T(8,128)S(1)} %get-tuple-element.28.refs_0_, f32[128,128]{1,0:T(8,128)S(1)} %get-tuple-element.29.refs_1_, bf16[256,128]{1,0:T(8,128)(2,1)S(1)} %add_convert_fusion.refs_2_, ...), custom_call_target="tpu_custom_call" | custom-call | tf_op jit(solution)/shard_map/sign_filter/pallas_call | solution.py:405
  78.6 1.8 %collective-permute-start.20 = (f32[16,640]{1,0:T(8,128)S(1)}, f32[16,640]{1,0:T(8,128)S(1)}, u32[]{:S(2)}, u32[]{:S(2)}) collective-permute-start(f32[16,640]{1,0:T(8,128)S(1)} %get-tuple-element.33), channel_id=1, source_target_pairs={{0,8},{4,12},{8,0},{12,4},{16,24},{20,28},{24,16},{28,20},{1,9},{5... | collective-permute-start | bytes 122888 | tf_op jit(solution)/shard_map/ppermute | solution.py:421
  80.4 2.2 %collective-permute-done.20.refs_2_ = f32[16,640]{1,0:T(8,128)S(1)} collective-permute-done((f32[16,640]{1,0:T(8,128)S(1)}, f32[16,640]{1,0:T(8,128)S(1)}, u32[]{:S(2)}, u32[]{:S(2)}) %collective-permute-start.20) | collective-permute-done | bytes 40992 | tf_op jit(solution)/shard_map/ppermute | solution.py:421
  82.7 1.2 %collective-permute-done.21.refs_3_ = f32[16,640]{1,0:T(8,128)S(1)} collective-permute-done((f32[16,640]{1,0:T(8,128)S(1)}, f32[16,640]{1,0:T(8,128)S(1)}, u32[]{:S(2)}, u32[]{:S(2)}) %collective-permute-start.21) | collective-permute-done | bytes 40992 | tf_op jit(solution)/shard_map/ppermute | solution.py:421
  83.9 1.2 %join.1 = f32[16,2560]{1,0:T(8,128)} custom-call(s32[14]{0:T(128)S(1)} %stack.55.refs_5_.refs_6_.places, f32[16,640]{1,0:T(8,128)S(1)} %get-tuple-element.31.refs_0_, f32[16,640]{1,0:T(8,128)S(1)} %collective-permute-done.19.refs_1_, f32[16,640]{1,0:T(8,128)S(1)} %collective-permute-done.20.refs_2_, f32[16,640]{1,0:T(8,128)S(1)} %collective-permute-done.21.refs_3_), custom_call_target="tpu_custom_call" | custom-call | tf_op jit(solution)/shard_map/join/pallas_call | solution.py:440
  (34 shorter events, 2.9 us)
Async XLA Ops:
  1.0 31.9 %copy-start = (f32[256,128]{1,0:T(8,128)S(1)}, f32[256,128]{1,0:T(8,128)}, u32[]{:S(2)}) copy-start(f32[256,128]{1,0:T(8,128)} %refs_5_.3) | copy-start | bytes 393220
  1.0 14.9 %collective-permute-start = (bf16[80,2560]{1,0:T(8,128)(2,1)S(1)}, bf16[80,2560]{1,0:T(8,128)(2,1)S(1)}, u32[]{:S(2)}, u32[]{:S(2)}) collective-permute-start(bf16[80,2560]{1,0:T(8,128)(2,1)S(1)} %slice.3), channel_id=1, source_target_pairs={{0,4},{4,8},{8,12},{12,16},{16,20},{20,24},{24,28},{1,5},{5,9},{9,... | collective-permute-start | bytes 1228808 | tf_op jit(solution)/shard_map/ppermute | solution.py:456
  3.6 1.0 %copy-start.1 = (bf16[1024,128]{1,0:T(8,128)(2,1)S(1)}, bf16[1024,128]{1,0:T(8,128)(2,1)}, u32[]{:S(2)}) copy-start(bf16[1024,128]{1,0:T(8,128)(2,1)} %refs_3_.1) | copy-start | bytes 786436
  4.5 0.7 copy-start.2
  5.2 0.7 copy-start.3
  17.7 4.4 %collective-permute-start.1 = (bf16[128,2560]{1,0:T(8,128)(2,1)S(1)}, bf16[128,2560]{1,0:T(8,128)(2,1)S(1)}, u32[]{:S(2)}, u32[]{:S(2)}) collective-permute-start(bf16[128,2560]{1,0:T(8,128)(2,1)S(1)} %front.3.own.refs_6_), channel_id=1, source_target_pairs={{0,4},{4,0},{8,12},{12,8},{16,20},{20,16},{24,28},{28,24},{1,5},{5... | collective-permute-start | bytes 1966088 | tf_op jit(solution)/shard_map/ppermute | solution.py:421
  20.4 20.9 %collective-permute-start.5 = (bf16[128,2560]{1,0:T(8,128)(2,1)S(1)}, bf16[128,2560]{1,0:T(8,128)(2,1)S(1)}, u32[]{:S(2)}, u32[]{:S(2)}) collective-permute-start(bf16[128,2560]{1,0:T(8,128)(2,1)S(1)} %front.3.own.refs_6_), channel_id=1, source_target_pairs={{0,8},{4,12},{8,0},{12,4},{16,24},{20,28},{24,16},{28,20},{1,9},{5... | collective-permute-start | bytes 1966088 | tf_op jit(solution)/shard_map/ppermute | solution.py:421
  23.0 6.7 %collective-permute-start.4 = (bf16[272,128]{1,0:T(8,128)(2,1)S(1)}, bf16[272,128]{1,0:T(8,128)(2,1)S(1)}, u32[]{:S(2)}, u32[]{:S(2)}) collective-permute-start(bf16[272,128]{1,0:T(8,128)(2,1)S(1)} %pair_gram.1.refs_0_), channel_id=1, source_target_pairs={{0,3},{1,2},{2,1},{3,0},{4,7},{5,6},{6,5},{7,4},{8,11},{9,10},{10,... | collective-permute-start | bytes 208904 | tf_op jit(solution)/shard_map/ppermute | solution.py:421
  26.6 6.3 %collective-permute-start.3 = (bf16[272,128]{1,0:T(8,128)(2,1)S(1)}, bf16[272,128]{1,0:T(8,128)(2,1)S(1)}, u32[]{:S(2)}, u32[]{:S(2)}) collective-permute-start(bf16[272,128]{1,0:T(8,128)(2,1)S(1)} %pair_gram.1.refs_0_), channel_id=1, source_target_pairs={{0,2},{1,3},{2,0},{3,1},{4,6},{5,7},{6,4},{7,5},{8,10},{9,11},{10,... | collective-permute-start | bytes 208904 | tf_op jit(solution)/shard_map/ppermute | solution.py:421
  26.6 6.3 %collective-permute-start.2 = (bf16[272,128]{1,0:T(8,128)(2,1)S(1)}, bf16[272,128]{1,0:T(8,128)(2,1)S(1)}, u32[]{:S(2)}, u32[]{:S(2)}) collective-permute-start(bf16[272,128]{1,0:T(8,128)(2,1)S(1)} %pair_gram.1.refs_0_), channel_id=1, source_target_pairs={{0,1},{1,0},{2,3},{3,2},{4,5},{5,4},{6,7},{7,6},{8,9},{9,8},{10,11... | collective-permute-start | bytes 208904 | tf_op jit(solution)/shard_map/ppermute | solution.py:421
  39.6 9.2 %collective-permute-start.12 = (bf16[128,1280]{1,0:T(8,128)(2,1)S(1)}, bf16[128,1280]{1,0:T(8,128)(2,1)S(1)}, u32[]{:S(2)}, u32[]{:S(2)}) collective-permute-start(bf16[128,1280]{1,0:T(8,128)(2,1)S(1)} %get-tuple-element.27.refs_7_.own), channel_id=1, source_target_pairs={{0,16},{4,20},{8,24},{12,28},{16,0},{20,4},{24,8},{28,12},{1,17},{... | collective-permute-start | bytes 983048 | tf_op jit(solution)/shard_map/ppermute | solution.py:421
  41.2 8.9 %collective-permute-start.11 = (bf16[128,1280]{1,0:T(8,128)(2,1)S(1)}, bf16[128,1280]{1,0:T(8,128)(2,1)S(1)}, u32[]{:S(2)}, u32[]{:S(2)}) collective-permute-start(bf16[128,1280]{1,0:T(8,128)(2,1)S(1)} %get-tuple-element.27.refs_7_.own), channel_id=1, source_target_pairs={{0,8},{4,12},{8,0},{12,4},{16,24},{20,28},{24,16},{28,20},{1,9},{5... | collective-permute-start | bytes 983048 | tf_op jit(solution)/shard_map/ppermute | solution.py:421
  41.8 8.7 %collective-permute-start.8 = (bf16[256,128]{1,0:T(8,128)(2,1)S(1)}, bf16[256,128]{1,0:T(8,128)(2,1)S(1)}, u32[]{:S(2)}, u32[]{:S(2)}) collective-permute-start(bf16[256,128]{1,0:T(8,128)(2,1)S(1)} %ahead_gram.2), channel_id=1, source_target_pairs={{0,3},{1,2},{2,1},{3,0},{4,7},{5,6},{6,5},{7,4},{8,11},{9,10},{10,... | collective-permute-start | bytes 196616 | tf_op jit(solution)/shard_map/ppermute | solution.py:421
  44.4 6.1 %collective-permute-start.7 = (bf16[256,128]{1,0:T(8,128)(2,1)S(1)}, bf16[256,128]{1,0:T(8,128)(2,1)S(1)}, u32[]{:S(2)}, u32[]{:S(2)}) collective-permute-start(bf16[256,128]{1,0:T(8,128)(2,1)S(1)} %ahead_gram.2), channel_id=1, source_target_pairs={{0,2},{1,3},{2,0},{3,1},{4,6},{5,7},{6,4},{7,5},{8,10},{9,11},{10,... | collective-permute-start | bytes 196616 | tf_op jit(solution)/shard_map/ppermute | solution.py:421
  44.4 6.1 %collective-permute-start.6 = (bf16[256,128]{1,0:T(8,128)(2,1)S(1)}, bf16[256,128]{1,0:T(8,128)(2,1)S(1)}, u32[]{:S(2)}, u32[]{:S(2)}) collective-permute-start(bf16[256,128]{1,0:T(8,128)(2,1)S(1)} %ahead_gram.2), channel_id=1, source_target_pairs={{0,1},{1,0},{2,3},{3,2},{4,5},{5,4},{6,7},{7,6},{8,9},{9,8},{10,11... | collective-permute-start | bytes 196616 | tf_op jit(solution)/shard_map/ppermute | solution.py:421
  50.4 1.9 %collective-permute-start.13 = (bf16[256,128]{1,0:T(8,128)(2,1)S(1)}, bf16[256,128]{1,0:T(8,128)(2,1)S(1)}, u32[]{:S(2)}, u32[]{:S(2)}) collective-permute-start(bf16[256,128]{1,0:T(8,128)(2,1)S(1)} %ahead_gram.3), channel_id=1, source_target_pairs={{0,4},{4,0},{8,12},{12,8},{16,20},{20,16},{24,28},{28,24},{1,5},{5... | collective-permute-start | bytes 196616 | tf_op jit(solution)/shard_map/ppermute | solution.py:421
  50.6 6.2 %collective-permute-start.9 = (bf16[256,128]{1,0:T(8,128)(2,1)S(1)}, bf16[256,128]{1,0:T(8,128)(2,1)S(1)}, u32[]{:S(2)}, u32[]{:S(2)}) collective-permute-start(bf16[256,128]{1,0:T(8,128)(2,1)S(1)} %add_convert_fusion.2.refs_2_), channel_id=1, source_target_pairs={{0,4},{4,0},{8,12},{12,8},{16,20},{20,16},{24,28},{28,24},{1,5},{5... | collective-permute-start | bytes 196616 | tf_op jit(solution)/shard_map/ppermute | solution.py:421
  51.1 5.6 %collective-permute-start.10 = (bf16[128,512]{1,0:T(8,128)(2,1)S(1)}, bf16[128,512]{1,0:T(8,128)(2,1)S(1)}, u32[]{:S(2)}, u32[]{:S(2)}) collective-permute-start(bf16[128,512]{1,0:T(8,128)(2,1)S(1)} %get-tuple-element.26), channel_id=1, source_target_pairs={{0,8},{4,12},{8,0},{12,4},{16,24},{20,28},{24,16},{28,20},{1,9},{5... | collective-permute-start | bytes 393224 | tf_op jit(solution)/shard_map/ppermute | solution.py:421
  52.3 12.6 %collective-permute-start.16 = (bf16[256,128]{1,0:T(8,128)(2,1)S(1)}, bf16[256,128]{1,0:T(8,128)(2,1)S(1)}, u32[]{:S(2)}, u32[]{:S(2)}) collective-permute-start(bf16[256,128]{1,0:T(8,128)(2,1)S(1)} %add_convert_fusion.1), channel_id=1, source_target_pairs={{0,3},{1,2},{2,1},{3,0},{4,7},{5,6},{6,5},{7,4},{8,11},{9,10},{10,... | collective-permute-start | bytes 196616 | tf_op jit(solution)/shard_map/ppermute | solution.py:421
  54.6 10.4 %collective-permute-start.15 = (bf16[256,128]{1,0:T(8,128)(2,1)S(1)}, bf16[256,128]{1,0:T(8,128)(2,1)S(1)}, u32[]{:S(2)}, u32[]{:S(2)}) collective-permute-start(bf16[256,128]{1,0:T(8,128)(2,1)S(1)} %add_convert_fusion.1), channel_id=1, source_target_pairs={{0,2},{1,3},{2,0},{3,1},{4,6},{5,7},{6,4},{7,5},{8,10},{9,11},{10,... | collective-permute-start | bytes 196616 | tf_op jit(solution)/shard_map/ppermute | solution.py:421
  54.6 10.4 %collective-permute-start.14 = (bf16[256,128]{1,0:T(8,128)(2,1)S(1)}, bf16[256,128]{1,0:T(8,128)(2,1)S(1)}, u32[]{:S(2)}, u32[]{:S(2)}) collective-permute-start(bf16[256,128]{1,0:T(8,128)(2,1)S(1)} %add_convert_fusion.1), channel_id=1, source_target_pairs={{0,1},{1,0},{2,3},{3,2},{4,5},{5,4},{6,7},{7,6},{8,9},{9,8},{10,11... | collective-permute-start | bytes 196616 | tf_op jit(solution)/shard_map/ppermute | solution.py:421
  63.6 8.3 %collective-permute-start.18 = (bf16[128,1152]{1,0:T(8,128)(2,1)S(1)}, bf16[128,1152]{1,0:T(8,128)(2,1)S(1)}, u32[]{:S(2)}, u32[]{:S(2)}) collective-permute-start(bf16[128,1152]{1,0:T(8,128)(2,1)S(1)} %get-tuple-element.30.refs_7_), channel_id=1, source_target_pairs={{0,16},{4,20},{8,24},{12,28},{16,0},{20,4},{24,8},{28,12},{1,17},{... | collective-permute-start | bytes 884744 | tf_op jit(solution)/shard_map/ppermute | solution.py:421
  65.0 4.3 %collective-permute-start.17 = (bf16[256,128]{1,0:T(8,128)(2,1)S(1)}, bf16[256,128]{1,0:T(8,128)(2,1)S(1)}, u32[]{:S(2)}, u32[]{:S(2)}) collective-permute-start(bf16[256,128]{1,0:T(8,128)(2,1)S(1)} %add_convert_fusion.refs_2_), channel_id=1, source_target_pairs={{0,8},{4,12},{8,0},{12,4},{16,24},{20,28},{24,16},{28,20},{1,9},{5... | collective-permute-start | bytes 196616 | tf_op jit(solution)/shard_map/ppermute | solution.py:421
  78.5 1.9 %collective-permute-start.19 = (f32[16,640]{1,0:T(8,128)S(1)}, f32[16,640]{1,0:T(8,128)S(1)}, u32[]{:S(2)}, u32[]{:S(2)}) collective-permute-start(f32[16,640]{1,0:T(8,128)S(1)} %get-tuple-element.32), channel_id=1, source_target_pairs={{0,4},{4,0},{8,12},{12,8},{16,20},{20,16},{24,28},{28,24},{1,5},{5... | collective-permute-start | bytes 122888 | tf_op jit(solution)/shard_map/ppermute | solution.py:421
  78.6 4.1 %collective-permute-start.20 = (f32[16,640]{1,0:T(8,128)S(1)}, f32[16,640]{1,0:T(8,128)S(1)}, u32[]{:S(2)}, u32[]{:S(2)}) collective-permute-start(f32[16,640]{1,0:T(8,128)S(1)} %get-tuple-element.33), channel_id=1, source_target_pairs={{0,8},{4,12},{8,0},{12,4},{16,24},{20,28},{24,16},{28,20},{1,9},{5... | collective-permute-start | bytes 122888 | tf_op jit(solution)/shard_map/ppermute | solution.py:421
  80.3 3.5 %collective-permute-start.21 = (f32[16,640]{1,0:T(8,128)S(1)}, f32[16,640]{1,0:T(8,128)S(1)}, u32[]{:S(2)}, u32[]{:S(2)}) collective-permute-start(f32[16,640]{1,0:T(8,128)S(1)} %get-tuple-element.34), channel_id=1, source_target_pairs={{0,12},{4,8},{8,4},{12,0},{16,28},{20,24},{24,20},{28,16},{1,13},{... | collective-permute-start | bytes 122888 | tf_op jit(solution)/shard_map/ppermute | solution.py:421

commit v8 on v7

--- a/solution.py
+++ b/solution.py
@@ -86,10 +86,11 @@
                 copy.wait()
             turn = one_hot((TAPS, 256), lambda tap: TAPS - tap)
             line = dot(jnp.broadcast_to(taps[...], (8, TAPS)), turn)[0:1]
-            line = jnp.broadcast_to(line, (BLOCK, 256))
-            rolled = pltpu.roll(line, 0, 1, stride=1, stride_axis=0)[:, : BLOCK + TAPS]
+            line = jnp.broadcast_to(line, (BLOCK + GAUGE_MAX, 256))
+            rolled = pltpu.roll(line, 0, 1, stride=1, stride_axis=0)[:, : BLOCK + HALO]
+            order = one_hot((2 * BLOCK, BLOCK + GAUGE_MAX), lambda row: row // 8 + STEP * (row % 8))
+            band[...] = dot(order, rolled.astype(BF16)).astype(BF16)
             order = one_hot((BLOCK, BLOCK), lambda row: row // 8 + STEP * (row % 8))
-            band[...] = dot(order, rolled.astype(BF16)).astype(BF16)
             for block in range(projector.shape[0] // BLOCK):
                 part = slice(block * BLOCK, (block + 1) * BLOCK)
                 weights[:, part] = dot(order, projector[part, :]).T.astype(BF16)
@@ -103,43 +104,27 @@
     used = first * BLOCK
     if first > 0:
         head[...] = record[0:BLOCK, :]
-    top = lax.broadcasted_iota(jnp.int32, (STEP, 8, lane), 1) == 0
-
-    def later(rows):
-        return pltpu.roll(rows.reshape(STEP, 8, lane), 1, 1)
-
-    before = {}
-    for g in range(0, cols, group):
-        if first == 0:
-            result = dot(band[:, BLOCK + TAPS - HALO :], halo[:, g : g + group])
-        else:
-            result = dot(band[:, TAPS:], record[(first - 1) * BLOCK : first * BLOCK, g : g + group])
-        for c in range(0, group, lane):
-            before[g + c] = later(result[:, c : c + lane])
     for block in range(first, last):
         start = block * BLOCK
         for g in range(0, cols, group):
             if block == 0:
-                segment = jnp.concatenate(
-                    [halo[HALO - TAPS :, g : g + group], record[0:BLOCK, g : g + group]], 0
-                )
+                segment = jnp.concatenate([halo[:, g : g + group], record[0:BLOCK, g : g + group]], 0)
             else:
-                segment = record[start - TAPS : start + BLOCK, g : g + group]
+                segment = record[start - HALO : start + BLOCK, g : g + group]
             result = dot(band[...], segment)
             for c in range(0, group, lane):
                 line = pl.program_id(0) * lanes + (g + c) // lane
                 shift = GAUGE_MAX - lag[pl.ds(line, 1), :]
-                here = result[:, c : c + lane]
-                moved = later(here)
-                early = jnp.where(top, before[g + c], moved).reshape(BLOCK, lane)
-                before[g + c] = moved
-                picked = jnp.concatenate([early, here], 0)
+                wide = result[:, c : c + lane]
+                picked = wide
                 for step in (8, 4, 2, 1):
                     length = BLOCK + 8 * (step - 1)
                     picked = jnp.where(
                         (shift & step) != 0, picked[8 * step : 8 * step + length], picked[:length]
                     )
-                strain[start : start + BLOCK, g + c : g + c + lane] = (here - picked).astype(BF16)
+                strain[start : start + BLOCK, g + c : g + c + lane] = (wide[BLOCK:] - picked).astype(
+                    BF16
+                )
         done = start + BLOCK
         if done % CHUNK == 0 or block == last - 1:
             part = dot(weights[:, used:done], strain[used:done, :])
@@ -173,7 +158,7 @@
     tile = next((t for t in (512, 640, 256, 128) if cols % t == 0), cols)
     shapes = [
         jax.ShapeDtypeStruct((rank, cols), F32),
-        jax.ShapeDtypeStruct((BLOCK, BLOCK + TAPS), BF16),
+        jax.ShapeDtypeStruct((2 * BLOCK, BLOCK + HALO), BF16),
         jax.ShapeDtypeStruct((rank, BLOCK), BF16),
         jax.ShapeDtypeStruct((BLOCK, cols), BF16),
     ]
@@ -320,36 +305,35 @@
 
 def filter_kernel(count, first, last, used, base, *refs):
     grams, refs = refs[:count], refs[count:]
-    compress, places, own, other, refs = *refs[:4], refs[4:]
-    *out, pair, turned, sems = refs
-    if not last:
-        *sketch, packed, mix_out, level = out
-        place = packed.shape[1] - 4 * own.shape[0]
-        sketch = sketch[0] if sketch else packed
-    rank, width = own.shape[0], pair.shape[1]
-    if width < used:
-        span = pl.ds(pl.multiple_of(places[base], 128), width)
+    compress, places, refs = refs[0], refs[1], refs[2:]
+    if last:
+        mix_out, turned = refs
+        rank, share = compress.shape[1], mix_out.shape[0] // used
     else:
-        span = slice(0, width)
-    copies = [
-        pltpu.make_async_copy(source.at[:, span], pair.at[slice(i * rank, (i + 1) * rank)], sems.at[i])
-        for i, source in enumerate((own, other))
-    ]
-    for copy in copies:
-        copy.start()
+        own, other, sketch, packed, mix_out, level, pair, turned, sems = refs
+        rank, width = own.shape[0], pair.shape[1]
+        if width < used:
+            span = pl.ds(pl.multiple_of(places[base], 128), width)
+        else:
+            span = slice(0, width)
+        copies = [
+            pltpu.make_async_copy(
+                source.at[:, span], pair.at[slice(i * rank, (i + 1) * rank)], sems.at[i]
+            )
+            for i, source in enumerate((own, other))
+        ]
+        for copy in copies:
+            copy.start()
     flip = places[base + 1]
     for i in range(2):
         half = compress[pl.ds(pl.multiple_of((flip + i) % 2 * rank, 128), rank), :]
         turned[:, i * rank : (i + 1) * rank] = half.T
     if last:
-        share = out[0].shape[0]
-        compress_t = jnp.concatenate(
-            [
-                turned[pl.ds(pl.multiple_of(places[base + 2 + i] * share, 8), share), :]
-                for i in range(len(out))
-            ],
-            0,
-        )
+        parts = [
+            turned[pl.ds(pl.multiple_of(places[base + 2 + i] * share, 8), share), :]
+            for i in range(used)
+        ]
+        compress_t = jnp.concatenate(parts, 0) if used > 1 else parts[0]
     else:
         compress_t = turned[...]
     gram, mean = first_gram(grams) if first else later_gram(*grams)
@@ -365,47 +349,37 @@
         else:
             turn = dot3_split(*split(compress_t), zh, zl)
             mixing = 0.5 * (compress_t + dot3_split(*split(turn), *factor))
+    mix_out[...] = mixing
+    if last:
+        return
     for copy in copies:
         copy.wait()
     high, low = split(mixing)
     both = jnp.concatenate([high, low], 0)
-    rows = mixing.shape[0]
     tile = next((t for t in (640, 512, 256, 128) if width % t == 0), width)
     for c in range(0, width, tile):
         part = dot(both, pair[:, c : c + tile])
-        part = part[:rows] + part[rows:]
-        if last:
-            for i, piece in enumerate(out):
-                piece[:, c : c + tile] = part[i * share : (i + 1) * share]
-        else:
-            sketch[:, c : c + tile] = part.astype(BF16)
-    if not last:
-        block = dot3_nt(dot3(mixing, gram + mean * eye), mixing)
-        mix_out[...] = mixing
-        level[...] = block
-        packed[:, place : place + 2 * rank] = high
-        high, low = split(block)
-        packed[:, place + 2 * rank : place + 3 * rank] = high
-        packed[:, place + 3 * rank :] = low
-
-
-def filter_call(grams, compress, places, base, own, other, used, width, first, last, pieces, joint):
+        sketch[:, c : c + tile] = (part[:rank] + part[rank:]).astype(BF16)
+    block = dot3_nt(dot3(mixing, gram + mean * eye), mixing)
+    level[...] = block
+    packed[:, : 2 * rank] = high
+    high, low = split(block)
+    packed[:, 2 * rank : 3 * rank] = high
+    packed[:, 3 * rank :] = low
+
+
+def filter_call(grams, compress, places, base, own, other, used, width, first):
     rank = own.shape[0]
-    if last:
-        share = rank // lax.axis_size("tm")
-        out = [jax.ShapeDtypeStruct((share, width), F32)] * pieces
-    else:
-        out = [] if joint else [jax.ShapeDtypeStruct((rank, width), BF16)]
-        out += [
-            jax.ShapeDtypeStruct((rank, width * joint + 4 * rank), BF16),
+    args = [*grams, compress]
+    return pl.pallas_call(
+        functools.partial(filter_kernel, len(grams), first, False, used, base),
+        in_specs=[VMEM] * len(args) + [SMEM, ANY, ANY],
+        out_shape=[
+            jax.ShapeDtypeStruct((rank, width), BF16),
+            jax.ShapeDtypeStruct((rank, 4 * rank), BF16),
             jax.ShapeDtypeStruct((rank, 2 * rank), F32),
             jax.ShapeDtypeStruct((rank, rank), F32),
-        ]
-    args = [*grams, compress]
-    return pl.pallas_call(
-        functools.partial(filter_kernel, len(grams), first, last, used, base),
-        in_specs=[VMEM] * len(args) + [SMEM, ANY, ANY],
-        out_shape=out,
+        ],
         scratch_shapes=[
             pltpu.VMEM((2 * rank, width), BF16),
             pltpu.VMEM((rank, 2 * rank), F32),
@@ -414,6 +388,43 @@
         compiler_params=PARAMS,
         name="sign_filter",
     )(*args, places, own, other)
+
+
+def last_filter_call(grams, compress, places, base, first, share, pieces):
+    rank = compress.shape[1]
+    args = [*grams, compress]
+    return pl.pallas_call(
+        functools.partial(filter_kernel, len(grams), first, True, pieces, base),
+        in_specs=[VMEM] * len(args) + [SMEM],
+        out_shape=jax.ShapeDtypeStruct((share * pieces, 2 * rank), F32),
+        scratch_shapes=[pltpu.VMEM((rank, 2 * rank), F32)],
+        compiler_params=PARAMS,
+        name="sign_filter",
+    )(*args, places)
+
+
+def mix_kernel(mixing, own, other, *out):
+    rank = own.shape[0]
+    rows, share = mixing.shape[0], out[0].shape[0]
+    both = jnp.concatenate(split(mixing[...]), 0)
+    width = own.shape[1]
+    tile = next((t for t in (640, 512, 256, 128) if width % t == 0), width)
+    for c in range(0, width, tile):
+        span = slice(c, c + tile)
+        part = dot(both, jnp.concatenate([own[:, span], other[:, span]], 0))
+        part = part[:rows] + part[rows:]
+        for i, piece in enumerate(out):
+            piece[:, span] = part[i * share : (i + 1) * share]
+
+
+def mix(mixing, own, other, pieces):
+    shape = jax.ShapeDtypeStruct((mixing.shape[0] // pieces, own.shape[1]), F32)
+    return pl.pallas_call(
+        mix_kernel,
+        out_shape=[shape] * pieces,
+        compiler_params=pltpu.CompilerParams(vmem_limit_bytes=16 * 2**20),
+        name="mix",
+    )(mixing, own, other)
 
 
 def swap(value, axis, mask):
@@ -460,7 +471,7 @@
 
     widths = [cols]
     for depth in range(1, depths):
-        widths.append(widths[-1] // 2 if widths[-1] % 256 == 0 else widths[-1])
+        widths.append(cols // 2 if cols % 256 == 0 else cols)
     narrowed = [depth for depth in range(depths - 1) if widths[depth + 1] < widths[depth]]
     assert narrowed == list(range(len(narrowed)))
     span = 2 ** len(narrowed)
@@ -487,31 +498,25 @@
         if first:
             grams = gather_parts(pair_gram(sketch, other), "chan")
         else:
-            grams = [*kept, *ahead, other if packed is None else swap(packed, "tm", mask)]
+            packed, *kept = kept
+            grams = [*kept, *ahead, swap(packed, "tm", mask)]
         if last:
-            sketch, *kept = filter_call(
-                grams, compress, places, 2 * depth, sketch, other, here, here, first, last, span, False
-            )
-            continue
-        width = widths[depth + 1]
-        joint = depth + 1 == depths - 1
-        sent = sketch if sketch.shape[1] == here else sketch[:, :here]
-        part = ahead_gram(sketch, other, swap(sent, "tm", 2 * mask), here)
-        out = filter_call(
-            grams, compress, places, 2 * depth, sketch, other, here, width, first, last, span, joint
+            mixing = last_filter_call(grams, compress, places, 2 * depth, first, share, span)
+            pieces = mix(mixing, sketch, other, span)
+            break
+        part = ahead_gram(sketch, other, swap(sketch, "tm", 2 * mask), here)
+        merged, *kept = filter_call(
+            grams, compress, places, 2 * depth, sketch, other, here, widths[depth + 1], first
         )
         for bit in [b for b in narrowed if b < depth]:
             part = (part.astype(F32) + swap(part, "tm", 2**bit).astype(F32)).astype(BF16)
         parts = gather_parts(part, "chan")
         total = sum(piece.astype(F32) for piece in parts).astype(BF16)
         ahead = [total, swap(total, "tm", mask)]
-        sketch, *kept = out
-        packed = None if joint else kept.pop(0)
+        sketch = merged
     if span == 1:
-        return sketch
-    pieces = [sketch] + [
-        swap(piece, "tm", part) for part, piece in enumerate(kept, 1)
-    ]
+        return pieces[0]
+    pieces = [pieces[0]] + [swap(piece, "tm", part) for part, piece in enumerate(pieces[1:], 1)]
     return join(places, joined, pieces)
 
 

time: 85.4 us -> 83.4 us (0.977)
  Pallas kernels: 34.7 us -> 33.3 us
    pallas_call x2, Pallas kernels: 11.8 us -> 10.2 us  [front_call(): pl.pallas_call(functools.partial(front_kernel, *blocks), grid=(steps,), i...]
    ppermute x21 -> x20, starting transfers between devices: 25 us -> 24.6 us  [swap(): lax.ppermute(value, axis, [(source, source ^ mask) for source in range(co...]
    pallas_call x3 -> x4, Pallas kernels: 20 us -> 20.2 us  [the longest x2 13.9 us: filter_call(): pl.pallas_call(functools.partial(filter_kernel, len(grams), first, False,...]
    ppermute x21 -> x20, waiting for transfers between devices: 19.1 us -> 19 us  [swap(): lax.ppermute(value, axis, [(source, source ^ mask) for source in range(co...]
  transfers between devices with their start and end apart: 22 -> 21, of which waited for: 9 -> 7; matrix products, arithmetic and copies ran while one was open for 0% -> 0% of each run, Pallas kernels for 30% -> 37%
where the time goes in v8:
time: 83.4 us; the launch traced here: 83.1 us
  Pallas kernels  33.3 us (40%)
  starting transfers between devices  27.1 us (32%)
  waiting for transfers between devices  19 us (23%)
  local copies, waits for them, and re-layouts  3.43 us (4%)
    ppermute x20, starting transfers between devices, swap(): lax.ppermute(value, axis, [(source, source ^ mask) for source in range(co...  24.6 us
    ppermute x20, waiting for transfers between devices, swap(): lax.ppermute(value, axis, [(source, source ^ mask) for source in range(co...  19 us
    pallas_call x2, Pallas kernels, filter_call(): pl.pallas_call(functools.partial(filter_kernel, len(grams), first, False,...  13.9 us
    pallas_call x2, Pallas kernels, front_call(): pl.pallas_call(functools.partial(front_kernel, *blocks), grid=(steps,), i...  10.2 us
    pallas_call x1, Pallas kernels, last_filter_call(): pl.pallas_call(functools.partial(filter_kernel, len(grams), first, True,...  6.09 us
    ppermute x1, starting transfers between devices, on_device(): lax.ppermute(record[rows - HALO:], 'tm', [(source, source + 1) for source...  2.51 us
    unnamed x8, local copies, waits for them, and re-layouts  2.31 us
  transfers between devices with their start and end apart: 21, of which 7 were waited for; matrix products, arithmetic and copies ran while one was open for 0% of the time, Pallas kernels for 37%

profile of v8, /device:TPU:0, one launch (start us, length us, event | category | flops | bytes accessed | tf_op | source)
XLA Modules:
  0.0 83.1 jit_solution(7517810683461869582)
XLA Ops:
  0.0 1.0 %slice.3 = bf16[80,2560]{1,0:T(8,128)(2,1)S(1)} slice(bf16[1024,2560]{1,0:T(8,128)(2,1)} %refs_0_.1), slice={[944:1024], [0:2560]} | slice | bytes 819200 | tf_op jit(solution)/shard_map/slice | solution.py:468
  1.0 2.5 %collective-permute-start = (bf16[80,2560]{1,0:T(8,128)(2,1)S(1)}, bf16[80,2560]{1,0:T(8,128)(2,1)S(1)}, u32[]{:S(2)}, u32[]{:S(2)}) collective-permute-start(bf16[80,2560]{1,0:T(8,128)(2,1)S(1)} %slice.3), channel_id=1, source_target_pairs={{0,4},{4,8},{8,12},{12,16},{16,20},{20,24},{24,28},{1,5},{5,9},{9,... | collective-permute-start | bytes 1228808 | tf_op jit(solution)/shard_map/ppermute | solution.py:467
  3.6 0.9 %copy-done.1 = bf16[1024,128]{1,0:T(8,128)(2,1)S(1)} copy-done((bf16[1024,128]{1,0:T(8,128)(2,1)S(1)}, bf16[1024,128]{1,0:T(8,128)(2,1)}, u32[]{:S(2)}) %copy-start.1) | copy-done | bytes 262168
  4.5 0.7 copy-done.2
  5.2 0.7 copy-done.3
  5.9 8.8 %front.2 = (f32[128,2560]{1,0:T(8,128)S(1)}, bf16[256,208]{1,0:T(8,128)(2,1)S(1)}, bf16[128,128]{1,0:T(8,128)(2,1)S(1)}, bf16[128,2560]{1,0:T(8,128)(2,1)S(1)}) custom-call(bf16[1024,2560]{1,0:T(8,128)(2,1)} %refs_0_.1, s32[20,128]{1,0:T(8,128)S(1)} %bitcast.9, bf16[1,64]{1,0:T(2,128)(2,1)S(1)} %bitcast.11, bf16[1024,128]{1,0:T(8,128)(2,1)S(1)} %copy-done.1), custom_call_target="tpu_custom_call" | custom-call | tf_op jit(solution)/shard_map/front/pallas_call | solution.py:140
  14.7 1.4 %front.3.own.refs_6_ = bf16[128,2560]{1,0:T(8,128)(2,1)S(1)} custom-call(bf16[128,2560]{1,0:T(8,128)(2,1)S(1)} %get-tuple-element.19.refs_0_, bf16[80,2560]{1,0:T(8,128)(2,1)S(1)} %collective-permute-done.refs_1_, s32[20,128]{1,0:T(8,128)S(1)} %bitcast.10, bf16[256,208]{1,0:T(8,128)(2,1)S(1)} %get-tuple-element.20.refs_3_, ...), custom_call_target="tpu_custom_call" | custom-call | tf_op jit(solution)/shard_map/front/pallas_call | solution.py:140
  16.1 2.6 %collective-permute-start.1 = (bf16[128,2560]{1,0:T(8,128)(2,1)S(1)}, bf16[128,2560]{1,0:T(8,128)(2,1)S(1)}, u32[]{:S(2)}, u32[]{:S(2)}) collective-permute-start(bf16[128,2560]{1,0:T(8,128)(2,1)S(1)} %front.3.own.refs_6_), channel_id=1, source_target_pairs={{0,4},{4,0},{8,12},{12,8},{16,20},{20,16},{24,28},{28,24},{1,5},{5... | collective-permute-start | bytes 1966088 | tf_op jit(solution)/shard_map/ppermute | solution.py:432
  18.7 1.5 %collective-permute-start.5 = (bf16[128,2560]{1,0:T(8,128)(2,1)S(1)}, bf16[128,2560]{1,0:T(8,128)(2,1)S(1)}, u32[]{:S(2)}, u32[]{:S(2)}) collective-permute-start(bf16[128,2560]{1,0:T(8,128)(2,1)S(1)} %front.3.own.refs_6_), channel_id=1, source_target_pairs={{0,8},{4,12},{8,0},{12,4},{16,24},{20,28},{24,16},{28,20},{1,9},{5... | collective-permute-start | bytes 1966088 | tf_op jit(solution)/shard_map/ppermute | solution.py:432
  20.5 0.8 pair_gram.1.refs_0_
  21.3 3.7 %collective-permute-start.4 = (bf16[272,128]{1,0:T(8,128)(2,1)S(1)}, bf16[272,128]{1,0:T(8,128)(2,1)S(1)}, u32[]{:S(2)}, u32[]{:S(2)}) collective-permute-start(bf16[272,128]{1,0:T(8,128)(2,1)S(1)} %pair_gram.1.refs_0_), channel_id=1, source_target_pairs={{0,3},{1,2},{2,1},{3,0},{4,7},{5,6},{6,5},{7,4},{8,11},{9,10},{10,... | collective-permute-start | bytes 208904 | tf_op jit(solution)/shard_map/ppermute | solution.py:432
  25.0 0.8 collective-permute-start.2
  25.8 2.2 %collective-permute-done.4.refs_3_ = bf16[272,128]{1,0:T(8,128)(2,1)S(1)} collective-permute-done((bf16[272,128]{1,0:T(8,128)(2,1)S(1)}, bf16[272,128]{1,0:T(8,128)(2,1)S(1)}, u32[]{:S(2)}, u32[]{:S(2)}) %collective-permute-start.4) | collective-permute-done | bytes 69664 | tf_op jit(solution)/shard_map/ppermute | solution.py:432
  28.0 3.3 %collective-permute-done.3.refs_2_ = bf16[272,128]{1,0:T(8,128)(2,1)S(1)} collective-permute-done((bf16[272,128]{1,0:T(8,128)(2,1)S(1)}, bf16[272,128]{1,0:T(8,128)(2,1)S(1)}, u32[]{:S(2)}, u32[]{:S(2)}) %collective-permute-start.3) | collective-permute-done | bytes 69664 | tf_op jit(solution)/shard_map/ppermute | solution.py:432
  31.3 6.6 %sign_filter.3 = (bf16[128,1280]{1,0:T(8,128)(2,1)S(1)}, bf16[128,512]{1,0:T(8,128)(2,1)S(1)}, f32[128,256]{1,0:T(8,128)S(1)}, f32[128,128]{1,0:T(8,128)S(1)}) custom-call(bf16[272,128]{1,0:T(8,128)(2,1)S(1)} %pair_gram.1.refs_0_, bf16[272,128]{1,0:T(8,128)(2,1)S(1)} %collective-permute-done.2.refs_1_, bf16[272,128]{1,0:T(8,128)(2,1)S(1)} %collective-permute-done.3.refs_2_, ...), custom_call_target="tpu_custom_call" | custom-call | tf_op jit(solution)/shard_map/sign_filter/pallas_call | solution.py:374
  38.0 1.6 %collective-permute-start.12 = (bf16[128,1280]{1,0:T(8,128)(2,1)S(1)}, bf16[128,1280]{1,0:T(8,128)(2,1)S(1)}, u32[]{:S(2)}, u32[]{:S(2)}) collective-permute-start(bf16[128,1280]{1,0:T(8,128)(2,1)S(1)} %get-tuple-element.26.refs_7_.own), channel_id=1, source_target_pairs={{0,16},{4,20},{8,24},{12,28},{16,0},{20,4},{24,8},{28,12},{1,17},{... | collective-permute-start | bytes 983048 | tf_op jit(solution)/shard_map/ppermute | solution.py:432
  40.2 2.6 %collective-permute-start.8 = (bf16[256,128]{1,0:T(8,128)(2,1)S(1)}, bf16[256,128]{1,0:T(8,128)(2,1)S(1)}, u32[]{:S(2)}, u32[]{:S(2)}) collective-permute-start(bf16[256,128]{1,0:T(8,128)(2,1)S(1)} %ahead_gram.2), channel_id=1, source_target_pairs={{0,3},{1,2},{2,1},{3,0},{4,7},{5,6},{6,5},{7,4},{8,11},{9,10},{10,... | collective-permute-start | bytes 196616 | tf_op jit(solution)/shard_map/ppermute | solution.py:432
  42.8 1.9 %collective-permute-start.6 = (bf16[256,128]{1,0:T(8,128)(2,1)S(1)}, bf16[256,128]{1,0:T(8,128)(2,1)S(1)}, u32[]{:S(2)}, u32[]{:S(2)}) collective-permute-start(bf16[256,128]{1,0:T(8,128)(2,1)S(1)} %ahead_gram.2), channel_id=1, source_target_pairs={{0,1},{1,0},{2,3},{3,2},{4,5},{5,4},{6,7},{7,6},{8,9},{9,8},{10,11... | collective-permute-start | bytes 196616 | tf_op jit(solution)/shard_map/ppermute | solution.py:432
  44.6 2.6 %collective-permute-done.12.partner = bf16[128,1280]{1,0:T(8,128)(2,1)S(1)} collective-permute-done((bf16[128,1280]{1,0:T(8,128)(2,1)S(1)}, bf16[128,1280]{1,0:T(8,128)(2,1)S(1)}, u32[]{:S(2)}, u32[]{:S(2)}) %collective-permute-start.12) | collective-permute-done | bytes 327712 | tf_op jit(solution)/shard_map/ppermute | solution.py:432
  47.2 1.2 %collective-permute-done.11.refs_8_.sibling = bf16[128,1280]{1,0:T(8,128)(2,1)S(1)} collective-permute-done((bf16[128,1280]{1,0:T(8,128)(2,1)S(1)}, bf16[128,1280]{1,0:T(8,128)(2,1)S(1)}, u32[]{:S(2)}, u32[]{:S(2)}) %collective-permute-start.11) | collective-permute-done | bytes 327712 | tf_op jit(solution)/shard_map/ppermute | solution.py:432
  48.9 0.5 collective-permute-start.9
  49.5 1.2 %collective-permute-start.10 = (bf16[128,512]{1,0:T(8,128)(2,1)S(1)}, bf16[128,512]{1,0:T(8,128)(2,1)S(1)}, u32[]{:S(2)}, u32[]{:S(2)}) collective-permute-start(bf16[128,512]{1,0:T(8,128)(2,1)S(1)} %get-tuple-element.25), channel_id=1, source_target_pairs={{0,8},{4,12},{8,0},{12,4},{16,24},{20,28},{24,16},{28,20},{1,9},{5... | collective-permute-start | bytes 393224 | tf_op jit(solution)/shard_map/ppermute | solution.py:432
  50.7 2.2 %collective-permute-start.16 = (bf16[256,128]{1,0:T(8,128)(2,1)S(1)}, bf16[256,128]{1,0:T(8,128)(2,1)S(1)}, u32[]{:S(2)}, u32[]{:S(2)}) collective-permute-start(bf16[256,128]{1,0:T(8,128)(2,1)S(1)} %add_convert_fusion.1), channel_id=1, source_target_pairs={{0,3},{1,2},{2,1},{3,0},{4,7},{5,6},{6,5},{7,4},{8,11},{9,10},{10,... | collective-permute-start | bytes 196616 | tf_op jit(solution)/shard_map/ppermute | solution.py:432
  52.9 2.2 %collective-permute-start.14 = (bf16[256,128]{1,0:T(8,128)(2,1)S(1)}, bf16[256,128]{1,0:T(8,128)(2,1)S(1)}, u32[]{:S(2)}, u32[]{:S(2)}) collective-permute-start(bf16[256,128]{1,0:T(8,128)(2,1)S(1)} %add_convert_fusion.1), channel_id=1, source_target_pairs={{0,1},{1,0},{2,3},{3,2},{4,5},{5,4},{6,7},{7,6},{8,9},{9,8},{10,11... | collective-permute-start | bytes 196616 | tf_op jit(solution)/shard_map/ppermute | solution.py:432
  55.1 7.3 %sign_filter.4 = (bf16[128,1280]{1,0:T(8,128)(2,1)S(1)}, bf16[128,512]{1,0:T(8,128)(2,1)S(1)}, f32[128,256]{1,0:T(8,128)S(1)}, f32[128,128]{1,0:T(8,128)S(1)}) custom-call(f32[128,256]{1,0:T(8,128)S(1)} %get-tuple-element.23.refs_0_, f32[128,128]{1,0:T(8,128)S(1)} %get-tuple-element.24.refs_1_, bf16[256,128]{1,0:T(8,128)(2,1)S(1)} %add_convert_fusion.2.refs_2_, ...), custom_call_target="tpu_custom_call" | custom-call | tf_op jit(solution)/shard_map/sign_filter/pallas_call | solution.py:374
  62.4 1.4 %collective-permute-start.19 = (bf16[128,1280]{1,0:T(8,128)(2,1)S(1)}, bf16[128,1280]{1,0:T(8,128)(2,1)S(1)}, u32[]{:S(2)}, u32[]{:S(2)}) collective-permute-start(bf16[128,1280]{1,0:T(8,128)(2,1)S(1)} %get-tuple-element.30.own), channel_id=1, source_target_pairs={{0,16},{4,20},{8,24},{12,28},{16,0},{20,4},{24,8},{28,12},{1,17},{... | collective-permute-start | bytes 983048 | tf_op jit(solution)/shard_map/ppermute | solution.py:432
  63.8 0.7 collective-permute-start.18
  64.6 1.4 %collective-permute-start.17 = (bf16[256,128]{1,0:T(8,128)(2,1)S(1)}, bf16[256,128]{1,0:T(8,128)(2,1)S(1)}, u32[]{:S(2)}, u32[]{:S(2)}) collective-permute-start(bf16[256,128]{1,0:T(8,128)(2,1)S(1)} %add_convert_fusion.refs_2_), channel_id=1, source_target_pairs={{0,8},{4,12},{8,0},{12,4},{16,24},{20,28},{24,16},{28,20},{1,9},{5... | collective-permute-start | bytes 196616 | tf_op jit(solution)/shard_map/ppermute | solution.py:432
  66.0 8.2 %collective-permute-done.18.refs_4_ = bf16[128,512]{1,0:T(8,128)(2,1)S(1)} collective-permute-done((bf16[128,512]{1,0:T(8,128)(2,1)S(1)}, bf16[128,512]{1,0:T(8,128)(2,1)S(1)}, u32[]{:S(2)}, u32[]{:S(2)}) %collective-permute-start.18) | collective-permute-done | bytes 131104 | tf_op jit(solution)/shard_map/ppermute | solution.py:432
  74.2 6.1 %sign_filter.5.mixing = f32[32,256]{1,0:T(8,128)S(1)} custom-call(f32[128,256]{1,0:T(8,128)S(1)} %get-tuple-element.27.refs_0_, f32[128,128]{1,0:T(8,128)S(1)} %get-tuple-element.28.refs_1_, bf16[256,128]{1,0:T(8,128)(2,1)S(1)} %add_convert_fusion.refs_2_, bf16[256,128]{1,0:T(8,128)(2,1)S(1)} %collective-permute-done.17.refs_3_, ...), custom_call_target="tpu_custom_call" | custom-call | tf_op jit(solution)/shard_map/sign_filter/pallas_call | solution.py:396
  80.6 1.3 %collective-permute-done.20.refs_1_ = f32[16,1280]{1,0:T(8,128)S(1)} collective-permute-done((f32[16,1280]{1,0:T(8,128)S(1)}, f32[16,1280]{1,0:T(8,128)S(1)}, u32[]{:S(2)}, u32[]{:S(2)}) %collective-permute-start.20) | collective-permute-done | bytes 81952 | tf_op jit(solution)/shard_map/ppermute | solution.py:432
  81.9 1.2 %join.1 = f32[16,2560]{1,0:T(8,128)} custom-call(s32[10]{0:T(128)S(1)} %stack.32.refs_5_.refs_6_.places, f32[16,1280]{1,0:T(8,128)S(1)} %get-tuple-element.31.refs_0_, f32[16,1280]{1,0:T(8,128)S(1)} %collective-permute-done.20.refs_1_), custom_call_target="tpu_custom_call" | custom-call | tf_op jit(solution)/shard_map/join/pallas_call | solution.py:451
  (33 shorter events, 1.8 us)
Async XLA Ops:
  1.0 30.3 %copy-start = (f32[256,128]{1,0:T(8,128)S(1)}, f32[256,128]{1,0:T(8,128)}, u32[]{:S(2)}) copy-start(f32[256,128]{1,0:T(8,128)} %refs_5_.3) | copy-start | bytes 393220
  1.0 13.7 %collective-permute-start = (bf16[80,2560]{1,0:T(8,128)(2,1)S(1)}, bf16[80,2560]{1,0:T(8,128)(2,1)S(1)}, u32[]{:S(2)}, u32[]{:S(2)}) collective-permute-start(bf16[80,2560]{1,0:T(8,128)(2,1)S(1)} %slice.3), channel_id=1, source_target_pairs={{0,4},{4,8},{8,12},{12,16},{16,20},{20,24},{24,28},{1,5},{5,9},{9,... | collective-permute-start | bytes 1228808 | tf_op jit(solution)/shard_map/ppermute | solution.py:467
  3.6 1.0 %copy-start.1 = (bf16[1024,128]{1,0:T(8,128)(2,1)S(1)}, bf16[1024,128]{1,0:T(8,128)(2,1)}, u32[]{:S(2)}) copy-start(bf16[1024,128]{1,0:T(8,128)(2,1)} %refs_3_.1) | copy-start | bytes 786436
  4.5 0.7 copy-start.2
  5.2 0.7 copy-start.3
  16.1 4.4 %collective-permute-start.1 = (bf16[128,2560]{1,0:T(8,128)(2,1)S(1)}, bf16[128,2560]{1,0:T(8,128)(2,1)S(1)}, u32[]{:S(2)}, u32[]{:S(2)}) collective-permute-start(bf16[128,2560]{1,0:T(8,128)(2,1)S(1)} %front.3.own.refs_6_), channel_id=1, source_target_pairs={{0,4},{4,0},{8,12},{12,8},{16,20},{20,16},{24,28},{28,24},{1,5},{5... | collective-permute-start | bytes 1966088 | tf_op jit(solution)/shard_map/ppermute | solution.py:432
  18.7 21.0 %collective-permute-start.5 = (bf16[128,2560]{1,0:T(8,128)(2,1)S(1)}, bf16[128,2560]{1,0:T(8,128)(2,1)S(1)}, u32[]{:S(2)}, u32[]{:S(2)}) collective-permute-start(bf16[128,2560]{1,0:T(8,128)(2,1)S(1)} %front.3.own.refs_6_), channel_id=1, source_target_pairs={{0,8},{4,12},{8,0},{12,4},{16,24},{20,28},{24,16},{28,20},{1,9},{5... | collective-permute-start | bytes 1966088 | tf_op jit(solution)/shard_map/ppermute | solution.py:432
  21.3 6.7 %collective-permute-start.4 = (bf16[272,128]{1,0:T(8,128)(2,1)S(1)}, bf16[272,128]{1,0:T(8,128)(2,1)S(1)}, u32[]{:S(2)}, u32[]{:S(2)}) collective-permute-start(bf16[272,128]{1,0:T(8,128)(2,1)S(1)} %pair_gram.1.refs_0_), channel_id=1, source_target_pairs={{0,3},{1,2},{2,1},{3,0},{4,7},{5,6},{6,5},{7,4},{8,11},{9,10},{10,... | collective-permute-start | bytes 208904 | tf_op jit(solution)/shard_map/ppermute | solution.py:432
  25.0 6.3 %collective-permute-start.3 = (bf16[272,128]{1,0:T(8,128)(2,1)S(1)}, bf16[272,128]{1,0:T(8,128)(2,1)S(1)}, u32[]{:S(2)}, u32[]{:S(2)}) collective-permute-start(bf16[272,128]{1,0:T(8,128)(2,1)S(1)} %pair_gram.1.refs_0_), channel_id=1, source_target_pairs={{0,2},{1,3},{2,0},{3,1},{4,6},{5,7},{6,4},{7,5},{8,10},{9,11},{10,... | collective-permute-start | bytes 208904 | tf_op jit(solution)/shard_map/ppermute | solution.py:432
  25.0 6.3 %collective-permute-start.2 = (bf16[272,128]{1,0:T(8,128)(2,1)S(1)}, bf16[272,128]{1,0:T(8,128)(2,1)S(1)}, u32[]{:S(2)}, u32[]{:S(2)}) collective-permute-start(bf16[272,128]{1,0:T(8,128)(2,1)S(1)} %pair_gram.1.refs_0_), channel_id=1, source_target_pairs={{0,1},{1,0},{2,3},{3,2},{4,5},{5,4},{6,7},{7,6},{8,9},{9,8},{10,11... | collective-permute-start | bytes 208904 | tf_op jit(solution)/shard_map/ppermute | solution.py:432
  38.0 9.2 %collective-permute-start.12 = (bf16[128,1280]{1,0:T(8,128)(2,1)S(1)}, bf16[128,1280]{1,0:T(8,128)(2,1)S(1)}, u32[]{:S(2)}, u32[]{:S(2)}) collective-permute-start(bf16[128,1280]{1,0:T(8,128)(2,1)S(1)} %get-tuple-element.26.refs_7_.own), channel_id=1, source_target_pairs={{0,16},{4,20},{8,24},{12,28},{16,0},{20,4},{24,8},{28,12},{1,17},{... | collective-permute-start | bytes 983048 | tf_op jit(solution)/shard_map/ppermute | solution.py:432
  39.5 8.9 %collective-permute-start.11 = (bf16[128,1280]{1,0:T(8,128)(2,1)S(1)}, bf16[128,1280]{1,0:T(8,128)(2,1)S(1)}, u32[]{:S(2)}, u32[]{:S(2)}) collective-permute-start(bf16[128,1280]{1,0:T(8,128)(2,1)S(1)} %get-tuple-element.26.refs_7_.own), channel_id=1, source_target_pairs={{0,8},{4,12},{8,0},{12,4},{16,24},{20,28},{24,16},{28,20},{1,9},{5... | collective-permute-start | bytes 983048 | tf_op jit(solution)/shard_map/ppermute | solution.py:432
  40.2 8.7 %collective-permute-start.8 = (bf16[256,128]{1,0:T(8,128)(2,1)S(1)}, bf16[256,128]{1,0:T(8,128)(2,1)S(1)}, u32[]{:S(2)}, u32[]{:S(2)}) collective-permute-start(bf16[256,128]{1,0:T(8,128)(2,1)S(1)} %ahead_gram.2), channel_id=1, source_target_pairs={{0,3},{1,2},{2,1},{3,0},{4,7},{5,6},{6,5},{7,4},{8,11},{9,10},{10,... | collective-permute-start | bytes 196616 | tf_op jit(solution)/shard_map/ppermute | solution.py:432
  42.8 6.1 %collective-permute-start.7 = (bf16[256,128]{1,0:T(8,128)(2,1)S(1)}, bf16[256,128]{1,0:T(8,128)(2,1)S(1)}, u32[]{:S(2)}, u32[]{:S(2)}) collective-permute-start(bf16[256,128]{1,0:T(8,128)(2,1)S(1)} %ahead_gram.2), channel_id=1, source_target_pairs={{0,2},{1,3},{2,0},{3,1},{4,6},{5,7},{6,4},{7,5},{8,10},{9,11},{10,... | collective-permute-start | bytes 196616 | tf_op jit(solution)/shard_map/ppermute | solution.py:432
  42.8 6.1 %collective-permute-start.6 = (bf16[256,128]{1,0:T(8,128)(2,1)S(1)}, bf16[256,128]{1,0:T(8,128)(2,1)S(1)}, u32[]{:S(2)}, u32[]{:S(2)}) collective-permute-start(bf16[256,128]{1,0:T(8,128)(2,1)S(1)} %ahead_gram.2), channel_id=1, source_target_pairs={{0,1},{1,0},{2,3},{3,2},{4,5},{5,4},{6,7},{7,6},{8,9},{9,8},{10,11... | collective-permute-start | bytes 196616 | tf_op jit(solution)/shard_map/ppermute | solution.py:432
  48.8 1.9 %collective-permute-start.13 = (bf16[256,128]{1,0:T(8,128)(2,1)S(1)}, bf16[256,128]{1,0:T(8,128)(2,1)S(1)}, u32[]{:S(2)}, u32[]{:S(2)}) collective-permute-start(bf16[256,128]{1,0:T(8,128)(2,1)S(1)} %ahead_gram.3), channel_id=1, source_target_pairs={{0,4},{4,0},{8,12},{12,8},{16,20},{20,16},{24,28},{28,24},{1,5},{5... | collective-permute-start | bytes 196616 | tf_op jit(solution)/shard_map/ppermute | solution.py:432
  48.9 6.2 %collective-permute-start.9 = (bf16[256,128]{1,0:T(8,128)(2,1)S(1)}, bf16[256,128]{1,0:T(8,128)(2,1)S(1)}, u32[]{:S(2)}, u32[]{:S(2)}) collective-permute-start(bf16[256,128]{1,0:T(8,128)(2,1)S(1)} %add_convert_fusion.2.refs_2_), channel_id=1, source_target_pairs={{0,4},{4,0},{8,12},{12,8},{16,20},{20,16},{24,28},{28,24},{1,5},{5... | collective-permute-start | bytes 196616 | tf_op jit(solution)/shard_map/ppermute | solution.py:432
  49.5 5.7 %collective-permute-start.10 = (bf16[128,512]{1,0:T(8,128)(2,1)S(1)}, bf16[128,512]{1,0:T(8,128)(2,1)S(1)}, u32[]{:S(2)}, u32[]{:S(2)}) collective-permute-start(bf16[128,512]{1,0:T(8,128)(2,1)S(1)} %get-tuple-element.25), channel_id=1, source_target_pairs={{0,8},{4,12},{8,0},{12,4},{16,24},{20,28},{24,16},{28,20},{1,9},{5... | collective-permute-start | bytes 393224 | tf_op jit(solution)/shard_map/ppermute | solution.py:432
  50.7 13.8 %collective-permute-start.16 = (bf16[256,128]{1,0:T(8,128)(2,1)S(1)}, bf16[256,128]{1,0:T(8,128)(2,1)S(1)}, u32[]{:S(2)}, u32[]{:S(2)}) collective-permute-start(bf16[256,128]{1,0:T(8,128)(2,1)S(1)} %add_convert_fusion.1), channel_id=1, source_target_pairs={{0,3},{1,2},{2,1},{3,0},{4,7},{5,6},{6,5},{7,4},{8,11},{9,10},{10,... | collective-permute-start | bytes 196616 | tf_op jit(solution)/shard_map/ppermute | solution.py:432
  52.9 11.6 %collective-permute-start.15 = (bf16[256,128]{1,0:T(8,128)(2,1)S(1)}, bf16[256,128]{1,0:T(8,128)(2,1)S(1)}, u32[]{:S(2)}, u32[]{:S(2)}) collective-permute-start(bf16[256,128]{1,0:T(8,128)(2,1)S(1)} %add_convert_fusion.1), channel_id=1, source_target_pairs={{0,2},{1,3},{2,0},{3,1},{4,6},{5,7},{6,4},{7,5},{8,10},{9,11},{10,... | collective-permute-start | bytes 196616 | tf_op jit(solution)/shard_map/ppermute | solution.py:432
  52.9 11.6 %collective-permute-start.14 = (bf16[256,128]{1,0:T(8,128)(2,1)S(1)}, bf16[256,128]{1,0:T(8,128)(2,1)S(1)}, u32[]{:S(2)}, u32[]{:S(2)}) collective-permute-start(bf16[256,128]{1,0:T(8,128)(2,1)S(1)} %add_convert_fusion.1), channel_id=1, source_target_pairs={{0,1},{1,0},{2,3},{3,2},{4,5},{5,4},{6,7},{7,6},{8,9},{9,8},{10,11... | collective-permute-start | bytes 196616 | tf_op jit(solution)/shard_map/ppermute | solution.py:432
  62.4 17.9 %collective-permute-start.19 = (bf16[128,1280]{1,0:T(8,128)(2,1)S(1)}, bf16[128,1280]{1,0:T(8,128)(2,1)S(1)}, u32[]{:S(2)}, u32[]{:S(2)}) collective-permute-start(bf16[128,1280]{1,0:T(8,128)(2,1)S(1)} %get-tuple-element.30.own), channel_id=1, source_target_pairs={{0,16},{4,20},{8,24},{12,28},{16,0},{20,4},{24,8},{28,12},{1,17},{... | collective-permute-start | bytes 983048 | tf_op jit(solution)/shard_map/ppermute | solution.py:432
  63.8 10.4 %collective-permute-start.18 = (bf16[128,512]{1,0:T(8,128)(2,1)S(1)}, bf16[128,512]{1,0:T(8,128)(2,1)S(1)}, u32[]{:S(2)}, u32[]{:S(2)}) collective-permute-start(bf16[128,512]{1,0:T(8,128)(2,1)S(1)} %get-tuple-element.29), channel_id=1, source_target_pairs={{0,16},{4,20},{8,24},{12,28},{16,0},{20,4},{24,8},{28,12},{1,17},{... | collective-permute-start | bytes 393224 | tf_op jit(solution)/shard_map/ppermute | solution.py:432
  64.6 9.7 %collective-permute-start.17 = (bf16[256,128]{1,0:T(8,128)(2,1)S(1)}, bf16[256,128]{1,0:T(8,128)(2,1)S(1)}, u32[]{:S(2)}, u32[]{:S(2)}) collective-permute-start(bf16[256,128]{1,0:T(8,128)(2,1)S(1)} %add_convert_fusion.refs_2_), channel_id=1, source_target_pairs={{0,8},{4,12},{8,0},{12,4},{16,24},{20,28},{24,16},{28,20},{1,9},{5... | collective-permute-start | bytes 196616 | tf_op jit(solution)/shard_map/ppermute | solution.py:432
  80.6 1.3 %collective-permute-start.20 = (f32[16,1280]{1,0:T(8,128)S(1)}, f32[16,1280]{1,0:T(8,128)S(1)}, u32[]{:S(2)}, u32[]{:S(2)}) collective-permute-start(f32[16,1280]{1,0:T(8,128)S(1)} %get-tuple-element.32), channel_id=1, source_target_pairs={{0,4},{4,0},{8,12},{12,8},{16,20},{20,16},{24,28},{28,24},{1,5},{5... | collective-permute-start | bytes 245768 | tf_op jit(solution)/shard_map/ppermute | solution.py:432

commit v9 on v8

--- a/solution.py
+++ b/solution.py
@@ -256,6 +256,22 @@
     for part in parts[1:]:
         total = total + part[...].astype(F32)
     return total
+
+
+def hold_kernel(*refs):
+    pass
+
+
+def hold(value, *until):
+    return pl.pallas_call(
+        hold_kernel,
+        in_specs=[ANY] * (1 + len(until)),
+        out_specs=ANY,
+        out_shape=jax.ShapeDtypeStruct(value.shape, value.dtype),
+        input_output_aliases={0: 0},
+        compiler_params=pltpu.CompilerParams(vmem_limit_bytes=16 * 2**20),
+        name="hold",
+    )(value, *until)
 
 
 def square_of(aa, ab, bb):
@@ -399,6 +415,9 @@
         out_shape=jax.ShapeDtypeStruct((share * pieces, 2 * rank), F32),
         scratch_shapes=[pltpu.VMEM((rank, 2 * rank), F32)],
         compiler_params=PARAMS,
+        cost_estimate=pl.CostEstimate(
+            flops=50 * K_ITERS * (2 * rank) ** 3, bytes_accessed=0, transcendentals=0
+        ),
         name="sign_filter",
     )(*args, places)
 
@@ -494,13 +513,17 @@
         first, last = depth == 0, depth == depths - 1
         mask = 2**depth
         here = widths[depth]
-        other = swap(sketch, "tm", mask)
+        if not last:
+            other = swap(sketch, "tm", mask)
         if first:
             grams = gather_parts(pair_gram(sketch, other), "chan")
         else:
             packed, *kept = kept
             grams = [*kept, *ahead, swap(packed, "tm", mask)]
         if last:
+            if not first:
+                sketch = hold(sketch, *grams[-2:])
+            other = swap(sketch, "tm", mask)
             mixing = last_filter_call(grams, compress, places, 2 * depth, first, share, span)
             pieces = mix(mixing, sketch, other, span)
             break

time: 83.4 us -> 79.4 us (0.952)
  waiting for transfers between devices: 19 us -> 15.7 us
    ppermute x20, waiting for transfers between devices: 19 us -> 15.7 us  [swap(): lax.ppermute(value, axis, [(source, source ^ mask) for source in range(co...]
  transfers between devices with their start and end apart: 21 -> 21, of which waited for: 7 -> 9; matrix products, arithmetic and copies ran while one was open for 0% -> 0% of each run, Pallas kernels for 37% -> 39%
where the time goes in v9:
time: 79.4 us; the launch traced here: 79.1 us
  Pallas kernels  33.3 us (42%)
  starting transfers between devices  26.4 us (33%)
  waiting for transfers between devices  15.7 us (20%)
  local copies, waits for them, and re-layouts  3.43 us (4%)
    ppermute x20, starting transfers between devices, swap(): lax.ppermute(value, axis, [(source, source ^ mask) for source in range(co...  23.9 us
    ppermute x20, waiting for transfers between devices, swap(): lax.ppermute(value, axis, [(source, source ^ mask) for source in range(co...  15.7 us
    pallas_call x2, Pallas kernels, filter_call(): pl.pallas_call(functools.partial(filter_kernel, len(grams), first, False,...  13.9 us
    pallas_call x2, Pallas kernels, front_call(): pl.pallas_call(functools.partial(front_kernel, *blocks), grid=(steps,), i...  10.2 us
    pallas_call x1, Pallas kernels, last_filter_call(): pl.pallas_call(functools.partial(filter_kernel, len(grams), first, True,...  6.08 us
    ppermute x1, starting transfers between devices, on_device(): lax.ppermute(record[rows - HALO:], 'tm', [(source, source + 1) for source...  2.51 us
    unnamed x8, local copies, waits for them, and re-layouts  2.31 us
  transfers between devices with their start and end apart: 21, of which 9 were waited for; matrix products, arithmetic and copies ran while one was open for 0% of the time, Pallas kernels for 39%

profile of v9, /device:TPU:0, one launch (start us, length us, event | category | flops | bytes accessed | tf_op | source)
XLA Modules:
  0.0 79.1 jit_solution(2857440143621750968)
XLA Ops:
  0.0 1.0 %slice.3 = bf16[80,2560]{1,0:T(8,128)(2,1)S(1)} slice(bf16[1024,2560]{1,0:T(8,128)(2,1)} %refs_0_.1), slice={[944:1024], [0:2560]} | slice | bytes 819200 | tf_op jit(solution)/shard_map/slice | solution.py:487
  1.0 2.5 %collective-permute-start = (bf16[80,2560]{1,0:T(8,128)(2,1)S(1)}, bf16[80,2560]{1,0:T(8,128)(2,1)S(1)}, u32[]{:S(2)}, u32[]{:S(2)}) collective-permute-start(bf16[80,2560]{1,0:T(8,128)(2,1)S(1)} %slice.3), channel_id=1, source_target_pairs={{0,4},{4,8},{8,12},{12,16},{16,20},{20,24},{24,28},{1,5},{5,9},{9,... | collective-permute-start | bytes 1228808 | tf_op jit(solution)/shard_map/ppermute | solution.py:486
  3.6 0.9 %copy-done.1 = bf16[1024,128]{1,0:T(8,128)(2,1)S(1)} copy-done((bf16[1024,128]{1,0:T(8,128)(2,1)S(1)}, bf16[1024,128]{1,0:T(8,128)(2,1)}, u32[]{:S(2)}) %copy-start.1) | copy-done | bytes 262168
  4.5 0.7 copy-done.2
  5.9 8.8 %front.2 = (f32[128,2560]{1,0:T(8,128)S(1)}, bf16[256,208]{1,0:T(8,128)(2,1)S(1)}, bf16[128,128]{1,0:T(8,128)(2,1)S(1)}, bf16[128,2560]{1,0:T(8,128)(2,1)S(1)}) custom-call(bf16[1024,2560]{1,0:T(8,128)(2,1)} %refs_0_.1, s32[20,128]{1,0:T(8,128)S(1)} %bitcast.9, bf16[1,64]{1,0:T(2,128)(2,1)S(1)} %bitcast.11, bf16[1024,128]{1,0:T(8,128)(2,1)S(1)} %copy-done.1), custom_call_target="tpu_custom_call" | custom-call | tf_op jit(solution)/shard_map/front/pallas_call | solution.py:140
  14.7 1.4 %front.3.own.refs_6_ = bf16[128,2560]{1,0:T(8,128)(2,1)S(1)} custom-call(bf16[128,2560]{1,0:T(8,128)(2,1)S(1)} %get-tuple-element.19.refs_0_, bf16[80,2560]{1,0:T(8,128)(2,1)S(1)} %collective-permute-done.refs_1_, s32[20,128]{1,0:T(8,128)S(1)} %bitcast.10, bf16[256,208]{1,0:T(8,128)(2,1)S(1)} %get-tuple-element.20.refs_3_, ...), custom_call_target="tpu_custom_call" | custom-call | tf_op jit(solution)/shard_map/front/pallas_call | solution.py:140
  16.1 2.6 %collective-permute-start.1 = (bf16[128,2560]{1,0:T(8,128)(2,1)S(1)}, bf16[128,2560]{1,0:T(8,128)(2,1)S(1)}, u32[]{:S(2)}, u32[]{:S(2)}) collective-permute-start(bf16[128,2560]{1,0:T(8,128)(2,1)S(1)} %front.3.own.refs_6_), channel_id=1, source_target_pairs={{0,4},{4,0},{8,12},{12,8},{16,20},{20,16},{24,28},{28,24},{1,5},{5... | collective-permute-start | bytes 1966088 | tf_op jit(solution)/shard_map/ppermute | solution.py:451
  18.7 1.5 %collective-permute-start.5 = (bf16[128,2560]{1,0:T(8,128)(2,1)S(1)}, bf16[128,2560]{1,0:T(8,128)(2,1)S(1)}, u32[]{:S(2)}, u32[]{:S(2)}) collective-permute-start(bf16[128,2560]{1,0:T(8,128)(2,1)S(1)} %front.3.own.refs_6_), channel_id=1, source_target_pairs={{0,8},{4,12},{8,0},{12,4},{16,24},{20,28},{24,16},{28,20},{1,9},{5... | collective-permute-start | bytes 1966088 | tf_op jit(solution)/shard_map/ppermute | solution.py:451
  20.5 0.8 %pair_gram.1.refs_0_ = bf16[272,128]{1,0:T(8,128)(2,1)S(1)} custom-call(bf16[128,2560]{1,0:T(8,128)(2,1)S(1)} %front.3.own.refs_6_, bf16[128,2560]{1,0:T(8,128)(2,1)S(1)} %collective-permute-done.1.other.refs_7_.sibling), custom_call_target="tpu_custom_call" | custom-call | tf_op jit(solution)/shard_map/pair_gram/pallas_call | solution.py:229
  21.3 3.7 %collective-permute-start.4 = (bf16[272,128]{1,0:T(8,128)(2,1)S(1)}, bf16[272,128]{1,0:T(8,128)(2,1)S(1)}, u32[]{:S(2)}, u32[]{:S(2)}) collective-permute-start(bf16[272,128]{1,0:T(8,128)(2,1)S(1)} %pair_gram.1.refs_0_), channel_id=1, source_target_pairs={{0,3},{1,2},{2,1},{3,0},{4,7},{5,6},{6,5},{7,4},{8,11},{9,10},{10,... | collective-permute-start | bytes 208904 | tf_op jit(solution)/shard_map/ppermute | solution.py:451
  25.0 0.8 collective-permute-start.2
  25.8 2.2 %collective-permute-done.4.refs_3_ = bf16[272,128]{1,0:T(8,128)(2,1)S(1)} collective-permute-done((bf16[272,128]{1,0:T(8,128)(2,1)S(1)}, bf16[272,128]{1,0:T(8,128)(2,1)S(1)}, u32[]{:S(2)}, u32[]{:S(2)}) %collective-permute-start.4) | collective-permute-done | bytes 69664 | tf_op jit(solution)/shard_map/ppermute | solution.py:451
  28.0 3.3 %collective-permute-done.3.refs_2_ = bf16[272,128]{1,0:T(8,128)(2,1)S(1)} collective-permute-done((bf16[272,128]{1,0:T(8,128)(2,1)S(1)}, bf16[272,128]{1,0:T(8,128)(2,1)S(1)}, u32[]{:S(2)}, u32[]{:S(2)}) %collective-permute-start.3) | collective-permute-done | bytes 69664 | tf_op jit(solution)/shard_map/ppermute | solution.py:451
  31.3 6.6 %sign_filter.3 = (bf16[128,1280]{1,0:T(8,128)(2,1)S(1)}, bf16[128,512]{1,0:T(8,128)(2,1)S(1)}, f32[128,256]{1,0:T(8,128)S(1)}, f32[128,128]{1,0:T(8,128)S(1)}) custom-call(bf16[272,128]{1,0:T(8,128)(2,1)S(1)} %pair_gram.1.refs_0_, bf16[272,128]{1,0:T(8,128)(2,1)S(1)} %collective-permute-done.2.refs_1_, bf16[272,128]{1,0:T(8,128)(2,1)S(1)} %collective-permute-done.3.refs_2_, ...), custom_call_target="tpu_custom_call" | custom-call | tf_op jit(solution)/shard_map/sign_filter/pallas_call | solution.py:390
  38.0 1.6 %collective-permute-start.12 = (bf16[128,1280]{1,0:T(8,128)(2,1)S(1)}, bf16[128,1280]{1,0:T(8,128)(2,1)S(1)}, u32[]{:S(2)}, u32[]{:S(2)}) collective-permute-start(bf16[128,1280]{1,0:T(8,128)(2,1)S(1)} %get-tuple-element.26.refs_7_.own), channel_id=1, source_target_pairs={{0,16},{4,20},{8,24},{12,28},{16,0},{20,4},{24,8},{28,12},{1,17},{... | collective-permute-start | bytes 983048 | tf_op jit(solution)/shard_map/ppermute | solution.py:451
  40.2 2.6 %collective-permute-start.8 = (bf16[256,128]{1,0:T(8,128)(2,1)S(1)}, bf16[256,128]{1,0:T(8,128)(2,1)S(1)}, u32[]{:S(2)}, u32[]{:S(2)}) collective-permute-start(bf16[256,128]{1,0:T(8,128)(2,1)S(1)} %ahead_gram.2), channel_id=1, source_target_pairs={{0,3},{1,2},{2,1},{3,0},{4,7},{5,6},{6,5},{7,4},{8,11},{9,10},{10,... | collective-permute-start | bytes 196616 | tf_op jit(solution)/shard_map/ppermute | solution.py:451
  42.8 1.9 %collective-permute-start.6 = (bf16[256,128]{1,0:T(8,128)(2,1)S(1)}, bf16[256,128]{1,0:T(8,128)(2,1)S(1)}, u32[]{:S(2)}, u32[]{:S(2)}) collective-permute-start(bf16[256,128]{1,0:T(8,128)(2,1)S(1)} %ahead_gram.2), channel_id=1, source_target_pairs={{0,1},{1,0},{2,3},{3,2},{4,5},{5,4},{6,7},{7,6},{8,9},{9,8},{10,11... | collective-permute-start | bytes 196616 | tf_op jit(solution)/shard_map/ppermute | solution.py:451
  44.6 2.6 %collective-permute-done.12.partner = bf16[128,1280]{1,0:T(8,128)(2,1)S(1)} collective-permute-done((bf16[128,1280]{1,0:T(8,128)(2,1)S(1)}, bf16[128,1280]{1,0:T(8,128)(2,1)S(1)}, u32[]{:S(2)}, u32[]{:S(2)}) %collective-permute-start.12) | collective-permute-done | bytes 327712 | tf_op jit(solution)/shard_map/ppermute | solution.py:451
  47.2 1.2 %collective-permute-done.11.refs_8_.sibling = bf16[128,1280]{1,0:T(8,128)(2,1)S(1)} collective-permute-done((bf16[128,1280]{1,0:T(8,128)(2,1)S(1)}, bf16[128,1280]{1,0:T(8,128)(2,1)S(1)}, u32[]{:S(2)}, u32[]{:S(2)}) %collective-permute-start.11) | collective-permute-done | bytes 327712 | tf_op jit(solution)/shard_map/ppermute | solution.py:451
  49.5 1.2 %collective-permute-start.10 = (bf16[128,512]{1,0:T(8,128)(2,1)S(1)}, bf16[128,512]{1,0:T(8,128)(2,1)S(1)}, u32[]{:S(2)}, u32[]{:S(2)}) collective-permute-start(bf16[128,512]{1,0:T(8,128)(2,1)S(1)} %get-tuple-element.25), channel_id=1, source_target_pairs={{0,8},{4,12},{8,0},{12,4},{16,24},{20,28},{24,16},{28,20},{1,9},{5... | collective-permute-start | bytes 393224 | tf_op jit(solution)/shard_map/ppermute | solution.py:451
  50.7 2.2 %collective-permute-start.16 = (bf16[256,128]{1,0:T(8,128)(2,1)S(1)}, bf16[256,128]{1,0:T(8,128)(2,1)S(1)}, u32[]{:S(2)}, u32[]{:S(2)}) collective-permute-start(bf16[256,128]{1,0:T(8,128)(2,1)S(1)} %add_convert_fusion.1), channel_id=1, source_target_pairs={{0,3},{1,2},{2,1},{3,0},{4,7},{5,6},{6,5},{7,4},{8,11},{9,10},{10,... | collective-permute-start | bytes 196616 | tf_op jit(solution)/shard_map/ppermute | solution.py:451
  52.9 2.2 %collective-permute-start.14 = (bf16[256,128]{1,0:T(8,128)(2,1)S(1)}, bf16[256,128]{1,0:T(8,128)(2,1)S(1)}, u32[]{:S(2)}, u32[]{:S(2)}) collective-permute-start(bf16[256,128]{1,0:T(8,128)(2,1)S(1)} %add_convert_fusion.1), channel_id=1, source_target_pairs={{0,1},{1,0},{2,3},{3,2},{4,5},{5,4},{6,7},{7,6},{8,9},{9,8},{10,11... | collective-permute-start | bytes 196616 | tf_op jit(solution)/shard_map/ppermute | solution.py:451
  55.1 7.3 %sign_filter.4 = (bf16[128,1280]{1,0:T(8,128)(2,1)S(1)}, bf16[128,512]{1,0:T(8,128)(2,1)S(1)}, f32[128,256]{1,0:T(8,128)S(1)}, f32[128,128]{1,0:T(8,128)S(1)}) custom-call(f32[128,256]{1,0:T(8,128)S(1)} %get-tuple-element.23.refs_0_, f32[128,128]{1,0:T(8,128)S(1)} %get-tuple-element.24.refs_1_, bf16[256,128]{1,0:T(8,128)(2,1)S(1)} %add_convert_fusion.2.refs_2_, ...), custom_call_target="tpu_custom_call" | custom-call | tf_op jit(solution)/shard_map/sign_filter/pallas_call | solution.py:390
  62.4 1.4 %collective-permute-start.18 = (bf16[128,512]{1,0:T(8,128)(2,1)S(1)}, bf16[128,512]{1,0:T(8,128)(2,1)S(1)}, u32[]{:S(2)}, u32[]{:S(2)}) collective-permute-start(bf16[128,512]{1,0:T(8,128)(2,1)S(1)} %get-tuple-element.29), channel_id=1, source_target_pairs={{0,16},{4,20},{8,24},{12,28},{16,0},{20,4},{24,8},{28,12},{1,17},{... | collective-permute-start | bytes 393224 | tf_op jit(solution)/shard_map/ppermute | solution.py:451
  63.9 0.7 collective-permute-start.17
  64.6 2.8 %collective-permute-done.18.refs_4_.refs_2_ = bf16[128,512]{1,0:T(8,128)(2,1)S(1)} collective-permute-done((bf16[128,512]{1,0:T(8,128)(2,1)S(1)}, bf16[128,512]{1,0:T(8,128)(2,1)S(1)}, u32[]{:S(2)}, u32[]{:S(2)}) %collective-permute-start.18) | collective-permute-done | bytes 131104 | tf_op jit(solution)/shard_map/ppermute | solution.py:451
  67.4 0.8 collective-permute-done.17.refs_3_.refs_1_
  68.2 0.7 collective-permute-start.19
  68.9 6.1 %sign_filter.5.mixing = f32[32,256]{1,0:T(8,128)S(1)} custom-call(f32[128,256]{1,0:T(8,128)S(1)} %get-tuple-element.27.refs_0_, f32[128,128]{1,0:T(8,128)S(1)} %get-tuple-element.28.refs_1_, bf16[256,128]{1,0:T(8,128)(2,1)S(1)} %add_convert_fusion.refs_2_, bf16[256,128]{1,0:T(8,128)(2,1)S(1)} %collective-permute-done.17.refs_3_.refs_1_, ...), custom_call_target="tpu_custom_call" | custom-call | flops 6710886400 | tf_op jit(solution)/shard_map/sign_filter/pallas_call | solution.py:412
  75.0 1.3 %collective-permute-done.19.other = bf16[128,1280]{1,0:T(8,128)(2,1)S(1)} collective-permute-done((bf16[128,1280]{1,0:T(8,128)(2,1)S(1)}, bf16[128,1280]{1,0:T(8,128)(2,1)S(1)}, u32[]{:S(2)}, u32[]{:S(2)}) %collective-permute-start.19) | collective-permute-done | bytes 327712 | tf_op jit(solution)/shard_map/ppermute | solution.py:451
  76.6 1.3 %collective-permute-done.20.refs_1_ = f32[16,1280]{1,0:T(8,128)S(1)} collective-permute-done((f32[16,1280]{1,0:T(8,128)S(1)}, f32[16,1280]{1,0:T(8,128)S(1)}, u32[]{:S(2)}, u32[]{:S(2)}) %collective-permute-start.20) | collective-permute-done | bytes 81952 | tf_op jit(solution)/shard_map/ppermute | solution.py:451
  77.9 1.2 %join.1 = f32[16,2560]{1,0:T(8,128)} custom-call(s32[10]{0:T(128)S(1)} %stack.32.refs_5_.refs_6_.places, f32[16,1280]{1,0:T(8,128)S(1)} %get-tuple-element.31.refs_0_, f32[16,1280]{1,0:T(8,128)S(1)} %collective-permute-done.20.refs_1_), custom_call_target="tpu_custom_call" | custom-call | tf_op jit(solution)/shard_map/join/pallas_call | solution.py:470
  (34 shorter events, 3.0 us)
Async XLA Ops:
  1.0 30.3 %copy-start = (f32[256,128]{1,0:T(8,128)S(1)}, f32[256,128]{1,0:T(8,128)}, u32[]{:S(2)}) copy-start(f32[256,128]{1,0:T(8,128)} %refs_5_.3) | copy-start | bytes 393220
  1.0 13.7 %collective-permute-start = (bf16[80,2560]{1,0:T(8,128)(2,1)S(1)}, bf16[80,2560]{1,0:T(8,128)(2,1)S(1)}, u32[]{:S(2)}, u32[]{:S(2)}) collective-permute-start(bf16[80,2560]{1,0:T(8,128)(2,1)S(1)} %slice.3), channel_id=1, source_target_pairs={{0,4},{4,8},{8,12},{12,16},{16,20},{20,24},{24,28},{1,5},{5,9},{9,... | collective-permute-start | bytes 1228808 | tf_op jit(solution)/shard_map/ppermute | solution.py:486
  3.6 1.0 %copy-start.1 = (bf16[1024,128]{1,0:T(8,128)(2,1)S(1)}, bf16[1024,128]{1,0:T(8,128)(2,1)}, u32[]{:S(2)}) copy-start(bf16[1024,128]{1,0:T(8,128)(2,1)} %refs_3_.1) | copy-start | bytes 786436
  4.5 0.7 copy-start.2
  5.2 0.7 copy-start.3
  16.1 4.4 %collective-permute-start.1 = (bf16[128,2560]{1,0:T(8,128)(2,1)S(1)}, bf16[128,2560]{1,0:T(8,128)(2,1)S(1)}, u32[]{:S(2)}, u32[]{:S(2)}) collective-permute-start(bf16[128,2560]{1,0:T(8,128)(2,1)S(1)} %front.3.own.refs_6_), channel_id=1, source_target_pairs={{0,4},{4,0},{8,12},{12,8},{16,20},{20,16},{24,28},{28,24},{1,5},{5... | collective-permute-start | bytes 1966088 | tf_op jit(solution)/shard_map/ppermute | solution.py:451
  18.7 21.0 %collective-permute-start.5 = (bf16[128,2560]{1,0:T(8,128)(2,1)S(1)}, bf16[128,2560]{1,0:T(8,128)(2,1)S(1)}, u32[]{:S(2)}, u32[]{:S(2)}) collective-permute-start(bf16[128,2560]{1,0:T(8,128)(2,1)S(1)} %front.3.own.refs_6_), channel_id=1, source_target_pairs={{0,8},{4,12},{8,0},{12,4},{16,24},{20,28},{24,16},{28,20},{1,9},{5... | collective-permute-start | bytes 1966088 | tf_op jit(solution)/shard_map/ppermute | solution.py:451
  21.3 6.7 %collective-permute-start.4 = (bf16[272,128]{1,0:T(8,128)(2,1)S(1)}, bf16[272,128]{1,0:T(8,128)(2,1)S(1)}, u32[]{:S(2)}, u32[]{:S(2)}) collective-permute-start(bf16[272,128]{1,0:T(8,128)(2,1)S(1)} %pair_gram.1.refs_0_), channel_id=1, source_target_pairs={{0,3},{1,2},{2,1},{3,0},{4,7},{5,6},{6,5},{7,4},{8,11},{9,10},{10,... | collective-permute-start | bytes 208904 | tf_op jit(solution)/shard_map/ppermute | solution.py:451
  25.0 6.3 %collective-permute-start.3 = (bf16[272,128]{1,0:T(8,128)(2,1)S(1)}, bf16[272,128]{1,0:T(8,128)(2,1)S(1)}, u32[]{:S(2)}, u32[]{:S(2)}) collective-permute-start(bf16[272,128]{1,0:T(8,128)(2,1)S(1)} %pair_gram.1.refs_0_), channel_id=1, source_target_pairs={{0,2},{1,3},{2,0},{3,1},{4,6},{5,7},{6,4},{7,5},{8,10},{9,11},{10,... | collective-permute-start | bytes 208904 | tf_op jit(solution)/shard_map/ppermute | solution.py:451
  25.0 6.3 %collective-permute-start.2 = (bf16[272,128]{1,0:T(8,128)(2,1)S(1)}, bf16[272,128]{1,0:T(8,128)(2,1)S(1)}, u32[]{:S(2)}, u32[]{:S(2)}) collective-permute-start(bf16[272,128]{1,0:T(8,128)(2,1)S(1)} %pair_gram.1.refs_0_), channel_id=1, source_target_pairs={{0,1},{1,0},{2,3},{3,2},{4,5},{5,4},{6,7},{7,6},{8,9},{9,8},{10,11... | collective-permute-start | bytes 208904 | tf_op jit(solution)/shard_map/ppermute | solution.py:451
  38.0 9.2 %collective-permute-start.12 = (bf16[128,1280]{1,0:T(8,128)(2,1)S(1)}, bf16[128,1280]{1,0:T(8,128)(2,1)S(1)}, u32[]{:S(2)}, u32[]{:S(2)}) collective-permute-start(bf16[128,1280]{1,0:T(8,128)(2,1)S(1)} %get-tuple-element.26.refs_7_.own), channel_id=1, source_target_pairs={{0,16},{4,20},{8,24},{12,28},{16,0},{20,4},{24,8},{28,12},{1,17},{... | collective-permute-start | bytes 983048 | tf_op jit(solution)/shard_map/ppermute | solution.py:451
  39.5 8.9 %collective-permute-start.11 = (bf16[128,1280]{1,0:T(8,128)(2,1)S(1)}, bf16[128,1280]{1,0:T(8,128)(2,1)S(1)}, u32[]{:S(2)}, u32[]{:S(2)}) collective-permute-start(bf16[128,1280]{1,0:T(8,128)(2,1)S(1)} %get-tuple-element.26.refs_7_.own), channel_id=1, source_target_pairs={{0,8},{4,12},{8,0},{12,4},{16,24},{20,28},{24,16},{28,20},{1,9},{5... | collective-permute-start | bytes 983048 | tf_op jit(solution)/shard_map/ppermute | solution.py:451
  40.2 8.7 %collective-permute-start.8 = (bf16[256,128]{1,0:T(8,128)(2,1)S(1)}, bf16[256,128]{1,0:T(8,128)(2,1)S(1)}, u32[]{:S(2)}, u32[]{:S(2)}) collective-permute-start(bf16[256,128]{1,0:T(8,128)(2,1)S(1)} %ahead_gram.2), channel_id=1, source_target_pairs={{0,3},{1,2},{2,1},{3,0},{4,7},{5,6},{6,5},{7,4},{8,11},{9,10},{10,... | collective-permute-start | bytes 196616 | tf_op jit(solution)/shard_map/ppermute | solution.py:451
  42.8 6.1 %collective-permute-start.7 = (bf16[256,128]{1,0:T(8,128)(2,1)S(1)}, bf16[256,128]{1,0:T(8,128)(2,1)S(1)}, u32[]{:S(2)}, u32[]{:S(2)}) collective-permute-start(bf16[256,128]{1,0:T(8,128)(2,1)S(1)} %ahead_gram.2), channel_id=1, source_target_pairs={{0,2},{1,3},{2,0},{3,1},{4,6},{5,7},{6,4},{7,5},{8,10},{9,11},{10,... | collective-permute-start | bytes 196616 | tf_op jit(solution)/shard_map/ppermute | solution.py:451
  42.8 6.1 %collective-permute-start.6 = (bf16[256,128]{1,0:T(8,128)(2,1)S(1)}, bf16[256,128]{1,0:T(8,128)(2,1)S(1)}, u32[]{:S(2)}, u32[]{:S(2)}) collective-permute-start(bf16[256,128]{1,0:T(8,128)(2,1)S(1)} %ahead_gram.2), channel_id=1, source_target_pairs={{0,1},{1,0},{2,3},{3,2},{4,5},{5,4},{6,7},{7,6},{8,9},{9,8},{10,11... | collective-permute-start | bytes 196616 | tf_op jit(solution)/shard_map/ppermute | solution.py:451
  48.8 1.9 %collective-permute-start.13 = (bf16[256,128]{1,0:T(8,128)(2,1)S(1)}, bf16[256,128]{1,0:T(8,128)(2,1)S(1)}, u32[]{:S(2)}, u32[]{:S(2)}) collective-permute-start(bf16[256,128]{1,0:T(8,128)(2,1)S(1)} %ahead_gram.3), channel_id=1, source_target_pairs={{0,4},{4,0},{8,12},{12,8},{16,20},{20,16},{24,28},{28,24},{1,5},{5... | collective-permute-start | bytes 196616 | tf_op jit(solution)/shard_map/ppermute | solution.py:451
  48.9 6.2 %collective-permute-start.9 = (bf16[256,128]{1,0:T(8,128)(2,1)S(1)}, bf16[256,128]{1,0:T(8,128)(2,1)S(1)}, u32[]{:S(2)}, u32[]{:S(2)}) collective-permute-start(bf16[256,128]{1,0:T(8,128)(2,1)S(1)} %add_convert_fusion.2.refs_2_), channel_id=1, source_target_pairs={{0,4},{4,0},{8,12},{12,8},{16,20},{20,16},{24,28},{28,24},{1,5},{5... | collective-permute-start | bytes 196616 | tf_op jit(solution)/shard_map/ppermute | solution.py:451
  49.5 5.6 %collective-permute-start.10 = (bf16[128,512]{1,0:T(8,128)(2,1)S(1)}, bf16[128,512]{1,0:T(8,128)(2,1)S(1)}, u32[]{:S(2)}, u32[]{:S(2)}) collective-permute-start(bf16[128,512]{1,0:T(8,128)(2,1)S(1)} %get-tuple-element.25), channel_id=1, source_target_pairs={{0,8},{4,12},{8,0},{12,4},{16,24},{20,28},{24,16},{28,20},{1,9},{5... | collective-permute-start | bytes 393224 | tf_op jit(solution)/shard_map/ppermute | solution.py:451
  50.7 13.1 %collective-permute-start.16 = (bf16[256,128]{1,0:T(8,128)(2,1)S(1)}, bf16[256,128]{1,0:T(8,128)(2,1)S(1)}, u32[]{:S(2)}, u32[]{:S(2)}) collective-permute-start(bf16[256,128]{1,0:T(8,128)(2,1)S(1)} %add_convert_fusion.1), channel_id=1, source_target_pairs={{0,3},{1,2},{2,1},{3,0},{4,7},{5,6},{6,5},{7,4},{8,11},{9,10},{10,... | collective-permute-start | bytes 196616 | tf_op jit(solution)/shard_map/ppermute | solution.py:451
  52.9 10.9 %collective-permute-start.15 = (bf16[256,128]{1,0:T(8,128)(2,1)S(1)}, bf16[256,128]{1,0:T(8,128)(2,1)S(1)}, u32[]{:S(2)}, u32[]{:S(2)}) collective-permute-start(bf16[256,128]{1,0:T(8,128)(2,1)S(1)} %add_convert_fusion.1), channel_id=1, source_target_pairs={{0,2},{1,3},{2,0},{3,1},{4,6},{5,7},{6,4},{7,5},{8,10},{9,11},{10,... | collective-permute-start | bytes 196616 | tf_op jit(solution)/shard_map/ppermute | solution.py:451
  52.9 10.9 %collective-permute-start.14 = (bf16[256,128]{1,0:T(8,128)(2,1)S(1)}, bf16[256,128]{1,0:T(8,128)(2,1)S(1)}, u32[]{:S(2)}, u32[]{:S(2)}) collective-permute-start(bf16[256,128]{1,0:T(8,128)(2,1)S(1)} %add_convert_fusion.1), channel_id=1, source_target_pairs={{0,1},{1,0},{2,3},{3,2},{4,5},{5,4},{6,7},{7,6},{8,9},{9,8},{10,11... | collective-permute-start | bytes 196616 | tf_op jit(solution)/shard_map/ppermute | solution.py:451
  62.4 5.0 %collective-permute-start.18 = (bf16[128,512]{1,0:T(8,128)(2,1)S(1)}, bf16[128,512]{1,0:T(8,128)(2,1)S(1)}, u32[]{:S(2)}, u32[]{:S(2)}) collective-permute-start(bf16[128,512]{1,0:T(8,128)(2,1)S(1)} %get-tuple-element.29), channel_id=1, source_target_pairs={{0,16},{4,20},{8,24},{12,28},{16,0},{20,4},{24,8},{28,12},{1,17},{... | collective-permute-start | bytes 393224 | tf_op jit(solution)/shard_map/ppermute | solution.py:451
  63.9 4.3 %collective-permute-start.17 = (bf16[256,128]{1,0:T(8,128)(2,1)S(1)}, bf16[256,128]{1,0:T(8,128)(2,1)S(1)}, u32[]{:S(2)}, u32[]{:S(2)}) collective-permute-start(bf16[256,128]{1,0:T(8,128)(2,1)S(1)} %add_convert_fusion.refs_2_), channel_id=1, source_target_pairs={{0,8},{4,12},{8,0},{12,4},{16,24},{20,28},{24,16},{28,20},{1,9},{5... | collective-permute-start | bytes 196616 | tf_op jit(solution)/shard_map/ppermute | solution.py:451
  68.2 8.1 %collective-permute-start.19 = (bf16[128,1280]{1,0:T(8,128)(2,1)S(1)}, bf16[128,1280]{1,0:T(8,128)(2,1)S(1)}, u32[]{:S(2)}, u32[]{:S(2)}) collective-permute-start(bf16[128,1280]{1,0:T(8,128)(2,1)S(1)} %hold.1.own), channel_id=1, source_target_pairs={{0,16},{4,20},{8,24},{12,28},{16,0},{20,4},{24,8},{28,12},{1,17},{... | collective-permute-start | bytes 983048 | tf_op jit(solution)/shard_map/ppermute | solution.py:451
  76.6 1.3 %collective-permute-start.20 = (f32[16,1280]{1,0:T(8,128)S(1)}, f32[16,1280]{1,0:T(8,128)S(1)}, u32[]{:S(2)}, u32[]{:S(2)}) collective-permute-start(f32[16,1280]{1,0:T(8,128)S(1)} %get-tuple-element.32), channel_id=1, source_target_pairs={{0,4},{4,0},{8,12},{12,8},{16,20},{20,16},{24,28},{28,24},{1,5},{5... | collective-permute-start | bytes 245768 | tf_op jit(solution)/shard_map/ppermute | solution.py:451

commit v10 on v9

--- a/solution.py
+++ b/solution.py
@@ -234,21 +234,23 @@
     )(own, other)
 
 
-def ahead_kernel(width, own, sibling, partner, out):
+def ahead_kernel(width, own, sibling, partner, *refs):
+    out = refs[-1]
     rank = own.shape[0]
     there = partner[:, :width]
     out[0:rank, :] = dot_nt(own[:, :width], there).astype(out.dtype)
     out[rank:, :] = dot_nt(sibling[:, :width], there).astype(out.dtype)
 
 
-def ahead_gram(own, sibling, partner, width):
+def ahead_gram(own, sibling, partner, width, *after):
     rank = own.shape[0]
     return pl.pallas_call(
         functools.partial(ahead_kernel, width),
+        in_specs=[VMEM] * 3 + [ANY] * len(after),
         out_shape=jax.ShapeDtypeStruct((2 * rank, rank), BF16),
         compiler_params=PARAMS,
         name="ahead_gram",
-    )(own, sibling, partner)
+    )(own, sibling, partner, *after)
 
 
 def summed(parts):
@@ -319,15 +321,19 @@
     return gram - jnp.where(diag, mean, 0.0), mean
 
 
-def filter_kernel(count, first, last, used, base, *refs):
+def filter_kernel(count, first, kind, used, base, *refs):
     grams, refs = refs[:count], refs[count:]
     compress, places, refs = refs[0], refs[1], refs[2:]
+    last = kind == "last"
+    rank = compress.shape[1]
     if last:
         mix_out, turned = refs
-        rank, share = compress.shape[1], mix_out.shape[0] // used
+        share = mix_out.shape[0] // used
+    elif kind == "level":
+        mix_out, packed, level, turned = refs
     else:
-        own, other, sketch, packed, mix_out, level, pair, turned, sems = refs
-        rank, width = own.shape[0], pair.shape[1]
+        own, other, mix_out, sketch, whole, pair, turned, sems = refs
+        width = pair.shape[1]
         if width < used:
             span = pl.ds(pl.multiple_of(places[base], 128), width)
         else:
@@ -368,33 +374,73 @@
     mix_out[...] = mixing
     if last:
         return
+    full = gram + mean * eye
+    if kind == "level":
+        pack_level(mixing, full, packed, level)
+        return
+    whole[...] = full
     for copy in copies:
         copy.wait()
-    high, low = split(mixing)
-    both = jnp.concatenate([high, low], 0)
+    both = jnp.concatenate(split(mixing), 0)
     tile = next((t for t in (640, 512, 256, 128) if width % t == 0), width)
     for c in range(0, width, tile):
         part = dot(both, pair[:, c : c + tile])
         sketch[:, c : c + tile] = (part[:rank] + part[rank:]).astype(BF16)
-    block = dot3_nt(dot3(mixing, gram + mean * eye), mixing)
+
+
+def pack_level(mixing, full, packed, level):
+    rank = mixing.shape[0]
+    block = dot3_nt(dot3(mixing, full), mixing)
     level[...] = block
-    packed[:, : 2 * rank] = high
+    packed[:, : 2 * rank] = mixing.astype(BF16)
     high, low = split(block)
     packed[:, 2 * rank : 3 * rank] = high
     packed[:, 3 * rank :] = low
 
 
+def level_kernel(mixing, full, packed, level):
+    pack_level(mixing[...], full[...], packed, level)
+
+
+def level_shapes(rank):
+    return [
+        jax.ShapeDtypeStruct((rank, 4 * rank), BF16),
+        jax.ShapeDtypeStruct((rank, rank), F32),
+    ]
+
+
+def level_call(mixing, full):
+    return pl.pallas_call(
+        level_kernel,
+        out_shape=level_shapes(mixing.shape[0]),
+        compiler_params=pltpu.CompilerParams(vmem_limit_bytes=16 * 2**20),
+        name="level",
+    )(mixing, full)
+
+
+def level_filter_call(grams, compress, places, base, first):
+    rank = compress.shape[1]
+    args = [*grams, compress]
+    return pl.pallas_call(
+        functools.partial(filter_kernel, len(grams), first, "level", 0, base),
+        in_specs=[VMEM] * len(args) + [SMEM],
+        out_shape=[jax.ShapeDtypeStruct((rank, 2 * rank), F32), *level_shapes(rank)],
+        scratch_shapes=[pltpu.VMEM((rank, 2 * rank), F32)],
+        compiler_params=PARAMS,
+        name="sign_filter",
+    )(*args, places)
+
+
 def filter_call(grams, compress, places, base, own, other, used, width, first):
     rank = own.shape[0]
     args = [*grams, compress]
     return pl.pallas_call(
-        functools.partial(filter_kernel, len(grams), first, False, used, base),
+        functools.partial(filter_kernel, len(grams), first, "sketch", used, base),
         in_specs=[VMEM] * len(args) + [SMEM, ANY, ANY],
         out_shape=[
+            jax.ShapeDtypeStruct((rank, 2 * rank), F32),
             jax.ShapeDtypeStruct((rank, width), BF16),
-            jax.ShapeDtypeStruct((rank, 4 * rank), BF16),
-            jax.ShapeDtypeStruct((rank, 2 * rank), F32),
-            jax.ShapeDtypeStruct((rank, rank), F32),
+            jax.ShapeDtypeStruct((2 * rank, 2 * rank), F32),
         ],
         scratch_shapes=[
             pltpu.VMEM((2 * rank, width), BF16),
@@ -410,7 +456,7 @@
     rank = compress.shape[1]
     args = [*grams, compress]
     return pl.pallas_call(
-        functools.partial(filter_kernel, len(grams), first, True, pieces, base),
+        functools.partial(filter_kernel, len(grams), first, "last", pieces, base),
         in_specs=[VMEM] * len(args) + [SMEM],
         out_shape=jax.ShapeDtypeStruct((share * pieces, 2 * rank), F32),
         scratch_shapes=[pltpu.VMEM((rank, 2 * rank), F32)],
@@ -433,11 +479,11 @@
         part = dot(both, jnp.concatenate([own[:, span], other[:, span]], 0))
         part = part[:rows] + part[rows:]
         for i, piece in enumerate(out):
-            piece[:, span] = part[i * share : (i + 1) * share]
-
-
-def mix(mixing, own, other, pieces):
-    shape = jax.ShapeDtypeStruct((mixing.shape[0] // pieces, own.shape[1]), F32)
+            piece[:, span] = part[i * share : (i + 1) * share].astype(piece.dtype)
+
+
+def mix(mixing, own, other, pieces, dtype):
+    shape = jax.ShapeDtypeStruct((mixing.shape[0] // pieces, own.shape[1]), dtype)
     return pl.pallas_call(
         mix_kernel,
         out_shape=[shape] * pieces,
@@ -525,12 +571,19 @@
                 sketch = hold(sketch, *grams[-2:])
             other = swap(sketch, "tm", mask)
             mixing = last_filter_call(grams, compress, places, 2 * depth, first, share, span)
-            pieces = mix(mixing, sketch, other, span)
+            pieces = mix(mixing, sketch, other, span, F32)
             break
-        part = ahead_gram(sketch, other, swap(sketch, "tm", 2 * mask), here)
-        merged, *kept = filter_call(
-            grams, compress, places, 2 * depth, sketch, other, here, widths[depth + 1], first
-        )
+        after = [] if first else [packed]
+        part = ahead_gram(sketch, other, swap(sketch, "tm", 2 * mask), here, *after)
+        if widths[depth + 1] == here and depth + 2 == depths:
+            mixing, packed, level = level_filter_call(grams, compress, places, 2 * depth, first)
+            (merged,) = mix(mixing, sketch, other, 1, BF16)
+        else:
+            mixing, merged, full = filter_call(
+                grams, compress, places, 2 * depth, sketch, other, here, widths[depth + 1], first
+            )
+            packed, level = level_call(mixing, full)
+        kept = packed, mixing, level
         for bit in [b for b in narrowed if b < depth]:
             part = (part.astype(F32) + swap(part, "tm", 2**bit).astype(F32)).astype(BF16)
         parts = gather_parts(part, "chan")

time: 79.4 us -> 79.9 us (level)
    pallas_call x5 -> x6, Pallas kernels: 20.8 us -> 20.5 us  [the longest x1 6.58 us: level_filter_call(): pl.pallas_call(functools.partial(filter_kernel, len(grams), first, 'level...]
  transfers between devices with their start and end apart: 21 -> 21, of which waited for: 9 -> 11; matrix products, arithmetic and copies ran while one was open for 0% -> 0% of each run, Pallas kernels for 39% -> 38%
where the time goes in v10:
time: 79.9 us; the launch traced here: 79.7 us
  Pallas kernels  33.3 us (42%)
  starting transfers between devices  27 us (34%)
  waiting for transfers between devices  15.6 us (20%)
  local copies, waits for them, and re-layouts  3.43 us (4%)
    ppermute x20, starting transfers between devices, swap(): lax.ppermute(value, axis, [(source, source ^ mask) for source in range(co...  24.5 us
    ppermute x20, waiting for transfers between devices, swap(): lax.ppermute(value, axis, [(source, source ^ mask) for source in range(co...  15.6 us
    pallas_call x2, Pallas kernels, front_call(): pl.pallas_call(functools.partial(front_kernel, *blocks), grid=(steps,), i...  10.2 us
    pallas_call x1, Pallas kernels, level_filter_call(): pl.pallas_call(functools.partial(filter_kernel, len(grams), first, 'level...  6.58 us
    pallas_call x1, Pallas kernels, filter_call(): pl.pallas_call(functools.partial(filter_kernel, len(grams), first, 'sketc...  6.53 us
    pallas_call x1, Pallas kernels, last_filter_call(): pl.pallas_call(functools.partial(filter_kernel, len(grams), first, 'last'...  6.08 us
    ppermute x1, starting transfers between devices, on_device(): lax.ppermute(record[rows - HALO:], 'tm', [(source, source + 1) for source...  2.51 us
    unnamed x8, local copies, waits for them, and re-layouts  2.31 us
  transfers between devices with their start and end apart: 21, of which 11 were waited for; matrix products, arithmetic and copies ran while one was open for 0% of the time, Pallas kernels for 38%

profile of v10, /device:TPU:0, one launch (start us, length us, event | category | flops | bytes accessed | tf_op | source)
XLA Modules:
  0.0 79.7 jit_solution(1129100829304907512)
XLA Ops:
  0.0 1.0 %slice.3 = bf16[80,2560]{1,0:T(8,128)(2,1)S(1)} slice(bf16[1024,2560]{1,0:T(8,128)(2,1)} %refs_0_.1), slice={[944:1024], [0:2560]} | slice | bytes 819200 | tf_op jit(solution)/shard_map/slice | solution.py:533
  1.0 2.5 %collective-permute-start = (bf16[80,2560]{1,0:T(8,128)(2,1)S(1)}, bf16[80,2560]{1,0:T(8,128)(2,1)S(1)}, u32[]{:S(2)}, u32[]{:S(2)}) collective-permute-start(bf16[80,2560]{1,0:T(8,128)(2,1)S(1)} %slice.3), channel_id=1, source_target_pairs={{0,4},{4,8},{8,12},{12,16},{16,20},{20,24},{24,28},{1,5},{5,9},{9,... | collective-permute-start | bytes 1228808 | tf_op jit(solution)/shard_map/ppermute | solution.py:532
  3.6 0.9 %copy-done.1 = bf16[1024,128]{1,0:T(8,128)(2,1)S(1)} copy-done((bf16[1024,128]{1,0:T(8,128)(2,1)S(1)}, bf16[1024,128]{1,0:T(8,128)(2,1)}, u32[]{:S(2)}) %copy-start.1) | copy-done | bytes 262168
  5.9 8.8 %front.2 = (f32[128,2560]{1,0:T(8,128)S(1)}, bf16[256,208]{1,0:T(8,128)(2,1)S(1)}, bf16[128,128]{1,0:T(8,128)(2,1)S(1)}, bf16[128,2560]{1,0:T(8,128)(2,1)S(1)}) custom-call(bf16[1024,2560]{1,0:T(8,128)(2,1)} %refs_0_.1, s32[20,128]{1,0:T(8,128)S(1)} %bitcast.9, bf16[1,64]{1,0:T(2,128)(2,1)S(1)} %bitcast.11, bf16[1024,128]{1,0:T(8,128)(2,1)S(1)} %copy-done.1), custom_call_target="tpu_custom_call" | custom-call | tf_op jit(solution)/shard_map/front/pallas_call | solution.py:140
  14.7 1.4 %front.3.own.refs_6_ = bf16[128,2560]{1,0:T(8,128)(2,1)S(1)} custom-call(bf16[128,2560]{1,0:T(8,128)(2,1)S(1)} %get-tuple-element.19.refs_0_, bf16[80,2560]{1,0:T(8,128)(2,1)S(1)} %collective-permute-done.refs_1_, s32[20,128]{1,0:T(8,128)S(1)} %bitcast.10, bf16[256,208]{1,0:T(8,128)(2,1)S(1)} %get-tuple-element.20.refs_3_, ...), custom_call_target="tpu_custom_call" | custom-call | tf_op jit(solution)/shard_map/front/pallas_call | solution.py:140
  16.1 2.6 %collective-permute-start.1 = (bf16[128,2560]{1,0:T(8,128)(2,1)S(1)}, bf16[128,2560]{1,0:T(8,128)(2,1)S(1)}, u32[]{:S(2)}, u32[]{:S(2)}) collective-permute-start(bf16[128,2560]{1,0:T(8,128)(2,1)S(1)} %front.3.own.refs_6_), channel_id=1, source_target_pairs={{0,4},{4,0},{8,12},{12,8},{16,20},{20,16},{24,28},{28,24},{1,5},{5... | collective-permute-start | bytes 1966088 | tf_op jit(solution)/shard_map/ppermute | solution.py:497
  18.7 1.5 %collective-permute-start.5 = (bf16[128,2560]{1,0:T(8,128)(2,1)S(1)}, bf16[128,2560]{1,0:T(8,128)(2,1)S(1)}, u32[]{:S(2)}, u32[]{:S(2)}) collective-permute-start(bf16[128,2560]{1,0:T(8,128)(2,1)S(1)} %front.3.own.refs_6_), channel_id=1, source_target_pairs={{0,8},{4,12},{8,0},{12,4},{16,24},{20,28},{24,16},{28,20},{1,9},{5... | collective-permute-start | bytes 1966088 | tf_op jit(solution)/shard_map/ppermute | solution.py:497
  20.5 0.8 %pair_gram.1.refs_0_ = bf16[272,128]{1,0:T(8,128)(2,1)S(1)} custom-call(bf16[128,2560]{1,0:T(8,128)(2,1)S(1)} %front.3.own.refs_6_, bf16[128,2560]{1,0:T(8,128)(2,1)S(1)} %collective-permute-done.1.other.refs_7_.sibling), custom_call_target="tpu_custom_call" | custom-call | tf_op jit(solution)/shard_map/pair_gram/pallas_call | solution.py:229
  21.3 1.7 %collective-permute-start.2 = (bf16[272,128]{1,0:T(8,128)(2,1)S(1)}, bf16[272,128]{1,0:T(8,128)(2,1)S(1)}, u32[]{:S(2)}, u32[]{:S(2)}) collective-permute-start(bf16[272,128]{1,0:T(8,128)(2,1)S(1)} %pair_gram.1.refs_0_), channel_id=1, source_target_pairs={{0,1},{1,0},{2,3},{3,2},{4,5},{5,4},{6,7},{7,6},{8,9},{9,8},{10,11... | collective-permute-start | bytes 208904 | tf_op jit(solution)/shard_map/ppermute | solution.py:497
  22.9 2.6 %collective-permute-start.3 = (bf16[272,128]{1,0:T(8,128)(2,1)S(1)}, bf16[272,128]{1,0:T(8,128)(2,1)S(1)}, u32[]{:S(2)}, u32[]{:S(2)}) collective-permute-start(bf16[272,128]{1,0:T(8,128)(2,1)S(1)} %pair_gram.1.refs_0_), channel_id=1, source_target_pairs={{0,2},{1,3},{2,0},{3,1},{4,6},{5,7},{6,4},{7,5},{8,10},{9,11},{10,... | collective-permute-start | bytes 208904 | tf_op jit(solution)/shard_map/ppermute | solution.py:497
  25.8 5.0 %collective-permute-done.3.refs_2_ = bf16[272,128]{1,0:T(8,128)(2,1)S(1)} collective-permute-done((bf16[272,128]{1,0:T(8,128)(2,1)S(1)}, bf16[272,128]{1,0:T(8,128)(2,1)S(1)}, u32[]{:S(2)}, u32[]{:S(2)}) %collective-permute-start.3) | collective-permute-done | bytes 69664 | tf_op jit(solution)/shard_map/ppermute | solution.py:497
  30.9 0.8 %collective-permute-done.4.refs_3_ = bf16[272,128]{1,0:T(8,128)(2,1)S(1)} collective-permute-done((bf16[272,128]{1,0:T(8,128)(2,1)S(1)}, bf16[272,128]{1,0:T(8,128)(2,1)S(1)}, u32[]{:S(2)}, u32[]{:S(2)}) %collective-permute-start.4) | collective-permute-done | bytes 69664 | tf_op jit(solution)/shard_map/ppermute | solution.py:497
  31.7 6.5 %sign_filter.3 = (f32[128,256]{1,0:T(8,128)S(1)}, bf16[128,1280]{1,0:T(8,128)(2,1)S(1)}, f32[256,256]{1,0:T(8,128)S(1)}) custom-call(bf16[272,128]{1,0:T(8,128)(2,1)S(1)} %pair_gram.1.refs_0_, bf16[272,128]{1,0:T(8,128)(2,1)S(1)} %collective-permute-done.2.refs_1_, bf16[272,128]{1,0:T(8,128)(2,1)S(1)} %collective-permute-done.3.refs_2_, ...), custom_call_target="tpu_custom_call" | custom-call | tf_op jit(solution)/shard_map/sign_filter/pallas_call | solution.py:437
  38.2 1.6 %collective-permute-start.11 = (bf16[128,1280]{1,0:T(8,128)(2,1)S(1)}, bf16[128,1280]{1,0:T(8,128)(2,1)S(1)}, u32[]{:S(2)}, u32[]{:S(2)}) collective-permute-start(bf16[128,1280]{1,0:T(8,128)(2,1)S(1)} %get-tuple-element.29.own), channel_id=1, source_target_pairs={{0,8},{4,12},{8,0},{12,4},{16,24},{20,28},{24,16},{28,20},{1,9},{5... | collective-permute-start | bytes 983048 | tf_op jit(solution)/shard_map/ppermute | solution.py:497
  40.7 1.2 %collective-permute-start.6 = (bf16[256,128]{1,0:T(8,128)(2,1)S(1)}, bf16[256,128]{1,0:T(8,128)(2,1)S(1)}, u32[]{:S(2)}, u32[]{:S(2)}) collective-permute-start(bf16[256,128]{1,0:T(8,128)(2,1)S(1)} %ahead_gram.2), channel_id=1, source_target_pairs={{0,1},{1,0},{2,3},{3,2},{4,5},{5,4},{6,7},{7,6},{8,9},{9,8},{10,11... | collective-permute-start | bytes 196616 | tf_op jit(solution)/shard_map/ppermute | solution.py:497
  41.9 1.7 %collective-permute-start.7 = (bf16[256,128]{1,0:T(8,128)(2,1)S(1)}, bf16[256,128]{1,0:T(8,128)(2,1)S(1)}, u32[]{:S(2)}, u32[]{:S(2)}) collective-permute-start(bf16[256,128]{1,0:T(8,128)(2,1)S(1)} %ahead_gram.2), channel_id=1, source_target_pairs={{0,2},{1,3},{2,0},{3,1},{4,6},{5,7},{6,4},{7,5},{8,10},{9,11},{10,... | collective-permute-start | bytes 196616 | tf_op jit(solution)/shard_map/ppermute | solution.py:497
  43.6 1.6 %collective-permute-start.8 = (bf16[256,128]{1,0:T(8,128)(2,1)S(1)}, bf16[256,128]{1,0:T(8,128)(2,1)S(1)}, u32[]{:S(2)}, u32[]{:S(2)}) collective-permute-start(bf16[256,128]{1,0:T(8,128)(2,1)S(1)} %ahead_gram.2), channel_id=1, source_target_pairs={{0,3},{1,2},{2,1},{3,0},{4,7},{5,6},{6,5},{7,4},{8,11},{9,10},{10,... | collective-permute-start | bytes 196616 | tf_op jit(solution)/shard_map/ppermute | solution.py:497
  45.6 0.9 %collective-permute-done.11.sibling.other = bf16[128,1280]{1,0:T(8,128)(2,1)S(1)} collective-permute-done((bf16[128,1280]{1,0:T(8,128)(2,1)S(1)}, bf16[128,1280]{1,0:T(8,128)(2,1)S(1)}, u32[]{:S(2)}, u32[]{:S(2)}) %collective-permute-start.11) | collective-permute-done | bytes 327712 | tf_op jit(solution)/shard_map/ppermute | solution.py:497
  46.5 1.2 %collective-permute-done.12.partner = bf16[128,1280]{1,0:T(8,128)(2,1)S(1)} collective-permute-done((bf16[128,1280]{1,0:T(8,128)(2,1)S(1)}, bf16[128,1280]{1,0:T(8,128)(2,1)S(1)}, u32[]{:S(2)}, u32[]{:S(2)}) %collective-permute-start.12) | collective-permute-done | bytes 327712 | tf_op jit(solution)/shard_map/ppermute | solution.py:497
  48.6 1.1 %collective-permute-done.8 = bf16[256,128]{1,0:T(8,128)(2,1)S(1)} collective-permute-done((bf16[256,128]{1,0:T(8,128)(2,1)S(1)}, bf16[256,128]{1,0:T(8,128)(2,1)S(1)}, u32[]{:S(2)}, u32[]{:S(2)}) %collective-permute-start.8) | collective-permute-done | bytes 65568 | tf_op jit(solution)/shard_map/ppermute | solution.py:497
  49.9 2.0 %collective-permute-start.10 = (bf16[128,512]{1,0:T(8,128)(2,1)S(1)}, bf16[128,512]{1,0:T(8,128)(2,1)S(1)}, u32[]{:S(2)}, u32[]{:S(2)}) collective-permute-start(bf16[128,512]{1,0:T(8,128)(2,1)S(1)} %get-tuple-element.26.refs_0_), channel_id=1, source_target_pairs={{0,8},{4,12},{8,0},{12,4},{16,24},{20,28},{24,16},{28,20},{1,9},{5... | collective-permute-start | bytes 393224 | tf_op jit(solution)/shard_map/ppermute | solution.py:497
  52.5 1.3 %collective-permute-start.15 = (bf16[256,128]{1,0:T(8,128)(2,1)S(1)}, bf16[256,128]{1,0:T(8,128)(2,1)S(1)}, u32[]{:S(2)}, u32[]{:S(2)}) collective-permute-start(bf16[256,128]{1,0:T(8,128)(2,1)S(1)} %add_convert_fusion.1), channel_id=1, source_target_pairs={{0,2},{1,3},{2,0},{3,1},{4,6},{5,7},{6,4},{7,5},{8,10},{9,11},{10,... | collective-permute-start | bytes 196616 | tf_op jit(solution)/shard_map/ppermute | solution.py:497
  53.8 2.5 %collective-permute-start.16 = (bf16[256,128]{1,0:T(8,128)(2,1)S(1)}, bf16[256,128]{1,0:T(8,128)(2,1)S(1)}, u32[]{:S(2)}, u32[]{:S(2)}) collective-permute-start(bf16[256,128]{1,0:T(8,128)(2,1)S(1)} %add_convert_fusion.1), channel_id=1, source_target_pairs={{0,3},{1,2},{2,1},{3,0},{4,7},{5,6},{6,5},{7,4},{8,11},{9,10},{10,... | collective-permute-start | bytes 196616 | tf_op jit(solution)/shard_map/ppermute | solution.py:497
  56.3 6.6 %sign_filter.4 = (f32[128,256]{1,0:T(8,128)S(1)}, bf16[128,512]{1,0:T(8,128)(2,1)S(1)}, f32[128,128]{1,0:T(8,128)S(1)}) custom-call(f32[128,256]{1,0:T(8,128)S(1)} %get-tuple-element.23.mixing.refs_0_, f32[128,128]{1,0:T(8,128)S(1)} %get-tuple-element.25.refs_1_, bf16[256,128]{1,0:T(8,128)(2,1)S(1)} %add_convert_fusion.2.refs_2_, ...), custom_call_target="tpu_custom_call" | custom-call | tf_op jit(solution)/shard_map/sign_filter/pallas_call | solution.py:424
  62.9 1.4 %collective-permute-start.18 = (bf16[128,512]{1,0:T(8,128)(2,1)S(1)}, bf16[128,512]{1,0:T(8,128)(2,1)S(1)}, u32[]{:S(2)}, u32[]{:S(2)}) collective-permute-start(bf16[128,512]{1,0:T(8,128)(2,1)S(1)} %get-tuple-element.30), channel_id=1, source_target_pairs={{0,16},{4,20},{8,24},{12,28},{16,0},{20,4},{24,8},{28,12},{1,17},{... | collective-permute-start | bytes 393224 | tf_op jit(solution)/shard_map/ppermute | solution.py:497
  64.4 0.7 collective-permute-start.17
  65.5 2.5 %collective-permute-done.18.refs_4_.refs_2_ = bf16[128,512]{1,0:T(8,128)(2,1)S(1)} collective-permute-done((bf16[128,512]{1,0:T(8,128)(2,1)S(1)}, bf16[128,512]{1,0:T(8,128)(2,1)S(1)}, u32[]{:S(2)}, u32[]{:S(2)}) %collective-permute-start.18) | collective-permute-done | bytes 131104 | tf_op jit(solution)/shard_map/ppermute | solution.py:497
  68.0 0.7 collective-permute-done.17.refs_3_.refs_1_
  69.4 6.1 %sign_filter.5.mixing = f32[32,256]{1,0:T(8,128)S(1)} custom-call(f32[128,256]{1,0:T(8,128)S(1)} %get-tuple-element.27.refs_0_.mixing, f32[128,128]{1,0:T(8,128)S(1)} %get-tuple-element.28.refs_1_, bf16[256,128]{1,0:T(8,128)(2,1)S(1)} %add_convert_fusion.refs_2_, bf16[256,128]{1,0:T(8,128)(2,1)S(1)} %collective-permute-done.17.refs_3_.refs_1_, ...), custom_call_target="tpu_custom_call" | custom-call | flops 6710886400 | tf_op jit(solution)/shard_map/sign_filter/pallas_call | solution.py:458
  75.5 1.3 %collective-permute-done.19.other = bf16[128,1280]{1,0:T(8,128)(2,1)S(1)} collective-permute-done((bf16[128,1280]{1,0:T(8,128)(2,1)S(1)}, bf16[128,1280]{1,0:T(8,128)(2,1)S(1)}, u32[]{:S(2)}, u32[]{:S(2)}) %collective-permute-start.19) | collective-permute-done | bytes 327712 | tf_op jit(solution)/shard_map/ppermute | solution.py:497
  77.2 1.3 %collective-permute-done.20.refs_1_ = f32[16,1280]{1,0:T(8,128)S(1)} collective-permute-done((f32[16,1280]{1,0:T(8,128)S(1)}, f32[16,1280]{1,0:T(8,128)S(1)}, u32[]{:S(2)}, u32[]{:S(2)}) %collective-permute-start.20) | collective-permute-done | bytes 81952 | tf_op jit(solution)/shard_map/ppermute | solution.py:497
  78.4 1.2 %join.1 = f32[16,2560]{1,0:T(8,128)} custom-call(s32[10]{0:T(128)S(1)} %stack.32.refs_5_.refs_6_.places, f32[16,1280]{1,0:T(8,128)S(1)} %get-tuple-element.31.refs_0_, f32[16,1280]{1,0:T(8,128)S(1)} %collective-permute-done.20.refs_1_), custom_call_target="tpu_custom_call" | custom-call | tf_op jit(solution)/shard_map/join/pallas_call | solution.py:516
  (36 shorter events, 6.3 us)
Async XLA Ops:
  1.0 30.7 %copy-start = (f32[256,128]{1,0:T(8,128)S(1)}, f32[256,128]{1,0:T(8,128)}, u32[]{:S(2)}) copy-start(f32[256,128]{1,0:T(8,128)} %refs_5_.3) | copy-start | bytes 393220
  1.0 13.7 %collective-permute-start = (bf16[80,2560]{1,0:T(8,128)(2,1)S(1)}, bf16[80,2560]{1,0:T(8,128)(2,1)S(1)}, u32[]{:S(2)}, u32[]{:S(2)}) collective-permute-start(bf16[80,2560]{1,0:T(8,128)(2,1)S(1)} %slice.3), channel_id=1, source_target_pairs={{0,4},{4,8},{8,12},{12,16},{16,20},{20,24},{24,28},{1,5},{5,9},{9,... | collective-permute-start | bytes 1228808 | tf_op jit(solution)/shard_map/ppermute | solution.py:532
  3.6 1.0 %copy-start.1 = (bf16[1024,128]{1,0:T(8,128)(2,1)S(1)}, bf16[1024,128]{1,0:T(8,128)(2,1)}, u32[]{:S(2)}) copy-start(bf16[1024,128]{1,0:T(8,128)(2,1)} %refs_3_.1) | copy-start | bytes 786436
  4.5 0.7 copy-start.2
  5.2 0.7 copy-start.3
  16.1 4.4 %collective-permute-start.1 = (bf16[128,2560]{1,0:T(8,128)(2,1)S(1)}, bf16[128,2560]{1,0:T(8,128)(2,1)S(1)}, u32[]{:S(2)}, u32[]{:S(2)}) collective-permute-start(bf16[128,2560]{1,0:T(8,128)(2,1)S(1)} %front.3.own.refs_6_), channel_id=1, source_target_pairs={{0,4},{4,0},{8,12},{12,8},{16,20},{20,16},{24,28},{28,24},{1,5},{5... | collective-permute-start | bytes 1966088 | tf_op jit(solution)/shard_map/ppermute | solution.py:497
  18.7 21.4 %collective-permute-start.5 = (bf16[128,2560]{1,0:T(8,128)(2,1)S(1)}, bf16[128,2560]{1,0:T(8,128)(2,1)S(1)}, u32[]{:S(2)}, u32[]{:S(2)}) collective-permute-start(bf16[128,2560]{1,0:T(8,128)(2,1)S(1)} %front.3.own.refs_6_), channel_id=1, source_target_pairs={{0,8},{4,12},{8,0},{12,4},{16,24},{20,28},{24,16},{28,20},{1,9},{5... | collective-permute-start | bytes 1966088 | tf_op jit(solution)/shard_map/ppermute | solution.py:497
  21.3 4.6 %collective-permute-start.2 = (bf16[272,128]{1,0:T(8,128)(2,1)S(1)}, bf16[272,128]{1,0:T(8,128)(2,1)S(1)}, u32[]{:S(2)}, u32[]{:S(2)}) collective-permute-start(bf16[272,128]{1,0:T(8,128)(2,1)S(1)} %pair_gram.1.refs_0_), channel_id=1, source_target_pairs={{0,1},{1,0},{2,3},{3,2},{4,5},{5,4},{6,7},{7,6},{8,9},{9,8},{10,11... | collective-permute-start | bytes 208904 | tf_op jit(solution)/shard_map/ppermute | solution.py:497
  22.9 7.9 %collective-permute-start.3 = (bf16[272,128]{1,0:T(8,128)(2,1)S(1)}, bf16[272,128]{1,0:T(8,128)(2,1)S(1)}, u32[]{:S(2)}, u32[]{:S(2)}) collective-permute-start(bf16[272,128]{1,0:T(8,128)(2,1)S(1)} %pair_gram.1.refs_0_), channel_id=1, source_target_pairs={{0,2},{1,3},{2,0},{3,1},{4,6},{5,7},{6,4},{7,5},{8,10},{9,11},{10,... | collective-permute-start | bytes 208904 | tf_op jit(solution)/shard_map/ppermute | solution.py:497
  25.5 6.2 %collective-permute-start.4 = (bf16[272,128]{1,0:T(8,128)(2,1)S(1)}, bf16[272,128]{1,0:T(8,128)(2,1)S(1)}, u32[]{:S(2)}, u32[]{:S(2)}) collective-permute-start(bf16[272,128]{1,0:T(8,128)(2,1)S(1)} %pair_gram.1.refs_0_), channel_id=1, source_target_pairs={{0,3},{1,2},{2,1},{3,0},{4,7},{5,6},{6,5},{7,4},{8,11},{9,10},{10,... | collective-permute-start | bytes 208904 | tf_op jit(solution)/shard_map/ppermute | solution.py:497
  38.2 8.3 %collective-permute-start.11 = (bf16[128,1280]{1,0:T(8,128)(2,1)S(1)}, bf16[128,1280]{1,0:T(8,128)(2,1)S(1)}, u32[]{:S(2)}, u32[]{:S(2)}) collective-permute-start(bf16[128,1280]{1,0:T(8,128)(2,1)S(1)} %get-tuple-element.29.own), channel_id=1, source_target_pairs={{0,8},{4,12},{8,0},{12,4},{16,24},{20,28},{24,16},{28,20},{1,9},{5... | collective-permute-start | bytes 983048 | tf_op jit(solution)/shard_map/ppermute | solution.py:497
  39.8 7.9 %collective-permute-start.12 = (bf16[128,1280]{1,0:T(8,128)(2,1)S(1)}, bf16[128,1280]{1,0:T(8,128)(2,1)S(1)}, u32[]{:S(2)}, u32[]{:S(2)}) collective-permute-start(bf16[128,1280]{1,0:T(8,128)(2,1)S(1)} %get-tuple-element.29.own), channel_id=1, source_target_pairs={{0,16},{4,20},{8,24},{12,28},{16,0},{20,4},{24,8},{28,12},{1,17},{... | collective-permute-start | bytes 983048 | tf_op jit(solution)/shard_map/ppermute | solution.py:497
  40.7 7.5 %collective-permute-start.6 = (bf16[256,128]{1,0:T(8,128)(2,1)S(1)}, bf16[256,128]{1,0:T(8,128)(2,1)S(1)}, u32[]{:S(2)}, u32[]{:S(2)}) collective-permute-start(bf16[256,128]{1,0:T(8,128)(2,1)S(1)} %ahead_gram.2), channel_id=1, source_target_pairs={{0,1},{1,0},{2,3},{3,2},{4,5},{5,4},{6,7},{7,6},{8,9},{9,8},{10,11... | collective-permute-start | bytes 196616 | tf_op jit(solution)/shard_map/ppermute | solution.py:497
  41.9 6.7 %collective-permute-start.7 = (bf16[256,128]{1,0:T(8,128)(2,1)S(1)}, bf16[256,128]{1,0:T(8,128)(2,1)S(1)}, u32[]{:S(2)}, u32[]{:S(2)}) collective-permute-start(bf16[256,128]{1,0:T(8,128)(2,1)S(1)} %ahead_gram.2), channel_id=1, source_target_pairs={{0,2},{1,3},{2,0},{3,1},{4,6},{5,7},{6,4},{7,5},{8,10},{9,11},{10,... | collective-permute-start | bytes 196616 | tf_op jit(solution)/shard_map/ppermute | solution.py:497
  43.6 6.2 %collective-permute-start.8 = (bf16[256,128]{1,0:T(8,128)(2,1)S(1)}, bf16[256,128]{1,0:T(8,128)(2,1)S(1)}, u32[]{:S(2)}, u32[]{:S(2)}) collective-permute-start(bf16[256,128]{1,0:T(8,128)(2,1)S(1)} %ahead_gram.2), channel_id=1, source_target_pairs={{0,3},{1,2},{2,1},{3,0},{4,7},{5,6},{6,5},{7,4},{8,11},{9,10},{10,... | collective-permute-start | bytes 196616 | tf_op jit(solution)/shard_map/ppermute | solution.py:497
  48.1 3.8 %collective-permute-start.13 = (bf16[256,128]{1,0:T(8,128)(2,1)S(1)}, bf16[256,128]{1,0:T(8,128)(2,1)S(1)}, u32[]{:S(2)}, u32[]{:S(2)}) collective-permute-start(bf16[256,128]{1,0:T(8,128)(2,1)S(1)} %ahead_gram.3), channel_id=1, source_target_pairs={{0,4},{4,0},{8,12},{12,8},{16,20},{20,16},{24,28},{28,24},{1,5},{5... | collective-permute-start | bytes 196616 | tf_op jit(solution)/shard_map/ppermute | solution.py:497
  49.8 6.6 %collective-permute-start.9 = (bf16[256,128]{1,0:T(8,128)(2,1)S(1)}, bf16[256,128]{1,0:T(8,128)(2,1)S(1)}, u32[]{:S(2)}, u32[]{:S(2)}) collective-permute-start(bf16[256,128]{1,0:T(8,128)(2,1)S(1)} %add_convert_fusion.2.refs_2_), channel_id=1, source_target_pairs={{0,4},{4,0},{8,12},{12,8},{16,20},{20,16},{24,28},{28,24},{1,5},{5... | collective-permute-start | bytes 196616 | tf_op jit(solution)/shard_map/ppermute | solution.py:497
  49.9 6.5 %collective-permute-start.10 = (bf16[128,512]{1,0:T(8,128)(2,1)S(1)}, bf16[128,512]{1,0:T(8,128)(2,1)S(1)}, u32[]{:S(2)}, u32[]{:S(2)}) collective-permute-start(bf16[128,512]{1,0:T(8,128)(2,1)S(1)} %get-tuple-element.26.refs_0_), channel_id=1, source_target_pairs={{0,8},{4,12},{8,0},{12,4},{16,24},{20,28},{24,16},{28,20},{1,9},{5... | collective-permute-start | bytes 393224 | tf_op jit(solution)/shard_map/ppermute | solution.py:497
  51.9 12.4 %collective-permute-start.14 = (bf16[256,128]{1,0:T(8,128)(2,1)S(1)}, bf16[256,128]{1,0:T(8,128)(2,1)S(1)}, u32[]{:S(2)}, u32[]{:S(2)}) collective-permute-start(bf16[256,128]{1,0:T(8,128)(2,1)S(1)} %add_convert_fusion.1), channel_id=1, source_target_pairs={{0,1},{1,0},{2,3},{3,2},{4,5},{5,4},{6,7},{7,6},{8,9},{9,8},{10,11... | collective-permute-start | bytes 196616 | tf_op jit(solution)/shard_map/ppermute | solution.py:497
  52.5 11.8 %collective-permute-start.15 = (bf16[256,128]{1,0:T(8,128)(2,1)S(1)}, bf16[256,128]{1,0:T(8,128)(2,1)S(1)}, u32[]{:S(2)}, u32[]{:S(2)}) collective-permute-start(bf16[256,128]{1,0:T(8,128)(2,1)S(1)} %add_convert_fusion.1), channel_id=1, source_target_pairs={{0,2},{1,3},{2,0},{3,1},{4,6},{5,7},{6,4},{7,5},{8,10},{9,11},{10,... | collective-permute-start | bytes 196616 | tf_op jit(solution)/shard_map/ppermute | solution.py:497
  53.8 10.5 %collective-permute-start.16 = (bf16[256,128]{1,0:T(8,128)(2,1)S(1)}, bf16[256,128]{1,0:T(8,128)(2,1)S(1)}, u32[]{:S(2)}, u32[]{:S(2)}) collective-permute-start(bf16[256,128]{1,0:T(8,128)(2,1)S(1)} %add_convert_fusion.1), channel_id=1, source_target_pairs={{0,3},{1,2},{2,1},{3,0},{4,7},{5,6},{6,5},{7,4},{8,11},{9,10},{10,... | collective-permute-start | bytes 196616 | tf_op jit(solution)/shard_map/ppermute | solution.py:497
  62.9 5.0 %collective-permute-start.18 = (bf16[128,512]{1,0:T(8,128)(2,1)S(1)}, bf16[128,512]{1,0:T(8,128)(2,1)S(1)}, u32[]{:S(2)}, u32[]{:S(2)}) collective-permute-start(bf16[128,512]{1,0:T(8,128)(2,1)S(1)} %get-tuple-element.30), channel_id=1, source_target_pairs={{0,16},{4,20},{8,24},{12,28},{16,0},{20,4},{24,8},{28,12},{1,17},{... | collective-permute-start | bytes 393224 | tf_op jit(solution)/shard_map/ppermute | solution.py:497
  64.4 4.3 %collective-permute-start.17 = (bf16[256,128]{1,0:T(8,128)(2,1)S(1)}, bf16[256,128]{1,0:T(8,128)(2,1)S(1)}, u32[]{:S(2)}, u32[]{:S(2)}) collective-permute-start(bf16[256,128]{1,0:T(8,128)(2,1)S(1)} %add_convert_fusion.refs_2_), channel_id=1, source_target_pairs={{0,8},{4,12},{8,0},{12,4},{16,24},{20,28},{24,16},{28,20},{1,9},{5... | collective-permute-start | bytes 196616 | tf_op jit(solution)/shard_map/ppermute | solution.py:497
  68.7 8.1 %collective-permute-start.19 = (bf16[128,1280]{1,0:T(8,128)(2,1)S(1)}, bf16[128,1280]{1,0:T(8,128)(2,1)S(1)}, u32[]{:S(2)}, u32[]{:S(2)}) collective-permute-start(bf16[128,1280]{1,0:T(8,128)(2,1)S(1)} %hold.1.own), channel_id=1, source_target_pairs={{0,16},{4,20},{8,24},{12,28},{16,0},{20,4},{24,8},{28,12},{1,17},{... | collective-permute-start | bytes 983048 | tf_op jit(solution)/shard_map/ppermute | solution.py:497
  77.1 1.3 %collective-permute-start.20 = (f32[16,1280]{1,0:T(8,128)S(1)}, f32[16,1280]{1,0:T(8,128)S(1)}, u32[]{:S(2)}, u32[]{:S(2)}) collective-permute-start(f32[16,1280]{1,0:T(8,128)S(1)} %get-tuple-element.32), channel_id=1, source_target_pairs={{0,4},{4,0},{8,12},{12,8},{16,20},{20,16},{24,28},{28,24},{1,5},{5... | collective-permute-start | bytes 245768 | tf_op jit(solution)/shard_map/ppermute | solution.py:497

commit v11 on v10

--- a/solution.py
+++ b/solution.py
@@ -274,6 +274,20 @@
         compiler_params=pltpu.CompilerParams(vmem_limit_bytes=16 * 2**20),
         name="hold",
     )(value, *until)
+
+
+def add_kernel(one, two, _, out):
+    out[...] = (one[...].astype(F32) + two[...].astype(F32)).astype(BF16)
+
+
+def add_after(one, two, after):
+    return pl.pallas_call(
+        add_kernel,
+        in_specs=[VMEM, VMEM, ANY],
+        out_shape=jax.ShapeDtypeStruct(one.shape, BF16),
+        compiler_params=pltpu.CompilerParams(vmem_limit_bytes=16 * 2**20),
+        name="add_after",
+    )(one, two, after)
 
 
 def square_of(aa, ab, bb):
@@ -585,7 +599,7 @@
             packed, level = level_call(mixing, full)
         kept = packed, mixing, level
         for bit in [b for b in narrowed if b < depth]:
-            part = (part.astype(F32) + swap(part, "tm", 2**bit).astype(F32)).astype(BF16)
+            part = add_after(part, swap(part, "tm", 2**bit), grams[-1])
         parts = gather_parts(part, "chan")
         total = sum(piece.astype(F32) for piece in parts).astype(BF16)
         ahead = [total, swap(total, "tm", mask)]

time: 79.9 us -> 79.4 us (level)
  waiting for transfers between devices: 15.6 us -> 14.8 us
    ppermute x20, waiting for transfers between devices: 15.6 us -> 14.8 us  [swap(): lax.ppermute(value, axis, [(source, source ^ mask) for source in range(co...]
  transfers between devices with their start and end apart: 21 -> 21, of which waited for: 11 -> 10; matrix products, arithmetic and copies ran while one was open for 0% -> 0% of each run, Pallas kernels for 38% -> 39%
where the time goes in v11:
time: 79.4 us; the launch traced here: 79.1 us
  Pallas kernels  33.3 us (42%)
  starting transfers between devices  27.2 us (34%)
  waiting for transfers between devices  14.8 us (19%)
  local copies, waits for them, and re-layouts  3.43 us (4%)
    ppermute x20, starting transfers between devices, swap(): lax.ppermute(value, axis, [(source, source ^ mask) for source in range(co...  24.7 us
    ppermute x20, waiting for transfers between devices, swap(): lax.ppermute(value, axis, [(source, source ^ mask) for source in range(co...  14.8 us
    pallas_call x2, Pallas kernels, front_call(): pl.pallas_call(functools.partial(front_kernel, *blocks), grid=(steps,), i...  10.2 us
    pallas_call x1, Pallas kernels, level_filter_call(): pl.pallas_call(functools.partial(filter_kernel, len(grams), first, 'level...  6.58 us
    pallas_call x1, Pallas kernels, filter_call(): pl.pallas_call(functools.partial(filter_kernel, len(grams), first, 'sketc...  6.53 us
    pallas_call x1, Pallas kernels, last_filter_call(): pl.pallas_call(functools.partial(filter_kernel, len(grams), first, 'last'...  6.08 us
    ppermute x1, starting transfers between devices, on_device(): lax.ppermute(record[rows - HALO:], 'tm', [(source, source + 1) for source...  2.51 us
    unnamed x8, local copies, waits for them, and re-layouts  2.31 us
  transfers between devices with their start and end apart: 21, of which 10 were waited for; matrix products, arithmetic and copies ran while one was open for 0% of the time, Pallas kernels for 39%

profile of v11, /device:TPU:0, one launch (start us, length us, event | category | flops | bytes accessed | tf_op | source)
XLA Modules:
  0.0 79.1 jit_solution(13628093131270920013)
XLA Ops:
  0.0 1.0 %slice.3 = bf16[80,2560]{1,0:T(8,128)(2,1)S(1)} slice(bf16[1024,2560]{1,0:T(8,128)(2,1)} %refs_0_.1), slice={[944:1024], [0:2560]} | slice | bytes 819200 | tf_op jit(solution)/shard_map/slice | solution.py:547
  1.0 2.5 %collective-permute-start = (bf16[80,2560]{1,0:T(8,128)(2,1)S(1)}, bf16[80,2560]{1,0:T(8,128)(2,1)S(1)}, u32[]{:S(2)}, u32[]{:S(2)}) collective-permute-start(bf16[80,2560]{1,0:T(8,128)(2,1)S(1)} %slice.3), channel_id=1, source_target_pairs={{0,4},{4,8},{8,12},{12,16},{16,20},{20,24},{24,28},{1,5},{5,9},{9,... | collective-permute-start | bytes 1228808 | tf_op jit(solution)/shard_map/ppermute | solution.py:546
  3.6 0.9 %copy-done.1 = bf16[1024,128]{1,0:T(8,128)(2,1)S(1)} copy-done((bf16[1024,128]{1,0:T(8,128)(2,1)S(1)}, bf16[1024,128]{1,0:T(8,128)(2,1)}, u32[]{:S(2)}) %copy-start.1) | copy-done | bytes 262168
  4.5 0.7 copy-done.2
  5.9 8.8 %front.2 = (f32[128,2560]{1,0:T(8,128)S(1)}, bf16[256,208]{1,0:T(8,128)(2,1)S(1)}, bf16[128,128]{1,0:T(8,128)(2,1)S(1)}, bf16[128,2560]{1,0:T(8,128)(2,1)S(1)}) custom-call(bf16[1024,2560]{1,0:T(8,128)(2,1)} %refs_0_.1, s32[20,128]{1,0:T(8,128)S(1)} %bitcast.9, bf16[1,64]{1,0:T(2,128)(2,1)S(1)} %bitcast.11, bf16[1024,128]{1,0:T(8,128)(2,1)S(1)} %copy-done.1), custom_call_target="tpu_custom_call" | custom-call | tf_op jit(solution)/shard_map/front/pallas_call | solution.py:140
  14.7 1.4 %front.3.own.refs_6_ = bf16[128,2560]{1,0:T(8,128)(2,1)S(1)} custom-call(bf16[128,2560]{1,0:T(8,128)(2,1)S(1)} %get-tuple-element.19.refs_0_, bf16[80,2560]{1,0:T(8,128)(2,1)S(1)} %collective-permute-done.refs_1_, s32[20,128]{1,0:T(8,128)S(1)} %bitcast.10, bf16[256,208]{1,0:T(8,128)(2,1)S(1)} %get-tuple-element.20.refs_3_, ...), custom_call_target="tpu_custom_call" | custom-call | tf_op jit(solution)/shard_map/front/pallas_call | solution.py:140
  16.1 2.6 %collective-permute-start.1 = (bf16[128,2560]{1,0:T(8,128)(2,1)S(1)}, bf16[128,2560]{1,0:T(8,128)(2,1)S(1)}, u32[]{:S(2)}, u32[]{:S(2)}) collective-permute-start(bf16[128,2560]{1,0:T(8,128)(2,1)S(1)} %front.3.own.refs_6_), channel_id=1, source_target_pairs={{0,4},{4,0},{8,12},{12,8},{16,20},{20,16},{24,28},{28,24},{1,5},{5... | collective-permute-start | bytes 1966088 | tf_op jit(solution)/shard_map/ppermute | solution.py:511
  18.7 1.5 %collective-permute-start.5 = (bf16[128,2560]{1,0:T(8,128)(2,1)S(1)}, bf16[128,2560]{1,0:T(8,128)(2,1)S(1)}, u32[]{:S(2)}, u32[]{:S(2)}) collective-permute-start(bf16[128,2560]{1,0:T(8,128)(2,1)S(1)} %front.3.own.refs_6_), channel_id=1, source_target_pairs={{0,8},{4,12},{8,0},{12,4},{16,24},{20,28},{24,16},{28,20},{1,9},{5... | collective-permute-start | bytes 1966088 | tf_op jit(solution)/shard_map/ppermute | solution.py:511
  20.5 0.8 %pair_gram.1.refs_0_ = bf16[272,128]{1,0:T(8,128)(2,1)S(1)} custom-call(bf16[128,2560]{1,0:T(8,128)(2,1)S(1)} %front.3.own.refs_6_, bf16[128,2560]{1,0:T(8,128)(2,1)S(1)} %collective-permute-done.1.other.refs_7_.sibling), custom_call_target="tpu_custom_call" | custom-call | tf_op jit(solution)/shard_map/pair_gram/pallas_call | solution.py:229
  21.3 1.7 %collective-permute-start.2 = (bf16[272,128]{1,0:T(8,128)(2,1)S(1)}, bf16[272,128]{1,0:T(8,128)(2,1)S(1)}, u32[]{:S(2)}, u32[]{:S(2)}) collective-permute-start(bf16[272,128]{1,0:T(8,128)(2,1)S(1)} %pair_gram.1.refs_0_), channel_id=1, source_target_pairs={{0,1},{1,0},{2,3},{3,2},{4,5},{5,4},{6,7},{7,6},{8,9},{9,8},{10,11... | collective-permute-start | bytes 208904 | tf_op jit(solution)/shard_map/ppermute | solution.py:511
  22.9 2.6 %collective-permute-start.3 = (bf16[272,128]{1,0:T(8,128)(2,1)S(1)}, bf16[272,128]{1,0:T(8,128)(2,1)S(1)}, u32[]{:S(2)}, u32[]{:S(2)}) collective-permute-start(bf16[272,128]{1,0:T(8,128)(2,1)S(1)} %pair_gram.1.refs_0_), channel_id=1, source_target_pairs={{0,2},{1,3},{2,0},{3,1},{4,6},{5,7},{6,4},{7,5},{8,10},{9,11},{10,... | collective-permute-start | bytes 208904 | tf_op jit(solution)/shard_map/ppermute | solution.py:511
  25.8 5.0 %collective-permute-done.3.refs_2_ = bf16[272,128]{1,0:T(8,128)(2,1)S(1)} collective-permute-done((bf16[272,128]{1,0:T(8,128)(2,1)S(1)}, bf16[272,128]{1,0:T(8,128)(2,1)S(1)}, u32[]{:S(2)}, u32[]{:S(2)}) %collective-permute-start.3) | collective-permute-done | bytes 69664 | tf_op jit(solution)/shard_map/ppermute | solution.py:511
  30.9 0.8 %collective-permute-done.4.refs_3_ = bf16[272,128]{1,0:T(8,128)(2,1)S(1)} collective-permute-done((bf16[272,128]{1,0:T(8,128)(2,1)S(1)}, bf16[272,128]{1,0:T(8,128)(2,1)S(1)}, u32[]{:S(2)}, u32[]{:S(2)}) %collective-permute-start.4) | collective-permute-done | bytes 69664 | tf_op jit(solution)/shard_map/ppermute | solution.py:511
  31.7 6.5 %sign_filter.3 = (f32[128,256]{1,0:T(8,128)S(1)}, bf16[128,1280]{1,0:T(8,128)(2,1)S(1)}, f32[256,256]{1,0:T(8,128)S(1)}) custom-call(bf16[272,128]{1,0:T(8,128)(2,1)S(1)} %pair_gram.1.refs_0_, bf16[272,128]{1,0:T(8,128)(2,1)S(1)} %collective-permute-done.2.refs_1_, bf16[272,128]{1,0:T(8,128)(2,1)S(1)} %collective-permute-done.3.refs_2_, ...), custom_call_target="tpu_custom_call" | custom-call | tf_op jit(solution)/shard_map/sign_filter/pallas_call | solution.py:451
  38.2 1.6 %collective-permute-start.11 = (bf16[128,1280]{1,0:T(8,128)(2,1)S(1)}, bf16[128,1280]{1,0:T(8,128)(2,1)S(1)}, u32[]{:S(2)}, u32[]{:S(2)}) collective-permute-start(bf16[128,1280]{1,0:T(8,128)(2,1)S(1)} %get-tuple-element.29.own), channel_id=1, source_target_pairs={{0,8},{4,12},{8,0},{12,4},{16,24},{20,28},{24,16},{28,20},{1,9},{5... | collective-permute-start | bytes 983048 | tf_op jit(solution)/shard_map/ppermute | solution.py:511
  40.7 1.2 %collective-permute-start.6 = (bf16[256,128]{1,0:T(8,128)(2,1)S(1)}, bf16[256,128]{1,0:T(8,128)(2,1)S(1)}, u32[]{:S(2)}, u32[]{:S(2)}) collective-permute-start(bf16[256,128]{1,0:T(8,128)(2,1)S(1)} %ahead_gram.2), channel_id=1, source_target_pairs={{0,1},{1,0},{2,3},{3,2},{4,5},{5,4},{6,7},{7,6},{8,9},{9,8},{10,11... | collective-permute-start | bytes 196616 | tf_op jit(solution)/shard_map/ppermute | solution.py:511
  41.9 1.7 %collective-permute-start.7 = (bf16[256,128]{1,0:T(8,128)(2,1)S(1)}, bf16[256,128]{1,0:T(8,128)(2,1)S(1)}, u32[]{:S(2)}, u32[]{:S(2)}) collective-permute-start(bf16[256,128]{1,0:T(8,128)(2,1)S(1)} %ahead_gram.2), channel_id=1, source_target_pairs={{0,2},{1,3},{2,0},{3,1},{4,6},{5,7},{6,4},{7,5},{8,10},{9,11},{10,... | collective-permute-start | bytes 196616 | tf_op jit(solution)/shard_map/ppermute | solution.py:511
  43.6 1.6 %collective-permute-start.8 = (bf16[256,128]{1,0:T(8,128)(2,1)S(1)}, bf16[256,128]{1,0:T(8,128)(2,1)S(1)}, u32[]{:S(2)}, u32[]{:S(2)}) collective-permute-start(bf16[256,128]{1,0:T(8,128)(2,1)S(1)} %ahead_gram.2), channel_id=1, source_target_pairs={{0,3},{1,2},{2,1},{3,0},{4,7},{5,6},{6,5},{7,4},{8,11},{9,10},{10,... | collective-permute-start | bytes 196616 | tf_op jit(solution)/shard_map/ppermute | solution.py:511
  45.6 0.9 %collective-permute-done.11.sibling.other = bf16[128,1280]{1,0:T(8,128)(2,1)S(1)} collective-permute-done((bf16[128,1280]{1,0:T(8,128)(2,1)S(1)}, bf16[128,1280]{1,0:T(8,128)(2,1)S(1)}, u32[]{:S(2)}, u32[]{:S(2)}) %collective-permute-start.11) | collective-permute-done | bytes 327712 | tf_op jit(solution)/shard_map/ppermute | solution.py:511
  46.5 1.5 %collective-permute-start.10 = (bf16[128,512]{1,0:T(8,128)(2,1)S(1)}, bf16[128,512]{1,0:T(8,128)(2,1)S(1)}, u32[]{:S(2)}, u32[]{:S(2)}) collective-permute-start(bf16[128,512]{1,0:T(8,128)(2,1)S(1)} %get-tuple-element.26.refs_0_), channel_id=1, source_target_pairs={{0,8},{4,12},{8,0},{12,4},{16,24},{20,28},{24,16},{28,20},{1,9},{5... | collective-permute-start | bytes 393224 | tf_op jit(solution)/shard_map/ppermute | solution.py:511
  48.6 1.1 %collective-permute-done.8 = bf16[256,128]{1,0:T(8,128)(2,1)S(1)} collective-permute-done((bf16[256,128]{1,0:T(8,128)(2,1)S(1)}, bf16[256,128]{1,0:T(8,128)(2,1)S(1)}, u32[]{:S(2)}, u32[]{:S(2)}) %collective-permute-start.8) | collective-permute-done | bytes 65568 | tf_op jit(solution)/shard_map/ppermute | solution.py:511
  49.8 1.6 %collective-permute-done.10.refs_4_._ = bf16[128,512]{1,0:T(8,128)(2,1)S(1)} collective-permute-done((bf16[128,512]{1,0:T(8,128)(2,1)S(1)}, bf16[128,512]{1,0:T(8,128)(2,1)S(1)}, u32[]{:S(2)}, u32[]{:S(2)}) %collective-permute-start.10) | collective-permute-done | bytes 131104 | tf_op jit(solution)/shard_map/ppermute | solution.py:511
  51.5 2.5 %collective-permute-start.14 = (bf16[256,128]{1,0:T(8,128)(2,1)S(1)}, bf16[256,128]{1,0:T(8,128)(2,1)S(1)}, u32[]{:S(2)}, u32[]{:S(2)}) collective-permute-start(bf16[256,128]{1,0:T(8,128)(2,1)S(1)} %add_after.1), channel_id=1, source_target_pairs={{0,1},{1,0},{2,3},{3,2},{4,5},{5,4},{6,7},{7,6},{8,9},{9,8},{10,11... | collective-permute-start | bytes 196616 | tf_op jit(solution)/shard_map/ppermute | solution.py:511
  54.7 1.8 %collective-permute-start.16 = (bf16[256,128]{1,0:T(8,128)(2,1)S(1)}, bf16[256,128]{1,0:T(8,128)(2,1)S(1)}, u32[]{:S(2)}, u32[]{:S(2)}) collective-permute-start(bf16[256,128]{1,0:T(8,128)(2,1)S(1)} %add_after.1), channel_id=1, source_target_pairs={{0,3},{1,2},{2,1},{3,0},{4,7},{5,6},{6,5},{7,4},{8,11},{9,10},{10,... | collective-permute-start | bytes 196616 | tf_op jit(solution)/shard_map/ppermute | solution.py:511
  56.4 6.6 %sign_filter.4 = (f32[128,256]{1,0:T(8,128)S(1)}, bf16[128,512]{1,0:T(8,128)(2,1)S(1)}, f32[128,128]{1,0:T(8,128)S(1)}) custom-call(f32[128,256]{1,0:T(8,128)S(1)} %get-tuple-element.23.mixing.refs_0_, f32[128,128]{1,0:T(8,128)S(1)} %get-tuple-element.25.refs_1_, bf16[256,128]{1,0:T(8,128)(2,1)S(1)} %add_convert_fusion.1.refs_2_, ...), custom_call_target="tpu_custom_call" | custom-call | tf_op jit(solution)/shard_map/sign_filter/pallas_call | solution.py:438
  63.0 1.6 %collective-permute-start.18 = (bf16[128,512]{1,0:T(8,128)(2,1)S(1)}, bf16[128,512]{1,0:T(8,128)(2,1)S(1)}, u32[]{:S(2)}, u32[]{:S(2)}) collective-permute-start(bf16[128,512]{1,0:T(8,128)(2,1)S(1)} %get-tuple-element.30), channel_id=1, source_target_pairs={{0,16},{4,20},{8,24},{12,28},{16,0},{20,4},{24,8},{28,12},{1,17},{... | collective-permute-start | bytes 393224 | tf_op jit(solution)/shard_map/ppermute | solution.py:511
  65.4 2.7 %collective-permute-done.18.refs_4_.refs_2_ = bf16[128,512]{1,0:T(8,128)(2,1)S(1)} collective-permute-done((bf16[128,512]{1,0:T(8,128)(2,1)S(1)}, bf16[128,512]{1,0:T(8,128)(2,1)S(1)}, u32[]{:S(2)}, u32[]{:S(2)}) %collective-permute-start.18) | collective-permute-done | bytes 131104 | tf_op jit(solution)/shard_map/ppermute | solution.py:511
  68.0 0.9 %collective-permute-done.17.refs_3_.refs_1_ = bf16[256,128]{1,0:T(8,128)(2,1)S(1)} collective-permute-done((bf16[256,128]{1,0:T(8,128)(2,1)S(1)}, bf16[256,128]{1,0:T(8,128)(2,1)S(1)}, u32[]{:S(2)}, u32[]{:S(2)}) %collective-permute-start.17) | collective-permute-done | bytes 65568 | tf_op jit(solution)/shard_map/ppermute | solution.py:511
  69.0 1.2 %collective-permute-start.19 = (bf16[128,1280]{1,0:T(8,128)(2,1)S(1)}, bf16[128,1280]{1,0:T(8,128)(2,1)S(1)}, u32[]{:S(2)}, u32[]{:S(2)}) collective-permute-start(bf16[128,1280]{1,0:T(8,128)(2,1)S(1)} %hold.1.own), channel_id=1, source_target_pairs={{0,16},{4,20},{8,24},{12,28},{16,0},{20,4},{24,8},{28,12},{1,17},{... | collective-permute-start | bytes 983048 | tf_op jit(solution)/shard_map/ppermute | solution.py:511
  70.2 6.1 %sign_filter.5.mixing = f32[32,256]{1,0:T(8,128)S(1)} custom-call(f32[128,256]{1,0:T(8,128)S(1)} %get-tuple-element.27.refs_0_.mixing, f32[128,128]{1,0:T(8,128)S(1)} %get-tuple-element.28.refs_1_, bf16[256,128]{1,0:T(8,128)(2,1)S(1)} %add_convert_fusion.refs_2_, bf16[256,128]{1,0:T(8,128)(2,1)S(1)} %collective-permute-done.17.refs_3_.refs_1_, ...), custom_call_target="tpu_custom_call" | custom-call | flops 6710886400 | tf_op jit(solution)/shard_map/sign_filter/pallas_call | solution.py:472
  76.6 1.3 %collective-permute-done.20.refs_1_ = f32[16,1280]{1,0:T(8,128)S(1)} collective-permute-done((f32[16,1280]{1,0:T(8,128)S(1)}, f32[16,1280]{1,0:T(8,128)S(1)}, u32[]{:S(2)}, u32[]{:S(2)}) %collective-permute-start.20) | collective-permute-done | bytes 81952 | tf_op jit(solution)/shard_map/ppermute | solution.py:511
  77.9 1.2 %join.1 = f32[16,2560]{1,0:T(8,128)} custom-call(s32[10]{0:T(128)S(1)} %stack.32.refs_5_.refs_6_.places, f32[16,1280]{1,0:T(8,128)S(1)} %get-tuple-element.31.refs_0_, f32[16,1280]{1,0:T(8,128)S(1)} %collective-permute-done.20.refs_1_), custom_call_target="tpu_custom_call" | custom-call | tf_op jit(solution)/shard_map/join/pallas_call | solution.py:530
  (36 shorter events, 5.0 us)
Async XLA Ops:
  1.0 30.7 %copy-start = (f32[256,128]{1,0:T(8,128)S(1)}, f32[256,128]{1,0:T(8,128)}, u32[]{:S(2)}) copy-start(f32[256,128]{1,0:T(8,128)} %refs_5_.3) | copy-start | bytes 393220
  1.0 13.7 %collective-permute-start = (bf16[80,2560]{1,0:T(8,128)(2,1)S(1)}, bf16[80,2560]{1,0:T(8,128)(2,1)S(1)}, u32[]{:S(2)}, u32[]{:S(2)}) collective-permute-start(bf16[80,2560]{1,0:T(8,128)(2,1)S(1)} %slice.3), channel_id=1, source_target_pairs={{0,4},{4,8},{8,12},{12,16},{16,20},{20,24},{24,28},{1,5},{5,9},{9,... | collective-permute-start | bytes 1228808 | tf_op jit(solution)/shard_map/ppermute | solution.py:546
  3.6 1.0 %copy-start.1 = (bf16[1024,128]{1,0:T(8,128)(2,1)S(1)}, bf16[1024,128]{1,0:T(8,128)(2,1)}, u32[]{:S(2)}) copy-start(bf16[1024,128]{1,0:T(8,128)(2,1)} %refs_3_.1) | copy-start | bytes 786436
  4.5 0.7 copy-start.2
  5.2 0.7 copy-start.3
  16.1 4.4 %collective-permute-start.1 = (bf16[128,2560]{1,0:T(8,128)(2,1)S(1)}, bf16[128,2560]{1,0:T(8,128)(2,1)S(1)}, u32[]{:S(2)}, u32[]{:S(2)}) collective-permute-start(bf16[128,2560]{1,0:T(8,128)(2,1)S(1)} %front.3.own.refs_6_), channel_id=1, source_target_pairs={{0,4},{4,0},{8,12},{12,8},{16,20},{20,16},{24,28},{28,24},{1,5},{5... | collective-permute-start | bytes 1966088 | tf_op jit(solution)/shard_map/ppermute | solution.py:511
  18.7 21.4 %collective-permute-start.5 = (bf16[128,2560]{1,0:T(8,128)(2,1)S(1)}, bf16[128,2560]{1,0:T(8,128)(2,1)S(1)}, u32[]{:S(2)}, u32[]{:S(2)}) collective-permute-start(bf16[128,2560]{1,0:T(8,128)(2,1)S(1)} %front.3.own.refs_6_), channel_id=1, source_target_pairs={{0,8},{4,12},{8,0},{12,4},{16,24},{20,28},{24,16},{28,20},{1,9},{5... | collective-permute-start | bytes 1966088 | tf_op jit(solution)/shard_map/ppermute | solution.py:511
  21.3 4.6 %collective-permute-start.2 = (bf16[272,128]{1,0:T(8,128)(2,1)S(1)}, bf16[272,128]{1,0:T(8,128)(2,1)S(1)}, u32[]{:S(2)}, u32[]{:S(2)}) collective-permute-start(bf16[272,128]{1,0:T(8,128)(2,1)S(1)} %pair_gram.1.refs_0_), channel_id=1, source_target_pairs={{0,1},{1,0},{2,3},{3,2},{4,5},{5,4},{6,7},{7,6},{8,9},{9,8},{10,11... | collective-permute-start | bytes 208904 | tf_op jit(solution)/shard_map/ppermute | solution.py:511
  22.9 7.9 %collective-permute-start.3 = (bf16[272,128]{1,0:T(8,128)(2,1)S(1)}, bf16[272,128]{1,0:T(8,128)(2,1)S(1)}, u32[]{:S(2)}, u32[]{:S(2)}) collective-permute-start(bf16[272,128]{1,0:T(8,128)(2,1)S(1)} %pair_gram.1.refs_0_), channel_id=1, source_target_pairs={{0,2},{1,3},{2,0},{3,1},{4,6},{5,7},{6,4},{7,5},{8,10},{9,11},{10,... | collective-permute-start | bytes 208904 | tf_op jit(solution)/shard_map/ppermute | solution.py:511
  25.5 6.2 %collective-permute-start.4 = (bf16[272,128]{1,0:T(8,128)(2,1)S(1)}, bf16[272,128]{1,0:T(8,128)(2,1)S(1)}, u32[]{:S(2)}, u32[]{:S(2)}) collective-permute-start(bf16[272,128]{1,0:T(8,128)(2,1)S(1)} %pair_gram.1.refs_0_), channel_id=1, source_target_pairs={{0,3},{1,2},{2,1},{3,0},{4,7},{5,6},{6,5},{7,4},{8,11},{9,10},{10,... | collective-permute-start | bytes 208904 | tf_op jit(solution)/shard_map/ppermute | solution.py:511
  38.2 8.3 %collective-permute-start.11 = (bf16[128,1280]{1,0:T(8,128)(2,1)S(1)}, bf16[128,1280]{1,0:T(8,128)(2,1)S(1)}, u32[]{:S(2)}, u32[]{:S(2)}) collective-permute-start(bf16[128,1280]{1,0:T(8,128)(2,1)S(1)} %get-tuple-element.29.own), channel_id=1, source_target_pairs={{0,8},{4,12},{8,0},{12,4},{16,24},{20,28},{24,16},{28,20},{1,9},{5... | collective-permute-start | bytes 983048 | tf_op jit(solution)/shard_map/ppermute | solution.py:511
  39.8 8.2 %collective-permute-start.12 = (bf16[128,1280]{1,0:T(8,128)(2,1)S(1)}, bf16[128,1280]{1,0:T(8,128)(2,1)S(1)}, u32[]{:S(2)}, u32[]{:S(2)}) collective-permute-start(bf16[128,1280]{1,0:T(8,128)(2,1)S(1)} %get-tuple-element.29.own), channel_id=1, source_target_pairs={{0,16},{4,20},{8,24},{12,28},{16,0},{20,4},{24,8},{28,12},{1,17},{... | collective-permute-start | bytes 983048 | tf_op jit(solution)/shard_map/ppermute | solution.py:511
  40.7 7.7 %collective-permute-start.6 = (bf16[256,128]{1,0:T(8,128)(2,1)S(1)}, bf16[256,128]{1,0:T(8,128)(2,1)S(1)}, u32[]{:S(2)}, u32[]{:S(2)}) collective-permute-start(bf16[256,128]{1,0:T(8,128)(2,1)S(1)} %ahead_gram.2), channel_id=1, source_target_pairs={{0,1},{1,0},{2,3},{3,2},{4,5},{5,4},{6,7},{7,6},{8,9},{9,8},{10,11... | collective-permute-start | bytes 196616 | tf_op jit(solution)/shard_map/ppermute | solution.py:511
  41.9 6.7 %collective-permute-start.7 = (bf16[256,128]{1,0:T(8,128)(2,1)S(1)}, bf16[256,128]{1,0:T(8,128)(2,1)S(1)}, u32[]{:S(2)}, u32[]{:S(2)}) collective-permute-start(bf16[256,128]{1,0:T(8,128)(2,1)S(1)} %ahead_gram.2), channel_id=1, source_target_pairs={{0,2},{1,3},{2,0},{3,1},{4,6},{5,7},{6,4},{7,5},{8,10},{9,11},{10,... | collective-permute-start | bytes 196616 | tf_op jit(solution)/shard_map/ppermute | solution.py:511
  43.6 6.2 %collective-permute-start.8 = (bf16[256,128]{1,0:T(8,128)(2,1)S(1)}, bf16[256,128]{1,0:T(8,128)(2,1)S(1)}, u32[]{:S(2)}, u32[]{:S(2)}) collective-permute-start(bf16[256,128]{1,0:T(8,128)(2,1)S(1)} %ahead_gram.2), channel_id=1, source_target_pairs={{0,3},{1,2},{2,1},{3,0},{4,7},{5,6},{6,5},{7,4},{8,11},{9,10},{10,... | collective-permute-start | bytes 196616 | tf_op jit(solution)/shard_map/ppermute | solution.py:511
  46.5 5.0 %collective-permute-start.10 = (bf16[128,512]{1,0:T(8,128)(2,1)S(1)}, bf16[128,512]{1,0:T(8,128)(2,1)S(1)}, u32[]{:S(2)}, u32[]{:S(2)}) collective-permute-start(bf16[128,512]{1,0:T(8,128)(2,1)S(1)} %get-tuple-element.26.refs_0_), channel_id=1, source_target_pairs={{0,8},{4,12},{8,0},{12,4},{16,24},{20,28},{24,16},{28,20},{1,9},{5... | collective-permute-start | bytes 393224 | tf_op jit(solution)/shard_map/ppermute | solution.py:511
  48.3 3.1 %collective-permute-start.13 = (bf16[256,128]{1,0:T(8,128)(2,1)S(1)}, bf16[256,128]{1,0:T(8,128)(2,1)S(1)}, u32[]{:S(2)}, u32[]{:S(2)}) collective-permute-start(bf16[256,128]{1,0:T(8,128)(2,1)S(1)} %ahead_gram.3.one), channel_id=1, source_target_pairs={{0,4},{4,0},{8,12},{12,8},{16,20},{20,16},{24,28},{28,24},{1,5},{5... | collective-permute-start | bytes 196616 | tf_op jit(solution)/shard_map/ppermute | solution.py:511
  49.8 6.7 %collective-permute-start.9 = (bf16[256,128]{1,0:T(8,128)(2,1)S(1)}, bf16[256,128]{1,0:T(8,128)(2,1)S(1)}, u32[]{:S(2)}, u32[]{:S(2)}) collective-permute-start(bf16[256,128]{1,0:T(8,128)(2,1)S(1)} %add_convert_fusion.1.refs_2_), channel_id=1, source_target_pairs={{0,4},{4,0},{8,12},{12,8},{16,20},{20,16},{24,28},{28,24},{1,5},{5... | collective-permute-start | bytes 196616 | tf_op jit(solution)/shard_map/ppermute | solution.py:511
  51.5 13.1 %collective-permute-start.14 = (bf16[256,128]{1,0:T(8,128)(2,1)S(1)}, bf16[256,128]{1,0:T(8,128)(2,1)S(1)}, u32[]{:S(2)}, u32[]{:S(2)}) collective-permute-start(bf16[256,128]{1,0:T(8,128)(2,1)S(1)} %add_after.1), channel_id=1, source_target_pairs={{0,1},{1,0},{2,3},{3,2},{4,5},{5,4},{6,7},{7,6},{8,9},{9,8},{10,11... | collective-permute-start | bytes 196616 | tf_op jit(solution)/shard_map/ppermute | solution.py:511
  54.0 10.6 %collective-permute-start.15 = (bf16[256,128]{1,0:T(8,128)(2,1)S(1)}, bf16[256,128]{1,0:T(8,128)(2,1)S(1)}, u32[]{:S(2)}, u32[]{:S(2)}) collective-permute-start(bf16[256,128]{1,0:T(8,128)(2,1)S(1)} %add_after.1), channel_id=1, source_target_pairs={{0,2},{1,3},{2,0},{3,1},{4,6},{5,7},{6,4},{7,5},{8,10},{9,11},{10,... | collective-permute-start | bytes 196616 | tf_op jit(solution)/shard_map/ppermute | solution.py:511
  54.7 9.9 %collective-permute-start.16 = (bf16[256,128]{1,0:T(8,128)(2,1)S(1)}, bf16[256,128]{1,0:T(8,128)(2,1)S(1)}, u32[]{:S(2)}, u32[]{:S(2)}) collective-permute-start(bf16[256,128]{1,0:T(8,128)(2,1)S(1)} %add_after.1), channel_id=1, source_target_pairs={{0,3},{1,2},{2,1},{3,0},{4,7},{5,6},{6,5},{7,4},{8,11},{9,10},{10,... | collective-permute-start | bytes 196616 | tf_op jit(solution)/shard_map/ppermute | solution.py:511
  63.0 5.0 %collective-permute-start.18 = (bf16[128,512]{1,0:T(8,128)(2,1)S(1)}, bf16[128,512]{1,0:T(8,128)(2,1)S(1)}, u32[]{:S(2)}, u32[]{:S(2)}) collective-permute-start(bf16[128,512]{1,0:T(8,128)(2,1)S(1)} %get-tuple-element.30), channel_id=1, source_target_pairs={{0,16},{4,20},{8,24},{12,28},{16,0},{20,4},{24,8},{28,12},{1,17},{... | collective-permute-start | bytes 393224 | tf_op jit(solution)/shard_map/ppermute | solution.py:511
  64.7 4.3 %collective-permute-start.17 = (bf16[256,128]{1,0:T(8,128)(2,1)S(1)}, bf16[256,128]{1,0:T(8,128)(2,1)S(1)}, u32[]{:S(2)}, u32[]{:S(2)}) collective-permute-start(bf16[256,128]{1,0:T(8,128)(2,1)S(1)} %add_convert_fusion.refs_2_), channel_id=1, source_target_pairs={{0,8},{4,12},{8,0},{12,4},{16,24},{20,28},{24,16},{28,20},{1,9},{5... | collective-permute-start | bytes 196616 | tf_op jit(solution)/shard_map/ppermute | solution.py:511
  69.0 7.3 %collective-permute-start.19 = (bf16[128,1280]{1,0:T(8,128)(2,1)S(1)}, bf16[128,1280]{1,0:T(8,128)(2,1)S(1)}, u32[]{:S(2)}, u32[]{:S(2)}) collective-permute-start(bf16[128,1280]{1,0:T(8,128)(2,1)S(1)} %hold.1.own), channel_id=1, source_target_pairs={{0,16},{4,20},{8,24},{12,28},{16,0},{20,4},{24,8},{28,12},{1,17},{... | collective-permute-start | bytes 983048 | tf_op jit(solution)/shard_map/ppermute | solution.py:511
  76.5 1.3 %collective-permute-start.20 = (f32[16,1280]{1,0:T(8,128)S(1)}, f32[16,1280]{1,0:T(8,128)S(1)}, u32[]{:S(2)}, u32[]{:S(2)}) collective-permute-start(f32[16,1280]{1,0:T(8,128)S(1)} %get-tuple-element.32), channel_id=1, source_target_pairs={{0,4},{4,0},{8,12},{12,8},{16,20},{20,16},{24,28},{28,24},{1,5},{5... | collective-permute-start | bytes 245768 | tf_op jit(solution)/shard_map/ppermute | solution.py:511

commit v12 on v11

--- a/solution.py
+++ b/solution.py
@@ -13,7 +13,7 @@
 HALO = TAPS + GAUGE_MAX
 BLOCK = 128
 STEP = 16
-CHUNK = 256
+CHUNK = 512
 EXTRA = 16
 F32 = jnp.float32
 BF16 = jnp.bfloat16

time: 79.4 us -> 78.2 us (0.985)
  Pallas kernels: 33.3 us -> 32 us
    pallas_call x2, Pallas kernels: 10.2 us -> 8.91 us  [front_call(): pl.pallas_call(functools.partial(front_kernel, *blocks), grid=(steps,), i...]
  transfers between devices with their start and end apart: 21 -> 21, of which waited for: 10 -> 10; matrix products, arithmetic and copies ran while one was open for 0% -> 0% of each run, Pallas kernels for 39% -> 38%
where the time goes in v12:
time: 78.2 us; the launch traced here: 77.8 us
  Pallas kernels  32 us (41%)
  starting transfers between devices  27.2 us (35%)
  waiting for transfers between devices  14.8 us (19%)
  local copies, waits for them, and re-layouts  3.43 us (4%)
    ppermute x20, starting transfers between devices, swap(): lax.ppermute(value, axis, [(source, source ^ mask) for source in range(co...  24.7 us
    ppermute x20, waiting for transfers between devices, swap(): lax.ppermute(value, axis, [(source, source ^ mask) for source in range(co...  14.8 us
    pallas_call x2, Pallas kernels, front_call(): pl.pallas_call(functools.partial(front_kernel, *blocks), grid=(steps,), i...  8.91 us
    pallas_call x1, Pallas kernels, level_filter_call(): pl.pallas_call(functools.partial(filter_kernel, len(grams), first, 'level...  6.58 us
    pallas_call x1, Pallas kernels, filter_call(): pl.pallas_call(functools.partial(filter_kernel, len(grams), first, 'sketc...  6.53 us
    pallas_call x1, Pallas kernels, last_filter_call(): pl.pallas_call(functools.partial(filter_kernel, len(grams), first, 'last'...  6.08 us
    ppermute x1, starting transfers between devices, on_device(): lax.ppermute(record[rows - HALO:], 'tm', [(source, source + 1) for source...  2.51 us
    unnamed x8, local copies, waits for them, and re-layouts  2.31 us
  transfers between devices with their start and end apart: 21, of which 10 were waited for; matrix products, arithmetic and copies ran while one was open for 0% of the time, Pallas kernels for 38%

profile of v12, /device:TPU:0, one launch (start us, length us, event | category | flops | bytes accessed | tf_op | source)
XLA Modules:
  0.0 77.8 jit_solution(5495738739804618432)
XLA Ops:
  0.0 1.0 %slice.3 = bf16[80,2560]{1,0:T(8,128)(2,1)S(1)} slice(bf16[1024,2560]{1,0:T(8,128)(2,1)} %refs_0_.1), slice={[944:1024], [0:2560]} | slice | bytes 819200 | tf_op jit(solution)/shard_map/slice | solution.py:547
  1.0 2.5 %collective-permute-start = (bf16[80,2560]{1,0:T(8,128)(2,1)S(1)}, bf16[80,2560]{1,0:T(8,128)(2,1)S(1)}, u32[]{:S(2)}, u32[]{:S(2)}) collective-permute-start(bf16[80,2560]{1,0:T(8,128)(2,1)S(1)} %slice.3), channel_id=1, source_target_pairs={{0,4},{4,8},{8,12},{12,16},{16,20},{20,24},{24,28},{1,5},{5,9},{9,... | collective-permute-start | bytes 1228808 | tf_op jit(solution)/shard_map/ppermute | solution.py:546
  3.6 0.9 %copy-done.1 = bf16[1024,128]{1,0:T(8,128)(2,1)S(1)} copy-done((bf16[1024,128]{1,0:T(8,128)(2,1)S(1)}, bf16[1024,128]{1,0:T(8,128)(2,1)}, u32[]{:S(2)}) %copy-start.1) | copy-done | bytes 262168
  4.5 0.7 copy-done.2
  5.9 7.5 %front.2 = (f32[128,2560]{1,0:T(8,128)S(1)}, bf16[256,208]{1,0:T(8,128)(2,1)S(1)}, bf16[128,128]{1,0:T(8,128)(2,1)S(1)}, bf16[128,2560]{1,0:T(8,128)(2,1)S(1)}) custom-call(bf16[1024,2560]{1,0:T(8,128)(2,1)} %refs_0_.1, s32[20,128]{1,0:T(8,128)S(1)} %bitcast.9, bf16[1,64]{1,0:T(2,128)(2,1)S(1)} %bitcast.11, bf16[1024,128]{1,0:T(8,128)(2,1)S(1)} %copy-done.1), custom_call_target="tpu_custom_call" | custom-call | tf_op jit(solution)/shard_map/front/pallas_call | solution.py:140
  13.4 1.4 %front.3.own.refs_6_ = bf16[128,2560]{1,0:T(8,128)(2,1)S(1)} custom-call(bf16[128,2560]{1,0:T(8,128)(2,1)S(1)} %get-tuple-element.19.refs_0_, bf16[80,2560]{1,0:T(8,128)(2,1)S(1)} %collective-permute-done.refs_1_, s32[20,128]{1,0:T(8,128)S(1)} %bitcast.10, bf16[256,208]{1,0:T(8,128)(2,1)S(1)} %get-tuple-element.20.refs_3_, ...), custom_call_target="tpu_custom_call" | custom-call | tf_op jit(solution)/shard_map/front/pallas_call | solution.py:140
  14.8 2.6 %collective-permute-start.1 = (bf16[128,2560]{1,0:T(8,128)(2,1)S(1)}, bf16[128,2560]{1,0:T(8,128)(2,1)S(1)}, u32[]{:S(2)}, u32[]{:S(2)}) collective-permute-start(bf16[128,2560]{1,0:T(8,128)(2,1)S(1)} %front.3.own.refs_6_), channel_id=1, source_target_pairs={{0,4},{4,0},{8,12},{12,8},{16,20},{20,16},{24,28},{28,24},{1,5},{5... | collective-permute-start | bytes 1966088 | tf_op jit(solution)/shard_map/ppermute | solution.py:511
  17.5 1.5 %collective-permute-start.5 = (bf16[128,2560]{1,0:T(8,128)(2,1)S(1)}, bf16[128,2560]{1,0:T(8,128)(2,1)S(1)}, u32[]{:S(2)}, u32[]{:S(2)}) collective-permute-start(bf16[128,2560]{1,0:T(8,128)(2,1)S(1)} %front.3.own.refs_6_), channel_id=1, source_target_pairs={{0,8},{4,12},{8,0},{12,4},{16,24},{20,28},{24,16},{28,20},{1,9},{5... | collective-permute-start | bytes 1966088 | tf_op jit(solution)/shard_map/ppermute | solution.py:511
  19.2 0.8 %pair_gram.1.refs_0_ = bf16[272,128]{1,0:T(8,128)(2,1)S(1)} custom-call(bf16[128,2560]{1,0:T(8,128)(2,1)S(1)} %front.3.own.refs_6_, bf16[128,2560]{1,0:T(8,128)(2,1)S(1)} %collective-permute-done.1.other.refs_7_.sibling), custom_call_target="tpu_custom_call" | custom-call | tf_op jit(solution)/shard_map/pair_gram/pallas_call | solution.py:229
  20.0 1.6 %collective-permute-start.2 = (bf16[272,128]{1,0:T(8,128)(2,1)S(1)}, bf16[272,128]{1,0:T(8,128)(2,1)S(1)}, u32[]{:S(2)}, u32[]{:S(2)}) collective-permute-start(bf16[272,128]{1,0:T(8,128)(2,1)S(1)} %pair_gram.1.refs_0_), channel_id=1, source_target_pairs={{0,1},{1,0},{2,3},{3,2},{4,5},{5,4},{6,7},{7,6},{8,9},{9,8},{10,11... | collective-permute-start | bytes 208904 | tf_op jit(solution)/shard_map/ppermute | solution.py:511
  21.7 2.6 %collective-permute-start.3 = (bf16[272,128]{1,0:T(8,128)(2,1)S(1)}, bf16[272,128]{1,0:T(8,128)(2,1)S(1)}, u32[]{:S(2)}, u32[]{:S(2)}) collective-permute-start(bf16[272,128]{1,0:T(8,128)(2,1)S(1)} %pair_gram.1.refs_0_), channel_id=1, source_target_pairs={{0,2},{1,3},{2,0},{3,1},{4,6},{5,7},{6,4},{7,5},{8,10},{9,11},{10,... | collective-permute-start | bytes 208904 | tf_op jit(solution)/shard_map/ppermute | solution.py:511
  24.6 5.0 %collective-permute-done.3.refs_2_ = bf16[272,128]{1,0:T(8,128)(2,1)S(1)} collective-permute-done((bf16[272,128]{1,0:T(8,128)(2,1)S(1)}, bf16[272,128]{1,0:T(8,128)(2,1)S(1)}, u32[]{:S(2)}, u32[]{:S(2)}) %collective-permute-start.3) | collective-permute-done | bytes 69664 | tf_op jit(solution)/shard_map/ppermute | solution.py:511
  29.6 0.8 %collective-permute-done.4.refs_3_ = bf16[272,128]{1,0:T(8,128)(2,1)S(1)} collective-permute-done((bf16[272,128]{1,0:T(8,128)(2,1)S(1)}, bf16[272,128]{1,0:T(8,128)(2,1)S(1)}, u32[]{:S(2)}, u32[]{:S(2)}) %collective-permute-start.4) | collective-permute-done | bytes 69664 | tf_op jit(solution)/shard_map/ppermute | solution.py:511
  30.4 6.5 %sign_filter.3 = (f32[128,256]{1,0:T(8,128)S(1)}, bf16[128,1280]{1,0:T(8,128)(2,1)S(1)}, f32[256,256]{1,0:T(8,128)S(1)}) custom-call(bf16[272,128]{1,0:T(8,128)(2,1)S(1)} %pair_gram.1.refs_0_, bf16[272,128]{1,0:T(8,128)(2,1)S(1)} %collective-permute-done.2.refs_1_, bf16[272,128]{1,0:T(8,128)(2,1)S(1)} %collective-permute-done.3.refs_2_, ...), custom_call_target="tpu_custom_call" | custom-call | tf_op jit(solution)/shard_map/sign_filter/pallas_call | solution.py:451
  37.0 1.5 %collective-permute-start.11 = (bf16[128,1280]{1,0:T(8,128)(2,1)S(1)}, bf16[128,1280]{1,0:T(8,128)(2,1)S(1)}, u32[]{:S(2)}, u32[]{:S(2)}) collective-permute-start(bf16[128,1280]{1,0:T(8,128)(2,1)S(1)} %get-tuple-element.29.own), channel_id=1, source_target_pairs={{0,8},{4,12},{8,0},{12,4},{16,24},{20,28},{24,16},{28,20},{1,9},{5... | collective-permute-start | bytes 983048 | tf_op jit(solution)/shard_map/ppermute | solution.py:511
  39.4 1.2 %collective-permute-start.6 = (bf16[256,128]{1,0:T(8,128)(2,1)S(1)}, bf16[256,128]{1,0:T(8,128)(2,1)S(1)}, u32[]{:S(2)}, u32[]{:S(2)}) collective-permute-start(bf16[256,128]{1,0:T(8,128)(2,1)S(1)} %ahead_gram.2), channel_id=1, source_target_pairs={{0,1},{1,0},{2,3},{3,2},{4,5},{5,4},{6,7},{7,6},{8,9},{9,8},{10,11... | collective-permute-start | bytes 196616 | tf_op jit(solution)/shard_map/ppermute | solution.py:511
  40.6 1.6 %collective-permute-start.7 = (bf16[256,128]{1,0:T(8,128)(2,1)S(1)}, bf16[256,128]{1,0:T(8,128)(2,1)S(1)}, u32[]{:S(2)}, u32[]{:S(2)}) collective-permute-start(bf16[256,128]{1,0:T(8,128)(2,1)S(1)} %ahead_gram.2), channel_id=1, source_target_pairs={{0,2},{1,3},{2,0},{3,1},{4,6},{5,7},{6,4},{7,5},{8,10},{9,11},{10,... | collective-permute-start | bytes 196616 | tf_op jit(solution)/shard_map/ppermute | solution.py:511
  42.3 1.6 %collective-permute-start.8 = (bf16[256,128]{1,0:T(8,128)(2,1)S(1)}, bf16[256,128]{1,0:T(8,128)(2,1)S(1)}, u32[]{:S(2)}, u32[]{:S(2)}) collective-permute-start(bf16[256,128]{1,0:T(8,128)(2,1)S(1)} %ahead_gram.2), channel_id=1, source_target_pairs={{0,3},{1,2},{2,1},{3,0},{4,7},{5,6},{6,5},{7,4},{8,11},{9,10},{10,... | collective-permute-start | bytes 196616 | tf_op jit(solution)/shard_map/ppermute | solution.py:511
  44.3 0.9 %collective-permute-done.11.sibling.other = bf16[128,1280]{1,0:T(8,128)(2,1)S(1)} collective-permute-done((bf16[128,1280]{1,0:T(8,128)(2,1)S(1)}, bf16[128,1280]{1,0:T(8,128)(2,1)S(1)}, u32[]{:S(2)}, u32[]{:S(2)}) %collective-permute-start.11) | collective-permute-done | bytes 327712 | tf_op jit(solution)/shard_map/ppermute | solution.py:511
  45.2 1.5 %collective-permute-start.10 = (bf16[128,512]{1,0:T(8,128)(2,1)S(1)}, bf16[128,512]{1,0:T(8,128)(2,1)S(1)}, u32[]{:S(2)}, u32[]{:S(2)}) collective-permute-start(bf16[128,512]{1,0:T(8,128)(2,1)S(1)} %get-tuple-element.26.refs_0_), channel_id=1, source_target_pairs={{0,8},{4,12},{8,0},{12,4},{16,24},{20,28},{24,16},{28,20},{1,9},{5... | collective-permute-start | bytes 393224 | tf_op jit(solution)/shard_map/ppermute | solution.py:511
  47.3 1.1 %collective-permute-done.8 = bf16[256,128]{1,0:T(8,128)(2,1)S(1)} collective-permute-done((bf16[256,128]{1,0:T(8,128)(2,1)S(1)}, bf16[256,128]{1,0:T(8,128)(2,1)S(1)}, u32[]{:S(2)}, u32[]{:S(2)}) %collective-permute-start.8) | collective-permute-done | bytes 65568 | tf_op jit(solution)/shard_map/ppermute | solution.py:511
  48.6 1.6 %collective-permute-done.10.refs_4_._ = bf16[128,512]{1,0:T(8,128)(2,1)S(1)} collective-permute-done((bf16[128,512]{1,0:T(8,128)(2,1)S(1)}, bf16[128,512]{1,0:T(8,128)(2,1)S(1)}, u32[]{:S(2)}, u32[]{:S(2)}) %collective-permute-start.10) | collective-permute-done | bytes 131104 | tf_op jit(solution)/shard_map/ppermute | solution.py:511
  50.2 2.5 %collective-permute-start.14 = (bf16[256,128]{1,0:T(8,128)(2,1)S(1)}, bf16[256,128]{1,0:T(8,128)(2,1)S(1)}, u32[]{:S(2)}, u32[]{:S(2)}) collective-permute-start(bf16[256,128]{1,0:T(8,128)(2,1)S(1)} %add_after.1), channel_id=1, source_target_pairs={{0,1},{1,0},{2,3},{3,2},{4,5},{5,4},{6,7},{7,6},{8,9},{9,8},{10,11... | collective-permute-start | bytes 196616 | tf_op jit(solution)/shard_map/ppermute | solution.py:511
  53.4 1.8 %collective-permute-start.16 = (bf16[256,128]{1,0:T(8,128)(2,1)S(1)}, bf16[256,128]{1,0:T(8,128)(2,1)S(1)}, u32[]{:S(2)}, u32[]{:S(2)}) collective-permute-start(bf16[256,128]{1,0:T(8,128)(2,1)S(1)} %add_after.1), channel_id=1, source_target_pairs={{0,3},{1,2},{2,1},{3,0},{4,7},{5,6},{6,5},{7,4},{8,11},{9,10},{10,... | collective-permute-start | bytes 196616 | tf_op jit(solution)/shard_map/ppermute | solution.py:511
  55.1 6.6 %sign_filter.4 = (f32[128,256]{1,0:T(8,128)S(1)}, bf16[128,512]{1,0:T(8,128)(2,1)S(1)}, f32[128,128]{1,0:T(8,128)S(1)}) custom-call(f32[128,256]{1,0:T(8,128)S(1)} %get-tuple-element.23.mixing.refs_0_, f32[128,128]{1,0:T(8,128)S(1)} %get-tuple-element.25.refs_1_, bf16[256,128]{1,0:T(8,128)(2,1)S(1)} %add_convert_fusion.1.refs_2_, ...), custom_call_target="tpu_custom_call" | custom-call | tf_op jit(solution)/shard_map/sign_filter/pallas_call | solution.py:438
  61.7 1.6 %collective-permute-start.18 = (bf16[128,512]{1,0:T(8,128)(2,1)S(1)}, bf16[128,512]{1,0:T(8,128)(2,1)S(1)}, u32[]{:S(2)}, u32[]{:S(2)}) collective-permute-start(bf16[128,512]{1,0:T(8,128)(2,1)S(1)} %get-tuple-element.30), channel_id=1, source_target_pairs={{0,16},{4,20},{8,24},{12,28},{16,0},{20,4},{24,8},{28,12},{1,17},{... | collective-permute-start | bytes 393224 | tf_op jit(solution)/shard_map/ppermute | solution.py:511
  64.1 2.7 %collective-permute-done.18.refs_4_.refs_2_ = bf16[128,512]{1,0:T(8,128)(2,1)S(1)} collective-permute-done((bf16[128,512]{1,0:T(8,128)(2,1)S(1)}, bf16[128,512]{1,0:T(8,128)(2,1)S(1)}, u32[]{:S(2)}, u32[]{:S(2)}) %collective-permute-start.18) | collective-permute-done | bytes 131104 | tf_op jit(solution)/shard_map/ppermute | solution.py:511
  66.8 0.9 %collective-permute-done.17.refs_3_.refs_1_ = bf16[256,128]{1,0:T(8,128)(2,1)S(1)} collective-permute-done((bf16[256,128]{1,0:T(8,128)(2,1)S(1)}, bf16[256,128]{1,0:T(8,128)(2,1)S(1)}, u32[]{:S(2)}, u32[]{:S(2)}) %collective-permute-start.17) | collective-permute-done | bytes 65568 | tf_op jit(solution)/shard_map/ppermute | solution.py:511
  67.7 1.2 %collective-permute-start.19 = (bf16[128,1280]{1,0:T(8,128)(2,1)S(1)}, bf16[128,1280]{1,0:T(8,128)(2,1)S(1)}, u32[]{:S(2)}, u32[]{:S(2)}) collective-permute-start(bf16[128,1280]{1,0:T(8,128)(2,1)S(1)} %hold.1.own), channel_id=1, source_target_pairs={{0,16},{4,20},{8,24},{12,28},{16,0},{20,4},{24,8},{28,12},{1,17},{... | collective-permute-start | bytes 983048 | tf_op jit(solution)/shard_map/ppermute | solution.py:511
  68.9 6.1 %sign_filter.5.mixing = f32[32,256]{1,0:T(8,128)S(1)} custom-call(f32[128,256]{1,0:T(8,128)S(1)} %get-tuple-element.27.refs_0_.mixing, f32[128,128]{1,0:T(8,128)S(1)} %get-tuple-element.28.refs_1_, bf16[256,128]{1,0:T(8,128)(2,1)S(1)} %add_convert_fusion.refs_2_, bf16[256,128]{1,0:T(8,128)(2,1)S(1)} %collective-permute-done.17.refs_3_.refs_1_, ...), custom_call_target="tpu_custom_call" | custom-call | flops 6710886400 | tf_op jit(solution)/shard_map/sign_filter/pallas_call | solution.py:472
  75.3 1.3 %collective-permute-done.20.refs_1_ = f32[16,1280]{1,0:T(8,128)S(1)} collective-permute-done((f32[16,1280]{1,0:T(8,128)S(1)}, f32[16,1280]{1,0:T(8,128)S(1)}, u32[]{:S(2)}, u32[]{:S(2)}) %collective-permute-start.20) | collective-permute-done | bytes 81952 | tf_op jit(solution)/shard_map/ppermute | solution.py:511
  76.6 1.2 %join.1 = f32[16,2560]{1,0:T(8,128)} custom-call(s32[10]{0:T(128)S(1)} %stack.32.refs_5_.refs_6_.places, f32[16,1280]{1,0:T(8,128)S(1)} %get-tuple-element.31.refs_0_, f32[16,1280]{1,0:T(8,128)S(1)} %collective-permute-done.20.refs_1_), custom_call_target="tpu_custom_call" | custom-call | tf_op jit(solution)/shard_map/join/pallas_call | solution.py:530
  (36 shorter events, 5.0 us)
Async XLA Ops:
  1.0 29.4 %copy-start = (f32[256,128]{1,0:T(8,128)S(1)}, f32[256,128]{1,0:T(8,128)}, u32[]{:S(2)}) copy-start(f32[256,128]{1,0:T(8,128)} %refs_5_.3) | copy-start | bytes 393220
  1.0 12.4 %collective-permute-start = (bf16[80,2560]{1,0:T(8,128)(2,1)S(1)}, bf16[80,2560]{1,0:T(8,128)(2,1)S(1)}, u32[]{:S(2)}, u32[]{:S(2)}) collective-permute-start(bf16[80,2560]{1,0:T(8,128)(2,1)S(1)} %slice.3), channel_id=1, source_target_pairs={{0,4},{4,8},{8,12},{12,16},{16,20},{20,24},{24,28},{1,5},{5,9},{9,... | collective-permute-start | bytes 1228808 | tf_op jit(solution)/shard_map/ppermute | solution.py:546
  3.6 1.0 %copy-start.1 = (bf16[1024,128]{1,0:T(8,128)(2,1)S(1)}, bf16[1024,128]{1,0:T(8,128)(2,1)}, u32[]{:S(2)}) copy-start(bf16[1024,128]{1,0:T(8,128)(2,1)} %refs_3_.1) | copy-start | bytes 786436
  4.5 0.7 copy-start.2
  5.2 0.7 copy-start.3
  14.8 4.4 %collective-permute-start.1 = (bf16[128,2560]{1,0:T(8,128)(2,1)S(1)}, bf16[128,2560]{1,0:T(8,128)(2,1)S(1)}, u32[]{:S(2)}, u32[]{:S(2)}) collective-permute-start(bf16[128,2560]{1,0:T(8,128)(2,1)S(1)} %front.3.own.refs_6_), channel_id=1, source_target_pairs={{0,4},{4,0},{8,12},{12,8},{16,20},{20,16},{24,28},{28,24},{1,5},{5... | collective-permute-start | bytes 1966088 | tf_op jit(solution)/shard_map/ppermute | solution.py:511
  17.5 21.4 %collective-permute-start.5 = (bf16[128,2560]{1,0:T(8,128)(2,1)S(1)}, bf16[128,2560]{1,0:T(8,128)(2,1)S(1)}, u32[]{:S(2)}, u32[]{:S(2)}) collective-permute-start(bf16[128,2560]{1,0:T(8,128)(2,1)S(1)} %front.3.own.refs_6_), channel_id=1, source_target_pairs={{0,8},{4,12},{8,0},{12,4},{16,24},{20,28},{24,16},{28,20},{1,9},{5... | collective-permute-start | bytes 1966088 | tf_op jit(solution)/shard_map/ppermute | solution.py:511
  20.0 4.6 %collective-permute-start.2 = (bf16[272,128]{1,0:T(8,128)(2,1)S(1)}, bf16[272,128]{1,0:T(8,128)(2,1)S(1)}, u32[]{:S(2)}, u32[]{:S(2)}) collective-permute-start(bf16[272,128]{1,0:T(8,128)(2,1)S(1)} %pair_gram.1.refs_0_), channel_id=1, source_target_pairs={{0,1},{1,0},{2,3},{3,2},{4,5},{5,4},{6,7},{7,6},{8,9},{9,8},{10,11... | collective-permute-start | bytes 208904 | tf_op jit(solution)/shard_map/ppermute | solution.py:511
  21.7 7.9 %collective-permute-start.3 = (bf16[272,128]{1,0:T(8,128)(2,1)S(1)}, bf16[272,128]{1,0:T(8,128)(2,1)S(1)}, u32[]{:S(2)}, u32[]{:S(2)}) collective-permute-start(bf16[272,128]{1,0:T(8,128)(2,1)S(1)} %pair_gram.1.refs_0_), channel_id=1, source_target_pairs={{0,2},{1,3},{2,0},{3,1},{4,6},{5,7},{6,4},{7,5},{8,10},{9,11},{10,... | collective-permute-start | bytes 208904 | tf_op jit(solution)/shard_map/ppermute | solution.py:511
  24.3 6.2 %collective-permute-start.4 = (bf16[272,128]{1,0:T(8,128)(2,1)S(1)}, bf16[272,128]{1,0:T(8,128)(2,1)S(1)}, u32[]{:S(2)}, u32[]{:S(2)}) collective-permute-start(bf16[272,128]{1,0:T(8,128)(2,1)S(1)} %pair_gram.1.refs_0_), channel_id=1, source_target_pairs={{0,3},{1,2},{2,1},{3,0},{4,7},{5,6},{6,5},{7,4},{8,11},{9,10},{10,... | collective-permute-start | bytes 208904 | tf_op jit(solution)/shard_map/ppermute | solution.py:511
  37.0 8.3 %collective-permute-start.11 = (bf16[128,1280]{1,0:T(8,128)(2,1)S(1)}, bf16[128,1280]{1,0:T(8,128)(2,1)S(1)}, u32[]{:S(2)}, u32[]{:S(2)}) collective-permute-start(bf16[128,1280]{1,0:T(8,128)(2,1)S(1)} %get-tuple-element.29.own), channel_id=1, source_target_pairs={{0,8},{4,12},{8,0},{12,4},{16,24},{20,28},{24,16},{28,20},{1,9},{5... | collective-permute-start | bytes 983048 | tf_op jit(solution)/shard_map/ppermute | solution.py:511
  38.5 8.2 %collective-permute-start.12 = (bf16[128,1280]{1,0:T(8,128)(2,1)S(1)}, bf16[128,1280]{1,0:T(8,128)(2,1)S(1)}, u32[]{:S(2)}, u32[]{:S(2)}) collective-permute-start(bf16[128,1280]{1,0:T(8,128)(2,1)S(1)} %get-tuple-element.29.own), channel_id=1, source_target_pairs={{0,16},{4,20},{8,24},{12,28},{16,0},{20,4},{24,8},{28,12},{1,17},{... | collective-permute-start | bytes 983048 | tf_op jit(solution)/shard_map/ppermute | solution.py:511
  39.4 7.8 %collective-permute-start.6 = (bf16[256,128]{1,0:T(8,128)(2,1)S(1)}, bf16[256,128]{1,0:T(8,128)(2,1)S(1)}, u32[]{:S(2)}, u32[]{:S(2)}) collective-permute-start(bf16[256,128]{1,0:T(8,128)(2,1)S(1)} %ahead_gram.2), channel_id=1, source_target_pairs={{0,1},{1,0},{2,3},{3,2},{4,5},{5,4},{6,7},{7,6},{8,9},{9,8},{10,11... | collective-permute-start | bytes 196616 | tf_op jit(solution)/shard_map/ppermute | solution.py:511
  40.6 6.7 %collective-permute-start.7 = (bf16[256,128]{1,0:T(8,128)(2,1)S(1)}, bf16[256,128]{1,0:T(8,128)(2,1)S(1)}, u32[]{:S(2)}, u32[]{:S(2)}) collective-permute-start(bf16[256,128]{1,0:T(8,128)(2,1)S(1)} %ahead_gram.2), channel_id=1, source_target_pairs={{0,2},{1,3},{2,0},{3,1},{4,6},{5,7},{6,4},{7,5},{8,10},{9,11},{10,... | collective-permute-start | bytes 196616 | tf_op jit(solution)/shard_map/ppermute | solution.py:511
  42.3 6.2 %collective-permute-start.8 = (bf16[256,128]{1,0:T(8,128)(2,1)S(1)}, bf16[256,128]{1,0:T(8,128)(2,1)S(1)}, u32[]{:S(2)}, u32[]{:S(2)}) collective-permute-start(bf16[256,128]{1,0:T(8,128)(2,1)S(1)} %ahead_gram.2), channel_id=1, source_target_pairs={{0,3},{1,2},{2,1},{3,0},{4,7},{5,6},{6,5},{7,4},{8,11},{9,10},{10,... | collective-permute-start | bytes 196616 | tf_op jit(solution)/shard_map/ppermute | solution.py:511
  45.2 5.0 %collective-permute-start.10 = (bf16[128,512]{1,0:T(8,128)(2,1)S(1)}, bf16[128,512]{1,0:T(8,128)(2,1)S(1)}, u32[]{:S(2)}, u32[]{:S(2)}) collective-permute-start(bf16[128,512]{1,0:T(8,128)(2,1)S(1)} %get-tuple-element.26.refs_0_), channel_id=1, source_target_pairs={{0,8},{4,12},{8,0},{12,4},{16,24},{20,28},{24,16},{28,20},{1,9},{5... | collective-permute-start | bytes 393224 | tf_op jit(solution)/shard_map/ppermute | solution.py:511
  47.1 3.1 %collective-permute-start.13 = (bf16[256,128]{1,0:T(8,128)(2,1)S(1)}, bf16[256,128]{1,0:T(8,128)(2,1)S(1)}, u32[]{:S(2)}, u32[]{:S(2)}) collective-permute-start(bf16[256,128]{1,0:T(8,128)(2,1)S(1)} %ahead_gram.3.one), channel_id=1, source_target_pairs={{0,4},{4,0},{8,12},{12,8},{16,20},{20,16},{24,28},{28,24},{1,5},{5... | collective-permute-start | bytes 196616 | tf_op jit(solution)/shard_map/ppermute | solution.py:511
  48.5 6.7 %collective-permute-start.9 = (bf16[256,128]{1,0:T(8,128)(2,1)S(1)}, bf16[256,128]{1,0:T(8,128)(2,1)S(1)}, u32[]{:S(2)}, u32[]{:S(2)}) collective-permute-start(bf16[256,128]{1,0:T(8,128)(2,1)S(1)} %add_convert_fusion.1.refs_2_), channel_id=1, source_target_pairs={{0,4},{4,0},{8,12},{12,8},{16,20},{20,16},{24,28},{28,24},{1,5},{5... | collective-permute-start | bytes 196616 | tf_op jit(solution)/shard_map/ppermute | solution.py:511
  50.2 13.1 %collective-permute-start.14 = (bf16[256,128]{1,0:T(8,128)(2,1)S(1)}, bf16[256,128]{1,0:T(8,128)(2,1)S(1)}, u32[]{:S(2)}, u32[]{:S(2)}) collective-permute-start(bf16[256,128]{1,0:T(8,128)(2,1)S(1)} %add_after.1), channel_id=1, source_target_pairs={{0,1},{1,0},{2,3},{3,2},{4,5},{5,4},{6,7},{7,6},{8,9},{9,8},{10,11... | collective-permute-start | bytes 196616 | tf_op jit(solution)/shard_map/ppermute | solution.py:511
  52.7 10.6 %collective-permute-start.15 = (bf16[256,128]{1,0:T(8,128)(2,1)S(1)}, bf16[256,128]{1,0:T(8,128)(2,1)S(1)}, u32[]{:S(2)}, u32[]{:S(2)}) collective-permute-start(bf16[256,128]{1,0:T(8,128)(2,1)S(1)} %add_after.1), channel_id=1, source_target_pairs={{0,2},{1,3},{2,0},{3,1},{4,6},{5,7},{6,4},{7,5},{8,10},{9,11},{10,... | collective-permute-start | bytes 196616 | tf_op jit(solution)/shard_map/ppermute | solution.py:511
  53.4 9.9 %collective-permute-start.16 = (bf16[256,128]{1,0:T(8,128)(2,1)S(1)}, bf16[256,128]{1,0:T(8,128)(2,1)S(1)}, u32[]{:S(2)}, u32[]{:S(2)}) collective-permute-start(bf16[256,128]{1,0:T(8,128)(2,1)S(1)} %add_after.1), channel_id=1, source_target_pairs={{0,3},{1,2},{2,1},{3,0},{4,7},{5,6},{6,5},{7,4},{8,11},{9,10},{10,... | collective-permute-start | bytes 196616 | tf_op jit(solution)/shard_map/ppermute | solution.py:511
  61.7 5.0 %collective-permute-start.18 = (bf16[128,512]{1,0:T(8,128)(2,1)S(1)}, bf16[128,512]{1,0:T(8,128)(2,1)S(1)}, u32[]{:S(2)}, u32[]{:S(2)}) collective-permute-start(bf16[128,512]{1,0:T(8,128)(2,1)S(1)} %get-tuple-element.30), channel_id=1, source_target_pairs={{0,16},{4,20},{8,24},{12,28},{16,0},{20,4},{24,8},{28,12},{1,17},{... | collective-permute-start | bytes 393224 | tf_op jit(solution)/shard_map/ppermute | solution.py:511
  63.4 4.3 %collective-permute-start.17 = (bf16[256,128]{1,0:T(8,128)(2,1)S(1)}, bf16[256,128]{1,0:T(8,128)(2,1)S(1)}, u32[]{:S(2)}, u32[]{:S(2)}) collective-permute-start(bf16[256,128]{1,0:T(8,128)(2,1)S(1)} %add_convert_fusion.refs_2_), channel_id=1, source_target_pairs={{0,8},{4,12},{8,0},{12,4},{16,24},{20,28},{24,16},{28,20},{1,9},{5... | collective-permute-start | bytes 196616 | tf_op jit(solution)/shard_map/ppermute | solution.py:511
  67.7 7.3 %collective-permute-start.19 = (bf16[128,1280]{1,0:T(8,128)(2,1)S(1)}, bf16[128,1280]{1,0:T(8,128)(2,1)S(1)}, u32[]{:S(2)}, u32[]{:S(2)}) collective-permute-start(bf16[128,1280]{1,0:T(8,128)(2,1)S(1)} %hold.1.own), channel_id=1, source_target_pairs={{0,16},{4,20},{8,24},{12,28},{16,0},{20,4},{24,8},{28,12},{1,17},{... | collective-permute-start | bytes 983048 | tf_op jit(solution)/shard_map/ppermute | solution.py:511
  75.2 1.3 %collective-permute-start.20 = (f32[16,1280]{1,0:T(8,128)S(1)}, f32[16,1280]{1,0:T(8,128)S(1)}, u32[]{:S(2)}, u32[]{:S(2)}) collective-permute-start(f32[16,1280]{1,0:T(8,128)S(1)} %get-tuple-element.32), channel_id=1, source_target_pairs={{0,4},{4,0},{8,12},{12,8},{16,20},{20,16},{24,28},{28,24},{1,5},{5... | collective-permute-start | bytes 245768 | tf_op jit(solution)/shard_map/ppermute | solution.py:511

commit v13 on v12

--- a/solution.py
+++ b/solution.py
@@ -13,7 +13,7 @@
 HALO = TAPS + GAUGE_MAX
 BLOCK = 128
 STEP = 16
-CHUNK = 512
+CHUNK = 1024
 EXTRA = 16
 F32 = jnp.float32
 BF16 = jnp.bfloat16

time: 78.2 us -> 78 us (level)
  transfers between devices with their start and end apart: 21 -> 21, of which waited for: 10 -> 10; matrix products, arithmetic and copies ran while one was open for 0% -> 0% of each run, Pallas kernels for 38% -> 37%
where the time goes in v13:
time: 78 us; the launch traced here: 77.6 us
  Pallas kernels  31.8 us (41%)
  starting transfers between devices  27.3 us (35%)
  waiting for transfers between devices  14.8 us (19%)
  local copies, waits for them, and re-layouts  3.43 us (4%)
    ppermute x20, starting transfers between devices, swap(): lax.ppermute(value, axis, [(source, source ^ mask) for source in range(co...  24.8 us
    ppermute x20, waiting for transfers between devices, swap(): lax.ppermute(value, axis, [(source, source ^ mask) for source in range(co...  14.8 us
    pallas_call x2, Pallas kernels, front_call(): pl.pallas_call(functools.partial(front_kernel, *blocks), grid=(steps,), i...  8.69 us
    pallas_call x1, Pallas kernels, level_filter_call(): pl.pallas_call(functools.partial(filter_kernel, len(grams), first, 'level...  6.58 us
    pallas_call x1, Pallas kernels, filter_call(): pl.pallas_call(functools.partial(filter_kernel, len(grams), first, 'sketc...  6.53 us
    pallas_call x1, Pallas kernels, last_filter_call(): pl.pallas_call(functools.partial(filter_kernel, len(grams), first, 'last'...  6.08 us
    ppermute x1, starting transfers between devices, on_device(): lax.ppermute(record[rows - HALO:], 'tm', [(source, source + 1) for source...  2.51 us
    unnamed x8, local copies, waits for them, and re-layouts  2.31 us
  transfers between devices with their start and end apart: 21, of which 10 were waited for; matrix products, arithmetic and copies ran while one was open for 0% of the time, Pallas kernels for 37%

profile of v13, /device:TPU:0, one launch (start us, length us, event | category | flops | bytes accessed | tf_op | source)
XLA Modules:
  0.0 77.6 jit_solution(15314264296866852589)
XLA Ops:
  0.0 1.0 %slice.3 = bf16[80,2560]{1,0:T(8,128)(2,1)S(1)} slice(bf16[1024,2560]{1,0:T(8,128)(2,1)} %refs_0_.1), slice={[944:1024], [0:2560]} | slice | bytes 819200 | tf_op jit(solution)/shard_map/slice | solution.py:547
  1.0 2.5 %collective-permute-start = (bf16[80,2560]{1,0:T(8,128)(2,1)S(1)}, bf16[80,2560]{1,0:T(8,128)(2,1)S(1)}, u32[]{:S(2)}, u32[]{:S(2)}) collective-permute-start(bf16[80,2560]{1,0:T(8,128)(2,1)S(1)} %slice.3), channel_id=1, source_target_pairs={{0,4},{4,8},{8,12},{12,16},{16,20},{20,24},{24,28},{1,5},{5,9},{9,... | collective-permute-start | bytes 1228808 | tf_op jit(solution)/shard_map/ppermute | solution.py:546
  3.6 0.9 %copy-done.1 = bf16[1024,128]{1,0:T(8,128)(2,1)S(1)} copy-done((bf16[1024,128]{1,0:T(8,128)(2,1)S(1)}, bf16[1024,128]{1,0:T(8,128)(2,1)}, u32[]{:S(2)}) %copy-start.1) | copy-done | bytes 262168
  4.5 0.7 copy-done.2
  5.9 7.3 %front.2 = (f32[128,2560]{1,0:T(8,128)S(1)}, bf16[256,208]{1,0:T(8,128)(2,1)S(1)}, bf16[128,128]{1,0:T(8,128)(2,1)S(1)}, bf16[128,2560]{1,0:T(8,128)(2,1)S(1)}) custom-call(bf16[1024,2560]{1,0:T(8,128)(2,1)} %refs_0_.1, s32[20,128]{1,0:T(8,128)S(1)} %bitcast.9, bf16[1,64]{1,0:T(2,128)(2,1)S(1)} %bitcast.11, bf16[1024,128]{1,0:T(8,128)(2,1)S(1)} %copy-done.1), custom_call_target="tpu_custom_call" | custom-call | tf_op jit(solution)/shard_map/front/pallas_call | solution.py:140
  13.2 1.4 %front.3.own.refs_6_ = bf16[128,2560]{1,0:T(8,128)(2,1)S(1)} custom-call(bf16[128,2560]{1,0:T(8,128)(2,1)S(1)} %get-tuple-element.19.refs_0_, bf16[80,2560]{1,0:T(8,128)(2,1)S(1)} %collective-permute-done.refs_1_, s32[20,128]{1,0:T(8,128)S(1)} %bitcast.10, bf16[256,208]{1,0:T(8,128)(2,1)S(1)} %get-tuple-element.20.refs_3_, ...), custom_call_target="tpu_custom_call" | custom-call | tf_op jit(solution)/shard_map/front/pallas_call | solution.py:140
  14.6 2.7 %collective-permute-start.1 = (bf16[128,2560]{1,0:T(8,128)(2,1)S(1)}, bf16[128,2560]{1,0:T(8,128)(2,1)S(1)}, u32[]{:S(2)}, u32[]{:S(2)}) collective-permute-start(bf16[128,2560]{1,0:T(8,128)(2,1)S(1)} %front.3.own.refs_6_), channel_id=1, source_target_pairs={{0,4},{4,0},{8,12},{12,8},{16,20},{20,16},{24,28},{28,24},{1,5},{5... | collective-permute-start | bytes 1966088 | tf_op jit(solution)/shard_map/ppermute | solution.py:511
  17.3 1.5 %collective-permute-start.5 = (bf16[128,2560]{1,0:T(8,128)(2,1)S(1)}, bf16[128,2560]{1,0:T(8,128)(2,1)S(1)}, u32[]{:S(2)}, u32[]{:S(2)}) collective-permute-start(bf16[128,2560]{1,0:T(8,128)(2,1)S(1)} %front.3.own.refs_6_), channel_id=1, source_target_pairs={{0,8},{4,12},{8,0},{12,4},{16,24},{20,28},{24,16},{28,20},{1,9},{5... | collective-permute-start | bytes 1966088 | tf_op jit(solution)/shard_map/ppermute | solution.py:511
  19.0 0.8 %pair_gram.1.refs_0_ = bf16[272,128]{1,0:T(8,128)(2,1)S(1)} custom-call(bf16[128,2560]{1,0:T(8,128)(2,1)S(1)} %front.3.own.refs_6_, bf16[128,2560]{1,0:T(8,128)(2,1)S(1)} %collective-permute-done.1.other.refs_7_.sibling), custom_call_target="tpu_custom_call" | custom-call | tf_op jit(solution)/shard_map/pair_gram/pallas_call | solution.py:229
  19.8 1.7 %collective-permute-start.2 = (bf16[272,128]{1,0:T(8,128)(2,1)S(1)}, bf16[272,128]{1,0:T(8,128)(2,1)S(1)}, u32[]{:S(2)}, u32[]{:S(2)}) collective-permute-start(bf16[272,128]{1,0:T(8,128)(2,1)S(1)} %pair_gram.1.refs_0_), channel_id=1, source_target_pairs={{0,1},{1,0},{2,3},{3,2},{4,5},{5,4},{6,7},{7,6},{8,9},{9,8},{10,11... | collective-permute-start | bytes 208904 | tf_op jit(solution)/shard_map/ppermute | solution.py:511
  21.5 2.6 %collective-permute-start.3 = (bf16[272,128]{1,0:T(8,128)(2,1)S(1)}, bf16[272,128]{1,0:T(8,128)(2,1)S(1)}, u32[]{:S(2)}, u32[]{:S(2)}) collective-permute-start(bf16[272,128]{1,0:T(8,128)(2,1)S(1)} %pair_gram.1.refs_0_), channel_id=1, source_target_pairs={{0,2},{1,3},{2,0},{3,1},{4,6},{5,7},{6,4},{7,5},{8,10},{9,11},{10,... | collective-permute-start | bytes 208904 | tf_op jit(solution)/shard_map/ppermute | solution.py:511
  24.4 5.0 %collective-permute-done.3.refs_2_ = bf16[272,128]{1,0:T(8,128)(2,1)S(1)} collective-permute-done((bf16[272,128]{1,0:T(8,128)(2,1)S(1)}, bf16[272,128]{1,0:T(8,128)(2,1)S(1)}, u32[]{:S(2)}, u32[]{:S(2)}) %collective-permute-start.3) | collective-permute-done | bytes 69664 | tf_op jit(solution)/shard_map/ppermute | solution.py:511
  29.4 0.8 %collective-permute-done.4.refs_3_ = bf16[272,128]{1,0:T(8,128)(2,1)S(1)} collective-permute-done((bf16[272,128]{1,0:T(8,128)(2,1)S(1)}, bf16[272,128]{1,0:T(8,128)(2,1)S(1)}, u32[]{:S(2)}, u32[]{:S(2)}) %collective-permute-start.4) | collective-permute-done | bytes 69664 | tf_op jit(solution)/shard_map/ppermute | solution.py:511
  30.2 6.5 %sign_filter.3 = (f32[128,256]{1,0:T(8,128)S(1)}, bf16[128,1280]{1,0:T(8,128)(2,1)S(1)}, f32[256,256]{1,0:T(8,128)S(1)}) custom-call(bf16[272,128]{1,0:T(8,128)(2,1)S(1)} %pair_gram.1.refs_0_, bf16[272,128]{1,0:T(8,128)(2,1)S(1)} %collective-permute-done.2.refs_1_, bf16[272,128]{1,0:T(8,128)(2,1)S(1)} %collective-permute-done.3.refs_2_, ...), custom_call_target="tpu_custom_call" | custom-call | tf_op jit(solution)/shard_map/sign_filter/pallas_call | solution.py:451
  36.8 1.6 %collective-permute-start.11 = (bf16[128,1280]{1,0:T(8,128)(2,1)S(1)}, bf16[128,1280]{1,0:T(8,128)(2,1)S(1)}, u32[]{:S(2)}, u32[]{:S(2)}) collective-permute-start(bf16[128,1280]{1,0:T(8,128)(2,1)S(1)} %get-tuple-element.29.own), channel_id=1, source_target_pairs={{0,8},{4,12},{8,0},{12,4},{16,24},{20,28},{24,16},{28,20},{1,9},{5... | collective-permute-start | bytes 983048 | tf_op jit(solution)/shard_map/ppermute | solution.py:511
  39.2 1.2 %collective-permute-start.6 = (bf16[256,128]{1,0:T(8,128)(2,1)S(1)}, bf16[256,128]{1,0:T(8,128)(2,1)S(1)}, u32[]{:S(2)}, u32[]{:S(2)}) collective-permute-start(bf16[256,128]{1,0:T(8,128)(2,1)S(1)} %ahead_gram.2), channel_id=1, source_target_pairs={{0,1},{1,0},{2,3},{3,2},{4,5},{5,4},{6,7},{7,6},{8,9},{9,8},{10,11... | collective-permute-start | bytes 196616 | tf_op jit(solution)/shard_map/ppermute | solution.py:511
  40.4 1.6 %collective-permute-start.7 = (bf16[256,128]{1,0:T(8,128)(2,1)S(1)}, bf16[256,128]{1,0:T(8,128)(2,1)S(1)}, u32[]{:S(2)}, u32[]{:S(2)}) collective-permute-start(bf16[256,128]{1,0:T(8,128)(2,1)S(1)} %ahead_gram.2), channel_id=1, source_target_pairs={{0,2},{1,3},{2,0},{3,1},{4,6},{5,7},{6,4},{7,5},{8,10},{9,11},{10,... | collective-permute-start | bytes 196616 | tf_op jit(solution)/shard_map/ppermute | solution.py:511
  42.1 1.6 %collective-permute-start.8 = (bf16[256,128]{1,0:T(8,128)(2,1)S(1)}, bf16[256,128]{1,0:T(8,128)(2,1)S(1)}, u32[]{:S(2)}, u32[]{:S(2)}) collective-permute-start(bf16[256,128]{1,0:T(8,128)(2,1)S(1)} %ahead_gram.2), channel_id=1, source_target_pairs={{0,3},{1,2},{2,1},{3,0},{4,7},{5,6},{6,5},{7,4},{8,11},{9,10},{10,... | collective-permute-start | bytes 196616 | tf_op jit(solution)/shard_map/ppermute | solution.py:511
  44.1 0.9 %collective-permute-done.11.sibling.other = bf16[128,1280]{1,0:T(8,128)(2,1)S(1)} collective-permute-done((bf16[128,1280]{1,0:T(8,128)(2,1)S(1)}, bf16[128,1280]{1,0:T(8,128)(2,1)S(1)}, u32[]{:S(2)}, u32[]{:S(2)}) %collective-permute-start.11) | collective-permute-done | bytes 327712 | tf_op jit(solution)/shard_map/ppermute | solution.py:511
  45.0 1.5 %collective-permute-start.10 = (bf16[128,512]{1,0:T(8,128)(2,1)S(1)}, bf16[128,512]{1,0:T(8,128)(2,1)S(1)}, u32[]{:S(2)}, u32[]{:S(2)}) collective-permute-start(bf16[128,512]{1,0:T(8,128)(2,1)S(1)} %get-tuple-element.26.refs_0_), channel_id=1, source_target_pairs={{0,8},{4,12},{8,0},{12,4},{16,24},{20,28},{24,16},{28,20},{1,9},{5... | collective-permute-start | bytes 393224 | tf_op jit(solution)/shard_map/ppermute | solution.py:511
  47.1 1.1 %collective-permute-done.8 = bf16[256,128]{1,0:T(8,128)(2,1)S(1)} collective-permute-done((bf16[256,128]{1,0:T(8,128)(2,1)S(1)}, bf16[256,128]{1,0:T(8,128)(2,1)S(1)}, u32[]{:S(2)}, u32[]{:S(2)}) %collective-permute-start.8) | collective-permute-done | bytes 65568 | tf_op jit(solution)/shard_map/ppermute | solution.py:511
  48.4 1.6 %collective-permute-done.10.refs_4_._ = bf16[128,512]{1,0:T(8,128)(2,1)S(1)} collective-permute-done((bf16[128,512]{1,0:T(8,128)(2,1)S(1)}, bf16[128,512]{1,0:T(8,128)(2,1)S(1)}, u32[]{:S(2)}, u32[]{:S(2)}) %collective-permute-start.10) | collective-permute-done | bytes 131104 | tf_op jit(solution)/shard_map/ppermute | solution.py:511
  50.0 2.5 %collective-permute-start.14 = (bf16[256,128]{1,0:T(8,128)(2,1)S(1)}, bf16[256,128]{1,0:T(8,128)(2,1)S(1)}, u32[]{:S(2)}, u32[]{:S(2)}) collective-permute-start(bf16[256,128]{1,0:T(8,128)(2,1)S(1)} %add_after.1), channel_id=1, source_target_pairs={{0,1},{1,0},{2,3},{3,2},{4,5},{5,4},{6,7},{7,6},{8,9},{9,8},{10,11... | collective-permute-start | bytes 196616 | tf_op jit(solution)/shard_map/ppermute | solution.py:511
  53.2 1.8 %collective-permute-start.16 = (bf16[256,128]{1,0:T(8,128)(2,1)S(1)}, bf16[256,128]{1,0:T(8,128)(2,1)S(1)}, u32[]{:S(2)}, u32[]{:S(2)}) collective-permute-start(bf16[256,128]{1,0:T(8,128)(2,1)S(1)} %add_after.1), channel_id=1, source_target_pairs={{0,3},{1,2},{2,1},{3,0},{4,7},{5,6},{6,5},{7,4},{8,11},{9,10},{10,... | collective-permute-start | bytes 196616 | tf_op jit(solution)/shard_map/ppermute | solution.py:511
  54.9 6.6 %sign_filter.4 = (f32[128,256]{1,0:T(8,128)S(1)}, bf16[128,512]{1,0:T(8,128)(2,1)S(1)}, f32[128,128]{1,0:T(8,128)S(1)}) custom-call(f32[128,256]{1,0:T(8,128)S(1)} %get-tuple-element.23.mixing.refs_0_, f32[128,128]{1,0:T(8,128)S(1)} %get-tuple-element.25.refs_1_, bf16[256,128]{1,0:T(8,128)(2,1)S(1)} %add_convert_fusion.1.refs_2_, ...), custom_call_target="tpu_custom_call" | custom-call | tf_op jit(solution)/shard_map/sign_filter/pallas_call | solution.py:438
  61.5 1.6 %collective-permute-start.18 = (bf16[128,512]{1,0:T(8,128)(2,1)S(1)}, bf16[128,512]{1,0:T(8,128)(2,1)S(1)}, u32[]{:S(2)}, u32[]{:S(2)}) collective-permute-start(bf16[128,512]{1,0:T(8,128)(2,1)S(1)} %get-tuple-element.30), channel_id=1, source_target_pairs={{0,16},{4,20},{8,24},{12,28},{16,0},{20,4},{24,8},{28,12},{1,17},{... | collective-permute-start | bytes 393224 | tf_op jit(solution)/shard_map/ppermute | solution.py:511
  63.9 2.6 %collective-permute-done.18.refs_4_.refs_2_ = bf16[128,512]{1,0:T(8,128)(2,1)S(1)} collective-permute-done((bf16[128,512]{1,0:T(8,128)(2,1)S(1)}, bf16[128,512]{1,0:T(8,128)(2,1)S(1)}, u32[]{:S(2)}, u32[]{:S(2)}) %collective-permute-start.18) | collective-permute-done | bytes 131104 | tf_op jit(solution)/shard_map/ppermute | solution.py:511
  66.6 0.9 %collective-permute-done.17.refs_3_.refs_1_ = bf16[256,128]{1,0:T(8,128)(2,1)S(1)} collective-permute-done((bf16[256,128]{1,0:T(8,128)(2,1)S(1)}, bf16[256,128]{1,0:T(8,128)(2,1)S(1)}, u32[]{:S(2)}, u32[]{:S(2)}) %collective-permute-start.17) | collective-permute-done | bytes 65568 | tf_op jit(solution)/shard_map/ppermute | solution.py:511
  67.5 1.2 %collective-permute-start.19 = (bf16[128,1280]{1,0:T(8,128)(2,1)S(1)}, bf16[128,1280]{1,0:T(8,128)(2,1)S(1)}, u32[]{:S(2)}, u32[]{:S(2)}) collective-permute-start(bf16[128,1280]{1,0:T(8,128)(2,1)S(1)} %hold.1.own), channel_id=1, source_target_pairs={{0,16},{4,20},{8,24},{12,28},{16,0},{20,4},{24,8},{28,12},{1,17},{... | collective-permute-start | bytes 983048 | tf_op jit(solution)/shard_map/ppermute | solution.py:511
  68.7 6.1 %sign_filter.5.mixing = f32[32,256]{1,0:T(8,128)S(1)} custom-call(f32[128,256]{1,0:T(8,128)S(1)} %get-tuple-element.27.refs_0_.mixing, f32[128,128]{1,0:T(8,128)S(1)} %get-tuple-element.28.refs_1_, bf16[256,128]{1,0:T(8,128)(2,1)S(1)} %add_convert_fusion.refs_2_, bf16[256,128]{1,0:T(8,128)(2,1)S(1)} %collective-permute-done.17.refs_3_.refs_1_, ...), custom_call_target="tpu_custom_call" | custom-call | flops 6710886400 | tf_op jit(solution)/shard_map/sign_filter/pallas_call | solution.py:472
  75.1 1.3 %collective-permute-done.20.refs_1_ = f32[16,1280]{1,0:T(8,128)S(1)} collective-permute-done((f32[16,1280]{1,0:T(8,128)S(1)}, f32[16,1280]{1,0:T(8,128)S(1)}, u32[]{:S(2)}, u32[]{:S(2)}) %collective-permute-start.20) | collective-permute-done | bytes 81952 | tf_op jit(solution)/shard_map/ppermute | solution.py:511
  76.4 1.2 %join.1 = f32[16,2560]{1,0:T(8,128)} custom-call(s32[10]{0:T(128)S(1)} %stack.32.refs_5_.refs_6_.places, f32[16,1280]{1,0:T(8,128)S(1)} %get-tuple-element.31.refs_0_, f32[16,1280]{1,0:T(8,128)S(1)} %collective-permute-done.20.refs_1_), custom_call_target="tpu_custom_call" | custom-call | tf_op jit(solution)/shard_map/join/pallas_call | solution.py:530
  (36 shorter events, 5.0 us)
Async XLA Ops:
  1.0 29.2 %copy-start = (f32[256,128]{1,0:T(8,128)S(1)}, f32[256,128]{1,0:T(8,128)}, u32[]{:S(2)}) copy-start(f32[256,128]{1,0:T(8,128)} %refs_5_.3) | copy-start | bytes 393220
  1.0 12.2 %collective-permute-start = (bf16[80,2560]{1,0:T(8,128)(2,1)S(1)}, bf16[80,2560]{1,0:T(8,128)(2,1)S(1)}, u32[]{:S(2)}, u32[]{:S(2)}) collective-permute-start(bf16[80,2560]{1,0:T(8,128)(2,1)S(1)} %slice.3), channel_id=1, source_target_pairs={{0,4},{4,8},{8,12},{12,16},{16,20},{20,24},{24,28},{1,5},{5,9},{9,... | collective-permute-start | bytes 1228808 | tf_op jit(solution)/shard_map/ppermute | solution.py:546
  3.6 1.0 %copy-start.1 = (bf16[1024,128]{1,0:T(8,128)(2,1)S(1)}, bf16[1024,128]{1,0:T(8,128)(2,1)}, u32[]{:S(2)}) copy-start(bf16[1024,128]{1,0:T(8,128)(2,1)} %refs_3_.1) | copy-start | bytes 786436
  4.5 0.7 copy-start.2
  5.2 0.7 copy-start.3
  14.6 4.4 %collective-permute-start.1 = (bf16[128,2560]{1,0:T(8,128)(2,1)S(1)}, bf16[128,2560]{1,0:T(8,128)(2,1)S(1)}, u32[]{:S(2)}, u32[]{:S(2)}) collective-permute-start(bf16[128,2560]{1,0:T(8,128)(2,1)S(1)} %front.3.own.refs_6_), channel_id=1, source_target_pairs={{0,4},{4,0},{8,12},{12,8},{16,20},{20,16},{24,28},{28,24},{1,5},{5... | collective-permute-start | bytes 1966088 | tf_op jit(solution)/shard_map/ppermute | solution.py:511
  17.3 21.4 %collective-permute-start.5 = (bf16[128,2560]{1,0:T(8,128)(2,1)S(1)}, bf16[128,2560]{1,0:T(8,128)(2,1)S(1)}, u32[]{:S(2)}, u32[]{:S(2)}) collective-permute-start(bf16[128,2560]{1,0:T(8,128)(2,1)S(1)} %front.3.own.refs_6_), channel_id=1, source_target_pairs={{0,8},{4,12},{8,0},{12,4},{16,24},{20,28},{24,16},{28,20},{1,9},{5... | collective-permute-start | bytes 1966088 | tf_op jit(solution)/shard_map/ppermute | solution.py:511
  19.8 4.6 %collective-permute-start.2 = (bf16[272,128]{1,0:T(8,128)(2,1)S(1)}, bf16[272,128]{1,0:T(8,128)(2,1)S(1)}, u32[]{:S(2)}, u32[]{:S(2)}) collective-permute-start(bf16[272,128]{1,0:T(8,128)(2,1)S(1)} %pair_gram.1.refs_0_), channel_id=1, source_target_pairs={{0,1},{1,0},{2,3},{3,2},{4,5},{5,4},{6,7},{7,6},{8,9},{9,8},{10,11... | collective-permute-start | bytes 208904 | tf_op jit(solution)/shard_map/ppermute | solution.py:511
  21.5 7.9 %collective-permute-start.3 = (bf16[272,128]{1,0:T(8,128)(2,1)S(1)}, bf16[272,128]{1,0:T(8,128)(2,1)S(1)}, u32[]{:S(2)}, u32[]{:S(2)}) collective-permute-start(bf16[272,128]{1,0:T(8,128)(2,1)S(1)} %pair_gram.1.refs_0_), channel_id=1, source_target_pairs={{0,2},{1,3},{2,0},{3,1},{4,6},{5,7},{6,4},{7,5},{8,10},{9,11},{10,... | collective-permute-start | bytes 208904 | tf_op jit(solution)/shard_map/ppermute | solution.py:511
  24.0 6.2 %collective-permute-start.4 = (bf16[272,128]{1,0:T(8,128)(2,1)S(1)}, bf16[272,128]{1,0:T(8,128)(2,1)S(1)}, u32[]{:S(2)}, u32[]{:S(2)}) collective-permute-start(bf16[272,128]{1,0:T(8,128)(2,1)S(1)} %pair_gram.1.refs_0_), channel_id=1, source_target_pairs={{0,3},{1,2},{2,1},{3,0},{4,7},{5,6},{6,5},{7,4},{8,11},{9,10},{10,... | collective-permute-start | bytes 208904 | tf_op jit(solution)/shard_map/ppermute | solution.py:511
  36.8 8.3 %collective-permute-start.11 = (bf16[128,1280]{1,0:T(8,128)(2,1)S(1)}, bf16[128,1280]{1,0:T(8,128)(2,1)S(1)}, u32[]{:S(2)}, u32[]{:S(2)}) collective-permute-start(bf16[128,1280]{1,0:T(8,128)(2,1)S(1)} %get-tuple-element.29.own), channel_id=1, source_target_pairs={{0,8},{4,12},{8,0},{12,4},{16,24},{20,28},{24,16},{28,20},{1,9},{5... | collective-permute-start | bytes 983048 | tf_op jit(solution)/shard_map/ppermute | solution.py:511
  38.3 8.2 %collective-permute-start.12 = (bf16[128,1280]{1,0:T(8,128)(2,1)S(1)}, bf16[128,1280]{1,0:T(8,128)(2,1)S(1)}, u32[]{:S(2)}, u32[]{:S(2)}) collective-permute-start(bf16[128,1280]{1,0:T(8,128)(2,1)S(1)} %get-tuple-element.29.own), channel_id=1, source_target_pairs={{0,16},{4,20},{8,24},{12,28},{16,0},{20,4},{24,8},{28,12},{1,17},{... | collective-permute-start | bytes 983048 | tf_op jit(solution)/shard_map/ppermute | solution.py:511
  39.2 7.8 %collective-permute-start.6 = (bf16[256,128]{1,0:T(8,128)(2,1)S(1)}, bf16[256,128]{1,0:T(8,128)(2,1)S(1)}, u32[]{:S(2)}, u32[]{:S(2)}) collective-permute-start(bf16[256,128]{1,0:T(8,128)(2,1)S(1)} %ahead_gram.2), channel_id=1, source_target_pairs={{0,1},{1,0},{2,3},{3,2},{4,5},{5,4},{6,7},{7,6},{8,9},{9,8},{10,11... | collective-permute-start | bytes 196616 | tf_op jit(solution)/shard_map/ppermute | solution.py:511
  40.4 6.7 %collective-permute-start.7 = (bf16[256,128]{1,0:T(8,128)(2,1)S(1)}, bf16[256,128]{1,0:T(8,128)(2,1)S(1)}, u32[]{:S(2)}, u32[]{:S(2)}) collective-permute-start(bf16[256,128]{1,0:T(8,128)(2,1)S(1)} %ahead_gram.2), channel_id=1, source_target_pairs={{0,2},{1,3},{2,0},{3,1},{4,6},{5,7},{6,4},{7,5},{8,10},{9,11},{10,... | collective-permute-start | bytes 196616 | tf_op jit(solution)/shard_map/ppermute | solution.py:511
  42.1 6.2 %collective-permute-start.8 = (bf16[256,128]{1,0:T(8,128)(2,1)S(1)}, bf16[256,128]{1,0:T(8,128)(2,1)S(1)}, u32[]{:S(2)}, u32[]{:S(2)}) collective-permute-start(bf16[256,128]{1,0:T(8,128)(2,1)S(1)} %ahead_gram.2), channel_id=1, source_target_pairs={{0,3},{1,2},{2,1},{3,0},{4,7},{5,6},{6,5},{7,4},{8,11},{9,10},{10,... | collective-permute-start | bytes 196616 | tf_op jit(solution)/shard_map/ppermute | solution.py:511
  45.0 5.0 %collective-permute-start.10 = (bf16[128,512]{1,0:T(8,128)(2,1)S(1)}, bf16[128,512]{1,0:T(8,128)(2,1)S(1)}, u32[]{:S(2)}, u32[]{:S(2)}) collective-permute-start(bf16[128,512]{1,0:T(8,128)(2,1)S(1)} %get-tuple-element.26.refs_0_), channel_id=1, source_target_pairs={{0,8},{4,12},{8,0},{12,4},{16,24},{20,28},{24,16},{28,20},{1,9},{5... | collective-permute-start | bytes 393224 | tf_op jit(solution)/shard_map/ppermute | solution.py:511
  46.9 3.1 %collective-permute-start.13 = (bf16[256,128]{1,0:T(8,128)(2,1)S(1)}, bf16[256,128]{1,0:T(8,128)(2,1)S(1)}, u32[]{:S(2)}, u32[]{:S(2)}) collective-permute-start(bf16[256,128]{1,0:T(8,128)(2,1)S(1)} %ahead_gram.3.one), channel_id=1, source_target_pairs={{0,4},{4,0},{8,12},{12,8},{16,20},{20,16},{24,28},{28,24},{1,5},{5... | collective-permute-start | bytes 196616 | tf_op jit(solution)/shard_map/ppermute | solution.py:511
  48.3 6.6 %collective-permute-start.9 = (bf16[256,128]{1,0:T(8,128)(2,1)S(1)}, bf16[256,128]{1,0:T(8,128)(2,1)S(1)}, u32[]{:S(2)}, u32[]{:S(2)}) collective-permute-start(bf16[256,128]{1,0:T(8,128)(2,1)S(1)} %add_convert_fusion.1.refs_2_), channel_id=1, source_target_pairs={{0,4},{4,0},{8,12},{12,8},{16,20},{20,16},{24,28},{28,24},{1,5},{5... | collective-permute-start | bytes 196616 | tf_op jit(solution)/shard_map/ppermute | solution.py:511
  50.0 13.1 %collective-permute-start.14 = (bf16[256,128]{1,0:T(8,128)(2,1)S(1)}, bf16[256,128]{1,0:T(8,128)(2,1)S(1)}, u32[]{:S(2)}, u32[]{:S(2)}) collective-permute-start(bf16[256,128]{1,0:T(8,128)(2,1)S(1)} %add_after.1), channel_id=1, source_target_pairs={{0,1},{1,0},{2,3},{3,2},{4,5},{5,4},{6,7},{7,6},{8,9},{9,8},{10,11... | collective-permute-start | bytes 196616 | tf_op jit(solution)/shard_map/ppermute | solution.py:511
  52.5 10.6 %collective-permute-start.15 = (bf16[256,128]{1,0:T(8,128)(2,1)S(1)}, bf16[256,128]{1,0:T(8,128)(2,1)S(1)}, u32[]{:S(2)}, u32[]{:S(2)}) collective-permute-start(bf16[256,128]{1,0:T(8,128)(2,1)S(1)} %add_after.1), channel_id=1, source_target_pairs={{0,2},{1,3},{2,0},{3,1},{4,6},{5,7},{6,4},{7,5},{8,10},{9,11},{10,... | collective-permute-start | bytes 196616 | tf_op jit(solution)/shard_map/ppermute | solution.py:511
  53.2 10.0 %collective-permute-start.16 = (bf16[256,128]{1,0:T(8,128)(2,1)S(1)}, bf16[256,128]{1,0:T(8,128)(2,1)S(1)}, u32[]{:S(2)}, u32[]{:S(2)}) collective-permute-start(bf16[256,128]{1,0:T(8,128)(2,1)S(1)} %add_after.1), channel_id=1, source_target_pairs={{0,3},{1,2},{2,1},{3,0},{4,7},{5,6},{6,5},{7,4},{8,11},{9,10},{10,... | collective-permute-start | bytes 196616 | tf_op jit(solution)/shard_map/ppermute | solution.py:511
  61.5 5.0 %collective-permute-start.18 = (bf16[128,512]{1,0:T(8,128)(2,1)S(1)}, bf16[128,512]{1,0:T(8,128)(2,1)S(1)}, u32[]{:S(2)}, u32[]{:S(2)}) collective-permute-start(bf16[128,512]{1,0:T(8,128)(2,1)S(1)} %get-tuple-element.30), channel_id=1, source_target_pairs={{0,16},{4,20},{8,24},{12,28},{16,0},{20,4},{24,8},{28,12},{1,17},{... | collective-permute-start | bytes 393224 | tf_op jit(solution)/shard_map/ppermute | solution.py:511
  63.2 4.3 %collective-permute-start.17 = (bf16[256,128]{1,0:T(8,128)(2,1)S(1)}, bf16[256,128]{1,0:T(8,128)(2,1)S(1)}, u32[]{:S(2)}, u32[]{:S(2)}) collective-permute-start(bf16[256,128]{1,0:T(8,128)(2,1)S(1)} %add_convert_fusion.refs_2_), channel_id=1, source_target_pairs={{0,8},{4,12},{8,0},{12,4},{16,24},{20,28},{24,16},{28,20},{1,9},{5... | collective-permute-start | bytes 196616 | tf_op jit(solution)/shard_map/ppermute | solution.py:511
  67.5 7.3 %collective-permute-start.19 = (bf16[128,1280]{1,0:T(8,128)(2,1)S(1)}, bf16[128,1280]{1,0:T(8,128)(2,1)S(1)}, u32[]{:S(2)}, u32[]{:S(2)}) collective-permute-start(bf16[128,1280]{1,0:T(8,128)(2,1)S(1)} %hold.1.own), channel_id=1, source_target_pairs={{0,16},{4,20},{8,24},{12,28},{16,0},{20,4},{24,8},{28,12},{1,17},{... | collective-permute-start | bytes 983048 | tf_op jit(solution)/shard_map/ppermute | solution.py:511
  75.0 1.3 %collective-permute-start.20 = (f32[16,1280]{1,0:T(8,128)S(1)}, f32[16,1280]{1,0:T(8,128)S(1)}, u32[]{:S(2)}, u32[]{:S(2)}) collective-permute-start(f32[16,1280]{1,0:T(8,128)S(1)} %get-tuple-element.32), channel_id=1, source_target_pairs={{0,4},{4,0},{8,12},{12,8},{16,20},{20,16},{24,28},{28,24},{1,5},{5... | collective-permute-start | bytes 245768 | tf_op jit(solution)/shard_map/ppermute | solution.py:511

commit v14 on v13

--- a/solution.py
+++ b/solution.py
@@ -155,7 +155,7 @@
     lag = lag.reshape(cols // 128, 128) if cols % 128 == 0 else lag[None, :]
     whole = lambda a: pl.BlockSpec(a.shape, lambda i: (0, 0))
     columns = lambda count, tile: pl.BlockSpec((count, tile), lambda i: (0, i))
-    tile = next((t for t in (512, 640, 256, 128) if cols % t == 0), cols)
+    tile = next((t for t in (1280, 640, 512, 256, 128) if cols % t == 0), cols)
     shapes = [
         jax.ShapeDtypeStruct((rank, cols), F32),
         jax.ShapeDtypeStruct((2 * BLOCK, BLOCK + HALO), BF16),

time: 78 us -> 77 us (0.987)
  Pallas kernels: 31.8 us -> 31 us
    pallas_call x2, Pallas kernels: 8.69 us -> 7.85 us  [front_call(): pl.pallas_call(functools.partial(front_kernel, *blocks), grid=(steps,), i...]
where the time goes in v14:
time: 77 us; the launch traced here: 76.8 us
  Pallas kernels  31 us (40%)
  starting transfers between devices  27.2 us (35%)
  waiting for transfers between devices  14.8 us (19%)
  local copies, waits for them, and re-layouts  3.43 us (4%)
    ppermute x20, starting transfers between devices, swap(): lax.ppermute(value, axis, [(source, source ^ mask) for source in range(co...  24.7 us
    ppermute x20, waiting for transfers between devices, swap(): lax.ppermute(value, axis, [(source, source ^ mask) for source in range(co...  14.8 us
    pallas_call x2, Pallas kernels, front_call(): pl.pallas_call(functools.partial(front_kernel, *blocks), grid=(steps,), i...  7.85 us
    pallas_call x1, Pallas kernels, level_filter_call(): pl.pallas_call(functools.partial(filter_kernel, len(grams), first, 'level...  6.58 us
    pallas_call x1, Pallas kernels, filter_call(): pl.pallas_call(functools.partial(filter_kernel, len(grams), first, 'sketc...  6.53 us
    pallas_call x1, Pallas kernels, last_filter_call(): pl.pallas_call(functools.partial(filter_kernel, len(grams), first, 'last'...  6.08 us
    ppermute x1, starting transfers between devices, on_device(): lax.ppermute(record[rows - HALO:], 'tm', [(source, source + 1) for source...  2.51 us
    unnamed x8, local copies, waits for them, and re-layouts  2.31 us
  transfers between devices with their start and end apart: 21, of which 10 were waited for; matrix products, arithmetic and copies ran while one was open for 0% of the time, Pallas kernels for 37%

profile of v14, /device:TPU:0, one launch (start us, length us, event | category | flops | bytes accessed | tf_op | source)
XLA Modules:
  0.0 76.8 jit_solution(2262848494601593968)
XLA Ops:
  0.0 1.0 %slice.3 = bf16[80,2560]{1,0:T(8,128)(2,1)S(1)} slice(bf16[1024,2560]{1,0:T(8,128)(2,1)} %refs_0_.1), slice={[944:1024], [0:2560]} | slice | bytes 819200 | tf_op jit(solution)/shard_map/slice | solution.py:547
  1.0 2.5 %collective-permute-start = (bf16[80,2560]{1,0:T(8,128)(2,1)S(1)}, bf16[80,2560]{1,0:T(8,128)(2,1)S(1)}, u32[]{:S(2)}, u32[]{:S(2)}) collective-permute-start(bf16[80,2560]{1,0:T(8,128)(2,1)S(1)} %slice.3), channel_id=1, source_target_pairs={{0,4},{4,8},{8,12},{12,16},{16,20},{20,24},{24,28},{1,5},{5,9},{9,... | collective-permute-start | bytes 1228808 | tf_op jit(solution)/shard_map/ppermute | solution.py:546
  3.6 0.9 %copy-done.1 = bf16[1024,128]{1,0:T(8,128)(2,1)S(1)} copy-done((bf16[1024,128]{1,0:T(8,128)(2,1)S(1)}, bf16[1024,128]{1,0:T(8,128)(2,1)}, u32[]{:S(2)}) %copy-start.1) | copy-done | bytes 262168
  4.5 0.7 copy-done.2
  5.9 6.5 %front.2 = (f32[128,2560]{1,0:T(8,128)S(1)}, bf16[256,208]{1,0:T(8,128)(2,1)S(1)}, bf16[128,128]{1,0:T(8,128)(2,1)S(1)}, bf16[128,2560]{1,0:T(8,128)(2,1)S(1)}) custom-call(bf16[1024,2560]{1,0:T(8,128)(2,1)} %refs_0_.1, s32[20,128]{1,0:T(8,128)S(1)} %bitcast.9, bf16[1,64]{1,0:T(2,128)(2,1)S(1)} %bitcast.11, bf16[1024,128]{1,0:T(8,128)(2,1)S(1)} %copy-done.1), custom_call_target="tpu_custom_call" | custom-call | tf_op jit(solution)/shard_map/front/pallas_call | solution.py:140
  12.4 1.4 %front.3.own.refs_6_ = bf16[128,2560]{1,0:T(8,128)(2,1)S(1)} custom-call(bf16[128,2560]{1,0:T(8,128)(2,1)S(1)} %get-tuple-element.19.refs_0_, bf16[80,2560]{1,0:T(8,128)(2,1)S(1)} %collective-permute-done.refs_1_, s32[20,128]{1,0:T(8,128)S(1)} %bitcast.10, bf16[256,208]{1,0:T(8,128)(2,1)S(1)} %get-tuple-element.20.refs_3_, ...), custom_call_target="tpu_custom_call" | custom-call | tf_op jit(solution)/shard_map/front/pallas_call | solution.py:140
  13.8 2.6 %collective-permute-start.1 = (bf16[128,2560]{1,0:T(8,128)(2,1)S(1)}, bf16[128,2560]{1,0:T(8,128)(2,1)S(1)}, u32[]{:S(2)}, u32[]{:S(2)}) collective-permute-start(bf16[128,2560]{1,0:T(8,128)(2,1)S(1)} %front.3.own.refs_6_), channel_id=1, source_target_pairs={{0,4},{4,0},{8,12},{12,8},{16,20},{20,16},{24,28},{28,24},{1,5},{5... | collective-permute-start | bytes 1966088 | tf_op jit(solution)/shard_map/ppermute | solution.py:511
  16.4 1.5 %collective-permute-start.5 = (bf16[128,2560]{1,0:T(8,128)(2,1)S(1)}, bf16[128,2560]{1,0:T(8,128)(2,1)S(1)}, u32[]{:S(2)}, u32[]{:S(2)}) collective-permute-start(bf16[128,2560]{1,0:T(8,128)(2,1)S(1)} %front.3.own.refs_6_), channel_id=1, source_target_pairs={{0,8},{4,12},{8,0},{12,4},{16,24},{20,28},{24,16},{28,20},{1,9},{5... | collective-permute-start | bytes 1966088 | tf_op jit(solution)/shard_map/ppermute | solution.py:511
  18.1 0.8 %pair_gram.1.refs_0_ = bf16[272,128]{1,0:T(8,128)(2,1)S(1)} custom-call(bf16[128,2560]{1,0:T(8,128)(2,1)S(1)} %front.3.own.refs_6_, bf16[128,2560]{1,0:T(8,128)(2,1)S(1)} %collective-permute-done.1.other.refs_7_.sibling), custom_call_target="tpu_custom_call" | custom-call | tf_op jit(solution)/shard_map/pair_gram/pallas_call | solution.py:229
  19.0 1.7 %collective-permute-start.2 = (bf16[272,128]{1,0:T(8,128)(2,1)S(1)}, bf16[272,128]{1,0:T(8,128)(2,1)S(1)}, u32[]{:S(2)}, u32[]{:S(2)}) collective-permute-start(bf16[272,128]{1,0:T(8,128)(2,1)S(1)} %pair_gram.1.refs_0_), channel_id=1, source_target_pairs={{0,1},{1,0},{2,3},{3,2},{4,5},{5,4},{6,7},{7,6},{8,9},{9,8},{10,11... | collective-permute-start | bytes 208904 | tf_op jit(solution)/shard_map/ppermute | solution.py:511
  20.6 2.6 %collective-permute-start.3 = (bf16[272,128]{1,0:T(8,128)(2,1)S(1)}, bf16[272,128]{1,0:T(8,128)(2,1)S(1)}, u32[]{:S(2)}, u32[]{:S(2)}) collective-permute-start(bf16[272,128]{1,0:T(8,128)(2,1)S(1)} %pair_gram.1.refs_0_), channel_id=1, source_target_pairs={{0,2},{1,3},{2,0},{3,1},{4,6},{5,7},{6,4},{7,5},{8,10},{9,11},{10,... | collective-permute-start | bytes 208904 | tf_op jit(solution)/shard_map/ppermute | solution.py:511
  23.5 5.0 %collective-permute-done.3.refs_2_ = bf16[272,128]{1,0:T(8,128)(2,1)S(1)} collective-permute-done((bf16[272,128]{1,0:T(8,128)(2,1)S(1)}, bf16[272,128]{1,0:T(8,128)(2,1)S(1)}, u32[]{:S(2)}, u32[]{:S(2)}) %collective-permute-start.3) | collective-permute-done | bytes 69664 | tf_op jit(solution)/shard_map/ppermute | solution.py:511
  28.5 0.8 %collective-permute-done.4.refs_3_ = bf16[272,128]{1,0:T(8,128)(2,1)S(1)} collective-permute-done((bf16[272,128]{1,0:T(8,128)(2,1)S(1)}, bf16[272,128]{1,0:T(8,128)(2,1)S(1)}, u32[]{:S(2)}, u32[]{:S(2)}) %collective-permute-start.4) | collective-permute-done | bytes 69664 | tf_op jit(solution)/shard_map/ppermute | solution.py:511
  29.4 6.5 %sign_filter.3 = (f32[128,256]{1,0:T(8,128)S(1)}, bf16[128,1280]{1,0:T(8,128)(2,1)S(1)}, f32[256,256]{1,0:T(8,128)S(1)}) custom-call(bf16[272,128]{1,0:T(8,128)(2,1)S(1)} %pair_gram.1.refs_0_, bf16[272,128]{1,0:T(8,128)(2,1)S(1)} %collective-permute-done.2.refs_1_, bf16[272,128]{1,0:T(8,128)(2,1)S(1)} %collective-permute-done.3.refs_2_, ...), custom_call_target="tpu_custom_call" | custom-call | tf_op jit(solution)/shard_map/sign_filter/pallas_call | solution.py:451
  35.9 1.6 %collective-permute-start.11 = (bf16[128,1280]{1,0:T(8,128)(2,1)S(1)}, bf16[128,1280]{1,0:T(8,128)(2,1)S(1)}, u32[]{:S(2)}, u32[]{:S(2)}) collective-permute-start(bf16[128,1280]{1,0:T(8,128)(2,1)S(1)} %get-tuple-element.29.own), channel_id=1, source_target_pairs={{0,8},{4,12},{8,0},{12,4},{16,24},{20,28},{24,16},{28,20},{1,9},{5... | collective-permute-start | bytes 983048 | tf_op jit(solution)/shard_map/ppermute | solution.py:511
  38.3 1.2 %collective-permute-start.6 = (bf16[256,128]{1,0:T(8,128)(2,1)S(1)}, bf16[256,128]{1,0:T(8,128)(2,1)S(1)}, u32[]{:S(2)}, u32[]{:S(2)}) collective-permute-start(bf16[256,128]{1,0:T(8,128)(2,1)S(1)} %ahead_gram.2), channel_id=1, source_target_pairs={{0,1},{1,0},{2,3},{3,2},{4,5},{5,4},{6,7},{7,6},{8,9},{9,8},{10,11... | collective-permute-start | bytes 196616 | tf_op jit(solution)/shard_map/ppermute | solution.py:511
  39.6 1.6 %collective-permute-start.7 = (bf16[256,128]{1,0:T(8,128)(2,1)S(1)}, bf16[256,128]{1,0:T(8,128)(2,1)S(1)}, u32[]{:S(2)}, u32[]{:S(2)}) collective-permute-start(bf16[256,128]{1,0:T(8,128)(2,1)S(1)} %ahead_gram.2), channel_id=1, source_target_pairs={{0,2},{1,3},{2,0},{3,1},{4,6},{5,7},{6,4},{7,5},{8,10},{9,11},{10,... | collective-permute-start | bytes 196616 | tf_op jit(solution)/shard_map/ppermute | solution.py:511
  41.2 1.6 %collective-permute-start.8 = (bf16[256,128]{1,0:T(8,128)(2,1)S(1)}, bf16[256,128]{1,0:T(8,128)(2,1)S(1)}, u32[]{:S(2)}, u32[]{:S(2)}) collective-permute-start(bf16[256,128]{1,0:T(8,128)(2,1)S(1)} %ahead_gram.2), channel_id=1, source_target_pairs={{0,3},{1,2},{2,1},{3,0},{4,7},{5,6},{6,5},{7,4},{8,11},{9,10},{10,... | collective-permute-start | bytes 196616 | tf_op jit(solution)/shard_map/ppermute | solution.py:511
  43.2 0.9 %collective-permute-done.11.sibling.other = bf16[128,1280]{1,0:T(8,128)(2,1)S(1)} collective-permute-done((bf16[128,1280]{1,0:T(8,128)(2,1)S(1)}, bf16[128,1280]{1,0:T(8,128)(2,1)S(1)}, u32[]{:S(2)}, u32[]{:S(2)}) %collective-permute-start.11) | collective-permute-done | bytes 327712 | tf_op jit(solution)/shard_map/ppermute | solution.py:511
  44.2 1.5 %collective-permute-start.10 = (bf16[128,512]{1,0:T(8,128)(2,1)S(1)}, bf16[128,512]{1,0:T(8,128)(2,1)S(1)}, u32[]{:S(2)}, u32[]{:S(2)}) collective-permute-start(bf16[128,512]{1,0:T(8,128)(2,1)S(1)} %get-tuple-element.26.refs_0_), channel_id=1, source_target_pairs={{0,8},{4,12},{8,0},{12,4},{16,24},{20,28},{24,16},{28,20},{1,9},{5... | collective-permute-start | bytes 393224 | tf_op jit(solution)/shard_map/ppermute | solution.py:511
  46.3 1.1 %collective-permute-done.8 = bf16[256,128]{1,0:T(8,128)(2,1)S(1)} collective-permute-done((bf16[256,128]{1,0:T(8,128)(2,1)S(1)}, bf16[256,128]{1,0:T(8,128)(2,1)S(1)}, u32[]{:S(2)}, u32[]{:S(2)}) %collective-permute-start.8) | collective-permute-done | bytes 65568 | tf_op jit(solution)/shard_map/ppermute | solution.py:511
  47.5 1.6 %collective-permute-done.10.refs_4_._ = bf16[128,512]{1,0:T(8,128)(2,1)S(1)} collective-permute-done((bf16[128,512]{1,0:T(8,128)(2,1)S(1)}, bf16[128,512]{1,0:T(8,128)(2,1)S(1)}, u32[]{:S(2)}, u32[]{:S(2)}) %collective-permute-start.10) | collective-permute-done | bytes 131104 | tf_op jit(solution)/shard_map/ppermute | solution.py:511
  49.2 2.5 %collective-permute-start.14 = (bf16[256,128]{1,0:T(8,128)(2,1)S(1)}, bf16[256,128]{1,0:T(8,128)(2,1)S(1)}, u32[]{:S(2)}, u32[]{:S(2)}) collective-permute-start(bf16[256,128]{1,0:T(8,128)(2,1)S(1)} %add_after.1), channel_id=1, source_target_pairs={{0,1},{1,0},{2,3},{3,2},{4,5},{5,4},{6,7},{7,6},{8,9},{9,8},{10,11... | collective-permute-start | bytes 196616 | tf_op jit(solution)/shard_map/ppermute | solution.py:511
  52.3 1.8 %collective-permute-start.16 = (bf16[256,128]{1,0:T(8,128)(2,1)S(1)}, bf16[256,128]{1,0:T(8,128)(2,1)S(1)}, u32[]{:S(2)}, u32[]{:S(2)}) collective-permute-start(bf16[256,128]{1,0:T(8,128)(2,1)S(1)} %add_after.1), channel_id=1, source_target_pairs={{0,3},{1,2},{2,1},{3,0},{4,7},{5,6},{6,5},{7,4},{8,11},{9,10},{10,... | collective-permute-start | bytes 196616 | tf_op jit(solution)/shard_map/ppermute | solution.py:511
  54.1 6.6 %sign_filter.4 = (f32[128,256]{1,0:T(8,128)S(1)}, bf16[128,512]{1,0:T(8,128)(2,1)S(1)}, f32[128,128]{1,0:T(8,128)S(1)}) custom-call(f32[128,256]{1,0:T(8,128)S(1)} %get-tuple-element.23.mixing.refs_0_, f32[128,128]{1,0:T(8,128)S(1)} %get-tuple-element.25.refs_1_, bf16[256,128]{1,0:T(8,128)(2,1)S(1)} %add_convert_fusion.1.refs_2_, ...), custom_call_target="tpu_custom_call" | custom-call | tf_op jit(solution)/shard_map/sign_filter/pallas_call | solution.py:438
  60.7 1.6 %collective-permute-start.18 = (bf16[128,512]{1,0:T(8,128)(2,1)S(1)}, bf16[128,512]{1,0:T(8,128)(2,1)S(1)}, u32[]{:S(2)}, u32[]{:S(2)}) collective-permute-start(bf16[128,512]{1,0:T(8,128)(2,1)S(1)} %get-tuple-element.30), channel_id=1, source_target_pairs={{0,16},{4,20},{8,24},{12,28},{16,0},{20,4},{24,8},{28,12},{1,17},{... | collective-permute-start | bytes 393224 | tf_op jit(solution)/shard_map/ppermute | solution.py:511
  63.1 2.7 %collective-permute-done.18.refs_4_.refs_2_ = bf16[128,512]{1,0:T(8,128)(2,1)S(1)} collective-permute-done((bf16[128,512]{1,0:T(8,128)(2,1)S(1)}, bf16[128,512]{1,0:T(8,128)(2,1)S(1)}, u32[]{:S(2)}, u32[]{:S(2)}) %collective-permute-start.18) | collective-permute-done | bytes 131104 | tf_op jit(solution)/shard_map/ppermute | solution.py:511
  65.7 0.9 %collective-permute-done.17.refs_3_.refs_1_ = bf16[256,128]{1,0:T(8,128)(2,1)S(1)} collective-permute-done((bf16[256,128]{1,0:T(8,128)(2,1)S(1)}, bf16[256,128]{1,0:T(8,128)(2,1)S(1)}, u32[]{:S(2)}, u32[]{:S(2)}) %collective-permute-start.17) | collective-permute-done | bytes 65568 | tf_op jit(solution)/shard_map/ppermute | solution.py:511
  66.7 1.2 %collective-permute-start.19 = (bf16[128,1280]{1,0:T(8,128)(2,1)S(1)}, bf16[128,1280]{1,0:T(8,128)(2,1)S(1)}, u32[]{:S(2)}, u32[]{:S(2)}) collective-permute-start(bf16[128,1280]{1,0:T(8,128)(2,1)S(1)} %hold.1.own), channel_id=1, source_target_pairs={{0,16},{4,20},{8,24},{12,28},{16,0},{20,4},{24,8},{28,12},{1,17},{... | collective-permute-start | bytes 983048 | tf_op jit(solution)/shard_map/ppermute | solution.py:511
  67.8 6.1 %sign_filter.5.mixing = f32[32,256]{1,0:T(8,128)S(1)} custom-call(f32[128,256]{1,0:T(8,128)S(1)} %get-tuple-element.27.refs_0_.mixing, f32[128,128]{1,0:T(8,128)S(1)} %get-tuple-element.28.refs_1_, bf16[256,128]{1,0:T(8,128)(2,1)S(1)} %add_convert_fusion.refs_2_, bf16[256,128]{1,0:T(8,128)(2,1)S(1)} %collective-permute-done.17.refs_3_.refs_1_, ...), custom_call_target="tpu_custom_call" | custom-call | flops 6710886400 | tf_op jit(solution)/shard_map/sign_filter/pallas_call | solution.py:472
  74.3 1.3 %collective-permute-done.20.refs_1_ = f32[16,1280]{1,0:T(8,128)S(1)} collective-permute-done((f32[16,1280]{1,0:T(8,128)S(1)}, f32[16,1280]{1,0:T(8,128)S(1)}, u32[]{:S(2)}, u32[]{:S(2)}) %collective-permute-start.20) | collective-permute-done | bytes 81952 | tf_op jit(solution)/shard_map/ppermute | solution.py:511
  75.5 1.2 %join.1 = f32[16,2560]{1,0:T(8,128)} custom-call(s32[10]{0:T(128)S(1)} %stack.32.refs_5_.refs_6_.places, f32[16,1280]{1,0:T(8,128)S(1)} %get-tuple-element.31.refs_0_, f32[16,1280]{1,0:T(8,128)S(1)} %collective-permute-done.20.refs_1_), custom_call_target="tpu_custom_call" | custom-call | tf_op jit(solution)/shard_map/join/pallas_call | solution.py:530
  (36 shorter events, 5.0 us)
Async XLA Ops:
  1.0 28.3 %copy-start = (f32[256,128]{1,0:T(8,128)S(1)}, f32[256,128]{1,0:T(8,128)}, u32[]{:S(2)}) copy-start(f32[256,128]{1,0:T(8,128)} %refs_5_.3) | copy-start | bytes 393220
  1.0 11.3 %collective-permute-start = (bf16[80,2560]{1,0:T(8,128)(2,1)S(1)}, bf16[80,2560]{1,0:T(8,128)(2,1)S(1)}, u32[]{:S(2)}, u32[]{:S(2)}) collective-permute-start(bf16[80,2560]{1,0:T(8,128)(2,1)S(1)} %slice.3), channel_id=1, source_target_pairs={{0,4},{4,8},{8,12},{12,16},{16,20},{20,24},{24,28},{1,5},{5,9},{9,... | collective-permute-start | bytes 1228808 | tf_op jit(solution)/shard_map/ppermute | solution.py:546
  3.6 1.0 %copy-start.1 = (bf16[1024,128]{1,0:T(8,128)(2,1)S(1)}, bf16[1024,128]{1,0:T(8,128)(2,1)}, u32[]{:S(2)}) copy-start(bf16[1024,128]{1,0:T(8,128)(2,1)} %refs_3_.1) | copy-start | bytes 786436
  4.5 0.7 copy-start.2
  5.2 0.7 copy-start.3
  13.8 4.4 %collective-permute-start.1 = (bf16[128,2560]{1,0:T(8,128)(2,1)S(1)}, bf16[128,2560]{1,0:T(8,128)(2,1)S(1)}, u32[]{:S(2)}, u32[]{:S(2)}) collective-permute-start(bf16[128,2560]{1,0:T(8,128)(2,1)S(1)} %front.3.own.refs_6_), channel_id=1, source_target_pairs={{0,4},{4,0},{8,12},{12,8},{16,20},{20,16},{24,28},{28,24},{1,5},{5... | collective-permute-start | bytes 1966088 | tf_op jit(solution)/shard_map/ppermute | solution.py:511
  16.4 21.4 %collective-permute-start.5 = (bf16[128,2560]{1,0:T(8,128)(2,1)S(1)}, bf16[128,2560]{1,0:T(8,128)(2,1)S(1)}, u32[]{:S(2)}, u32[]{:S(2)}) collective-permute-start(bf16[128,2560]{1,0:T(8,128)(2,1)S(1)} %front.3.own.refs_6_), channel_id=1, source_target_pairs={{0,8},{4,12},{8,0},{12,4},{16,24},{20,28},{24,16},{28,20},{1,9},{5... | collective-permute-start | bytes 1966088 | tf_op jit(solution)/shard_map/ppermute | solution.py:511
  19.0 4.6 %collective-permute-start.2 = (bf16[272,128]{1,0:T(8,128)(2,1)S(1)}, bf16[272,128]{1,0:T(8,128)(2,1)S(1)}, u32[]{:S(2)}, u32[]{:S(2)}) collective-permute-start(bf16[272,128]{1,0:T(8,128)(2,1)S(1)} %pair_gram.1.refs_0_), channel_id=1, source_target_pairs={{0,1},{1,0},{2,3},{3,2},{4,5},{5,4},{6,7},{7,6},{8,9},{9,8},{10,11... | collective-permute-start | bytes 208904 | tf_op jit(solution)/shard_map/ppermute | solution.py:511
  20.6 7.9 %collective-permute-start.3 = (bf16[272,128]{1,0:T(8,128)(2,1)S(1)}, bf16[272,128]{1,0:T(8,128)(2,1)S(1)}, u32[]{:S(2)}, u32[]{:S(2)}) collective-permute-start(bf16[272,128]{1,0:T(8,128)(2,1)S(1)} %pair_gram.1.refs_0_), channel_id=1, source_target_pairs={{0,2},{1,3},{2,0},{3,1},{4,6},{5,7},{6,4},{7,5},{8,10},{9,11},{10,... | collective-permute-start | bytes 208904 | tf_op jit(solution)/shard_map/ppermute | solution.py:511
  23.2 6.2 %collective-permute-start.4 = (bf16[272,128]{1,0:T(8,128)(2,1)S(1)}, bf16[272,128]{1,0:T(8,128)(2,1)S(1)}, u32[]{:S(2)}, u32[]{:S(2)}) collective-permute-start(bf16[272,128]{1,0:T(8,128)(2,1)S(1)} %pair_gram.1.refs_0_), channel_id=1, source_target_pairs={{0,3},{1,2},{2,1},{3,0},{4,7},{5,6},{6,5},{7,4},{8,11},{9,10},{10,... | collective-permute-start | bytes 208904 | tf_op jit(solution)/shard_map/ppermute | solution.py:511
  35.9 8.3 %collective-permute-start.11 = (bf16[128,1280]{1,0:T(8,128)(2,1)S(1)}, bf16[128,1280]{1,0:T(8,128)(2,1)S(1)}, u32[]{:S(2)}, u32[]{:S(2)}) collective-permute-start(bf16[128,1280]{1,0:T(8,128)(2,1)S(1)} %get-tuple-element.29.own), channel_id=1, source_target_pairs={{0,8},{4,12},{8,0},{12,4},{16,24},{20,28},{24,16},{28,20},{1,9},{5... | collective-permute-start | bytes 983048 | tf_op jit(solution)/shard_map/ppermute | solution.py:511
  37.5 8.2 %collective-permute-start.12 = (bf16[128,1280]{1,0:T(8,128)(2,1)S(1)}, bf16[128,1280]{1,0:T(8,128)(2,1)S(1)}, u32[]{:S(2)}, u32[]{:S(2)}) collective-permute-start(bf16[128,1280]{1,0:T(8,128)(2,1)S(1)} %get-tuple-element.29.own), channel_id=1, source_target_pairs={{0,16},{4,20},{8,24},{12,28},{16,0},{20,4},{24,8},{28,12},{1,17},{... | collective-permute-start | bytes 983048 | tf_op jit(solution)/shard_map/ppermute | solution.py:511
  38.3 7.8 %collective-permute-start.6 = (bf16[256,128]{1,0:T(8,128)(2,1)S(1)}, bf16[256,128]{1,0:T(8,128)(2,1)S(1)}, u32[]{:S(2)}, u32[]{:S(2)}) collective-permute-start(bf16[256,128]{1,0:T(8,128)(2,1)S(1)} %ahead_gram.2), channel_id=1, source_target_pairs={{0,1},{1,0},{2,3},{3,2},{4,5},{5,4},{6,7},{7,6},{8,9},{9,8},{10,11... | collective-permute-start | bytes 196616 | tf_op jit(solution)/shard_map/ppermute | solution.py:511
  39.6 6.7 %collective-permute-start.7 = (bf16[256,128]{1,0:T(8,128)(2,1)S(1)}, bf16[256,128]{1,0:T(8,128)(2,1)S(1)}, u32[]{:S(2)}, u32[]{:S(2)}) collective-permute-start(bf16[256,128]{1,0:T(8,128)(2,1)S(1)} %ahead_gram.2), channel_id=1, source_target_pairs={{0,2},{1,3},{2,0},{3,1},{4,6},{5,7},{6,4},{7,5},{8,10},{9,11},{10,... | collective-permute-start | bytes 196616 | tf_op jit(solution)/shard_map/ppermute | solution.py:511
  41.2 6.2 %collective-permute-start.8 = (bf16[256,128]{1,0:T(8,128)(2,1)S(1)}, bf16[256,128]{1,0:T(8,128)(2,1)S(1)}, u32[]{:S(2)}, u32[]{:S(2)}) collective-permute-start(bf16[256,128]{1,0:T(8,128)(2,1)S(1)} %ahead_gram.2), channel_id=1, source_target_pairs={{0,3},{1,2},{2,1},{3,0},{4,7},{5,6},{6,5},{7,4},{8,11},{9,10},{10,... | collective-permute-start | bytes 196616 | tf_op jit(solution)/shard_map/ppermute | solution.py:511
  44.2 5.0 %collective-permute-start.10 = (bf16[128,512]{1,0:T(8,128)(2,1)S(1)}, bf16[128,512]{1,0:T(8,128)(2,1)S(1)}, u32[]{:S(2)}, u32[]{:S(2)}) collective-permute-start(bf16[128,512]{1,0:T(8,128)(2,1)S(1)} %get-tuple-element.26.refs_0_), channel_id=1, source_target_pairs={{0,8},{4,12},{8,0},{12,4},{16,24},{20,28},{24,16},{28,20},{1,9},{5... | collective-permute-start | bytes 393224 | tf_op jit(solution)/shard_map/ppermute | solution.py:511
  46.0 3.1 %collective-permute-start.13 = (bf16[256,128]{1,0:T(8,128)(2,1)S(1)}, bf16[256,128]{1,0:T(8,128)(2,1)S(1)}, u32[]{:S(2)}, u32[]{:S(2)}) collective-permute-start(bf16[256,128]{1,0:T(8,128)(2,1)S(1)} %ahead_gram.3.one), channel_id=1, source_target_pairs={{0,4},{4,0},{8,12},{12,8},{16,20},{20,16},{24,28},{28,24},{1,5},{5... | collective-permute-start | bytes 196616 | tf_op jit(solution)/shard_map/ppermute | solution.py:511
  47.4 6.7 %collective-permute-start.9 = (bf16[256,128]{1,0:T(8,128)(2,1)S(1)}, bf16[256,128]{1,0:T(8,128)(2,1)S(1)}, u32[]{:S(2)}, u32[]{:S(2)}) collective-permute-start(bf16[256,128]{1,0:T(8,128)(2,1)S(1)} %add_convert_fusion.1.refs_2_), channel_id=1, source_target_pairs={{0,4},{4,0},{8,12},{12,8},{16,20},{20,16},{24,28},{28,24},{1,5},{5... | collective-permute-start | bytes 196616 | tf_op jit(solution)/shard_map/ppermute | solution.py:511
  49.2 13.1 %collective-permute-start.14 = (bf16[256,128]{1,0:T(8,128)(2,1)S(1)}, bf16[256,128]{1,0:T(8,128)(2,1)S(1)}, u32[]{:S(2)}, u32[]{:S(2)}) collective-permute-start(bf16[256,128]{1,0:T(8,128)(2,1)S(1)} %add_after.1), channel_id=1, source_target_pairs={{0,1},{1,0},{2,3},{3,2},{4,5},{5,4},{6,7},{7,6},{8,9},{9,8},{10,11... | collective-permute-start | bytes 196616 | tf_op jit(solution)/shard_map/ppermute | solution.py:511
  51.7 10.6 %collective-permute-start.15 = (bf16[256,128]{1,0:T(8,128)(2,1)S(1)}, bf16[256,128]{1,0:T(8,128)(2,1)S(1)}, u32[]{:S(2)}, u32[]{:S(2)}) collective-permute-start(bf16[256,128]{1,0:T(8,128)(2,1)S(1)} %add_after.1), channel_id=1, source_target_pairs={{0,2},{1,3},{2,0},{3,1},{4,6},{5,7},{6,4},{7,5},{8,10},{9,11},{10,... | collective-permute-start | bytes 196616 | tf_op jit(solution)/shard_map/ppermute | solution.py:511
  52.3 9.9 %collective-permute-start.16 = (bf16[256,128]{1,0:T(8,128)(2,1)S(1)}, bf16[256,128]{1,0:T(8,128)(2,1)S(1)}, u32[]{:S(2)}, u32[]{:S(2)}) collective-permute-start(bf16[256,128]{1,0:T(8,128)(2,1)S(1)} %add_after.1), channel_id=1, source_target_pairs={{0,3},{1,2},{2,1},{3,0},{4,7},{5,6},{6,5},{7,4},{8,11},{9,10},{10,... | collective-permute-start | bytes 196616 | tf_op jit(solution)/shard_map/ppermute | solution.py:511
  60.7 5.0 %collective-permute-start.18 = (bf16[128,512]{1,0:T(8,128)(2,1)S(1)}, bf16[128,512]{1,0:T(8,128)(2,1)S(1)}, u32[]{:S(2)}, u32[]{:S(2)}) collective-permute-start(bf16[128,512]{1,0:T(8,128)(2,1)S(1)} %get-tuple-element.30), channel_id=1, source_target_pairs={{0,16},{4,20},{8,24},{12,28},{16,0},{20,4},{24,8},{28,12},{1,17},{... | collective-permute-start | bytes 393224 | tf_op jit(solution)/shard_map/ppermute | solution.py:511
  62.3 4.3 %collective-permute-start.17 = (bf16[256,128]{1,0:T(8,128)(2,1)S(1)}, bf16[256,128]{1,0:T(8,128)(2,1)S(1)}, u32[]{:S(2)}, u32[]{:S(2)}) collective-permute-start(bf16[256,128]{1,0:T(8,128)(2,1)S(1)} %add_convert_fusion.refs_2_), channel_id=1, source_target_pairs={{0,8},{4,12},{8,0},{12,4},{16,24},{20,28},{24,16},{28,20},{1,9},{5... | collective-permute-start | bytes 196616 | tf_op jit(solution)/shard_map/ppermute | solution.py:511
  66.7 7.3 %collective-permute-start.19 = (bf16[128,1280]{1,0:T(8,128)(2,1)S(1)}, bf16[128,1280]{1,0:T(8,128)(2,1)S(1)}, u32[]{:S(2)}, u32[]{:S(2)}) collective-permute-start(bf16[128,1280]{1,0:T(8,128)(2,1)S(1)} %hold.1.own), channel_id=1, source_target_pairs={{0,16},{4,20},{8,24},{12,28},{16,0},{20,4},{24,8},{28,12},{1,17},{... | collective-permute-start | bytes 983048 | tf_op jit(solution)/shard_map/ppermute | solution.py:511
  74.2 1.3 %collective-permute-start.20 = (f32[16,1280]{1,0:T(8,128)S(1)}, f32[16,1280]{1,0:T(8,128)S(1)}, u32[]{:S(2)}, u32[]{:S(2)}) collective-permute-start(f32[16,1280]{1,0:T(8,128)S(1)} %get-tuple-element.32), channel_id=1, source_target_pairs={{0,4},{4,0},{8,12},{12,8},{16,20},{20,16},{24,28},{28,24},{1,5},{5... | collective-permute-start | bytes 245768 | tf_op jit(solution)/shard_map/ppermute | solution.py:511

commit v15 on v14

--- a/solution.py
+++ b/solution.py
@@ -179,7 +179,7 @@
         cols // tile,
         48,
     )
-    tile = cols // 2 if cols % 256 == 0 else cols
+    tile = cols
     return front_call(
         (0, 1),
         (head, halo, lag, band, weights, begun),

time: 77 us -> 76.4 us (level)
  no operation moved by 1% of the time
where the time goes in v15:
time: 76.4 us; the launch traced here: 76.2 us
  Pallas kernels  30.4 us (40%)
  starting transfers between devices  27.2 us (36%)
  waiting for transfers between devices  14.8 us (19%)
  local copies, waits for them, and re-layouts  3.43 us (4%)
    ppermute x20, starting transfers between devices, swap(): lax.ppermute(value, axis, [(source, source ^ mask) for source in range(co...  24.7 us
    ppermute x20, waiting for transfers between devices, swap(): lax.ppermute(value, axis, [(source, source ^ mask) for source in range(co...  14.8 us
    pallas_call x2, Pallas kernels, front_call(): pl.pallas_call(functools.partial(front_kernel, *blocks), grid=(steps,), i...  7.26 us
    pallas_call x1, Pallas kernels, level_filter_call(): pl.pallas_call(functools.partial(filter_kernel, len(grams), first, 'level...  6.58 us
    pallas_call x1, Pallas kernels, filter_call(): pl.pallas_call(functools.partial(filter_kernel, len(grams), first, 'sketc...  6.53 us
    pallas_call x1, Pallas kernels, last_filter_call(): pl.pallas_call(functools.partial(filter_kernel, len(grams), first, 'last'...  6.08 us
    ppermute x1, starting transfers between devices, on_device(): lax.ppermute(record[rows - HALO:], 'tm', [(source, source + 1) for source...  2.51 us
    unnamed x8, local copies, waits for them, and re-layouts  2.31 us
  transfers between devices with their start and end apart: 21, of which 10 were waited for; matrix products, arithmetic and copies ran while one was open for 0% of the time, Pallas kernels for 37%

profile of v15, /device:TPU:0, one launch (start us, length us, event | category | flops | bytes accessed | tf_op | source)
XLA Modules:
  0.0 76.2 jit_solution(16494666027077180857)
XLA Ops:
  0.0 1.0 %slice.3 = bf16[80,2560]{1,0:T(8,128)(2,1)S(1)} slice(bf16[1024,2560]{1,0:T(8,128)(2,1)} %refs_0_.1), slice={[944:1024], [0:2560]} | slice | bytes 819200 | tf_op jit(solution)/shard_map/slice | solution.py:547
  1.0 2.5 %collective-permute-start = (bf16[80,2560]{1,0:T(8,128)(2,1)S(1)}, bf16[80,2560]{1,0:T(8,128)(2,1)S(1)}, u32[]{:S(2)}, u32[]{:S(2)}) collective-permute-start(bf16[80,2560]{1,0:T(8,128)(2,1)S(1)} %slice.3), channel_id=1, source_target_pairs={{0,4},{4,8},{8,12},{12,16},{16,20},{20,24},{24,28},{1,5},{5,9},{9,... | collective-permute-start | bytes 1228808 | tf_op jit(solution)/shard_map/ppermute | solution.py:546
  3.6 0.9 %copy-done.1 = bf16[1024,128]{1,0:T(8,128)(2,1)S(1)} copy-done((bf16[1024,128]{1,0:T(8,128)(2,1)S(1)}, bf16[1024,128]{1,0:T(8,128)(2,1)}, u32[]{:S(2)}) %copy-start.1) | copy-done | bytes 262168
  4.5 0.7 copy-done.2
  5.9 6.5 %front.2 = (f32[128,2560]{1,0:T(8,128)S(1)}, bf16[256,208]{1,0:T(8,128)(2,1)S(1)}, bf16[128,128]{1,0:T(8,128)(2,1)S(1)}, bf16[128,2560]{1,0:T(8,128)(2,1)S(1)}) custom-call(bf16[1024,2560]{1,0:T(8,128)(2,1)} %refs_0_.1, s32[20,128]{1,0:T(8,128)S(1)} %bitcast.9, bf16[1,64]{1,0:T(2,128)(2,1)S(1)} %bitcast.11, bf16[1024,128]{1,0:T(8,128)(2,1)S(1)} %copy-done.1), custom_call_target="tpu_custom_call" | custom-call | tf_op jit(solution)/shard_map/front/pallas_call | solution.py:140
  12.4 0.8 %front.3.own.refs_6_ = bf16[128,2560]{1,0:T(8,128)(2,1)S(1)} custom-call(bf16[128,2560]{1,0:T(8,128)(2,1)S(1)} %get-tuple-element.19.refs_0_, bf16[80,2560]{1,0:T(8,128)(2,1)S(1)} %collective-permute-done.refs_1_, s32[20,128]{1,0:T(8,128)S(1)} %bitcast.10, bf16[256,208]{1,0:T(8,128)(2,1)S(1)} %get-tuple-element.20.refs_3_, ...), custom_call_target="tpu_custom_call" | custom-call | tf_op jit(solution)/shard_map/front/pallas_call | solution.py:140
  13.2 2.6 %collective-permute-start.1 = (bf16[128,2560]{1,0:T(8,128)(2,1)S(1)}, bf16[128,2560]{1,0:T(8,128)(2,1)S(1)}, u32[]{:S(2)}, u32[]{:S(2)}) collective-permute-start(bf16[128,2560]{1,0:T(8,128)(2,1)S(1)} %front.3.own.refs_6_), channel_id=1, source_target_pairs={{0,4},{4,0},{8,12},{12,8},{16,20},{20,16},{24,28},{28,24},{1,5},{5... | collective-permute-start | bytes 1966088 | tf_op jit(solution)/shard_map/ppermute | solution.py:511
  15.8 1.5 %collective-permute-start.5 = (bf16[128,2560]{1,0:T(8,128)(2,1)S(1)}, bf16[128,2560]{1,0:T(8,128)(2,1)S(1)}, u32[]{:S(2)}, u32[]{:S(2)}) collective-permute-start(bf16[128,2560]{1,0:T(8,128)(2,1)S(1)} %front.3.own.refs_6_), channel_id=1, source_target_pairs={{0,8},{4,12},{8,0},{12,4},{16,24},{20,28},{24,16},{28,20},{1,9},{5... | collective-permute-start | bytes 1966088 | tf_op jit(solution)/shard_map/ppermute | solution.py:511
  17.5 0.8 %pair_gram.1.refs_0_ = bf16[272,128]{1,0:T(8,128)(2,1)S(1)} custom-call(bf16[128,2560]{1,0:T(8,128)(2,1)S(1)} %front.3.own.refs_6_, bf16[128,2560]{1,0:T(8,128)(2,1)S(1)} %collective-permute-done.1.other.refs_7_.sibling), custom_call_target="tpu_custom_call" | custom-call | tf_op jit(solution)/shard_map/pair_gram/pallas_call | solution.py:229
  18.4 1.7 %collective-permute-start.2 = (bf16[272,128]{1,0:T(8,128)(2,1)S(1)}, bf16[272,128]{1,0:T(8,128)(2,1)S(1)}, u32[]{:S(2)}, u32[]{:S(2)}) collective-permute-start(bf16[272,128]{1,0:T(8,128)(2,1)S(1)} %pair_gram.1.refs_0_), channel_id=1, source_target_pairs={{0,1},{1,0},{2,3},{3,2},{4,5},{5,4},{6,7},{7,6},{8,9},{9,8},{10,11... | collective-permute-start | bytes 208904 | tf_op jit(solution)/shard_map/ppermute | solution.py:511
  20.0 2.6 %collective-permute-start.3 = (bf16[272,128]{1,0:T(8,128)(2,1)S(1)}, bf16[272,128]{1,0:T(8,128)(2,1)S(1)}, u32[]{:S(2)}, u32[]{:S(2)}) collective-permute-start(bf16[272,128]{1,0:T(8,128)(2,1)S(1)} %pair_gram.1.refs_0_), channel_id=1, source_target_pairs={{0,2},{1,3},{2,0},{3,1},{4,6},{5,7},{6,4},{7,5},{8,10},{9,11},{10,... | collective-permute-start | bytes 208904 | tf_op jit(solution)/shard_map/ppermute | solution.py:511
  22.9 5.0 %collective-permute-done.3.refs_2_ = bf16[272,128]{1,0:T(8,128)(2,1)S(1)} collective-permute-done((bf16[272,128]{1,0:T(8,128)(2,1)S(1)}, bf16[272,128]{1,0:T(8,128)(2,1)S(1)}, u32[]{:S(2)}, u32[]{:S(2)}) %collective-permute-start.3) | collective-permute-done | bytes 69664 | tf_op jit(solution)/shard_map/ppermute | solution.py:511
  27.9 0.8 %collective-permute-done.4.refs_3_ = bf16[272,128]{1,0:T(8,128)(2,1)S(1)} collective-permute-done((bf16[272,128]{1,0:T(8,128)(2,1)S(1)}, bf16[272,128]{1,0:T(8,128)(2,1)S(1)}, u32[]{:S(2)}, u32[]{:S(2)}) %collective-permute-start.4) | collective-permute-done | bytes 69664 | tf_op jit(solution)/shard_map/ppermute | solution.py:511
  28.8 6.5 %sign_filter.3 = (f32[128,256]{1,0:T(8,128)S(1)}, bf16[128,1280]{1,0:T(8,128)(2,1)S(1)}, f32[256,256]{1,0:T(8,128)S(1)}) custom-call(bf16[272,128]{1,0:T(8,128)(2,1)S(1)} %pair_gram.1.refs_0_, bf16[272,128]{1,0:T(8,128)(2,1)S(1)} %collective-permute-done.2.refs_1_, bf16[272,128]{1,0:T(8,128)(2,1)S(1)} %collective-permute-done.3.refs_2_, ...), custom_call_target="tpu_custom_call" | custom-call | tf_op jit(solution)/shard_map/sign_filter/pallas_call | solution.py:451
  35.3 1.6 %collective-permute-start.11 = (bf16[128,1280]{1,0:T(8,128)(2,1)S(1)}, bf16[128,1280]{1,0:T(8,128)(2,1)S(1)}, u32[]{:S(2)}, u32[]{:S(2)}) collective-permute-start(bf16[128,1280]{1,0:T(8,128)(2,1)S(1)} %get-tuple-element.29.own), channel_id=1, source_target_pairs={{0,8},{4,12},{8,0},{12,4},{16,24},{20,28},{24,16},{28,20},{1,9},{5... | collective-permute-start | bytes 983048 | tf_op jit(solution)/shard_map/ppermute | solution.py:511
  37.7 1.2 %collective-permute-start.6 = (bf16[256,128]{1,0:T(8,128)(2,1)S(1)}, bf16[256,128]{1,0:T(8,128)(2,1)S(1)}, u32[]{:S(2)}, u32[]{:S(2)}) collective-permute-start(bf16[256,128]{1,0:T(8,128)(2,1)S(1)} %ahead_gram.2), channel_id=1, source_target_pairs={{0,1},{1,0},{2,3},{3,2},{4,5},{5,4},{6,7},{7,6},{8,9},{9,8},{10,11... | collective-permute-start | bytes 196616 | tf_op jit(solution)/shard_map/ppermute | solution.py:511
  39.0 1.7 %collective-permute-start.7 = (bf16[256,128]{1,0:T(8,128)(2,1)S(1)}, bf16[256,128]{1,0:T(8,128)(2,1)S(1)}, u32[]{:S(2)}, u32[]{:S(2)}) collective-permute-start(bf16[256,128]{1,0:T(8,128)(2,1)S(1)} %ahead_gram.2), channel_id=1, source_target_pairs={{0,2},{1,3},{2,0},{3,1},{4,6},{5,7},{6,4},{7,5},{8,10},{9,11},{10,... | collective-permute-start | bytes 196616 | tf_op jit(solution)/shard_map/ppermute | solution.py:511
  40.6 1.6 %collective-permute-start.8 = (bf16[256,128]{1,0:T(8,128)(2,1)S(1)}, bf16[256,128]{1,0:T(8,128)(2,1)S(1)}, u32[]{:S(2)}, u32[]{:S(2)}) collective-permute-start(bf16[256,128]{1,0:T(8,128)(2,1)S(1)} %ahead_gram.2), channel_id=1, source_target_pairs={{0,3},{1,2},{2,1},{3,0},{4,7},{5,6},{6,5},{7,4},{8,11},{9,10},{10,... | collective-permute-start | bytes 196616 | tf_op jit(solution)/shard_map/ppermute | solution.py:511
  42.7 0.9 %collective-permute-done.11.sibling.other = bf16[128,1280]{1,0:T(8,128)(2,1)S(1)} collective-permute-done((bf16[128,1280]{1,0:T(8,128)(2,1)S(1)}, bf16[128,1280]{1,0:T(8,128)(2,1)S(1)}, u32[]{:S(2)}, u32[]{:S(2)}) %collective-permute-start.11) | collective-permute-done | bytes 327712 | tf_op jit(solution)/shard_map/ppermute | solution.py:511
  43.6 1.5 %collective-permute-start.10 = (bf16[128,512]{1,0:T(8,128)(2,1)S(1)}, bf16[128,512]{1,0:T(8,128)(2,1)S(1)}, u32[]{:S(2)}, u32[]{:S(2)}) collective-permute-start(bf16[128,512]{1,0:T(8,128)(2,1)S(1)} %get-tuple-element.26.refs_0_), channel_id=1, source_target_pairs={{0,8},{4,12},{8,0},{12,4},{16,24},{20,28},{24,16},{28,20},{1,9},{5... | collective-permute-start | bytes 393224 | tf_op jit(solution)/shard_map/ppermute | solution.py:511
  45.7 1.1 %collective-permute-done.8 = bf16[256,128]{1,0:T(8,128)(2,1)S(1)} collective-permute-done((bf16[256,128]{1,0:T(8,128)(2,1)S(1)}, bf16[256,128]{1,0:T(8,128)(2,1)S(1)}, u32[]{:S(2)}, u32[]{:S(2)}) %collective-permute-start.8) | collective-permute-done | bytes 65568 | tf_op jit(solution)/shard_map/ppermute | solution.py:511
  46.9 1.6 %collective-permute-done.10.refs_4_._ = bf16[128,512]{1,0:T(8,128)(2,1)S(1)} collective-permute-done((bf16[128,512]{1,0:T(8,128)(2,1)S(1)}, bf16[128,512]{1,0:T(8,128)(2,1)S(1)}, u32[]{:S(2)}, u32[]{:S(2)}) %collective-permute-start.10) | collective-permute-done | bytes 131104 | tf_op jit(solution)/shard_map/ppermute | solution.py:511
  48.6 2.5 %collective-permute-start.14 = (bf16[256,128]{1,0:T(8,128)(2,1)S(1)}, bf16[256,128]{1,0:T(8,128)(2,1)S(1)}, u32[]{:S(2)}, u32[]{:S(2)}) collective-permute-start(bf16[256,128]{1,0:T(8,128)(2,1)S(1)} %add_after.1), channel_id=1, source_target_pairs={{0,1},{1,0},{2,3},{3,2},{4,5},{5,4},{6,7},{7,6},{8,9},{9,8},{10,11... | collective-permute-start | bytes 196616 | tf_op jit(solution)/shard_map/ppermute | solution.py:511
  51.7 1.8 %collective-permute-start.16 = (bf16[256,128]{1,0:T(8,128)(2,1)S(1)}, bf16[256,128]{1,0:T(8,128)(2,1)S(1)}, u32[]{:S(2)}, u32[]{:S(2)}) collective-permute-start(bf16[256,128]{1,0:T(8,128)(2,1)S(1)} %add_after.1), channel_id=1, source_target_pairs={{0,3},{1,2},{2,1},{3,0},{4,7},{5,6},{6,5},{7,4},{8,11},{9,10},{10,... | collective-permute-start | bytes 196616 | tf_op jit(solution)/shard_map/ppermute | solution.py:511
  53.5 6.6 %sign_filter.4 = (f32[128,256]{1,0:T(8,128)S(1)}, bf16[128,512]{1,0:T(8,128)(2,1)S(1)}, f32[128,128]{1,0:T(8,128)S(1)}) custom-call(f32[128,256]{1,0:T(8,128)S(1)} %get-tuple-element.23.mixing.refs_0_, f32[128,128]{1,0:T(8,128)S(1)} %get-tuple-element.25.refs_1_, bf16[256,128]{1,0:T(8,128)(2,1)S(1)} %add_convert_fusion.1.refs_2_, ...), custom_call_target="tpu_custom_call" | custom-call | tf_op jit(solution)/shard_map/sign_filter/pallas_call | solution.py:438
  60.1 1.6 %collective-permute-start.18 = (bf16[128,512]{1,0:T(8,128)(2,1)S(1)}, bf16[128,512]{1,0:T(8,128)(2,1)S(1)}, u32[]{:S(2)}, u32[]{:S(2)}) collective-permute-start(bf16[128,512]{1,0:T(8,128)(2,1)S(1)} %get-tuple-element.30), channel_id=1, source_target_pairs={{0,16},{4,20},{8,24},{12,28},{16,0},{20,4},{24,8},{28,12},{1,17},{... | collective-permute-start | bytes 393224 | tf_op jit(solution)/shard_map/ppermute | solution.py:511
  62.5 2.7 %collective-permute-done.18.refs_4_.refs_2_ = bf16[128,512]{1,0:T(8,128)(2,1)S(1)} collective-permute-done((bf16[128,512]{1,0:T(8,128)(2,1)S(1)}, bf16[128,512]{1,0:T(8,128)(2,1)S(1)}, u32[]{:S(2)}, u32[]{:S(2)}) %collective-permute-start.18) | collective-permute-done | bytes 131104 | tf_op jit(solution)/shard_map/ppermute | solution.py:511
  65.1 0.9 %collective-permute-done.17.refs_3_.refs_1_ = bf16[256,128]{1,0:T(8,128)(2,1)S(1)} collective-permute-done((bf16[256,128]{1,0:T(8,128)(2,1)S(1)}, bf16[256,128]{1,0:T(8,128)(2,1)S(1)}, u32[]{:S(2)}, u32[]{:S(2)}) %collective-permute-start.17) | collective-permute-done | bytes 65568 | tf_op jit(solution)/shard_map/ppermute | solution.py:511
  66.1 1.2 %collective-permute-start.19 = (bf16[128,1280]{1,0:T(8,128)(2,1)S(1)}, bf16[128,1280]{1,0:T(8,128)(2,1)S(1)}, u32[]{:S(2)}, u32[]{:S(2)}) collective-permute-start(bf16[128,1280]{1,0:T(8,128)(2,1)S(1)} %hold.1.own), channel_id=1, source_target_pairs={{0,16},{4,20},{8,24},{12,28},{16,0},{20,4},{24,8},{28,12},{1,17},{... | collective-permute-start | bytes 983048 | tf_op jit(solution)/shard_map/ppermute | solution.py:511
  67.3 6.1 %sign_filter.5.mixing = f32[32,256]{1,0:T(8,128)S(1)} custom-call(f32[128,256]{1,0:T(8,128)S(1)} %get-tuple-element.27.refs_0_.mixing, f32[128,128]{1,0:T(8,128)S(1)} %get-tuple-element.28.refs_1_, bf16[256,128]{1,0:T(8,128)(2,1)S(1)} %add_convert_fusion.refs_2_, bf16[256,128]{1,0:T(8,128)(2,1)S(1)} %collective-permute-done.17.refs_3_.refs_1_, ...), custom_call_target="tpu_custom_call" | custom-call | flops 6710886400 | tf_op jit(solution)/shard_map/sign_filter/pallas_call | solution.py:472
  73.7 1.3 %collective-permute-done.20.refs_1_ = f32[16,1280]{1,0:T(8,128)S(1)} collective-permute-done((f32[16,1280]{1,0:T(8,128)S(1)}, f32[16,1280]{1,0:T(8,128)S(1)}, u32[]{:S(2)}, u32[]{:S(2)}) %collective-permute-start.20) | collective-permute-done | bytes 81952 | tf_op jit(solution)/shard_map/ppermute | solution.py:511
  74.9 1.2 %join.1 = f32[16,2560]{1,0:T(8,128)} custom-call(s32[10]{0:T(128)S(1)} %stack.32.refs_5_.refs_6_.places, f32[16,1280]{1,0:T(8,128)S(1)} %get-tuple-element.31.refs_0_, f32[16,1280]{1,0:T(8,128)S(1)} %collective-permute-done.20.refs_1_), custom_call_target="tpu_custom_call" | custom-call | tf_op jit(solution)/shard_map/join/pallas_call | solution.py:530
  (36 shorter events, 5.0 us)
Async XLA Ops:
  1.0 27.7 %copy-start = (f32[256,128]{1,0:T(8,128)S(1)}, f32[256,128]{1,0:T(8,128)}, u32[]{:S(2)}) copy-start(f32[256,128]{1,0:T(8,128)} %refs_5_.3) | copy-start | bytes 393220
  1.0 11.3 %collective-permute-start = (bf16[80,2560]{1,0:T(8,128)(2,1)S(1)}, bf16[80,2560]{1,0:T(8,128)(2,1)S(1)}, u32[]{:S(2)}, u32[]{:S(2)}) collective-permute-start(bf16[80,2560]{1,0:T(8,128)(2,1)S(1)} %slice.3), channel_id=1, source_target_pairs={{0,4},{4,8},{8,12},{12,16},{16,20},{20,24},{24,28},{1,5},{5,9},{9,... | collective-permute-start | bytes 1228808 | tf_op jit(solution)/shard_map/ppermute | solution.py:546
  3.6 1.0 %copy-start.1 = (bf16[1024,128]{1,0:T(8,128)(2,1)S(1)}, bf16[1024,128]{1,0:T(8,128)(2,1)}, u32[]{:S(2)}) copy-start(bf16[1024,128]{1,0:T(8,128)(2,1)} %refs_3_.1) | copy-start | bytes 786436
  4.5 0.7 copy-start.2
  5.2 0.7 copy-start.3
  13.2 4.4 %collective-permute-start.1 = (bf16[128,2560]{1,0:T(8,128)(2,1)S(1)}, bf16[128,2560]{1,0:T(8,128)(2,1)S(1)}, u32[]{:S(2)}, u32[]{:S(2)}) collective-permute-start(bf16[128,2560]{1,0:T(8,128)(2,1)S(1)} %front.3.own.refs_6_), channel_id=1, source_target_pairs={{0,4},{4,0},{8,12},{12,8},{16,20},{20,16},{24,28},{28,24},{1,5},{5... | collective-permute-start | bytes 1966088 | tf_op jit(solution)/shard_map/ppermute | solution.py:511
  15.8 21.4 %collective-permute-start.5 = (bf16[128,2560]{1,0:T(8,128)(2,1)S(1)}, bf16[128,2560]{1,0:T(8,128)(2,1)S(1)}, u32[]{:S(2)}, u32[]{:S(2)}) collective-permute-start(bf16[128,2560]{1,0:T(8,128)(2,1)S(1)} %front.3.own.refs_6_), channel_id=1, source_target_pairs={{0,8},{4,12},{8,0},{12,4},{16,24},{20,28},{24,16},{28,20},{1,9},{5... | collective-permute-start | bytes 1966088 | tf_op jit(solution)/shard_map/ppermute | solution.py:511
  18.4 4.6 %collective-permute-start.2 = (bf16[272,128]{1,0:T(8,128)(2,1)S(1)}, bf16[272,128]{1,0:T(8,128)(2,1)S(1)}, u32[]{:S(2)}, u32[]{:S(2)}) collective-permute-start(bf16[272,128]{1,0:T(8,128)(2,1)S(1)} %pair_gram.1.refs_0_), channel_id=1, source_target_pairs={{0,1},{1,0},{2,3},{3,2},{4,5},{5,4},{6,7},{7,6},{8,9},{9,8},{10,11... | collective-permute-start | bytes 208904 | tf_op jit(solution)/shard_map/ppermute | solution.py:511
  20.0 7.9 %collective-permute-start.3 = (bf16[272,128]{1,0:T(8,128)(2,1)S(1)}, bf16[272,128]{1,0:T(8,128)(2,1)S(1)}, u32[]{:S(2)}, u32[]{:S(2)}) collective-permute-start(bf16[272,128]{1,0:T(8,128)(2,1)S(1)} %pair_gram.1.refs_0_), channel_id=1, source_target_pairs={{0,2},{1,3},{2,0},{3,1},{4,6},{5,7},{6,4},{7,5},{8,10},{9,11},{10,... | collective-permute-start | bytes 208904 | tf_op jit(solution)/shard_map/ppermute | solution.py:511
  22.6 6.2 %collective-permute-start.4 = (bf16[272,128]{1,0:T(8,128)(2,1)S(1)}, bf16[272,128]{1,0:T(8,128)(2,1)S(1)}, u32[]{:S(2)}, u32[]{:S(2)}) collective-permute-start(bf16[272,128]{1,0:T(8,128)(2,1)S(1)} %pair_gram.1.refs_0_), channel_id=1, source_target_pairs={{0,3},{1,2},{2,1},{3,0},{4,7},{5,6},{6,5},{7,4},{8,11},{9,10},{10,... | collective-permute-start | bytes 208904 | tf_op jit(solution)/shard_map/ppermute | solution.py:511
  35.3 8.3 %collective-permute-start.11 = (bf16[128,1280]{1,0:T(8,128)(2,1)S(1)}, bf16[128,1280]{1,0:T(8,128)(2,1)S(1)}, u32[]{:S(2)}, u32[]{:S(2)}) collective-permute-start(bf16[128,1280]{1,0:T(8,128)(2,1)S(1)} %get-tuple-element.29.own), channel_id=1, source_target_pairs={{0,8},{4,12},{8,0},{12,4},{16,24},{20,28},{24,16},{28,20},{1,9},{5... | collective-permute-start | bytes 983048 | tf_op jit(solution)/shard_map/ppermute | solution.py:511
  36.9 8.2 %collective-permute-start.12 = (bf16[128,1280]{1,0:T(8,128)(2,1)S(1)}, bf16[128,1280]{1,0:T(8,128)(2,1)S(1)}, u32[]{:S(2)}, u32[]{:S(2)}) collective-permute-start(bf16[128,1280]{1,0:T(8,128)(2,1)S(1)} %get-tuple-element.29.own), channel_id=1, source_target_pairs={{0,16},{4,20},{8,24},{12,28},{16,0},{20,4},{24,8},{28,12},{1,17},{... | collective-permute-start | bytes 983048 | tf_op jit(solution)/shard_map/ppermute | solution.py:511
  37.7 7.8 %collective-permute-start.6 = (bf16[256,128]{1,0:T(8,128)(2,1)S(1)}, bf16[256,128]{1,0:T(8,128)(2,1)S(1)}, u32[]{:S(2)}, u32[]{:S(2)}) collective-permute-start(bf16[256,128]{1,0:T(8,128)(2,1)S(1)} %ahead_gram.2), channel_id=1, source_target_pairs={{0,1},{1,0},{2,3},{3,2},{4,5},{5,4},{6,7},{7,6},{8,9},{9,8},{10,11... | collective-permute-start | bytes 196616 | tf_op jit(solution)/shard_map/ppermute | solution.py:511
  39.0 6.7 %collective-permute-start.7 = (bf16[256,128]{1,0:T(8,128)(2,1)S(1)}, bf16[256,128]{1,0:T(8,128)(2,1)S(1)}, u32[]{:S(2)}, u32[]{:S(2)}) collective-permute-start(bf16[256,128]{1,0:T(8,128)(2,1)S(1)} %ahead_gram.2), channel_id=1, source_target_pairs={{0,2},{1,3},{2,0},{3,1},{4,6},{5,7},{6,4},{7,5},{8,10},{9,11},{10,... | collective-permute-start | bytes 196616 | tf_op jit(solution)/shard_map/ppermute | solution.py:511
  40.6 6.2 %collective-permute-start.8 = (bf16[256,128]{1,0:T(8,128)(2,1)S(1)}, bf16[256,128]{1,0:T(8,128)(2,1)S(1)}, u32[]{:S(2)}, u32[]{:S(2)}) collective-permute-start(bf16[256,128]{1,0:T(8,128)(2,1)S(1)} %ahead_gram.2), channel_id=1, source_target_pairs={{0,3},{1,2},{2,1},{3,0},{4,7},{5,6},{6,5},{7,4},{8,11},{9,10},{10,... | collective-permute-start | bytes 196616 | tf_op jit(solution)/shard_map/ppermute | solution.py:511
  43.6 5.0 %collective-permute-start.10 = (bf16[128,512]{1,0:T(8,128)(2,1)S(1)}, bf16[128,512]{1,0:T(8,128)(2,1)S(1)}, u32[]{:S(2)}, u32[]{:S(2)}) collective-permute-start(bf16[128,512]{1,0:T(8,128)(2,1)S(1)} %get-tuple-element.26.refs_0_), channel_id=1, source_target_pairs={{0,8},{4,12},{8,0},{12,4},{16,24},{20,28},{24,16},{28,20},{1,9},{5... | collective-permute-start | bytes 393224 | tf_op jit(solution)/shard_map/ppermute | solution.py:511
  45.4 3.1 %collective-permute-start.13 = (bf16[256,128]{1,0:T(8,128)(2,1)S(1)}, bf16[256,128]{1,0:T(8,128)(2,1)S(1)}, u32[]{:S(2)}, u32[]{:S(2)}) collective-permute-start(bf16[256,128]{1,0:T(8,128)(2,1)S(1)} %ahead_gram.3.one), channel_id=1, source_target_pairs={{0,4},{4,0},{8,12},{12,8},{16,20},{20,16},{24,28},{28,24},{1,5},{5... | collective-permute-start | bytes 196616 | tf_op jit(solution)/shard_map/ppermute | solution.py:511
  46.9 6.7 %collective-permute-start.9 = (bf16[256,128]{1,0:T(8,128)(2,1)S(1)}, bf16[256,128]{1,0:T(8,128)(2,1)S(1)}, u32[]{:S(2)}, u32[]{:S(2)}) collective-permute-start(bf16[256,128]{1,0:T(8,128)(2,1)S(1)} %add_convert_fusion.1.refs_2_), channel_id=1, source_target_pairs={{0,4},{4,0},{8,12},{12,8},{16,20},{20,16},{24,28},{28,24},{1,5},{5... | collective-permute-start | bytes 196616 | tf_op jit(solution)/shard_map/ppermute | solution.py:511
  48.6 13.1 %collective-permute-start.14 = (bf16[256,128]{1,0:T(8,128)(2,1)S(1)}, bf16[256,128]{1,0:T(8,128)(2,1)S(1)}, u32[]{:S(2)}, u32[]{:S(2)}) collective-permute-start(bf16[256,128]{1,0:T(8,128)(2,1)S(1)} %add_after.1), channel_id=1, source_target_pairs={{0,1},{1,0},{2,3},{3,2},{4,5},{5,4},{6,7},{7,6},{8,9},{9,8},{10,11... | collective-permute-start | bytes 196616 | tf_op jit(solution)/shard_map/ppermute | solution.py:511
  51.1 10.6 %collective-permute-start.15 = (bf16[256,128]{1,0:T(8,128)(2,1)S(1)}, bf16[256,128]{1,0:T(8,128)(2,1)S(1)}, u32[]{:S(2)}, u32[]{:S(2)}) collective-permute-start(bf16[256,128]{1,0:T(8,128)(2,1)S(1)} %add_after.1), channel_id=1, source_target_pairs={{0,2},{1,3},{2,0},{3,1},{4,6},{5,7},{6,4},{7,5},{8,10},{9,11},{10,... | collective-permute-start | bytes 196616 | tf_op jit(solution)/shard_map/ppermute | solution.py:511
  51.7 9.9 %collective-permute-start.16 = (bf16[256,128]{1,0:T(8,128)(2,1)S(1)}, bf16[256,128]{1,0:T(8,128)(2,1)S(1)}, u32[]{:S(2)}, u32[]{:S(2)}) collective-permute-start(bf16[256,128]{1,0:T(8,128)(2,1)S(1)} %add_after.1), channel_id=1, source_target_pairs={{0,3},{1,2},{2,1},{3,0},{4,7},{5,6},{6,5},{7,4},{8,11},{9,10},{10,... | collective-permute-start | bytes 196616 | tf_op jit(solution)/shard_map/ppermute | solution.py:511
  60.1 5.0 %collective-permute-start.18 = (bf16[128,512]{1,0:T(8,128)(2,1)S(1)}, bf16[128,512]{1,0:T(8,128)(2,1)S(1)}, u32[]{:S(2)}, u32[]{:S(2)}) collective-permute-start(bf16[128,512]{1,0:T(8,128)(2,1)S(1)} %get-tuple-element.30), channel_id=1, source_target_pairs={{0,16},{4,20},{8,24},{12,28},{16,0},{20,4},{24,8},{28,12},{1,17},{... | collective-permute-start | bytes 393224 | tf_op jit(solution)/shard_map/ppermute | solution.py:511
  61.7 4.3 %collective-permute-start.17 = (bf16[256,128]{1,0:T(8,128)(2,1)S(1)}, bf16[256,128]{1,0:T(8,128)(2,1)S(1)}, u32[]{:S(2)}, u32[]{:S(2)}) collective-permute-start(bf16[256,128]{1,0:T(8,128)(2,1)S(1)} %add_convert_fusion.refs_2_), channel_id=1, source_target_pairs={{0,8},{4,12},{8,0},{12,4},{16,24},{20,28},{24,16},{28,20},{1,9},{5... | collective-permute-start | bytes 196616 | tf_op jit(solution)/shard_map/ppermute | solution.py:511
  66.1 7.3 %collective-permute-start.19 = (bf16[128,1280]{1,0:T(8,128)(2,1)S(1)}, bf16[128,1280]{1,0:T(8,128)(2,1)S(1)}, u32[]{:S(2)}, u32[]{:S(2)}) collective-permute-start(bf16[128,1280]{1,0:T(8,128)(2,1)S(1)} %hold.1.own), channel_id=1, source_target_pairs={{0,16},{4,20},{8,24},{12,28},{16,0},{20,4},{24,8},{28,12},{1,17},{... | collective-permute-start | bytes 983048 | tf_op jit(solution)/shard_map/ppermute | solution.py:511
  73.6 1.3 %collective-permute-start.20 = (f32[16,1280]{1,0:T(8,128)S(1)}, f32[16,1280]{1,0:T(8,128)S(1)}, u32[]{:S(2)}, u32[]{:S(2)}) collective-permute-start(f32[16,1280]{1,0:T(8,128)S(1)} %get-tuple-element.32), channel_id=1, source_target_pairs={{0,4},{4,0},{8,12},{12,8},{16,20},{20,16},{24,28},{28,24},{1,5},{5... | collective-permute-start | bytes 245768 | tf_op jit(solution)/shard_map/ppermute | solution.py:511
